TPU v7x, 128 devices: a whole 4x4x4 slice. The times are simulated.
128 devices in a mesh: ctx: 16 (over y, x_hi, core), wt: 8 (over x_lo, z).
Axes of the slice: x: 4 (x_hi: 2, x_lo: 2; x = x_hi * 2 + x_lo), y: 4, z: 4, core: 2. Of those that a mesh axis runs over, the one named last changes fastest.
Arguments:
- inputs: bfloat16 [8, 4096, 512], P('wt', 'ctx'), may hold values from -6 to 6
- lengths: int32 [8], P('wt'), may hold values from 1024 to 4096, as said below
- cotangent: bfloat16 [8, 4096, 512], P('wt', 'ctx'), may hold values from -6 to 6
- glu_gain: bfloat16 [512], P('wt'), may hold values from 0.5 to 1.5
- glu_value: bfloat16 [512, 512], P('wt'), may hold values from -0.25 to 0.25
- glu_gate: bfloat16 [512, 512], P('wt'), may hold values from -0.25 to 0.25
- conv_gain: bfloat16 [512], P('wt'), may hold values from 0.5 to 1.5
- wide_weight: bfloat16 [512, 2048], P('wt'), may hold values from -0.25 to 0.25
- narrow_weight: bfloat16 [3, 512, 256], P(None, 'wt'), may hold values from -0.15625 to 0.15625
- mid_gain: bfloat16 [2048], P('wt'), may hold values from 0.5 to 1.5
- depth_weight: bfloat16 [9, 2048], P(None, 'wt'), may hold values from -2 to 2
- point_weight: bfloat16 [2048, 256], P('wt'), may hold values from -0.125 to 0.125
- attn_gain: bfloat16 [512], P('wt'), may hold values from 0.5 to 1.5
- query_weight: bfloat16 [512, 512], P('wt'), may hold values from -0.5 to 0.5
- key_weight: bfloat16 [512, 512], P('wt'), may hold values from -0.25 to 0.25
- value_weight: bfloat16 [512, 512], P('wt'), may hold values from -0.25 to 0.25
- output_weight: bfloat16 [512, 512], P('wt'), may hold values from -1.5 to 1.5
- ffn_gain: bfloat16 [512], P('wt'), may hold values from 0.5 to 1.5
- ffn_in: bfloat16 [512, 2048], P('wt'), may hold values from -0.25 to 0.25
- ffn_out: bfloat16 [2048, 512], P('wt'), may hold values from -0.125 to 0.125
Outputs:
- output: bfloat16 [8, 4096, 512], P('wt', 'ctx')
- input_grad: float32 [8, 4096, 512], P('wt', 'ctx')
- grad_glu_gain: float32 [512], P('wt')
- grad_glu_value: float32 [512, 512], P('wt')
- grad_glu_gate: float32 [512, 512], P('wt')
- grad_conv_gain: float32 [512], P('wt')
- grad_wide_weight: float32 [512, 2048], P('wt')
- grad_narrow_weight: float32 [3, 512, 256], P(None, 'wt')
- grad_mid_gain: float32 [2048], P('wt')
- grad_depth_weight: float32 [9, 2048], P(None, 'wt')
- grad_point_weight: float32 [2048, 256], P('wt')
- grad_attn_gain: float32 [512], P('wt')
- grad_query_weight: float32 [512, 512], P('wt')
- grad_key_weight: float32 [512, 512], P('wt')
- grad_value_weight: float32 [512, 512], P('wt')
- grad_output_weight: float32 [512, 512], P('wt')
- grad_ffn_gain: float32 [512], P('wt')
- grad_ffn_in: float32 [512, 2048], P('wt')
- grad_ffn_out: float32 [2048, 512], P('wt')
Inputs may be any that keep to these rules, and one draw needn't show every extreme that they name: `lengths`: valid slots of each sequence, which are its first slots; one sequence has exactly 4096 and one exactly 1024.
All inputs are finite; a program needn't handle non-finite values.
Results may differ from a plain program's by a relative error of at most 0.03.
Values may be sent and summed in bfloat16 or wider, within the bound.
No kernel may reach another device: no remote copies, remote signals or barrier semaphores. Data moves between devices by JAX's collectives and lax.ppermute only.
A program may use at most 256 MiB of HBM per device.

v0:
```python
import jax
import jax.numpy as jnp
from jax import lax
from jax.sharding import PartitionSpec as P

HEADS = 8
HEAD = 64


EPSILON = 1e-06


def with_halo(block, sides, width):
    for axis, dim in sides:
        count = lax.axis_size(axis)
        forward = [(i, i + 1) for i in range(count - 1)]
        backward = [(target, source) for source, target in forward]
        low = lax.ppermute(
            lax.slice_in_dim(block, block.shape[dim] - width, None, axis=dim), axis, forward
        )
        high = lax.ppermute(lax.slice_in_dim(block, 0, width, axis=dim), axis, backward)
        block = jnp.concatenate([low, block, high], axis=dim)
    return block


def matmul(left, right):
    return jnp.dot(left, right, preferred_element_type=jnp.float32)


def inner_rows(left, right):
    return lax.dot_general(
        left, right, (((0,), (0,)), ((), ())), preferred_element_type=jnp.float32
    )


def outer_cols(left, right):
    return lax.dot_general(
        left, right, (((1,), (1,)), ((), ())), preferred_element_type=jnp.float32
    )


def smooth_unit(value):
    return value * jax.nn.sigmoid(value)


def smooth_slope(value):
    sigma = jax.nn.sigmoid(value)
    return sigma * (1.0 + value * (1.0 - sigma))


def layer_norm(value, gain):
    average = jnp.mean(value, -1, keepdims=True)
    centred = value - average
    scale = lax.rsqrt(jnp.mean(centred * centred, -1, keepdims=True) + EPSILON)
    normal = centred * scale
    return (normal * gain.astype(jnp.float32), normal, scale)


def norm_back(incoming, normal, scale, gain):
    scaled = incoming * gain.astype(jnp.float32)
    gain_grad = jnp.sum(incoming * normal, 0)
    value_grad = scale * (
        scaled
        - jnp.mean(scaled, -1, keepdims=True)
        - normal * jnp.mean(scaled * normal, -1, keepdims=True)
    )
    return (value_grad, gain_grad)


def edges_forward(values, reach):
    return with_halo(values, (("ctx", 0),), reach)


def edges_backward(values, reach):
    return with_halo(values, (("ctx", 0),), reach)


def head_scores(queries, keys, key_valid, factor):
    logits = outer_cols(queries, keys) * factor
    return jnp.where(key_valid[None, :], logits, -1e30)


def shards(
    inputs,
    lengths,
    cotangent,
    glu_gain,
    glu_value,
    glu_gate,
    conv_gain,
    wide_weight,
    narrow_weight,
    mid_gain,
    depth_weight,
    point_weight,
    attn_gain,
    query_weight,
    key_weight,
    value_weight,
    output_weight,
    ffn_gain,
    ffn_in,
    ffn_out,
):
    rows = inputs.shape[1]
    width = inputs.shape[2]
    half = narrow_weight.shape[2]
    units = wide_weight.shape[1]
    total_rows = rows * lax.axis_size("ctx")
    factor = HEAD ** (-0.5)
    positions = lax.axis_index("ctx") * rows + jnp.arange(rows, dtype=jnp.int32)
    local_valid = positions < lengths[0]
    valid = local_valid.astype(jnp.float32)[:, None]
    key_valid = jnp.arange(total_rows, dtype=jnp.int32) < lengths[0]
    hidden = inputs[0].astype(jnp.float32)
    g_glu, w_val, w_gat = (
        lax.all_gather(glu_gain, "wt", axis=0, tiled=True),
        lax.all_gather(glu_value, "wt", axis=0, tiled=True),
        lax.all_gather(glu_gate, "wt", axis=0, tiled=True),
    )
    normed, glu_hat, glu_scale = layer_norm(hidden, g_glu)
    glu_in = normed.astype(jnp.bfloat16)
    value_part = matmul(glu_in, w_val)
    gate_part = matmul(glu_in, w_gat)
    sigma = jax.nn.sigmoid(gate_part)
    after_glu = hidden + value_part * sigma
    g_conv, w_wid, w_nar, g_mid, w_dep, w_pnt = (
        lax.all_gather(conv_gain, "wt", axis=0, tiled=True),
        lax.all_gather(wide_weight, "wt", axis=0, tiled=True),
        lax.all_gather(narrow_weight, "wt", axis=1, tiled=True),
        lax.all_gather(mid_gain, "wt", axis=0, tiled=True),
        lax.all_gather(depth_weight, "wt", axis=1, tiled=True),
        lax.all_gather(point_weight, "wt", axis=0, tiled=True),
    )
    normed, conv_hat, conv_scale = layer_norm(after_glu, g_conv)
    conv_in = (normed * valid).astype(jnp.bfloat16)
    wide_pre = matmul(conv_in, w_wid)
    conv_rim = edges_forward(conv_in, 1)
    stacked = jnp.concatenate(
        [conv_rim[0:rows], conv_rim[1 : rows + 1], conv_rim[2 : rows + 2]], axis=1
    )
    narrow_pre = matmul(stacked, w_nar.reshape(3 * width, half))
    mixed = smooth_unit(wide_pre) + jnp.pad(smooth_unit(narrow_pre), ((0, 0), (0, units - half)))
    normed, mid_hat, mid_scale = layer_norm(mixed, g_mid)
    mid_in = (normed * valid).astype(jnp.bfloat16)
    mid_rim = edges_forward(mid_in, 4)
    depth_float = w_dep.astype(jnp.float32)
    spread = sum(
        (mid_rim[tap : tap + rows].astype(jnp.float32) * depth_float[tap] for tap in range(9))
    )
    spread_in = spread.astype(jnp.bfloat16)
    separable = matmul(spread_in, w_pnt)
    after_conv = after_glu + jnp.pad(separable, ((0, 0), (0, width - half)))
    g_att, w_qry, w_key, w_vls, w_outp = (
        lax.all_gather(attn_gain, "wt", axis=0, tiled=True),
        lax.all_gather(query_weight, "wt", axis=0, tiled=True),
        lax.all_gather(key_weight, "wt", axis=0, tiled=True),
        lax.all_gather(value_weight, "wt", axis=0, tiled=True),
        lax.all_gather(output_weight, "wt", axis=0, tiled=True),
    )
    normed, attn_hat, attn_scale = layer_norm(after_conv, g_att)
    attn_in = normed.astype(jnp.bfloat16)
    queries = matmul(attn_in, w_qry).astype(jnp.bfloat16)
    keys_local = matmul(attn_in, w_key).astype(jnp.bfloat16)
    values_local = matmul(attn_in, w_vls).astype(jnp.bfloat16)
    keys_all, values_all = (
        lax.all_gather(keys_local, "ctx", axis=0, tiled=True),
        lax.all_gather(values_local, "ctx", axis=0, tiled=True),
    )
    head_outs = []
    head_lse = []
    for head_index in range(HEADS):
        cols = slice(head_index * HEAD, (head_index + 1) * HEAD)
        logits = head_scores(queries[:, cols], keys_all[:, cols], key_valid, factor)
        highest = jnp.max(logits, -1, keepdims=True)
        expo = jnp.exp(logits - highest)
        totals = jnp.sum(expo, -1, keepdims=True)
        probs = (expo / totals).astype(jnp.bfloat16)
        head_outs.append(matmul(probs, values_all[:, cols]))
        head_lse.append(highest + jnp.log(totals))
    heads_in = jnp.concatenate(head_outs, 1).astype(jnp.bfloat16)
    after_attn = after_conv + matmul(heads_in, w_outp)
    g_ffn, w_upper, w_lower = (
        lax.all_gather(ffn_gain, "wt", axis=0, tiled=True),
        lax.all_gather(ffn_in, "wt", axis=0, tiled=True),
        lax.all_gather(ffn_out, "wt", axis=0, tiled=True),
    )
    normed, ffn_hat, ffn_scale = layer_norm(after_attn, g_ffn)
    ffn_input = normed.astype(jnp.bfloat16)
    ffn_pre = matmul(ffn_input, w_upper)
    activated = smooth_unit(ffn_pre).astype(jnp.bfloat16)
    result = (after_attn + matmul(activated, w_lower)) * valid
    grad = cotangent[0].astype(jnp.float32) * valid
    grad_low = grad.astype(jnp.bfloat16)
    d_lower = inner_rows(activated, grad_low)
    d_pre = (outer_cols(grad_low, w_lower) * smooth_slope(ffn_pre)).astype(jnp.bfloat16)
    d_upper = inner_rows(ffn_input, d_pre)
    back, d_gffn = norm_back(outer_cols(d_pre, w_upper), ffn_hat, ffn_scale, g_ffn)
    grad = grad + back
    s_gffn, s_upper, s_lower = (
        lax.psum_scatter(d_gffn.astype(jnp.bfloat16), "wt", scatter_dimension=0, tiled=True).astype(
            jnp.float32
        ),
        lax.psum_scatter(
            d_upper.astype(jnp.bfloat16), "wt", scatter_dimension=0, tiled=True
        ).astype(jnp.float32),
        lax.psum_scatter(
            d_lower.astype(jnp.bfloat16), "wt", scatter_dimension=0, tiled=True
        ).astype(jnp.float32),
    )
    grad_low = grad.astype(jnp.bfloat16)
    d_outp = inner_rows(heads_in, grad_low)
    d_heads = outer_cols(grad_low, w_outp).astype(jnp.bfloat16)
    keys_back, values_back = (
        lax.all_gather(keys_local, "ctx", axis=0, tiled=True),
        lax.all_gather(values_local, "ctx", axis=0, tiled=True),
    )
    query_grads = []
    key_grads = []
    value_grads = []
    row_sums = []
    for head_index in range(HEADS):
        cols = slice(head_index * HEAD, (head_index + 1) * HEAD)
        logits = head_scores(queries[:, cols], keys_back[:, cols], key_valid, factor)
        probs_full = jnp.exp(logits - head_lse[head_index])
        d_probs = outer_cols(d_heads[:, cols], values_back[:, cols])
        row_total = jnp.sum(probs_full * d_probs, -1, keepdims=True)
        row_sums.append(row_total)
        d_scores = (probs_full * (d_probs - row_total)).astype(jnp.bfloat16)
        query_grads.append(matmul(d_scores, keys_back[:, cols]) * factor)
        probs = probs_full.astype(jnp.bfloat16)
        key_grads.append(inner_rows(d_scores, queries[:, cols]) * factor)
        value_grads.append(inner_rows(probs, d_heads[:, cols]))
    d_keys, d_values = (
        lax.psum_scatter(
            jnp.concatenate(key_grads, 1).astype(jnp.bfloat16),
            "ctx",
            scatter_dimension=0,
            tiled=True,
        ).astype(jnp.float32),
        lax.psum_scatter(
            jnp.concatenate(value_grads, 1).astype(jnp.bfloat16),
            "ctx",
            scatter_dimension=0,
            tiled=True,
        ).astype(jnp.float32),
    )
    dq_low = jnp.concatenate(query_grads, 1).astype(jnp.bfloat16)
    dk_low = d_keys.astype(jnp.bfloat16)
    dv_low = d_values.astype(jnp.bfloat16)
    d_qry = inner_rows(attn_in, dq_low)
    d_key = inner_rows(attn_in, dk_low)
    d_vls = inner_rows(attn_in, dv_low)
    d_norm = outer_cols(dq_low, w_qry) + outer_cols(dk_low, w_key) + outer_cols(dv_low, w_vls)
    back, d_gatt = norm_back(d_norm, attn_hat, attn_scale, g_att)
    grad = grad + back
    s_gatt, s_qry, s_key, s_vls, s_outp = (
        lax.psum_scatter(d_gatt.astype(jnp.bfloat16), "wt", scatter_dimension=0, tiled=True).astype(
            jnp.float32
        ),
        lax.psum_scatter(d_qry.astype(jnp.bfloat16), "wt", scatter_dimension=0, tiled=True).astype(
            jnp.float32
        ),
        lax.psum_scatter(d_key.astype(jnp.bfloat16), "wt", scatter_dimension=0, tiled=True).astype(
            jnp.float32
        ),
        lax.psum_scatter(d_vls.astype(jnp.bfloat16), "wt", scatter_dimension=0, tiled=True).astype(
            jnp.float32
        ),
        lax.psum_scatter(d_outp.astype(jnp.bfloat16), "wt", scatter_dimension=0, tiled=True).astype(
            jnp.float32
        ),
    )
    sep_grad = grad[:, :half].astype(jnp.bfloat16)
    d_pnt = inner_rows(spread_in, sep_grad)
    d_spread = outer_cols(sep_grad, w_pnt).astype(jnp.bfloat16)
    spread_float = d_spread.astype(jnp.float32)
    d_dep = jnp.stack(
        [
            jnp.sum(mid_rim[tap : tap + rows].astype(jnp.float32) * spread_float, 0)
            for tap in range(9)
        ]
    )
    spread_rim = edges_backward(d_spread, 4)
    d_mid = sum(
        (
            spread_rim[8 - tap : 8 - tap + rows].astype(jnp.float32) * depth_float[tap]
            for tap in range(9)
        )
    )
    back_mid, d_gmid = norm_back(d_mid * valid, mid_hat, mid_scale, g_mid)
    d_wide_pre = (back_mid * smooth_slope(wide_pre)).astype(jnp.bfloat16)
    d_nar_pre = (back_mid[:, :half] * smooth_slope(narrow_pre)).astype(jnp.bfloat16)
    d_wid = inner_rows(conv_in, d_wide_pre)
    d_nar = inner_rows(stacked, d_nar_pre).reshape(3, width, half)
    nar_rim = edges_backward(d_nar_pre, 1)
    back_stack = jnp.concatenate(
        [nar_rim[2 : rows + 2], nar_rim[1 : rows + 1], nar_rim[0:rows]], axis=1
    )
    d_conv = outer_cols(d_wide_pre, w_wid) + outer_cols(
        back_stack, w_nar.transpose(1, 0, 2).reshape(width, 3 * half)
    )
    back, d_gconv = norm_back(d_conv * valid, conv_hat, conv_scale, g_conv)
    grad = grad + back
    s_gconv, s_wid, s_nar, s_gmid, s_dep, s_pnt = (
        lax.psum_scatter(
            d_gconv.astype(jnp.bfloat16), "wt", scatter_dimension=0, tiled=True
        ).astype(jnp.float32),
        lax.psum_scatter(d_wid.astype(jnp.bfloat16), "wt", scatter_dimension=0, tiled=True).astype(
            jnp.float32
        ),
        lax.psum_scatter(d_nar.astype(jnp.bfloat16), "wt", scatter_dimension=1, tiled=True).astype(
            jnp.float32
        ),
        lax.psum_scatter(d_gmid.astype(jnp.bfloat16), "wt", scatter_dimension=0, tiled=True).astype(
            jnp.float32
        ),
        lax.psum_scatter(d_dep.astype(jnp.bfloat16), "wt", scatter_dimension=1, tiled=True).astype(
            jnp.float32
        ),
        lax.psum_scatter(d_pnt.astype(jnp.bfloat16), "wt", scatter_dimension=0, tiled=True).astype(
            jnp.float32
        ),
    )
    d_value = (grad * sigma).astype(jnp.bfloat16)
    d_gate = (grad * value_part * sigma * (1.0 - sigma)).astype(jnp.bfloat16)
    d_wval = inner_rows(glu_in, d_value)
    d_wgat = inner_rows(glu_in, d_gate)
    d_norm = outer_cols(d_value, w_val) + outer_cols(d_gate, w_gat)
    back, d_gglu = norm_back(d_norm, glu_hat, glu_scale, g_glu)
    grad = grad + back
    s_gglu, s_wval, s_wgat = (
        lax.psum_scatter(d_gglu.astype(jnp.bfloat16), "wt", scatter_dimension=0, tiled=True).astype(
            jnp.float32
        ),
        lax.psum_scatter(d_wval.astype(jnp.bfloat16), "wt", scatter_dimension=0, tiled=True).astype(
            jnp.float32
        ),
        lax.psum_scatter(d_wgat.astype(jnp.bfloat16), "wt", scatter_dimension=0, tiled=True).astype(
            jnp.float32
        ),
    )
    summed = (
        lax.psum(s_gglu.astype(jnp.bfloat16), "ctx").astype(jnp.float32),
        lax.psum(s_wval.astype(jnp.bfloat16), "ctx").astype(jnp.float32),
        lax.psum(s_wgat.astype(jnp.bfloat16), "ctx").astype(jnp.float32),
        lax.psum(s_gconv.astype(jnp.bfloat16), "ctx").astype(jnp.float32),
        lax.psum(s_wid.astype(jnp.bfloat16), "ctx").astype(jnp.float32),
        lax.psum(s_nar.astype(jnp.bfloat16), "ctx").astype(jnp.float32),
        lax.psum(s_gmid.astype(jnp.bfloat16), "ctx").astype(jnp.float32),
        lax.psum(s_dep.astype(jnp.bfloat16), "ctx").astype(jnp.float32),
        lax.psum(s_pnt.astype(jnp.bfloat16), "ctx").astype(jnp.float32),
        lax.psum(s_gatt.astype(jnp.bfloat16), "ctx").astype(jnp.float32),
        lax.psum(s_qry.astype(jnp.bfloat16), "ctx").astype(jnp.float32),
        lax.psum(s_key.astype(jnp.bfloat16), "ctx").astype(jnp.float32),
        lax.psum(s_vls.astype(jnp.bfloat16), "ctx").astype(jnp.float32),
        lax.psum(s_outp.astype(jnp.bfloat16), "ctx").astype(jnp.float32),
        lax.psum(s_gffn.astype(jnp.bfloat16), "ctx").astype(jnp.float32),
        lax.psum(s_upper.astype(jnp.bfloat16), "ctx").astype(jnp.float32),
        lax.psum(s_lower.astype(jnp.bfloat16), "ctx").astype(jnp.float32),
    )
    return (result.astype(jnp.bfloat16)[None], grad[None]) + tuple(summed)


def solution(mesh):
    return jax.shard_map(
        shards,
        mesh=mesh,
        in_specs=(
            P("wt", "ctx", None),
            P("wt"),
            P("wt", "ctx", None),
            P("wt"),
            P("wt", None),
            P("wt", None),
            P("wt"),
            P("wt", None),
            P(None, "wt", None),
            P("wt"),
            P(None, "wt"),
            P("wt", None),
            P("wt"),
            P("wt", None),
            P("wt", None),
            P("wt", None),
            P("wt", None),
            P("wt"),
            P("wt", None),
            P("wt", None),
        ),
        out_specs=(
            P("wt", "ctx", None),
            P("wt", "ctx", None),
            P("wt"),
            P("wt", None),
            P("wt", None),
            P("wt"),
            P("wt", None),
            P(None, "wt", None),
            P("wt"),
            P(None, "wt"),
            P("wt", None),
            P("wt"),
            P("wt", None),
            P("wt", None),
            P("wt", None),
            P("wt", None),
            P("wt"),
            P("wt", None),
            P("wt", None),
        ),
        check_vma=False,
    )
```

profile of v0, /device:TPU:1, one launch (start us, length us, event | category | flops | bytes accessed | tf_op | source)
XLA Modules:
  0.0 1289.0 jit_solution(4152932484720257702)
XLA Ops:
  14.0 18.5 %all-reduce.14 = (bf16[512]{0:T(512)(128)(2,1)S(1)}, bf16[512]{0:T(512)(128)(2,1)S(1)}, bf16[512]{0:T(512)(128)(2,1)S(1)}, bf16[512]{0:T(512)(128)(2,1)S(1)}) all-reduce(bf16[512]{0:T(512)(128)(2,1)S(1)} %dynamic-update-slice, bf16[512]{0:T(512)(128)(2,1)S(1)} %dynamic-update-slice.1, ...), channel_id=1, replica_groups=mesh['ctx'=16,'wt'=8] {'wt'}, use_global_device_ids=true, to_apply=%add.2 | all-reduce | flops 2048 | bytes 8192
  34.9 25.5 %all_gather.60 = bf16[512,512]{1,0:T(8,128)(2,1)S(1)} all-gather(bf16[64,512]{1,0:T(8,128)(2,1)} %param.24), channel_id=1, replica_groups=mesh['ctx'=16,'wt'=8] {'wt'}, dimensions={0}, use_global_device_ids=true | all-gather | bytes 589824 | tf_op jit(solution)/shard_map/all_gather | solution.py:118
  60.4 23.3 %all_gather.61 = bf16[512,512]{1,0:T(8,128)(2,1)S(1)} all-gather(bf16[64,512]{1,0:T(8,128)(2,1)} %param.25), channel_id=1, replica_groups=mesh['ctx'=16,'wt'=8] {'wt'}, dimensions={0}, use_global_device_ids=true | all-gather | bytes 589824 | tf_op jit(solution)/shard_map/all_gather | solution.py:119
  87.6 18.3 %collective-permute-start = (bf16[1,512]{1,0:T(2,128)(2,1)S(1)}, bf16[1,512]{1,0:T(2,128)(2,1)S(1)}, u32[]{:S(2)}, u32[]{:S(2)}) collective-permute-start(bf16[1,512]{1,0:T(2,128)(2,1)S(1)} %get-tuple-element.88), channel_id=1, source_target_pairs={{0,8},{8,16},{16,24},{24,32},{32,40},{40,48},{48,56},{56,64},{64,7... | collective-permute-start | bytes 3080 | tf_op jit(solution)/shard_map/ppermute | solution.py:18
  107.9 22.6 %all_gather.66 = bf16[9,2048]{1,0:T(8,128)(2,1)S(1)} all-gather(bf16[9,256]{1,0:T(8,128)(2,1)S(1)} %copy-done.142), channel_id=1, replica_groups=mesh['ctx'=16,'wt'=8] {'wt'}, dimensions={1}, use_global_device_ids=true | all-gather | bytes 41472 | tf_op jit(solution)/shard_map/all_gather | solution.py:132
  130.7 24.7 %all_gather.64 = bf16[3,512,256]{2,1,0:T(8,128)(2,1)S(1)} all-gather(bf16[3,64,256]{2,1,0:T(8,128)(2,1)S(1)} %copy-done.98), channel_id=1, replica_groups=mesh['ctx'=16,'wt'=8] {'wt'}, dimensions={1}, use_global_device_ids=true | all-gather | bytes 884736 | tf_op jit(solution)/shard_map/all_gather | solution.py:130
  155.4 12.0 all-gather
  168.5 3.8 fusion.267
  173.6 19.7 %collective-permute-start.2 = (bf16[4,2048]{1,0:T(4,128)(2,1)S(1)}, bf16[4,2048]{1,0:T(4,128)(2,1)S(1)}, u32[]{:S(2)}, u32[]{:S(2)}) collective-permute-start(bf16[4,2048]{1,0:T(4,128)(2,1)S(1)} %get-tuple-element.86), channel_id=1, source_target_pairs={{0,8},{8,16},{16,24},{24,32},{32,40},{40,48},{48,56},{56,64},{64,7... | collective-permute-start | bytes 49160 | tf_op jit(solution)/shard_map/ppermute | solution.py:18
  195.3 23.1 %all_gather.70 = bf16[512,512]{1,0:T(8,128)(2,1)S(1)} all-gather(bf16[64,512]{1,0:T(8,128)(2,1)S(1)} %copy-done.117), channel_id=1, replica_groups=mesh['ctx'=16,'wt'=8] {'wt'}, dimensions={0}, use_global_device_ids=true | all-gather | bytes 589824 | tf_op jit(solution)/shard_map/all_gather | solution.py:157
  218.5 2.8 fusion.57
  225.0 23.5 %all_gather.72 = bf16[512,512]{1,0:T(8,128)(2,1)S(1)} all-gather(bf16[64,512]{1,0:T(8,128)(2,1)S(1)} %copy-done.118), channel_id=1, replica_groups=mesh['ctx'=16,'wt'=8] {'wt'}, dimensions={0}, use_global_device_ids=true | all-gather | bytes 589824 | tf_op jit(solution)/shard_map/all_gather | solution.py:158
  250.8 25.2 %all_gather.69 = bf16[512,512]{1,0:T(8,128)(2,1)S(1)} all-gather(bf16[64,512]{1,0:T(8,128)(2,1)S(1)} %copy-done.119), channel_id=1, replica_groups=mesh['ctx'=16,'wt'=8] {'wt'}, dimensions={0}, use_global_device_ids=true | all-gather | bytes 589824 | tf_op jit(solution)/shard_map/all_gather | solution.py:156
  276.0 23.0 %all_gather.74 = bf16[512,512]{1,0:T(8,128)(2,1)S(1)} all-gather(bf16[64,512]{1,0:T(8,128)(2,1)S(1)} %copy-done.120), channel_id=1, replica_groups=mesh['ctx'=16,'wt'=8] {'wt'}, dimensions={0}, use_global_device_ids=true | all-gather | bytes 589824 | tf_op jit(solution)/shard_map/all_gather | solution.py:159
  334.5 9.0 all-gather.14.cloned.1.call-done
  343.5 3.6 fusion.128
  364.1 14.9 %all-gather.16.cloned.1.call-done = bf16[512,2048]{1,0:T(8,128)(2,1)} async-done(((bf16[64,2048]{1,0:T(8,128)(2,1)}), bf16[512,2048]{1,0:T(8,128)(2,1)}) %all-gather.16.cloned.1.call-update) | async-done | bytes 2097168 | tf_op jit(solution)/shard_map/all_gather | solution.py:185
  379.0 3.7 fusion.259
  382.7 38.6 %all-gather.18.cloned.1.call-done = bf16[2048,512]{1,0:T(8,128)(2,1)} async-done(((bf16[256,512]{1,0:T(8,128)(2,1)}), bf16[2048,512]{1,0:T(8,128)(2,1)}) %all-gather.18.cloned.1.call-update) | async-done | bytes 2097168 | tf_op jit(solution)/shard_map/all_gather | solution.py:186
  421.3 3.4 fusion.48
  451.3 3.2 multiply_reduce_fusion.6
  465.7 4.0 fusion.31
  488.9 2.9 fusion.105
  491.9 3.5 fusion.107
  505.8 3.8 convolution_convert_fusion.8
  516.8 32.5 %reduce-scatter.15.cloned.1.call-done = bf16[256,512]{0,1:T(8,128)(2,1)} async-done(((bf16[4096,512]{0,1:T(8,128)(2,1)}), bf16[256,512]{0,1:T(8,128)(2,1)}) %reduce-scatter.15.cloned.1.call-update) | async-done | bytes 262160 | tf_op jit(solution)/shard_map/reduce_scatter | solution.py:235
  550.8 82.4 %reduce-scatter.17.cloned.1.call-done = bf16[256,512]{0,1:T(8,128)(2,1)} async-done(((bf16[4096,512]{0,1:T(8,128)(2,1)}), bf16[256,512]{0,1:T(8,128)(2,1)}) %reduce-scatter.17.cloned.1.call-update) | async-done | bytes 262160 | tf_op jit(solution)/shard_map/reduce_scatter | solution.py:241
  637.1 11.4 fusion.80
  649.5 4.0 collective-permute-start.4
  653.5 3.3 collective-permute-start.5
  658.3 12.4 multiply_reduce_fusion.8
  674.4 5.2 collective-permute-start.7
  689.3 3.4 convolution_convert_fusion.10
  696.3 11.4 reduce-scatter.31.cloned.1.call-done
  707.7 43.9 %reduce-scatter.41.cloned.1.call-done = bf16[256,512]{1,0:T(8,128)(2,1)} async-done(((bf16[2048,512]{1,0:T(8,128)(2,1)}), bf16[256,512]{1,0:T(8,128)(2,1)}) %reduce-scatter.41.cloned.1.call-update) | async-done | bytes 262160 | tf_op jit(solution)/shard_map/reduce_scatter | solution.py:207
  751.6 43.7 %reduce-scatter.39.cloned.1.call-done = bf16[64,2048]{1,0:T(8,128)(2,1)} async-done(((bf16[512,2048]{1,0:T(8,128)(2,1)}), bf16[64,2048]{1,0:T(8,128)(2,1)}) %reduce-scatter.39.cloned.1.call-update) | async-done | bytes 262160 | tf_op jit(solution)/shard_map/reduce_scatter | solution.py:204
  795.3 39.0 %reduce-scatter.35.cloned.1.call-done = bf16[64,512]{1,0:T(8,128)(2,1)} async-done(((bf16[512,512]{1,0:T(8,128)(2,1)}), bf16[64,512]{1,0:T(8,128)(2,1)}) %reduce-scatter.35.cloned.1.call-update) | async-done | bytes 65552 | tf_op jit(solution)/shard_map/reduce_scatter | solution.py:267
  834.3 39.5 %reduce-scatter.33.cloned.1.call-done = bf16[64,512]{1,0:T(8,128)(2,1)} async-done(((bf16[512,512]{1,0:T(8,128)(2,1)}), bf16[64,512]{1,0:T(8,128)(2,1)}) %reduce-scatter.33.cloned.1.call-update) | async-done | bytes 65552 | tf_op jit(solution)/shard_map/reduce_scatter | solution.py:264
  873.8 39.4 %reduce-scatter.21.cloned.1.call-done = bf16[64,512]{1,0:T(8,128)(2,1)} async-done(((bf16[512,512]{1,0:T(8,128)(2,1)}), bf16[64,512]{1,0:T(8,128)(2,1)}) %reduce-scatter.21.cloned.1.call-update) | async-done | bytes 65552 | tf_op jit(solution)/shard_map/reduce_scatter | solution.py:339
  913.3 39.6 %reduce-scatter.19.cloned.1.call-done = bf16[64,512]{1,0:T(8,128)(2,1)} async-done(((bf16[512,512]{1,0:T(8,128)(2,1)}), bf16[64,512]{1,0:T(8,128)(2,1)}) %reduce-scatter.19.cloned.1.call-update) | async-done | bytes 65552 | tf_op jit(solution)/shard_map/reduce_scatter | solution.py:336
  952.8 39.4 %reduce-scatter.25.cloned.1.call-done = bf16[3,64,256]{2,1,0:T(8,128)(2,1)} async-done(((bf16[3,512,256]{2,1,0:T(8,128)(2,1)}), bf16[3,64,256]{2,1,0:T(8,128)(2,1)}) %reduce-scatter.25.cloned.1.call-update) | async-done | bytes 98320 | tf_op jit(solution)/shard_map/reduce_scatter | solution.py:312
  992.3 40.6 %reduce-scatter.29.cloned.1.call-done = bf16[256,256]{1,0:T(8,128)(2,1)} async-done(((bf16[2048,256]{1,0:T(8,128)(2,1)}), bf16[256,256]{1,0:T(8,128)(2,1)}) %reduce-scatter.29.cloned.1.call-update) | async-done | bytes 131088 | tf_op jit(solution)/shard_map/reduce_scatter | solution.py:321
  1032.9 43.7 %reduce-scatter.23.cloned.1.call-done = bf16[64,2048]{1,0:T(8,128)(2,1)} async-done(((bf16[512,2048]{1,0:T(8,128)(2,1)}), bf16[64,2048]{1,0:T(8,128)(2,1)}) %reduce-scatter.23.cloned.1.call-update) | async-done | bytes 262160 | tf_op jit(solution)/shard_map/reduce_scatter | solution.py:309
  1076.6 3.8 fusion.103
  1081.3 14.8 %all-reduce.13 = (bf16[512]{0:T(512)(128)(2,1)S(1)}, bf16[512]{0:T(512)(128)(2,1)S(1)}, bf16[2048]{0:T(1024)(128)(2,1)S(1)}, bf16[512]{0:T(512)(128)(2,1)S(1)}, bf16[512]{0:T(512)(128)(2,1)S(1)}) all-reduce(bf16[512]{0:T(512)(128)(2,1)S(1)} %get-tuple-element.41, ...), channel_id=4, replica_groups=mesh['ctx'=16,'wt'=8] {'wt'}, use_global_device_ids=true, to_apply=%region_47.48.clone | all-reduce | flops 4096 | bytes 16384
  1097.5 17.5 %reduce-scatter.27.cloned.1.call-done = bf16[9,256]{1,0:T(8,128)(2,1)} async-done(((bf16[9,2048]{1,0:T(8,128)(2,1)}), bf16[9,256]{1,0:T(8,128)(2,1)}) %reduce-scatter.27.cloned.1.call-update) | async-done | bytes 4624 | tf_op jit(solution)/shard_map/reduce_scatter | solution.py:318
  1115.0 65.3 %all-reduce.11 = (bf16[64]{0:T(256)(128)(2,1)S(1)}, bf16[64]{0:T(256)(128)(2,1)S(1)}, bf16[256]{0:T(256)(128)(2,1)S(1)}, bf16[9,256]{1,0:T(8,128)(2,1)S(1)}, bf1...) all-reduce(bf16[64]{0:T(256)(128)(2,1)S(1)} %dynamic-slice.5, ...), channel_id=1, replica_groups=mesh['ctx'=16,'wt'=8] {'ctx'}, use_global_device_ids=true, to_apply=%region_48.49 | all-reduce | flops 2816 | bytes 11264 | tf_op jit(solution)/shard_map/psum | solution.py:344
  1183.5 82.7 %all-reduce.17.cloned.1.call-done = (bf16[64,512]{1,0:T(8,128)(2,1)}, bf16[64,512]{1,0:T(8,128)(2,1)}, bf16[64,2048]{1,0:T(8,128)(2,1)}, bf16[3,64,256]{2,1,0:T(...) async-done(((bf16[64,512]{1,0:T(8,128)(2,1)}, ...) | async-done | bytes 1409040 | tf_op jit(solution)/shard_map/psum | solution.py:345
  (559 shorter events, 194.2 us)
Async XLA Ops:
  7.2 161.3 %all-gather.8.cloned.1.call-start = ((), (), s32[]{:S(2)}) async-start(), calls=%async_computation.14 | async-start | bytes 2359296 | tf_op jit(solution)/shard_map/all_gather | solution.py:129
  7.9 213.4 %all-gather.10.cloned.1.call-start = ((), (), s32[]{:S(2)}) async-start(), calls=%async_computation.15 | async-start | bytes 1179648 | tf_op jit(solution)/shard_map/all_gather | solution.py:133
  32.5 53.3 %copy-start.121 = (f32[512]{0:T(512)}, f32[512]{0:T(512)S(1)}, u32[]{:S(2)}) copy-start(f32[512]{0:T(512)S(1)} %convert_element_type.390) | copy-start | bytes 6148
  32.5 54.8 %copy-start.127 = (f32[512]{0:T(512)}, f32[512]{0:T(512)S(1)}, u32[]{:S(2)}) copy-start(f32[512]{0:T(512)S(1)} %convert_element_type.392) | copy-start | bytes 6148
  33.7 52.2 %copy-start.125 = (f32[256]{0:T(256)}, f32[256]{0:T(256)S(1)}, u32[]{:S(2)}) copy-start(f32[256]{0:T(256)S(1)} %broadcast_multiply_fusion.14) | copy-start | bytes 3076
  87.1 136.2 %copy-start.47 = (f32[256,512]{1,0:T(8,128)}, f32[256,512]{1,0:T(8,128)S(1)}, u32[]{:S(2)}) copy-start(f32[256,512]{1,0:T(8,128)S(1)} %get-tuple-element.83) | copy-start | bytes 1572868
  87.6 81.0 %copy-start.78 = (bf16[256,512]{1,0:T(8,128)(2,1)}, bf16[256,512]{1,0:T(8,128)(2,1)S(1)}, u32[]{:S(2)}) copy-start(bf16[256,512]{1,0:T(8,128)(2,1)S(1)} %multiply_convert_fusion.15) | copy-start | bytes 786436
  87.6 79.8 %collective-permute-start = (bf16[1,512]{1,0:T(2,128)(2,1)S(1)}, bf16[1,512]{1,0:T(2,128)(2,1)S(1)}, u32[]{:S(2)}, u32[]{:S(2)}) collective-permute-start(bf16[1,512]{1,0:T(2,128)(2,1)S(1)} %get-tuple-element.88), channel_id=1, source_target_pairs={{0,8},{8,16},{16,24},{24,32},{32,40},{40,48},{48,56},{56,64},{64,7... | collective-permute-start | bytes 3080 | tf_op jit(solution)/shard_map/ppermute | solution.py:18
  105.9 61.5 %collective-permute-start.1 = (bf16[1,512]{1,0:T(2,128)(2,1)S(1)}, bf16[1,512]{1,0:T(2,128)(2,1)S(1)}, u32[]{:S(2)}, u32[]{:S(2)}) collective-permute-start(bf16[1,512]{1,0:T(2,128)(2,1)S(1)} %get-tuple-element.89), channel_id=1, source_target_pairs={{8,0},{16,8},{24,16},{32,24},{40,32},{48,40},{56,48},{64,56},{72,6... | collective-permute-start | bytes 3080 | tf_op jit(solution)/shard_map/ppermute | solution.py:21
  107.8 192.2 %all-gather.12.cloned.1.call-start = ((), (), s32[]{:S(2)}) async-start(), calls=%async_computation.16 | async-start | bytes 4456448 | tf_op jit(solution)/shard_map/all_gather | solution.py:167
  130.6 87.8 %copy-start.99 = (f32[1,2048]{1,0:T(1,128)}, f32[1,2048]{1,0:T(1,128)S(1)}, u32[]{:S(2)}) copy-start(f32[1,2048]{1,0:T(1,128)S(1)} %get-tuple-element.92) | copy-start | bytes 24580
  130.6 87.8 %copy-start.101 = (f32[1,2048]{1,0:T(1,128)}, f32[1,2048]{1,0:T(1,128)S(1)}, u32[]{:S(2)}) copy-start(f32[1,2048]{1,0:T(1,128)S(1)} %get-tuple-element.93) | copy-start | bytes 24580
  130.6 87.8 %copy-start.103 = (f32[1,2048]{1,0:T(1,128)}, f32[1,2048]{1,0:T(1,128)S(1)}, u32[]{:S(2)}) copy-start(f32[1,2048]{1,0:T(1,128)S(1)} %get-tuple-element.94) | copy-start | bytes 24580
  130.6 87.8 %copy-start.105 = (f32[1,2048]{1,0:T(1,128)}, f32[1,2048]{1,0:T(1,128)S(1)}, u32[]{:S(2)}) copy-start(f32[1,2048]{1,0:T(1,128)S(1)} %get-tuple-element.95) | copy-start | bytes 24580
  130.6 87.8 %copy-start.107 = (f32[1,2048]{1,0:T(1,128)}, f32[1,2048]{1,0:T(1,128)S(1)}, u32[]{:S(2)}) copy-start(f32[1,2048]{1,0:T(1,128)S(1)} %get-tuple-element.96) | copy-start | bytes 24580
  130.6 87.8 %copy-start.109 = (f32[1,2048]{1,0:T(1,128)}, f32[1,2048]{1,0:T(1,128)S(1)}, u32[]{:S(2)}) copy-start(f32[1,2048]{1,0:T(1,128)S(1)} %get-tuple-element.97) | copy-start | bytes 24580
  130.6 87.8 %copy-start.111 = (f32[1,2048]{1,0:T(1,128)}, f32[1,2048]{1,0:T(1,128)S(1)}, u32[]{:S(2)}) copy-start(f32[1,2048]{1,0:T(1,128)S(1)} %get-tuple-element.98) | copy-start | bytes 24580
  130.6 87.8 %copy-start.113 = (f32[1,2048]{1,0:T(1,128)}, f32[1,2048]{1,0:T(1,128)S(1)}, u32[]{:S(2)}) copy-start(f32[1,2048]{1,0:T(1,128)S(1)} %get-tuple-element.99) | copy-start | bytes 24580
  130.6 87.8 %copy-start.115 = (f32[1,2048]{1,0:T(1,128)}, f32[1,2048]{1,0:T(1,128)S(1)}, u32[]{:S(2)}) copy-start(f32[1,2048]{1,0:T(1,128)S(1)} %get-tuple-element.100) | copy-start | bytes 24580
  173.6 44.7 %collective-permute-start.2 = (bf16[4,2048]{1,0:T(4,128)(2,1)S(1)}, bf16[4,2048]{1,0:T(4,128)(2,1)S(1)}, u32[]{:S(2)}, u32[]{:S(2)}) collective-permute-start(bf16[4,2048]{1,0:T(4,128)(2,1)S(1)} %get-tuple-element.86), channel_id=1, source_target_pairs={{0,8},{8,16},{16,24},{24,32},{32,40},{40,48},{48,56},{56,64},{64,7... | collective-permute-start | bytes 49160 | tf_op jit(solution)/shard_map/ppermute | solution.py:18
  193.3 25.0 %collective-permute-start.3 = (bf16[4,2048]{1,0:T(4,128)(2,1)S(1)}, bf16[4,2048]{1,0:T(4,128)(2,1)S(1)}, u32[]{:S(2)}, u32[]{:S(2)}) collective-permute-start(bf16[4,2048]{1,0:T(4,128)(2,1)S(1)} %get-tuple-element.87), channel_id=1, source_target_pairs={{8,0},{16,8},{24,16},{32,24},{40,32},{48,40},{56,48},{64,56},{72,6... | collective-permute-start | bytes 49160 | tf_op jit(solution)/shard_map/ppermute | solution.py:21
  223.9 52.1 %copy-start.120 = (bf16[64,512]{1,0:T(8,128)(2,1)S(1)}, bf16[64,512]{1,0:T(8,128)(2,1)}, u32[]{:S(2)}) copy-start(bf16[64,512]{1,0:T(8,128)(2,1)} %param.36) | copy-start | bytes 196612
  224.9 118.5 %all-gather.14.cloned.1.call-start = ((), (), s32[]{:S(2)}) async-start(), calls=%async_computation.17 | async-start | bytes 4456448 | tf_op jit(solution)/shard_map/all_gather | solution.py:168
  248.5 53.8 %copy-start.60 = (bf16[512,512]{1,0:T(8,128)(2,1)}, bf16[512,512]{1,0:T(8,128)(2,1)S(1)}, u32[]{:S(2)}) copy-start(bf16[512,512]{1,0:T(8,128)(2,1)S(1)} %all_gather.72) | copy-start | bytes 1572868
  249.6 129.4 %all-gather.16.cloned.1.call-start = ((), (), s32[]{:S(2)}) async-start(), calls=%async_computation.18 | async-start | bytes 2359296 | tf_op jit(solution)/shard_map/all_gather | solution.py:185
  250.2 171.1 %all-gather.18.cloned.1.call-start = ((), (), s32[]{:S(2)}) async-start(), calls=%async_computation.19 | async-start | bytes 2359296 | tf_op jit(solution)/shard_map/all_gather | solution.py:186
  250.7 298.5 %reduce-scatter.15.cloned.1.call-start = ((), (), s32[]{:S(2)}) async-start(), calls=%async_computation.20 | async-start | bytes 4456448 | tf_op jit(solution)/shard_map/reduce_scatter | solution.py:235
  364.0 57.2 %copy-start.94 = (bf16[1,256,512]{2,1,0:T(8,128)(2,1)S(1)}, bf16[1,256,512]{2,1,0:T(8,128)(2,1)}, u32[]{:S(2)}) copy-start(bf16[1,256,512]{2,1,0:T(8,128)(2,1)} %param.22) | copy-start | bytes 786436
  465.6 167.5 %reduce-scatter.17.cloned.1.call-start = ((), (), s32[]{:S(2)}) async-start(), calls=%async_computation.21 | async-start | bytes 4456448 | tf_op jit(solution)/shard_map/reduce_scatter | solution.py:241
  486.2 210.2 %reduce-scatter.37.cloned.1.call-start = ((), (), s32[]{:S(2)}) async-start(), calls=%async_computation.31 | async-start | bytes 589824 | tf_op jit(solution)/shard_map/reduce_scatter | solution.py:270
  488.5 219.3 %reduce-scatter.31.cloned.1.call-start = ((), (), s32[]{:S(2)}) async-start(), calls=%async_computation.28 | async-start | bytes 589824 | tf_op jit(solution)/shard_map/reduce_scatter | solution.py:261
  505.8 245.9 %reduce-scatter.41.cloned.1.call-start = ((), (), s32[]{:S(2)}) async-start(), calls=%async_computation.33 | async-start | bytes 2359296 | tf_op jit(solution)/shard_map/reduce_scatter | solution.py:207
  509.7 285.6 %reduce-scatter.39.cloned.1.call-start = ((), (), s32[]{:S(2)}) async-start(), calls=%async_computation.32 | async-start | bytes 2359296 | tf_op jit(solution)/shard_map/reduce_scatter | solution.py:204
  513.1 321.2 %reduce-scatter.35.cloned.1.call-start = ((), (), s32[]{:S(2)}) async-start(), calls=%async_computation.30 | async-start | bytes 589824 | tf_op jit(solution)/shard_map/reduce_scatter | solution.py:267
  513.1 120.0 %copy-start.61 = (bf16[512,512]{1,0:T(8,128)(2,1)S(1)}, bf16[512,512]{1,0:T(8,128)(2,1)}, u32[]{:S(2)}) copy-start(bf16[512,512]{1,0:T(8,128)(2,1)} %copy-done.60) | copy-start | bytes 1572868
  550.7 86.0 %copy-start.52 = (f32[256,512]{1,0:T(8,128)S(1)}, f32[256,512]{1,0:T(8,128)}, u32[]{:S(2)}) copy-start(f32[256,512]{1,0:T(8,128)} %copy-done.51) | copy-start | bytes 1572868
  636.5 237.4 %reduce-scatter.33.cloned.1.call-start = ((), (), s32[]{:S(2)}) async-start(), calls=%async_computation.29 | async-start | bytes 589824 | tf_op jit(solution)/shard_map/reduce_scatter | solution.py:264
  649.5 8.6 collective-permute-start.4
  653.5 4.6 collective-permute-start.5
  658.1 255.2 %reduce-scatter.21.cloned.1.call-start = ((), (), s32[]{:S(2)}) async-start(), calls=%async_computation.23 | async-start | bytes 589824 | tf_op jit(solution)/shard_map/reduce_scatter | solution.py:339
  672.3 8.1 collective-permute-start.6
  674.4 6.1 collective-permute-start.7
  683.9 269.0 %reduce-scatter.19.cloned.1.call-start = ((), (), s32[]{:S(2)}) async-start(), calls=%async_computation.22 | async-start | bytes 589824 | tf_op jit(solution)/shard_map/reduce_scatter | solution.py:336
  685.3 306.9 %reduce-scatter.25.cloned.1.call-start = ((), (), s32[]{:S(2)}) async-start(), calls=%async_computation.25 | async-start | bytes 884736 | tf_op jit(solution)/shard_map/reduce_scatter | solution.py:312
  687.5 345.4 %reduce-scatter.29.cloned.1.call-start = ((), (), s32[]{:S(2)}) async-start(), calls=%async_computation.27 | async-start | bytes 1179648 | tf_op jit(solution)/shard_map/reduce_scatter | solution.py:321
  689.1 387.5 %reduce-scatter.23.cloned.1.call-start = ((), (), s32[]{:S(2)}) async-start(), calls=%async_computation.24 | async-start | bytes 2359296 | tf_op jit(solution)/shard_map/reduce_scatter | solution.py:309
  692.8 422.2 %reduce-scatter.27.cloned.1.call-start = ((), (), s32[]{:S(2)}) async-start(), calls=%async_computation.26 | async-start | bytes 73728 | tf_op jit(solution)/shard_map/reduce_scatter | solution.py:318
  694.9 571.2 %all-reduce.17.cloned.1.call-start = ((), (), s32[]{:S(2)}) async-start(), calls=%async_computation.34 | async-start | bytes 2818048 | tf_op jit(solution)/shard_map/psum | solution.py:345
  (140 other events, 1174.1 us)
Sparse Core Ops, SparseCore 0:
  9.7 41.2 all-gather.7
  108.0 33.6 all-gather.9
  225.1 63.0 all-gather.11
  291.0 52.4 all-gather.13
  345.0 33.9 all-gather.15
  380.5 40.7 all-gather.17
  465.7 83.4 reduce-scatter.14
  553.8 79.2 reduce-scatter.16
  635.5 33.1 reduce-scatter.36
  671.0 36.6 reduce-scatter.30
  710.1 41.4 reduce-scatter.40
  753.9 41.3 reduce-scatter.38
  797.6 36.6 reduce-scatter.34
  837.2 36.5 reduce-scatter.32
  876.6 36.5 reduce-scatter.20
  916.2 36.6 reduce-scatter.18
  955.1 37.1 reduce-scatter.24
  994.6 38.1 reduce-scatter.28
  1035.4 41.0 reduce-scatter.22
  1079.4 35.5 reduce-scatter.26
  1118.5 147.6 all-reduce.16
where the time goes:
time: 1300 us; the launch traced here: 1290 us
  waiting for transfers between devices  660 us (51%)
  blocking collectives  301 us (23%)
  matrix products  146 us (11%)
  other arithmetic  58.9 us (5%)
  starting transfers between devices  58.1 us (4%)
  local copies, waits for them, and re-layouts  45.2 us (3%)
  between operations  19.4 us (1%)
    psum x1, waiting for transfers between devices, shards(): lax.psum(s_wval.astype(jnp.bfloat16), 'ctx').astype(jnp.float32)  82.7 us
    reduce_scatter x1, waiting for transfers between devices, shards(): lax.psum_scatter(jnp.concatenate(value_grads, 1).astype(jnp.bfloat16), 'c...  82.4 us
    psum x1, blocking collectives, shards(): lax.psum(s_gglu.astype(jnp.bfloat16), 'ctx').astype(jnp.float32)  65.3 us
    dot_general x27, matrix products, outer_cols(): lax.dot_general(left, right, (((1,), (1,)), ((), ())), preferred_element_...  52.7 us
    dot_general x27, matrix products, inner_rows(): lax.dot_general(left, right, (((0,), (0,)), ((), ())), preferred_element_...  47.8 us
    ppermute x4, starting transfers between devices, with_halo(): lax.ppermute(lax.slice_in_dim(block, block.shape[dim] - width, None, axis...  46.6 us
    dot_general x27, matrix products, matmul(): return jnp.dot(left, right, preferred_element_type=jnp.float32)  45.6 us
    reduce_scatter x1, waiting for transfers between devices, shards(): lax.psum_scatter(d_lower.astype(jnp.bfloat16), 'wt', scatter_dimension=0,...  43.9 us
  transfers between devices with their start and end apart: 29, of which 17 were waited for; matrix products, arithmetic and copies ran while one was open for 12% of the time, Pallas kernels for 0%

commit v1 on v0

v1 whole, which is shorter than its diff:
```python
import functools

import jax
import jax.numpy as jnp
import numpy as np
from jax import lax
from jax.experimental import pallas as pl
from jax.experimental.pallas import tpu as pltpu
from jax.sharding import Mesh
from jax.sharding import PartitionSpec as P

HEADS = 8
HEAD = 64
EPSILON = 1e-06
AXES = ("y", "xh", "core", "xl", "z")
SIZES = (4, 2, 2, 2, 4)
CTX = ("y", "xh", "core")
CHIPS = ("y", "xh")
WT = ("xl", "z")
LOG2E = 1.4426950408889634
BF = jnp.bfloat16
F32 = jnp.float32


def moves(target):
    pairs = []
    for source in range(int(np.prod(SIZES))):
        place = [int(v) for v in np.unravel_index(source, SIZES)]
        goal = target(*place)
        if goal is not None:
            pairs.append((source, int(np.ravel_multi_index(tuple(goal), SIZES))))
    return pairs


def shift(dy=0, dxh=0, dc=0, dxl=0, dz=0):
    return moves(
        lambda y, xh, c, xl, z: (
            (y + dy) % 4, (xh + dxh) % 2, (c + dc) % 2, (xl + dxl) % 2, (z + dz) % 4,
        )
    )


def along(step):
    def target(y, xh, c, xl, z):
        place = y * 4 + xh * 2 + c + step
        if place < 0 or place > 15:
            return None
        return (place // 4, place // 2 % 2, place % 2, xl, z)
    return moves(target)


def send(value, pairs):
    return lax.ppermute(value, AXES, pairs)


def matmul(left, right):
    return jnp.dot(left, right, preferred_element_type=F32)


def contract(left, right, ldim, rdim):
    return lax.dot_general(
        left, right, (((ldim,), (rdim,)), ((), ())), preferred_element_type=F32
    )


def inner_rows(left, right):
    return contract(left, right, 0, 0)


def outer_cols(left, right):
    return contract(left, right, 1, 1)


def smooth_unit(value):
    return value * jax.nn.sigmoid(value)


def smooth_slope(value):
    sigma = jax.nn.sigmoid(value)
    return sigma * (1.0 + value * (1.0 - sigma))


def layer_norm(value, gain):
    average = jnp.mean(value, -1, keepdims=True)
    centred = value - average
    scale = lax.rsqrt(jnp.mean(centred * centred, -1, keepdims=True) + EPSILON)
    normal = centred * scale
    return (normal * gain, normal, scale)


def norm_back(incoming, normal, scale, gain):
    scaled = incoming * gain
    gain_grad = jnp.sum(incoming * normal, 0)
    value_grad = scale * (
        scaled
        - jnp.mean(scaled, -1, keepdims=True)
        - normal * jnp.mean(scaled * normal, -1, keepdims=True)
    )
    return (value_grad, gain_grad)


def with_halo(block, width):
    low = send(block[block.shape[0] - width:], along(1))
    high = send(block[:width], along(-1))
    return jnp.concatenate([low, block, high], axis=0)


def rotate(stacked, amount):
    count = stacked.shape[0]
    return lax.dynamic_slice_in_dim(
        jnp.concatenate([stacked, stacked], 0), (count - amount) % count, count, 0
    )


def gather(own):
    core, xl, z = (lax.axis_index(a) for a in ("core", "xl", "z"))
    rows, cols = own.shape
    half, quarter = rows // 2, rows // 4
    mine = lax.dynamic_slice_in_dim(own, core * half, half, 0)
    other = send(mine, shift(dxl=1))
    two = jnp.where(xl == 0, jnp.stack([mine, other]), jnp.stack([other, mine]))
    up = send(two, shift(dz=1))
    down = send(two, shift(dz=-1))
    up2 = send(up[:, :quarter], shift(dz=1))
    down2 = send(down[:, quarter:], shift(dz=-1))
    far = jnp.concatenate([up2, down2], 1)
    placed = rotate(jnp.stack([two, down, far, up]), z)
    passed = send(placed, shift(dc=1))
    both = jnp.where(core == 0, jnp.stack([placed, passed]), jnp.stack([passed, placed]))
    return both.transpose(2, 1, 0, 3, 4).reshape(8, rows, cols)


def reduce_all(grads):
    y, core, xl, z = (lax.axis_index(a) for a in ("y", "core", "xl", "z"))
    _, rows, cols = grads.shape
    half, part = rows // 2, rows // 8
    work = grads.reshape(2, 4, rows, cols)
    give = lax.dynamic_slice_in_dim(work, (1 - core) * half, half, 2).astype(BF)
    work = lax.dynamic_slice_in_dim(work, core * half, half, 2) + send(give, shift(dc=1)).astype(F32)

    def pick(array, index, dim, size=1):
        return lax.dynamic_slice_in_dim(array, index * size, size, dim)

    parts = [
        send(pick(work, (z + d) % 4, 1)[:, 0].astype(BF), shift(dz=d)) for d in (1, 3, 2)
    ]
    work = pick(work, z, 1)[:, 0] + sum(p.astype(F32) for p in parts)
    give = pick(work, 1 - xl, 0)[0].astype(BF)
    work = pick(work, xl, 0)[0] + send(give, shift(dxl=1)).astype(F32)
    parts = [
        send(pick(work, (y + d) % 4, 0, part).astype(BF), shift(dy=d)) for d in (1, 3, 2)
    ]
    work = pick(work, y, 0, part) + sum(p.astype(F32) for p in parts)
    own = work.astype(BF)
    total = (own.astype(F32) + send(own, shift(dxh=1)).astype(F32)).astype(BF)
    rest = [send(total, shift(dy=-d)) for d in (1, 2, 3)]
    placed = rotate(jnp.stack([total] + rest), y).reshape(half, cols)
    passed = send(placed, shift(dc=1))
    return jnp.where(
        core == 0, jnp.concatenate([placed, passed], 0), jnp.concatenate([passed, placed], 0)
    )


def attend_kernel(chips, rows, length_ref, core_ref, near_ref, far_ref, o_ref, e_ref, l_ref,
                  keys_ref, values_ref):
    step = pl.program_id(0)
    span = chips * rows
    aug = 2 * HEAD

    @pl.when(step == 0)
    def _():
        length = length_ref[0]
        core = core_ref[0]
        ones = jnp.ones((16, rows), F32)
        for side in range(2):
            source = near_ref if side == 0 else far_ref
            base = HEAD if side == 0 else 0
            owner = core if side == 0 else 1 - core
            for chip in range(chips):
                cols = slice(side * span + chip * rows, side * span + (chip + 1) * rows)
                key = source[chip, base:base + HEAD, :]
                keys_ref[0:HEAD, cols] = key
                keys_ref[HEAD:aug, cols] = key
                place = (chip * 2 + owner) * rows + lax.broadcasted_iota(jnp.int32, (16, rows), 1)
                row = lax.broadcasted_iota(jnp.int32, (16, rows), 0)
                bias = jnp.where((place < length) | (row > 0), 0.0, -1e30)
                keys_ref[aug:aug + 16, cols] = bias.astype(BF)
                value = source[chip, base + HEAD:base + 2 * HEAD, :].astype(F32)
                stacked = jnp.concatenate([value, ones, jnp.zeros((48, rows), F32)], 0)
                values_ref[cols, :] = stacked.T.astype(BF)

    query = near_ref[step, 0:HEAD, :].astype(F32) * (LOG2E * HEAD ** -0.5)
    high = query.astype(BF)
    low = (query - high.astype(F32)).astype(BF)
    query = jnp.concatenate([high, low, jnp.ones((16, rows), BF)], 0)
    scores = contract(query, keys_ref[...], 0, 0)
    top = jnp.max(scores, 1, keepdims=True)
    expo = jnp.exp2(scores - top).astype(BF)
    e_ref[...] = expo
    out = matmul(expo, values_ref[...]).T
    inverse = 1.0 / out[HEAD:HEAD + 8]
    o_ref[0] = (out[0:HEAD] * inverse[0:1]).astype(BF)
    l_ref[0] = inverse


def attend(near, far, length, core):
    chips, _, rows = near.shape
    tokens = 2 * chips * rows
    return pl.pallas_call(
        functools.partial(attend_kernel, chips, rows),
        grid=(chips,),
        in_specs=[
            pl.BlockSpec(memory_space=pltpu.SMEM),
            pl.BlockSpec(memory_space=pltpu.SMEM),
            pl.BlockSpec(near.shape, lambda i: (0, 0, 0)),
            pl.BlockSpec(far.shape, lambda i: (0, 0, 0)),
        ],
        out_specs=[
            pl.BlockSpec((1, HEAD, rows), lambda i: (i, 0, 0)),
            pl.BlockSpec((rows, tokens), lambda i: (i, 0)),
            pl.BlockSpec((1, 8, rows), lambda i: (i, 0, 0)),
        ],
        out_shape=[
            jax.ShapeDtypeStruct((chips, HEAD, rows), BF),
            jax.ShapeDtypeStruct((chips * rows, tokens), BF),
            jax.ShapeDtypeStruct((chips, 8, rows), F32),
        ],
        scratch_shapes=[
            pltpu.VMEM((2 * HEAD + 16, tokens), BF),
            pltpu.VMEM((tokens, 2 * HEAD), BF),
        ],
        compiler_params=pltpu.CompilerParams(vmem_limit_bytes=48 * 2**20),
        name="attend",
    )(length, core, near, far)


def attend_back_kernel(chips, rows, near_ref, far_ref, e_ref, o_ref, l_ref, do_ref,
                       dq_ref, dk_ref, dv_ref, keys_ref, values_ref, dk_acc, dv_acc):
    step = pl.program_id(0)
    span = chips * rows

    @pl.when(step == 0)
    def _():
        row = lax.broadcasted_iota(jnp.int32, (16, rows), 0)
        ones = jnp.where(row < 3, 1.0, 0.0).astype(BF)
        for side in range(2):
            source = near_ref if side == 0 else far_ref
            base = HEAD if side == 0 else 0
            for chip in range(chips):
                cols = slice(side * span + chip * rows, side * span + (chip + 1) * rows)
                key = source[chip, base:base + HEAD, :].astype(F32)
                stacked = jnp.concatenate([key, jnp.zeros((HEAD, rows), F32)], 0)
                keys_ref[cols, :] = stacked.T.astype(BF)
                values_ref[0:HEAD, cols] = source[chip, base + HEAD:base + 2 * HEAD, :]
                values_ref[HEAD:HEAD + 16, cols] = ones
        dk_acc[...] = jnp.zeros_like(dk_acc)
        dv_acc[...] = jnp.zeros_like(dv_acc)

    inverse = l_ref[0, 0:1, :]
    grad = do_ref[0].astype(F32) * inverse
    total = -jnp.sum(grad * o_ref[0].astype(F32), 0, keepdims=True)
    high = total.astype(BF).astype(F32)
    mid = (total - high).astype(BF).astype(F32)
    low = total - high - mid
    grad_low = grad.astype(BF)
    row = lax.broadcasted_iota(jnp.int32, (16, rows), 0)
    extra = jnp.where(row == 0, high, jnp.where(row == 1, mid, jnp.where(row == 2, low, 0.0)))
    grads = jnp.concatenate([grad_low, extra.astype(BF)], 0)
    query = near_ref[step, 0:HEAD, :]
    block = 1024
    dq = jnp.zeros((rows, 2 * HEAD), F32)
    for start in range(0, 2 * span, block):
        cols = slice(start, start + block)
        expo = e_ref[:, cols]
        d_probs = contract(grads, values_ref[:, cols], 0, 0)
        d_scores = (expo.astype(F32) * d_probs).astype(BF)
        dq = dq + matmul(d_scores, keys_ref[cols, :])
        dk_acc[:, cols] += matmul(query, d_scores)
        dv_acc[:, cols] += matmul(grad_low, expo)
    dq_ref[0] = (dq.T[0:HEAD] * HEAD ** -0.5).astype(BF)

    @pl.when(step == chips - 1)
    def _():
        for side in range(2):
            for chip in range(chips):
                cols = slice(side * span + chip * rows, side * span + (chip + 1) * rows)
                dk_ref[side, chip] = (dk_acc[:, cols] * HEAD ** -0.5).astype(BF)
                dv_ref[side, chip] = dv_acc[:, cols].astype(BF)


def attend_back(near, far, expo, out, inverse, d_out):
    chips, _, rows = near.shape
    tokens = 2 * chips * rows
    whole = lambda i: (0, 0, 0)
    one = lambda i: (i, 0, 0)
    return pl.pallas_call(
        functools.partial(attend_back_kernel, chips, rows),
        grid=(chips,),
        in_specs=[
            pl.BlockSpec(near.shape, whole),
            pl.BlockSpec(far.shape, whole),
            pl.BlockSpec((rows, tokens), lambda i: (i, 0)),
            pl.BlockSpec((1, HEAD, rows), one),
            pl.BlockSpec((1, 8, rows), one),
            pl.BlockSpec((1, HEAD, rows), one),
        ],
        out_specs=[
            pl.BlockSpec((1, HEAD, rows), one),
            pl.BlockSpec((2, chips, HEAD, rows), lambda i: (0, 0, 0, 0)),
            pl.BlockSpec((2, chips, HEAD, rows), lambda i: (0, 0, 0, 0)),
        ],
        out_shape=[
            jax.ShapeDtypeStruct((chips, HEAD, rows), BF),
            jax.ShapeDtypeStruct((2, chips, HEAD, rows), BF),
            jax.ShapeDtypeStruct((2, chips, HEAD, rows), BF),
        ],
        scratch_shapes=[
            pltpu.VMEM((tokens, 2 * HEAD), BF),
            pltpu.VMEM((HEAD + 16, tokens), BF),
            pltpu.VMEM((HEAD, tokens), F32),
            pltpu.VMEM((HEAD, tokens), F32),
        ],
        compiler_params=pltpu.CompilerParams(vmem_limit_bytes=48 * 2**20),
        name="attend_back",
    )(near, far, expo, out, inverse, d_out)


def shards(
    inputs, lengths, cotangent, glu_gain, glu_value, glu_gate, conv_gain, wide_weight,
    narrow_weight, mid_gain, depth_weight, point_weight, attn_gain, query_weight, key_weight,
    value_weight, output_weight, ffn_gain, ffn_in, ffn_out,
):
    rows, width = inputs.shape[1], inputs.shape[2]
    half = narrow_weight.shape[2]
    units = wide_weight.shape[1]
    core = lax.axis_index("core")
    first = (lax.axis_index("y") * 4 + lax.axis_index("xh") * 2 + core) * rows
    valid = (first + jnp.arange(rows, dtype=jnp.int32) < lengths[0]).astype(F32)[:, None]
    hidden = inputs[0].astype(F32)

    gains = jnp.concatenate([glu_gain, conv_gain, attn_gain, ffn_gain])[None]
    small = jnp.concatenate([gains, mid_gain[None], depth_weight], 0)
    small = jnp.pad(small, ((0, 32 - small.shape[0]), (0, 0)))
    pack1 = jnp.concatenate(
        [glu_value, glu_gate, jnp.concatenate([small[:16], small[16:]], 1)], 0
    )
    full1 = gather(pack1)
    w_val = full1[:, 0:64].reshape(width, width)
    w_gat = full1[:, 64:128].reshape(width, width)
    small = full1[:, 128:144, :256].astype(F32)
    g_glu, g_conv, g_att, g_ffn = (small[:, 0, 64 * i:64 * i + 64].reshape(-1) for i in range(4))
    g_mid = small[:, 1].reshape(-1)
    depth_float = small[:, 2:11].transpose(1, 0, 2).reshape(9, units)

    narrow_flat = narrow_weight.reshape(-1, half)
    cut = narrow_flat.shape[0] // 2
    pack2 = jnp.concatenate(
        [wide_weight[:, 512 * i:512 * i + 512] for i in range(4)]
        + [jnp.concatenate([narrow_flat[:cut], narrow_flat[cut:]], 1)]
        + [jnp.concatenate([point_weight[:128], point_weight[128:]], 1)]
        + [query_weight, key_weight, value_weight], 0,
    )
    full2 = gather(pack2)
    w_wid = full2[:, 0:256].reshape(8, 4, 64, 512).transpose(0, 2, 1, 3).reshape(width, units)
    nar = full2[:, 256:352]
    nar = jnp.concatenate([nar[:, :, :half], nar[:, :, half:]], 1).reshape(8, 3, 64, half)
    w_nar = nar.transpose(1, 0, 2, 3).reshape(3, width, half)
    pnt = full2[:, 352:480]
    w_pnt = jnp.concatenate([pnt[:, :, :half], pnt[:, :, half:]], 1).reshape(units, half)
    w_qry, w_key, w_vls = (
        full2[:, 480 + 64 * i:544 + 64 * i].reshape(width, width) for i in range(3)
    )

    pack3 = jnp.concatenate(
        [output_weight] + [ffn_in[:, 512 * i:512 * i + 512] for i in range(4)] + [ffn_out], 0
    )
    full3 = gather(pack3)
    w_outp = full3[:, 0:64].reshape(width, width)
    w_upper = full3[:, 64:320].reshape(8, 4, 64, 512).transpose(0, 2, 1, 3).reshape(width, units)
    w_lower = full3[:, 320:576].reshape(units, width)

    normed, glu_hat, glu_scale = layer_norm(hidden, g_glu)
    glu_in = normed.astype(BF)
    value_part = matmul(glu_in, w_val)
    sigma = jax.nn.sigmoid(matmul(glu_in, w_gat))
    after_glu = hidden + value_part * sigma

    normed, conv_hat, conv_scale = layer_norm(after_glu, g_conv)
    conv_in = (normed * valid).astype(BF)
    wide_pre = matmul(conv_in, w_wid)
    conv_rim = with_halo(conv_in, 1)
    stacked = jnp.concatenate(
        [conv_rim[0:rows], conv_rim[1:rows + 1], conv_rim[2:rows + 2]], axis=1
    )
    narrow_pre = matmul(stacked, w_nar.reshape(3 * width, half))
    mixed = smooth_unit(wide_pre) + jnp.pad(smooth_unit(narrow_pre), ((0, 0), (0, units - half)))
    normed, mid_hat, mid_scale = layer_norm(mixed, g_mid)
    mid_in = (normed * valid).astype(BF)
    mid_rim = with_halo(mid_in, 4)
    spread = sum((mid_rim[tap:tap + rows].astype(F32) * depth_float[tap] for tap in range(9)))
    spread_in = spread.astype(BF)
    separable = matmul(spread_in, w_pnt)
    after_conv = after_glu + jnp.pad(separable, ((0, 0), (0, width - half)))

    normed, attn_hat, attn_scale = layer_norm(after_conv, g_att)
    attn_in = normed.astype(BF)
    qkv = jnp.concatenate(
        [contract(w, attn_in, 0, 1).astype(BF).reshape(HEADS, HEAD, rows)
         for w in (w_qry, w_key, w_vls)], 1,
    )
    near = lax.all_to_all(qkv, CHIPS, 0, 0, tiled=True)
    far = send(near[:, HEAD:], shift(dc=1))
    head_out, expo, inverse = attend(near, far, lengths, core[None])
    heads_in = lax.all_to_all(head_out, CHIPS, 0, 0, tiled=True).reshape(width, rows)
    after_attn = after_conv + contract(heads_in, w_outp, 0, 0)

    normed, ffn_hat, ffn_scale = layer_norm(after_attn, g_ffn)
    ffn_input = normed.astype(BF)
    ffn_pre = matmul(ffn_input, w_upper)
    activated = smooth_unit(ffn_pre).astype(BF)
    result = (after_attn + matmul(activated, w_lower)) * valid
    grad = cotangent[0].astype(F32) * valid
    grad_low = grad.astype(BF)
    d_lower = inner_rows(activated, grad_low)
    d_pre = (outer_cols(grad_low, w_lower) * smooth_slope(ffn_pre)).astype(BF)
    d_upper = inner_rows(ffn_input, d_pre)
    back, d_gffn = norm_back(outer_cols(d_pre, w_upper), ffn_hat, ffn_scale, g_ffn)
    grad = grad + back
    grad_low = grad.astype(BF)
    d_outp = contract(heads_in, grad_low, 1, 0)
    d_heads = contract(w_outp, grad_low, 1, 1).astype(BF).reshape(HEADS, HEAD, rows)
    d_near = lax.all_to_all(d_heads, CHIPS, 0, 0, tiled=True)

    def by_shard(array, count=8):
        return array.reshape((count, array.shape[0] // count) + array.shape[1:])

    def columns(array):
        return by_shard(array).reshape(8, 64, 4, 512).transpose(0, 2, 1, 3).reshape(8, 256, 512)

    early = jnp.concatenate([by_shard(d_outp), columns(d_upper), by_shard(d_lower)], 1)
    early = reduce_all(early)

    dq, dk, dv = attend_back(near, far, expo, head_out, inverse, d_near)
    d_far = send(jnp.concatenate([dk[1], dv[1]], 1), shift(dc=1)).astype(F32)
    d_near = jnp.concatenate([dk[0], dv[0]], 1).astype(F32)
    d_qkv = jnp.concatenate([dq, (d_near + d_far).astype(BF)], 1)
    d_qkv = lax.all_to_all(d_qkv, CHIPS, 0, 0, tiled=True)
    dq_low, dk_low, dv_low = (
        d_qkv[:, HEAD * i:HEAD * i + HEAD].reshape(width, rows) for i in range(3)
    )
    d_qry = contract(attn_in, dq_low, 0, 1)
    d_key = contract(attn_in, dk_low, 0, 1)
    d_vls = contract(attn_in, dv_low, 0, 1)
    d_norm = (
        contract(dq_low, w_qry, 0, 1) + contract(dk_low, w_key, 0, 1)
        + contract(dv_low, w_vls, 0, 1)
    )
    back, d_gatt = norm_back(d_norm, attn_hat, attn_scale, g_att)
    grad = grad + back

    sep_grad = grad[:, :half].astype(BF)
    d_pnt = inner_rows(spread_in, sep_grad)
    d_spread = outer_cols(sep_grad, w_pnt).astype(BF)
    spread_float = d_spread.astype(F32)
    d_dep = jnp.stack(
        [jnp.sum(mid_rim[tap:tap + rows].astype(F32) * spread_float, 0) for tap in range(9)]
    )
    spread_rim = with_halo(d_spread, 4)
    d_mid = sum(
        (spread_rim[8 - tap:8 - tap + rows].astype(F32) * depth_float[tap] for tap in range(9))
    )
    back_mid, d_gmid = norm_back(d_mid * valid, mid_hat, mid_scale, g_mid)
    d_wide_pre = (back_mid * smooth_slope(wide_pre)).astype(BF)
    d_nar_pre = (back_mid[:, :half] * smooth_slope(narrow_pre)).astype(BF)
    d_wid = inner_rows(conv_in, d_wide_pre)
    d_nar = inner_rows(stacked, d_nar_pre).reshape(3, width, half)
    nar_rim = with_halo(d_nar_pre, 1)
    back_stack = jnp.concatenate(
        [nar_rim[2:rows + 2], nar_rim[1:rows + 1], nar_rim[0:rows]], axis=1
    )
    d_conv = outer_cols(d_wide_pre, w_wid) + outer_cols(
        back_stack, w_nar.transpose(1, 0, 2).reshape(width, 3 * half)
    )
    back, d_gconv = norm_back(d_conv * valid, conv_hat, conv_scale, g_conv)
    grad = grad + back

    d_value = (grad * sigma).astype(BF)
    d_gate = (grad * value_part * sigma * (1.0 - sigma)).astype(BF)
    d_wval = inner_rows(glu_in, d_value)
    d_wgat = inner_rows(glu_in, d_gate)
    d_norm = outer_cols(d_value, w_val) + outer_cols(d_gate, w_gat)
    back, d_gglu = norm_back(d_norm, glu_hat, glu_scale, g_glu)
    grad = grad + back

    gains = jnp.concatenate([by_shard(g) for g in (d_gglu, d_gconv, d_gatt, d_gffn)], 1)[:, None]
    small = jnp.concatenate(
        [gains, by_shard(d_gmid)[:, None], d_dep.reshape(9, 8, 256).transpose(1, 0, 2)], 1
    )
    small = jnp.pad(small, ((0, 0), (0, 64 - small.shape[1]), (0, 0)))
    nar = d_nar.reshape(3, 8, 64, half).transpose(1, 0, 2, 3).reshape(8, 192, half)
    pnt = by_shard(d_pnt)
    late = jnp.concatenate(
        [by_shard(d_wval), by_shard(d_wgat), columns(d_wid),
         jnp.concatenate([nar[:, :96], nar[:, 96:]], 2),
         jnp.concatenate([pnt[:, :128], pnt[:, 128:]], 2),
         by_shard(d_qry), by_shard(d_key), by_shard(d_vls),
         jnp.concatenate([small[:, :32], small[:, 32:]], 2)], 1,
    )
    late = reduce_all(late).astype(F32)
    early = early.astype(F32)

    def wide_of(array):
        return array.reshape(4, 64, 512).transpose(1, 0, 2).reshape(64, 2048)

    s_wval, s_wgat = late[0:64], late[64:128]
    s_wid = wide_of(late[128:384])
    nar = late[384:480]
    s_nar = jnp.concatenate([nar[:, :half], nar[:, half:]], 0).reshape(3, 64, half)
    pnt = late[480:608]
    s_pnt = jnp.concatenate([pnt[:, :half], pnt[:, half:]], 0)
    s_qry, s_key, s_vls = late[608:672], late[672:736], late[736:800]
    small = late[800:832, :256]
    s_gglu, s_gconv, s_gatt, s_gffn = (small[0, 64 * i:64 * i + 64] for i in range(4))
    s_outp, s_upper, s_lower = early[0:64], wide_of(early[64:320]), early[320:576]
    return (
        result.astype(BF)[None], grad[None], s_gglu, s_wval, s_wgat, s_gconv, s_wid, s_nar,
        small[1], small[2:11], s_pnt, s_gatt, s_qry, s_key, s_vls, s_outp, s_gffn, s_upper,
        s_lower,
    )


def solution(mesh):
    fine = Mesh(mesh.devices.reshape(SIZES), AXES)
    flat, row, mid = P(WT), P(WT, None), P(None, WT, None)
    col = P(None, WT)
    tokens = P(WT, CTX, None)
    weights = (
        flat, row, row, flat, row, mid, flat, col, row, flat, row, row, row, row, flat, row, row,
    )
    return jax.shard_map(
        shards, mesh=fine, in_specs=(tokens, flat, tokens) + weights,
        out_specs=(tokens, tokens) + weights, check_vma=False,
    )
```

time: 1300 us -> 516 us (0.40)
  waiting for transfers between devices: 660 us -> 136 us
  blocking collectives: 301 us -> 0 us
  matrix products: 146 us -> 35 us
  local copies, waits for them, and re-layouts: 45.2 us -> 113 us
  starting transfers between devices: 58.1 us -> 116 us
  Pallas kernels: 0 us -> 32.3 us
  between operations: 19.4 us -> 4.49 us
    reduce_scatter x14 -> x0, waiting for transfers between devices: 513 us -> none  [the longest x1 82.4 us: shards(): lax.psum_scatter(jnp.concatenate(value_grads, 1).astype(jnp.bfloat16), 'c...]
    all_gather x9 -> x0, blocking collectives: 203 us -> none  [the longest x1 25.5 us: shards(): lax.all_gather(glu_value, 'wt', axis=0, tiled=True)]
    ppermute x8 -> x54, waiting for transfers between devices: 0.02 us -> 115 us  [send(): return lax.ppermute(value, AXES, pairs)]
    dot_general x81 -> x33, matrix products: 146 us -> 35 us  [the longest x26 25.2 us: contract(): lax.dot_general(left, right, (((ldim,), (rdim,)), ((), ())), preferred_el...]
    psum x1 -> x0, waiting for transfers between devices: 82.7 us -> none  [shards(): lax.psum(s_wval.astype(jnp.bfloat16), 'ctx').astype(jnp.float32)]
    psum x1 -> x0, blocking collectives: 65.3 us -> none  [shards(): lax.psum(s_gglu.astype(jnp.bfloat16), 'ctx').astype(jnp.float32)]
    all_gather x6 -> x0, waiting for transfers between devices: 62.5 us -> none  [the longest x1 38.6 us: shards(): lax.all_gather(ffn_out, 'wt', axis=0, tiled=True)]
    ppermute x8 -> x54, starting transfers between devices: 56.5 us -> 94.6 us  [send(): return lax.ppermute(value, AXES, pairs)]
  transfers between devices with their start and end apart: 29 -> 58, of which waited for: 17 -> 28; matrix products, arithmetic and copies ran while one was open for 12% -> 35% of each run, Pallas kernels for 0% -> 0%
where the time goes in v1:
time: 516 us; the launch traced here: 506 us
  waiting for transfers between devices  136 us (26%)
  starting transfers between devices  116 us (22%)
  local copies, waits for them, and re-layouts  113 us (22%)
  other arithmetic  69.3 us (13%)
  matrix products  35 us (7%)
  Pallas kernels  32.3 us (6%)
    ppermute x54, waiting for transfers between devices, send(): return lax.ppermute(value, AXES, pairs)  115 us
    ppermute x54, starting transfers between devices, send(): return lax.ppermute(value, AXES, pairs)  94.6 us
    unnamed x303, local copies, waits for them, and re-layouts  38.4 us
    dot_general x26, matrix products, contract(): lax.dot_general(left, right, (((ldim,), (rdim,)), ((), ())), preferred_el...  25.2 us
    pallas_call x1, Pallas kernels, attend_back(): pl.pallas_call(functools.partial(attend_back_kernel, chips, rows), grid=(...  18.3 us
    another operation x3, local copies, waits for them, and re-layouts, columns(): by_shard(array).reshape(8, 64, 4, 512).transpose(0, 2, 1, 3)  17.6 us
    pallas_call x1, Pallas kernels, attend(): pl.pallas_call(functools.partial(attend_kernel, chips, rows), grid=(chips...  14 us
    all_to_all x1, waiting for transfers between devices, shards(): near = lax.all_to_all(qkv, CHIPS, 0, 0, tiled=True)  12.4 us
  transfers between devices with their start and end apart: 58, of which 28 were waited for; matrix products, arithmetic and copies ran while one was open for 35% of the time, Pallas kernels for 0%

profile of v1, /device:TPU:1, one launch (start us, length us, event | category | flops | bytes accessed | tf_op | source)
XLA Modules:
  0.0 505.7 jit_solution(5210417775386170364)
XLA Ops:
  27.0 4.3 collective-permute-start.5
  41.2 5.2 %collective-permute-done.18 = bf16[2,288,512]{2,1,0:T(8,128)(2,1)S(1)} collective-permute-done((bf16[2,288,512]{2,1,0:T(8,128)(2,1)S(1)}, bf16[2,288,512]{2,1,0:T(8,128)(2,1)S(1)}, u32[]{:S(2)}, u32[]{:S(2)}) %collective-permute-start.18) | collective-permute-done | bytes 589856 | tf_op jit(solution)/shard_map/ppermute | solution.py:53
  47.2 3.4 collective-permute-start.21
  55.9 5.4 %collective-permute-done.7 = bf16[2,336,512]{2,1,0:T(8,128)(2,1)} collective-permute-done((bf16[2,336,512]{2,1,0:T(8,128)(2,1)}, bf16[2,336,512]{2,1,0:T(8,128)(2,1)}, u32[]{:S(2)}, u32[]{:S(2)}) %collective-permute-start.7) | collective-permute-done | bytes 688160 | tf_op jit(solution)/shard_map/ppermute | solution.py:53
  62.3 3.5 collective-permute-start.10
  68.4 6.5 %collective-permute-done.10 = bf16[2,168,512]{2,1,0:T(8,128)(2,1)S(1)} collective-permute-done((bf16[2,168,512]{2,1,0:T(8,128)(2,1)S(1)}, bf16[2,168,512]{2,1,0:T(8,128)(2,1)S(1)}, u32[]{:S(2)}, u32[]{:S(2)}) %collective-permute-start.10) | collective-permute-done | bytes 344096 | tf_op jit(solution)/shard_map/ppermute | solution.py:53
  85.4 4.4 collective-permute-start.12
  100.6 3.2 constant_dynamic-slice_fusion.2
  104.2 3.5 maximum_select_fusion
  115.6 5.1 %collective-permute-start.14 = (bf16[4,2048]{1,0:T(4,128)(2,1)S(1)}, bf16[4,2048]{1,0:T(4,128)(2,1)S(1)}, u32[]{:S(2)}, u32[]{:S(2)}) collective-permute-start(bf16[4,2048]{1,0:T(4,128)(2,1)S(1)} %get-tuple-element.116), channel_id=1, source_target_pairs={{0,8},{1,9},{2,10},{3,11},{4,12},{5,13},{6,14},{7,15},{8,16},{9,17... | collective-permute-start | bytes 49160 | tf_op jit(solution)/shard_map/ppermute | solution.py:53
  122.8 4.5 collective-permute-done.15
  133.4 6.9 %all-to-all-start = ((bf16[8,192,256]{2,1,0:T(8,128)(2,1)}), bf16[8,192,256]{2,1,0:T(8,128)(2,1)S(1)}, u32[]{:S(2)}, u32[]{:S(2)}) async-start(bf16[8,192,256]{2,1,0:T(8,128)(2,1)} %pad_maximum_fusion.11), calls=%async_computation | async-start | bytes 1572864 | tf_op jit(solution)/shard_map/all_to_all | solution.py:411
  140.5 12.4 %all-to-all-done.near_ref = bf16[8,192,256]{2,1,0:T(8,128)(2,1)S(1)} async-done(((bf16[8,192,256]{2,1,0:T(8,128)(2,1)}), bf16[8,192,256]{2,1,0:T(8,128)(2,1)S(1)}, u32[]{:S(2)}, u32[]{:S(2)}) %all-to-all-start) | async-done | bytes 786464 | tf_op jit(solution)/shard_map/all_to_all | solution.py:411
  154.8 3.2 fusion
  160.8 14.0 %attend.1 = (bf16[8,64,256]{2,1,0:T(8,128)(2,1)}, bf16[2048,4096]{1,0:T(8,128)(2,1)}, f32[8,8,256]{2,1,0:T(8,128)S(1)}) custom-call(s32[1]{0:T(128)} %copy.161.length_ref, s32[1]{0:T(128)} %bitcast.59.core_ref, bf16[8,192,256]{2,1,0:T(8,128)(2,1)S(1)} %all-to-all-done.near_ref, bf16[8,128,256]{2,1,0:T(8,128)(2,1)S(1)} %collective-permute-done.16.far_ref), custom_call_target="tpu_custom_call" | custom-call | tf_op jit(solution)/shard_map/attend/pallas_call | solution.py:209
  174.7 3.6 all-to-all-start.1
  178.3 3.9 fusion.145
  195.9 6.6 %all-to-all-start.2 = ((bf16[8,64,256]{2,1,0:T(8,128)(2,1)}), bf16[8,64,256]{2,1,0:T(8,128)(2,1)S(1)}, u32[]{:S(2)}, u32[]{:S(2)}) async-start(bf16[8,64,256]{2,1,0:T(8,128)(2,1)} %bitcast.85), calls=%async_computation.2 | async-start | bytes 524288 | tf_op jit(solution)/shard_map/all_to_all | solution.py:432
  203.5 6.6 %all-to-all-done.2.do_ref = bf16[8,64,256]{2,1,0:T(8,128)(2,1)S(1)} async-done(((bf16[8,64,256]{2,1,0:T(8,128)(2,1)}), bf16[8,64,256]{2,1,0:T(8,128)(2,1)S(1)}, u32[]{:S(2)}, u32[]{:S(2)}) %all-to-all-start.2) | async-done | bytes 262176 | tf_op jit(solution)/shard_map/all_to_all | solution.py:432
  210.1 18.3 %attend_back.1 = (bf16[8,64,256]{2,1,0:T(8,128)(2,1)S(1)}, bf16[2,8,64,256]{3,2,1,0:T(8,128)(2,1)S(1)}, bf16[2,8,64,256]{3,2,1,0:T(8,128)(2,1)S(1)}) custom-call(bf16[8,192,256]{2,1,0:T(8,128)(2,1)S(1)} %all-to-all-done.near_ref, bf16[8,128,256]{2,1,0:T(8,128)(2,1)S(1)} %collective-permute-done.16.far_ref, bf16[2048,4096]{1,0:T(8,128)(2,1)} %get-tuple-element.26.e_ref, ...), custom_call_target="tpu_custom_call" | custom-call | tf_op jit(solution)/shard_map/attend_back/pallas_call | solution.py:296
  232.7 2.9 fusion.135
  237.2 6.0 %reshape_reshape.15 = f32[8,64,4,512]{3,2,1,0:T(4,128)} reshape(f32[512,2048]{1,0:T(8,128)} %fusion.135) | data formatting | bytes 8388608 | tf_op jit(solution)/shard_map/reshape;reshape | solution.py:438
  243.2 5.5 %copy.84 = f32[8,4,64,512]{3,2,1,0:T(8,128)} copy(f32[8,4,64,512]{3,1,2,0:T(4,128)} %bitcast.433) | data formatting | bytes 8388608 | tf_op jit(solution)/shard_map/transpose | solution.py:438
  253.6 4.2 all-to-all-start.3
  258.2 8.6 %pad_maximum_fusion = f32[2,4,576,512]{3,2,1,0:T(8,128)} fusion(f32[2,4,256,512]{3,2,1,0:T(8,128)} %fusion.101, f32[2,4,256,512]{3,2,1,0:T(8,128)} %bitcast.434, f32[2,4,64,512]{3,2,1,0:T(8,128)S(1)} %bitcast.457), kind=kLoop, calls=%fused_computation | loop fusion | flops 4718592 | bytes 18874368 | tf_op jit(solution)/shard_map/concatenate | solution.py:440
  266.7 4.1 dynamic-slice_convert_fusion.1
  277.3 3.6 fusion.25
  283.7 4.5 collective-permute-start.25
  291.6 11.9 %multiply_reduce_fusion = (f32[2048]{0:T(1024)S(1)}, f32[256]{0:T(256)S(1)}, f32[256]{0:T(256)S(1)}, f32[256,2048]{1,0:T(8,128)S(1)}) fusion(f32[256,2048]{1,0:T(8,128)S(1)} %copy-done.1, f32[256]{0:T(256)S(1)} %add_rsqrt_fusion.2, f32[256]{0:T(256)S(1)} %broadcast_multiply_fusion.2, f32[2048]{0:T(1024)S(1)} %bitcast.514, f32[256]{0:T(256)S(1)} %copy-done.102, ...), kind=kLoop, calls=%fused_computation.60 | loop fusion | flops 30930432 | bytes 5370880 | tf_op jit(solution)/shard_map/reduce_sum | solution.py:93
  311.5 5.4 %collective-permute-start.27 = (bf16[1,256]{1,0:T(2,128)(2,1)S(1)}, bf16[1,256]{1,0:T(2,128)(2,1)S(1)}, u32[]{:S(2)}, u32[]{:S(2)}) collective-permute-start(bf16[1,256]{1,0:T(2,128)(2,1)S(1)} %get-tuple-element.136), channel_id=1, source_target_pairs={{0,8},{1,9},{2,10},{3,11},{4,12},{5,13},{6,14},{7,15},{8,16},{9,17... | collective-permute-start | bytes 1544 | tf_op jit(solution)/shard_map/ppermute | solution.py:53
  317.8 6.0 %reshape_reshape.13 = f32[8,64,4,512]{3,2,1,0:T(4,128)} reshape(f32[512,2048]{1,0:T(8,128)} %fusion.166) | data formatting | bytes 8388608 | tf_op jit(solution)/shard_map/reshape;reshape | solution.py:438
  323.8 5.6 %copy.78 = f32[8,64,4,512]{3,1,2,0:T(8,128)} copy(f32[8,64,4,512]{3,2,1,0:T(4,128)} %reshape_reshape.13) | data formatting | bytes 8388608 | tf_op jit(solution)/shard_map/reshape;reshape | solution.py:438
  341.2 4.9 copy-done.7
  348.3 3.8 convert_add_fusion.1
  354.6 4.6 collective-permute-start.44
  359.1 12.1 %collective-permute-done.42 = bf16[2,288,512]{2,1,0:T(8,128)(2,1)S(1)} collective-permute-done((bf16[2,288,512]{2,1,0:T(8,128)(2,1)S(1)}, bf16[2,288,512]{2,1,0:T(8,128)(2,1)S(1)}, u32[]{:S(2)}, u32[]{:S(2)}) %collective-permute-start.42) | collective-permute-done | bytes 589856 | tf_op jit(solution)/shard_map/ppermute | solution.py:53
  371.2 13.5 %collective-permute-done.44 = bf16[2,288,512]{2,1,0:T(8,128)(2,1)S(1)} collective-permute-done((bf16[2,288,512]{2,1,0:T(8,128)(2,1)S(1)}, bf16[2,288,512]{2,1,0:T(8,128)(2,1)S(1)}, u32[]{:S(2)}, u32[]{:S(2)}) %collective-permute-start.44) | collective-permute-done | bytes 589856 | tf_op jit(solution)/shard_map/ppermute | solution.py:53
  386.5 7.1 %collective-permute-done.45 = bf16[288,512]{1,0:T(8,128)(2,1)S(1)} collective-permute-done((bf16[288,512]{1,0:T(8,128)(2,1)S(1)}, bf16[288,512]{1,0:T(8,128)(2,1)S(1)}, u32[]{:S(2)}, u32[]{:S(2)}) %collective-permute-start.45) | collective-permute-done | bytes 294944 | tf_op jit(solution)/shard_map/ppermute | solution.py:53
  403.7 5.2 %convert_add_fusion = f32[2,4,416,512]{3,2,1,0:T(8,128)S(1)} fusion(bf16[2,4,416,512]{3,2,1,0:T(8,128)(2,1)} %collective-permute-done.28, f32[2,4,832,512]{3,2,1,0:T(8,128)} %copy-done.7, s32[]{:T(128)S(6)} %select_n.250), kind=kLoop, calls=%fused_computation.1 | loop fusion | flops 3407872 | bytes 17039364 | tf_op jit(solution)/shard_map/add | solution.py:139
  415.7 3.1 collective-permute-start.31
  419.4 3.1 collective-permute-start.50
  430.5 4.0 collective-permute-done.29
  434.5 19.4 %collective-permute-done.31 = bf16[2,416,512]{2,1,0:T(8,128)(2,1)S(1)} collective-permute-done((bf16[2,416,512]{2,1,0:T(8,128)(2,1)}, bf16[2,416,512]{2,1,0:T(8,128)(2,1)S(1)}, u32[]{:S(2)}, u32[]{:S(2)}) %collective-permute-start.31) | collective-permute-done | bytes 852000 | tf_op jit(solution)/shard_map/ppermute | solution.py:53
  457.1 9.1 %collective-permute-done.32 = bf16[416,512]{1,0:T(8,128)(2,1)S(1)} collective-permute-done((bf16[416,512]{1,0:T(8,128)(2,1)S(1)}, bf16[416,512]{1,0:T(8,128)(2,1)S(1)}, u32[]{:S(2)}, u32[]{:S(2)}) %collective-permute-start.32) | collective-permute-done | bytes 426016 | tf_op jit(solution)/shard_map/ppermute | solution.py:53
  466.9 3.9 collective-permute-start.35
  474.9 5.0 collective-permute-done.36
  481.3 5.7 %collective-permute-start.53 = (bf16[288,512]{1,0:T(8,128)(2,1)S(1)}, bf16[288,512]{1,0:T(8,128)(2,1)S(1)}, u32[]{:S(2)}, u32[]{:S(2)}) collective-permute-start(bf16[288,512]{1,0:T(8,128)(2,1)S(1)} %bitcast.496), channel_id=1, source_target_pairs={{0,8},{1,9},{2,10},{3,11},{4,12},{5,13},{6,14},{7,15},{8,0},{9,1},... | collective-permute-start | bytes 884744 | tf_op jit(solution)/shard_map/ppermute | solution.py:53
  488.7 5.4 %collective-permute-done.38 = bf16[104,512]{1,0:T(8,128)(2,1)S(1)} collective-permute-done((bf16[104,512]{1,0:T(8,128)(2,1)S(1)}, bf16[104,512]{1,0:T(8,128)(2,1)S(1)}, u32[]{:S(2)}, u32[]{:S(2)}) %collective-permute-start.38) | collective-permute-done | bytes 106528 | tf_op jit(solution)/shard_map/ppermute | solution.py:53
  (593 shorter events, 198.6 us)
Async XLA Ops:
  3.9 11.0 %collective-permute-start = (bf16[72,512]{1,0:T(8,128)(2,1)S(1)}, bf16[72,512]{1,0:T(8,128)(2,1)S(1)}, u32[]{:S(2)}, u32[]{:S(2)}) collective-permute-start(bf16[72,512]{1,0:T(8,128)(2,1)S(1)} %fusion.119), channel_id=1, source_target_pairs={{0,4},{1,5},{2,6},{3,7},{4,0},{5,1},{6,2},{7,3},{8,12},{9,13},{10,... | collective-permute-start | bytes 221192 | tf_op jit(solution)/shard_map/ppermute | solution.py:53
  12.0 12.2 %collective-permute-start.17 = (bf16[288,512]{1,0:T(8,128)(2,1)}, bf16[288,512]{1,0:T(8,128)(2,1)S(1)}, u32[]{:S(2)}, u32[]{:S(2)}) collective-permute-start(bf16[288,512]{1,0:T(8,128)(2,1)} %constant_dynamic-slice_fusion.3), channel_id=1, source_target_pairs={{0,4},{1,5},{2,6},{3,7},{4,0},{5,1},{6,2},{7,3},{8,12},{9,13},{10,... | collective-permute-start | bytes 884744 | tf_op jit(solution)/shard_map/ppermute | solution.py:53
  13.0 21.8 %collective-permute-start.6 = (bf16[336,512]{1,0:T(8,128)(2,1)}, bf16[336,512]{1,0:T(8,128)(2,1)S(1)}, u32[]{:S(2)}, u32[]{:S(2)}) collective-permute-start(bf16[336,512]{1,0:T(8,128)(2,1)} %constant_dynamic-slice_fusion.5), channel_id=1, source_target_pairs={{0,4},{1,5},{2,6},{3,7},{4,0},{5,1},{6,2},{7,3},{8,12},{9,13},{10,... | collective-permute-start | bytes 1032200 | tf_op jit(solution)/shard_map/ppermute | solution.py:53
  15.0 6.4 %collective-permute-start.2 = (bf16[2,72,512]{2,1,0:T(8,128)(2,1)S(1)}, bf16[2,72,512]{2,1,0:T(8,128)(2,1)S(1)}, u32[]{:S(2)}, u32[]{:S(2)}) collective-permute-start(bf16[2,72,512]{2,1,0:T(8,128)(2,1)S(1)} %maximum_select_fusion.10), channel_id=1, source_target_pairs={{0,1},{1,2},{2,3},{3,0},{4,5},{5,6},{6,7},{7,4},{8,9},{9,10},{10,1... | collective-permute-start | bytes 442376 | tf_op jit(solution)/shard_map/ppermute | solution.py:53
  24.3 15.1 %collective-permute-start.19 = (bf16[2,288,512]{2,1,0:T(8,128)(2,1)S(1)}, bf16[2,288,512]{2,1,0:T(8,128)(2,1)S(1)}, u32[]{:S(2)}, u32[]{:S(2)}) collective-permute-start(bf16[2,288,512]{2,1,0:T(8,128)(2,1)S(1)} %maximum_select_fusion.7), channel_id=1, source_target_pairs={{0,1},{1,2},{2,3},{3,0},{4,5},{5,6},{6,7},{7,4},{8,9},{9,10},{10,1... | collective-permute-start | bytes 1769480 | tf_op jit(solution)/shard_map/ppermute | solution.py:53
  27.0 13.2 %collective-permute-start.5 = (bf16[4,2,72,512]{3,2,0,1:T(8,128)(2,1)S(1)}, bf16[4,2,72,512]{3,2,0,1:T(8,128)(2,1)S(1)}, u32[]{:S(2)}, u32[]{:S(2)}) collective-permute-start(bf16[4,2,72,512]{3,2,0,1:T(8,128)(2,1)S(1)} %constant_dynamic-slice_fusion.6), channel_id=1, source_target_pairs={{0,8},{1,9},{2,10},{3,11},{4,12},{5,13},{6,14},{7,15},{8,0},{9,1},... | collective-permute-start | bytes 1769480 | tf_op jit(solution)/shard_map/ppermute | solution.py:53
  31.3 15.1 %collective-permute-start.18 = (bf16[2,288,512]{2,1,0:T(8,128)(2,1)S(1)}, bf16[2,288,512]{2,1,0:T(8,128)(2,1)S(1)}, u32[]{:S(2)}, u32[]{:S(2)}) collective-permute-start(bf16[2,288,512]{2,1,0:T(8,128)(2,1)S(1)} %maximum_select_fusion.7), channel_id=1, source_target_pairs={{0,3},{1,0},{2,1},{3,2},{4,7},{5,4},{6,5},{7,6},{8,11},{9,8},{10,9... | collective-permute-start | bytes 1769480 | tf_op jit(solution)/shard_map/ppermute | solution.py:53
  35.8 19.0 %collective-permute-start.8 = (bf16[2,336,512]{2,1,0:T(8,128)(2,1)}, bf16[2,336,512]{2,1,0:T(8,128)(2,1)}, u32[]{:S(2)}, u32[]{:S(2)}) collective-permute-start(bf16[2,336,512]{2,1,0:T(8,128)(2,1)} %maximum_select_fusion.5), channel_id=1, source_target_pairs={{0,1},{1,2},{2,3},{3,0},{4,5},{5,6},{6,7},{7,4},{8,9},{9,10},{10,1... | collective-permute-start | bytes 2064392 | tf_op jit(solution)/shard_map/ppermute | solution.py:53
  35.8 25.5 %collective-permute-start.7 = (bf16[2,336,512]{2,1,0:T(8,128)(2,1)}, bf16[2,336,512]{2,1,0:T(8,128)(2,1)}, u32[]{:S(2)}, u32[]{:S(2)}) collective-permute-start(bf16[2,336,512]{2,1,0:T(8,128)(2,1)} %maximum_select_fusion.5), channel_id=1, source_target_pairs={{0,3},{1,0},{2,1},{3,2},{4,7},{5,4},{6,5},{7,6},{8,11},{9,8},{10,9... | collective-permute-start | bytes 2064392 | tf_op jit(solution)/shard_map/ppermute | solution.py:53
  40.2 52.4 %collective-permute-start.20 = (bf16[2,144,512]{2,1,0:T(8,128)(2,1)}, bf16[2,144,512]{2,1,0:T(8,128)(2,1)}, u32[]{:S(2)}, u32[]{:S(2)}) collective-permute-start(bf16[2,144,512]{2,1,0:T(8,128)(2,1)} %slice.556), channel_id=1, source_target_pairs={{0,1},{1,2},{2,3},{3,0},{4,5},{5,6},{6,7},{7,4},{8,9},{9,10},{10,1... | collective-permute-start | bytes 884744 | tf_op jit(solution)/shard_map/ppermute | solution.py:53
  47.2 45.4 %collective-permute-start.21 = (bf16[2,144,512]{2,1,0:T(8,128)(2,1)}, bf16[2,144,512]{2,1,0:T(8,128)(2,1)}, u32[]{:S(2)}, u32[]{:S(2)}) collective-permute-start(bf16[2,144,512]{2,1,0:T(8,128)(2,1)} %slice.557), channel_id=1, source_target_pairs={{0,3},{1,0},{2,1},{3,2},{4,7},{5,4},{6,5},{7,6},{8,11},{9,8},{10,9... | collective-permute-start | bytes 884744 | tf_op jit(solution)/shard_map/ppermute | solution.py:53
  55.8 12.6 %collective-permute-start.9 = (bf16[2,168,512]{2,1,0:T(8,128)(2,1)S(1)}, bf16[2,168,512]{2,1,0:T(8,128)(2,1)S(1)}, u32[]{:S(2)}, u32[]{:S(2)}) collective-permute-start(bf16[2,168,512]{2,1,0:T(8,128)(2,1)S(1)} %slice.517), channel_id=1, source_target_pairs={{0,1},{1,2},{2,3},{3,0},{4,5},{5,6},{6,7},{7,4},{8,9},{9,10},{10,1... | collective-permute-start | bytes 1032200 | tf_op jit(solution)/shard_map/ppermute | solution.py:53
  62.3 12.6 %collective-permute-start.10 = (bf16[2,168,512]{2,1,0:T(8,128)(2,1)S(1)}, bf16[2,168,512]{2,1,0:T(8,128)(2,1)S(1)}, u32[]{:S(2)}, u32[]{:S(2)}) collective-permute-start(bf16[2,168,512]{2,1,0:T(8,128)(2,1)S(1)} %slice.518), channel_id=1, source_target_pairs={{0,3},{1,0},{2,1},{3,2},{4,7},{5,4},{6,5},{7,6},{8,11},{9,8},{10,9... | collective-permute-start | bytes 1032200 | tf_op jit(solution)/shard_map/ppermute | solution.py:53
  81.8 22.4 %collective-permute-start.11 = (bf16[4,2,336,512]{3,2,0,1:T(8,128)(2,1)}, bf16[4,2,336,512]{3,2,0,1:T(8,128)(2,1)}, u32[]{:S(2)}, u32[]{:S(2)}) collective-permute-start(bf16[4,2,336,512]{3,2,0,1:T(8,128)(2,1)} %constant_dynamic-slice_fusion.4), channel_id=1, source_target_pairs={{0,8},{1,9},{2,10},{3,11},{4,12},{5,13},{6,14},{7,15},{8,0},{9,1},... | collective-permute-start | bytes 8257544 | tf_op jit(solution)/shard_map/ppermute | solution.py:53
  85.4 25.3 %collective-permute-start.12 = (bf16[1,512]{1,0:T(2,128)(2,1)}, bf16[1,512]{1,0:T(2,128)(2,1)S(1)}, u32[]{:S(2)}, u32[]{:S(2)}) collective-permute-start(bf16[1,512]{1,0:T(2,128)(2,1)} %get-tuple-element.133), channel_id=1, source_target_pairs={{0,8},{1,9},{2,10},{3,11},{4,12},{5,13},{6,14},{7,15},{8,16},{9,17... | collective-permute-start | bytes 3080 | tf_op jit(solution)/shard_map/ppermute | solution.py:53
  89.7 20.9 %collective-permute-start.13 = (bf16[1,512]{1,0:T(2,128)(2,1)}, bf16[1,512]{1,0:T(2,128)(2,1)S(1)}, u32[]{:S(2)}, u32[]{:S(2)}) collective-permute-start(bf16[1,512]{1,0:T(2,128)(2,1)} %get-tuple-element.134), channel_id=1, source_target_pairs={{8,0},{9,1},{10,2},{11,3},{12,4},{13,5},{14,6},{15,7},{16,8},{17,9... | collective-permute-start | bytes 3080 | tf_op jit(solution)/shard_map/ppermute | solution.py:53
  103.8 51.0 %collective-permute-start.22 = (bf16[4,2,288,512]{3,2,1,0:T(8,128)(2,1)}, bf16[4,2,288,512]{3,2,1,0:T(8,128)(2,1)}, u32[]{:S(2)}, u32[]{:S(2)}) collective-permute-start(bf16[4,2,288,512]{3,2,1,0:T(8,128)(2,1)} %constant_dynamic-slice_fusion.2), channel_id=1, source_target_pairs={{0,8},{1,9},{2,10},{3,11},{4,12},{5,13},{6,14},{7,15},{8,0},{9,1},... | collective-permute-start | bytes 7077896 | tf_op jit(solution)/shard_map/ppermute | solution.py:53
  115.6 7.2 %collective-permute-start.14 = (bf16[4,2048]{1,0:T(4,128)(2,1)S(1)}, bf16[4,2048]{1,0:T(4,128)(2,1)S(1)}, u32[]{:S(2)}, u32[]{:S(2)}) collective-permute-start(bf16[4,2048]{1,0:T(4,128)(2,1)S(1)} %get-tuple-element.116), channel_id=1, source_target_pairs={{0,8},{1,9},{2,10},{3,11},{4,12},{5,13},{6,14},{7,15},{8,16},{9,17... | collective-permute-start | bytes 49160 | tf_op jit(solution)/shard_map/ppermute | solution.py:53
  120.8 6.6 %collective-permute-start.15 = (bf16[4,2048]{1,0:T(4,128)(2,1)S(1)}, bf16[4,2048]{1,0:T(4,128)(2,1)S(1)}, u32[]{:S(2)}, u32[]{:S(2)}) collective-permute-start(bf16[4,2048]{1,0:T(4,128)(2,1)S(1)} %get-tuple-element.117), channel_id=1, source_target_pairs={{8,0},{9,1},{10,2},{11,3},{12,4},{13,5},{14,6},{15,7},{16,8},{17,9... | collective-permute-start | bytes 49160 | tf_op jit(solution)/shard_map/ppermute | solution.py:53
  133.4 19.4 %all-to-all-start = ((bf16[8,192,256]{2,1,0:T(8,128)(2,1)}), bf16[8,192,256]{2,1,0:T(8,128)(2,1)S(1)}, u32[]{:S(2)}, u32[]{:S(2)}) async-start(bf16[8,192,256]{2,1,0:T(8,128)(2,1)} %pad_maximum_fusion.11), calls=%async_computation | async-start | bytes 1572864 | tf_op jit(solution)/shard_map/all_to_all | solution.py:411
  152.9 6.4 %collective-permute-start.16 = (bf16[8,128,256]{2,1,0:T(8,128)(2,1)S(1)}, bf16[8,128,256]{2,1,0:T(8,128)(2,1)S(1)}, u32[]{:S(2)}, u32[]{:S(2)}) collective-permute-start(bf16[8,128,256]{2,1,0:T(8,128)(2,1)S(1)} %slice.555), channel_id=1, source_target_pairs={{0,8},{1,9},{2,10},{3,11},{4,12},{5,13},{6,14},{7,15},{8,0},{9,1},... | collective-permute-start | bytes 1572872 | tf_op jit(solution)/shard_map/ppermute | solution.py:53
  174.7 13.4 %all-to-all-start.1 = ((bf16[8,64,256]{2,1,0:T(8,128)(2,1)}), bf16[8,64,256]{2,1,0:T(8,128)(2,1)S(1)}, u32[]{:S(2)}, u32[]{:S(2)}) async-start(bf16[8,64,256]{2,1,0:T(8,128)(2,1)} %get-tuple-element.25.o_ref), calls=%async_computation.1 | async-start | bytes 524288 | tf_op jit(solution)/shard_map/all_to_all | solution.py:414
  195.9 14.2 %all-to-all-start.2 = ((bf16[8,64,256]{2,1,0:T(8,128)(2,1)}), bf16[8,64,256]{2,1,0:T(8,128)(2,1)S(1)}, u32[]{:S(2)}, u32[]{:S(2)}) async-start(bf16[8,64,256]{2,1,0:T(8,128)(2,1)} %bitcast.85), calls=%async_computation.2 | async-start | bytes 524288 | tf_op jit(solution)/shard_map/all_to_all | solution.py:432
  230.1 21.4 %collective-permute-start.23 = (bf16[8,128,256]{2,1,0:T(8,128)(2,1)}, bf16[8,128,256]{2,1,0:T(8,128)(2,1)}, u32[]{:S(2)}, u32[]{:S(2)}) collective-permute-start(bf16[8,128,256]{2,1,0:T(8,128)(2,1)} %pad_maximum_fusion.13), channel_id=1, source_target_pairs={{0,8},{1,9},{2,10},{3,11},{4,12},{5,13},{6,14},{7,15},{8,0},{9,1},... | collective-permute-start | bytes 1572872 | tf_op jit(solution)/shard_map/ppermute | solution.py:53
  253.6 18.8 %all-to-all-start.3 = ((bf16[8,192,256]{2,1,0:T(8,128)(2,1)}), bf16[8,192,256]{2,1,0:T(8,128)(2,1)}, u32[]{:S(2)}, u32[]{:S(2)}) async-start(bf16[8,192,256]{2,1,0:T(8,128)(2,1)} %pad_maximum_fusion.12), calls=%async_computation.3 | async-start | bytes 1572864 | tf_op jit(solution)/shard_map/all_to_all | solution.py:447
  270.8 77.5 %collective-permute-start.41 = (bf16[2,4,288,512]{3,2,1,0:T(8,128)(2,1)}, bf16[2,4,288,512]{3,2,1,0:T(8,128)(2,1)}, u32[]{:S(2)}, u32[]{:S(2)}) collective-permute-start(bf16[2,4,288,512]{3,2,1,0:T(8,128)(2,1)} %dynamic-slice_convert_fusion.1), channel_id=1, source_target_pairs={{0,8},{1,9},{2,10},{3,11},{4,12},{5,13},{6,14},{7,15},{8,0},{9,1},... | collective-permute-start | bytes 7077896 | tf_op jit(solution)/shard_map/ppermute | solution.py:53
  280.9 10.6 %collective-permute-start.24 = (bf16[4,2048]{1,0:T(4,128)(2,1)S(1)}, bf16[4,2048]{1,0:T(4,128)(2,1)S(1)}, u32[]{:S(2)}, u32[]{:S(2)}) collective-permute-start(bf16[4,2048]{1,0:T(4,128)(2,1)S(1)} %get-tuple-element.114), channel_id=1, source_target_pairs={{8,0},{9,1},{10,2},{11,3},{12,4},{13,5},{14,6},{15,7},{16,8},{17,9... | collective-permute-start | bytes 49160 | tf_op jit(solution)/shard_map/ppermute | solution.py:53
  283.7 7.8 %collective-permute-start.25 = (bf16[4,2048]{1,0:T(4,128)(2,1)S(1)}, bf16[4,2048]{1,0:T(4,128)(2,1)S(1)}, u32[]{:S(2)}, u32[]{:S(2)}) collective-permute-start(bf16[4,2048]{1,0:T(4,128)(2,1)S(1)} %get-tuple-element.115), channel_id=1, source_target_pairs={{0,8},{1,9},{2,10},{3,11},{4,12},{5,13},{6,14},{7,15},{8,16},{9,17... | collective-permute-start | bytes 49160 | tf_op jit(solution)/shard_map/ppermute | solution.py:53
  309.6 19.8 %collective-permute-start.26 = (bf16[1,256]{1,0:T(2,128)(2,1)S(1)}, bf16[1,256]{1,0:T(2,128)(2,1)S(1)}, u32[]{:S(2)}, u32[]{:S(2)}) collective-permute-start(bf16[1,256]{1,0:T(2,128)(2,1)S(1)} %get-tuple-element.135), channel_id=1, source_target_pairs={{8,0},{9,1},{10,2},{11,3},{12,4},{13,5},{14,6},{15,7},{16,8},{17,9... | collective-permute-start | bytes 1544 | tf_op jit(solution)/shard_map/ppermute | solution.py:53
  311.5 17.9 %collective-permute-start.27 = (bf16[1,256]{1,0:T(2,128)(2,1)S(1)}, bf16[1,256]{1,0:T(2,128)(2,1)S(1)}, u32[]{:S(2)}, u32[]{:S(2)}) collective-permute-start(bf16[1,256]{1,0:T(2,128)(2,1)S(1)} %get-tuple-element.136), channel_id=1, source_target_pairs={{0,8},{1,9},{2,10},{3,11},{4,12},{5,13},{6,14},{7,15},{8,16},{9,17... | collective-permute-start | bytes 1544 | tf_op jit(solution)/shard_map/ppermute | solution.py:53
  348.3 55.4 %collective-permute-start.28 = (bf16[2,4,416,512]{3,2,1,0:T(8,128)(2,1)}, bf16[2,4,416,512]{3,2,1,0:T(8,128)(2,1)}, u32[]{:S(2)}, u32[]{:S(2)}) collective-permute-start(bf16[2,4,416,512]{3,2,1,0:T(8,128)(2,1)} %dynamic-slice_convert_fusion), channel_id=1, source_target_pairs={{0,8},{1,9},{2,10},{3,11},{4,12},{5,13},{6,14},{7,15},{8,0},{9,1},... | collective-permute-start | bytes 10223624 | tf_op jit(solution)/shard_map/ppermute | solution.py:53
  354.5 16.7 %collective-permute-start.42 = (bf16[2,288,512]{2,1,0:T(8,128)(2,1)S(1)}, bf16[2,288,512]{2,1,0:T(8,128)(2,1)S(1)}, u32[]{:S(2)}, u32[]{:S(2)}) collective-permute-start(bf16[2,288,512]{2,1,0:T(8,128)(2,1)S(1)} %get-tuple-element.88), channel_id=1, source_target_pairs={{0,1},{1,2},{2,3},{3,0},{4,5},{5,6},{6,7},{7,4},{8,9},{9,10},{10,1... | collective-permute-start | bytes 1769480 | tf_op jit(solution)/shard_map/ppermute | solution.py:53
  354.6 30.1 %collective-permute-start.44 = (bf16[2,288,512]{2,1,0:T(8,128)(2,1)S(1)}, bf16[2,288,512]{2,1,0:T(8,128)(2,1)S(1)}, u32[]{:S(2)}, u32[]{:S(2)}) collective-permute-start(bf16[2,288,512]{2,1,0:T(8,128)(2,1)S(1)} %get-tuple-element.89), channel_id=1, source_target_pairs={{0,2},{1,3},{2,0},{3,1},{4,6},{5,7},{6,4},{7,5},{8,10},{9,11},{10,... | collective-permute-start | bytes 1769480 | tf_op jit(solution)/shard_map/ppermute | solution.py:53
  359.1 25.6 %collective-permute-start.43 = (bf16[2,288,512]{2,1,0:T(8,128)(2,1)S(1)}, bf16[2,288,512]{2,1,0:T(8,128)(2,1)S(1)}, u32[]{:S(2)}, u32[]{:S(2)}) collective-permute-start(bf16[2,288,512]{2,1,0:T(8,128)(2,1)S(1)} %get-tuple-element.90), channel_id=1, source_target_pairs={{0,3},{1,0},{2,1},{3,2},{4,7},{5,4},{6,5},{7,6},{8,11},{9,8},{10,9... | collective-permute-start | bytes 1769480 | tf_op jit(solution)/shard_map/ppermute | solution.py:53
  386.3 7.2 %collective-permute-start.45 = (bf16[288,512]{1,0:T(8,128)(2,1)S(1)}, bf16[288,512]{1,0:T(8,128)(2,1)S(1)}, u32[]{:S(2)}, u32[]{:S(2)}) collective-permute-start(bf16[288,512]{1,0:T(8,128)(2,1)S(1)} %fusion.95), channel_id=1, source_target_pairs={{0,4},{1,5},{2,6},{3,7},{4,0},{5,1},{6,2},{7,3},{8,12},{9,13},{10,... | collective-permute-start | bytes 884744 | tf_op jit(solution)/shard_map/ppermute | solution.py:53
  393.7 5.7 %collective-permute-start.46 = (bf16[72,512]{1,0:T(8,128)(2,1)S(1)}, bf16[72,512]{1,0:T(8,128)(2,1)S(1)}, u32[]{:S(2)}, u32[]{:S(2)}) collective-permute-start(bf16[72,512]{1,0:T(8,128)(2,1)S(1)} %get-tuple-element.124), channel_id=1, source_target_pairs={{0,32},{1,33},{2,34},{3,35},{4,36},{5,37},{6,38},{7,39},{8,40},{9,... | collective-permute-start | bytes 221192 | tf_op jit(solution)/shard_map/ppermute | solution.py:53
  395.8 5.4 %collective-permute-start.48 = (bf16[72,512]{1,0:T(8,128)(2,1)S(1)}, bf16[72,512]{1,0:T(8,128)(2,1)S(1)}, u32[]{:S(2)}, u32[]{:S(2)}) collective-permute-start(bf16[72,512]{1,0:T(8,128)(2,1)S(1)} %get-tuple-element.125), channel_id=1, source_target_pairs={{0,64},{1,65},{2,66},{3,67},{4,68},{5,69},{6,70},{7,71},{8,72},{9,... | collective-permute-start | bytes 221192 | tf_op jit(solution)/shard_map/ppermute | solution.py:53
  402.6 16.2 %collective-permute-start.49 = (bf16[72,512]{1,0:T(8,128)(2,1)S(1)}, bf16[72,512]{1,0:T(8,128)(2,1)S(1)}, u32[]{:S(2)}, u32[]{:S(2)}) collective-permute-start(bf16[72,512]{1,0:T(8,128)(2,1)S(1)} %add_convert_fusion.4), channel_id=1, source_target_pairs={{0,16},{1,17},{2,18},{3,19},{4,20},{5,21},{6,22},{7,23},{8,24},{9,... | collective-permute-start | bytes 221192 | tf_op jit(solution)/shard_map/ppermute | solution.py:53
  413.2 21.3 %collective-permute-start.29 = (bf16[2,416,512]{2,1,0:T(8,128)(2,1)}, bf16[2,416,512]{2,1,0:T(8,128)(2,1)S(1)}, u32[]{:S(2)}, u32[]{:S(2)}) collective-permute-start(bf16[2,416,512]{2,1,0:T(8,128)(2,1)} %get-tuple-element.78), channel_id=1, source_target_pairs={{0,1},{1,2},{2,3},{3,0},{4,5},{5,6},{6,7},{7,4},{8,9},{9,10},{10,1... | collective-permute-start | bytes 2555912 | tf_op jit(solution)/shard_map/ppermute | solution.py:53
  415.7 38.2 %collective-permute-start.31 = (bf16[2,416,512]{2,1,0:T(8,128)(2,1)}, bf16[2,416,512]{2,1,0:T(8,128)(2,1)S(1)}, u32[]{:S(2)}, u32[]{:S(2)}) collective-permute-start(bf16[2,416,512]{2,1,0:T(8,128)(2,1)} %get-tuple-element.79), channel_id=1, source_target_pairs={{0,2},{1,3},{2,0},{3,1},{4,6},{5,7},{6,4},{7,5},{8,10},{9,11},{10,... | collective-permute-start | bytes 2555912 | tf_op jit(solution)/shard_map/ppermute | solution.py:53
  418.8 36.2 %collective-permute-start.30 = (bf16[2,416,512]{2,1,0:T(8,128)(2,1)S(1)}, bf16[2,416,512]{2,1,0:T(8,128)(2,1)S(1)}, u32[]{:S(2)}, u32[]{:S(2)}) collective-permute-start(bf16[2,416,512]{2,1,0:T(8,128)(2,1)S(1)} %get-tuple-element.80), channel_id=1, source_target_pairs={{0,3},{1,0},{2,1},{3,2},{4,7},{5,4},{6,5},{7,6},{8,11},{9,8},{10,9... | collective-permute-start | bytes 2555912 | tf_op jit(solution)/shard_map/ppermute | solution.py:53
  422.6 7.3 %collective-permute-start.52 = (bf16[72,512]{1,0:T(8,128)(2,1)S(1)}, bf16[72,512]{1,0:T(8,128)(2,1)S(1)}, u32[]{:S(2)}, u32[]{:S(2)}) collective-permute-start(bf16[72,512]{1,0:T(8,128)(2,1)S(1)} %get-tuple-element.64), channel_id=1, source_target_pairs={{0,32},{1,33},{2,34},{3,35},{4,36},{5,37},{6,38},{7,39},{8,40},{9,... | collective-permute-start | bytes 221192 | tf_op jit(solution)/shard_map/ppermute | solution.py:53
  457.0 9.3 %collective-permute-start.32 = (bf16[416,512]{1,0:T(8,128)(2,1)S(1)}, bf16[416,512]{1,0:T(8,128)(2,1)S(1)}, u32[]{:S(2)}, u32[]{:S(2)}) collective-permute-start(bf16[416,512]{1,0:T(8,128)(2,1)S(1)} %fusion.85), channel_id=1, source_target_pairs={{0,4},{1,5},{2,6},{3,7},{4,0},{5,1},{6,2},{7,3},{8,12},{9,13},{10,... | collective-permute-start | bytes 1277960 | tf_op jit(solution)/shard_map/ppermute | solution.py:53
  466.9 7.2 %collective-permute-start.35 = (bf16[104,512]{1,0:T(8,128)(2,1)S(1)}, bf16[104,512]{1,0:T(8,128)(2,1)S(1)}, u32[]{:S(2)}, u32[]{:S(2)}) collective-permute-start(bf16[104,512]{1,0:T(8,128)(2,1)S(1)} %get-tuple-element.119), channel_id=1, source_target_pairs={{0,64},{1,65},{2,66},{3,67},{4,68},{5,69},{6,70},{7,71},{8,72},{9,... | collective-permute-start | bytes 319496 | tf_op jit(solution)/shard_map/ppermute | solution.py:53
  479.9 8.8 %collective-permute-start.37 = (bf16[104,512]{1,0:T(8,128)(2,1)S(1)}, bf16[104,512]{1,0:T(8,128)(2,1)S(1)}, u32[]{:S(2)}, u32[]{:S(2)}) collective-permute-start(bf16[104,512]{1,0:T(8,128)(2,1)S(1)} %get-tuple-element.66), channel_id=1, source_target_pairs={{0,96},{1,97},{2,98},{3,99},{4,100},{5,101},{6,102},{7,103},{8,104... | collective-permute-start | bytes 319496 | tf_op jit(solution)/shard_map/ppermute | solution.py:53
  481.3 16.3 %collective-permute-start.53 = (bf16[288,512]{1,0:T(8,128)(2,1)S(1)}, bf16[288,512]{1,0:T(8,128)(2,1)S(1)}, u32[]{:S(2)}, u32[]{:S(2)}) collective-permute-start(bf16[288,512]{1,0:T(8,128)(2,1)S(1)} %bitcast.496), channel_id=1, source_target_pairs={{0,8},{1,9},{2,10},{3,11},{4,12},{5,13},{6,14},{7,15},{8,0},{9,1},... | collective-permute-start | bytes 884744 | tf_op jit(solution)/shard_map/ppermute | solution.py:53
  487.0 8.0 %collective-permute-start.39 = (bf16[104,512]{1,0:T(8,128)(2,1)S(1)}, bf16[104,512]{1,0:T(8,128)(2,1)S(1)}, u32[]{:S(2)}, u32[]{:S(2)}) collective-permute-start(bf16[104,512]{1,0:T(8,128)(2,1)S(1)} %get-tuple-element.66), channel_id=1, source_target_pairs={{0,32},{1,33},{2,34},{3,35},{4,36},{5,37},{6,38},{7,39},{8,40},{9,... | collective-permute-start | bytes 319496 | tf_op jit(solution)/shard_map/ppermute | solution.py:53
  487.5 6.6 %collective-permute-start.38 = (bf16[104,512]{1,0:T(8,128)(2,1)S(1)}, bf16[104,512]{1,0:T(8,128)(2,1)S(1)}, u32[]{:S(2)}, u32[]{:S(2)}) collective-permute-start(bf16[104,512]{1,0:T(8,128)(2,1)S(1)} %get-tuple-element.66), channel_id=1, source_target_pairs={{0,64},{1,65},{2,66},{3,67},{4,68},{5,69},{6,70},{7,71},{8,72},{9,... | collective-permute-start | bytes 319496 | tf_op jit(solution)/shard_map/ppermute | solution.py:53
  (143 other events, 1382.3 us)

commit v2 on v1

v2 whole, which is shorter than its diff:
```python
import functools

import jax
import jax.numpy as jnp
import numpy as np
from jax import lax
from jax.experimental import pallas as pl
from jax.experimental.pallas import tpu as pltpu
from jax.sharding import Mesh
from jax.sharding import PartitionSpec as P

HEADS = 8
HEAD = 64
EPSILON = 1e-06
AXES = ("y", "xh", "core", "xl", "z")
SIZES = (4, 2, 2, 2, 4)
CTX = ("y", "xh", "core")
CHIPS = ("y", "xh")
WT = ("xl", "z")
LOG2E = 1.4426950408889634
BF = jnp.bfloat16
F32 = jnp.float32


def moves(target):
    pairs = []
    for source in range(int(np.prod(SIZES))):
        place = [int(v) for v in np.unravel_index(source, SIZES)]
        goal = target(*place)
        if goal is not None:
            pairs.append((source, int(np.ravel_multi_index(tuple(goal), SIZES))))
    return pairs


def shift(dy=0, dxh=0, dc=0, dxl=0, dz=0):
    return moves(
        lambda y, xh, c, xl, z: (
            (y + dy) % 4, (xh + dxh) % 2, (c + dc) % 2, (xl + dxl) % 2, (z + dz) % 4,
        )
    )


def along(step):
    def target(y, xh, c, xl, z):
        place = y * 4 + xh * 2 + c + step
        if place < 0 or place > 15:
            return None
        return (place // 4, place // 2 % 2, place % 2, xl, z)
    return moves(target)


def send(value, pairs):
    return lax.ppermute(value, AXES, pairs)


def matmul(left, right):
    return jnp.dot(left, right, preferred_element_type=F32)


def contract(left, right, ldim, rdim):
    return lax.dot_general(
        left, right, (((ldim,), (rdim,)), ((), ())), preferred_element_type=F32
    )


def smooth_unit(value):
    return value * jax.nn.sigmoid(value)


def smooth_slope(value):
    sigma = jax.nn.sigmoid(value)
    return sigma * (1.0 + value * (1.0 - sigma))


def attend_kernel(chips, rows, length_ref, core_ref, near_ref, far_ref, o_ref, e_ref, l_ref,
                  keys_ref, values_ref):
    step = pl.program_id(0)
    span = chips * rows
    aug = 2 * HEAD

    @pl.when(step == 0)
    def _():
        length = length_ref[0]
        core = core_ref[0]
        ones = jnp.ones((16, rows), F32)
        for side in range(2):
            source = near_ref if side == 0 else far_ref
            base = HEAD if side == 0 else 0
            owner = core if side == 0 else 1 - core
            for chip in range(chips):
                cols = slice(side * span + chip * rows, side * span + (chip + 1) * rows)
                key = source[chip, base:base + HEAD, :]
                keys_ref[0:HEAD, cols] = key
                keys_ref[HEAD:aug, cols] = key
                place = (chip * 2 + owner) * rows + lax.broadcasted_iota(jnp.int32, (16, rows), 1)
                row = lax.broadcasted_iota(jnp.int32, (16, rows), 0)
                bias = jnp.where((place < length) | (row > 0), 0.0, -1e30)
                keys_ref[aug:aug + 16, cols] = bias.astype(BF)
                value = source[chip, base + HEAD:base + 2 * HEAD, :].astype(F32)
                stacked = jnp.concatenate([value, ones, jnp.zeros((48, rows), F32)], 0)
                values_ref[cols, :] = stacked.T.astype(BF)

    query = near_ref[step, 0:HEAD, :].astype(F32) * (LOG2E * HEAD ** -0.5)
    high = query.astype(BF)
    low = (query - high.astype(F32)).astype(BF)
    query = jnp.concatenate([high, low, jnp.ones((16, rows), BF)], 0)
    scores = contract(query, keys_ref[...], 0, 0)
    top = jnp.max(scores, 1, keepdims=True)
    expo = jnp.exp2(scores - top).astype(BF)
    e_ref[...] = expo
    out = matmul(expo, values_ref[...]).T
    inverse = 1.0 / out[HEAD:HEAD + 8]
    o_ref[0] = (out[0:HEAD] * inverse[0:1]).astype(BF)
    l_ref[0] = inverse


def attend(near, far, length, core):
    chips, _, rows = near.shape
    tokens = 2 * chips * rows
    return pl.pallas_call(
        functools.partial(attend_kernel, chips, rows),
        grid=(chips,),
        in_specs=[
            pl.BlockSpec(memory_space=pltpu.SMEM),
            pl.BlockSpec(memory_space=pltpu.SMEM),
            pl.BlockSpec(near.shape, lambda i: (0, 0, 0)),
            pl.BlockSpec(far.shape, lambda i: (0, 0, 0)),
        ],
        out_specs=[
            pl.BlockSpec((1, HEAD, rows), lambda i: (i, 0, 0)),
            pl.BlockSpec((rows, tokens), lambda i: (i, 0)),
            pl.BlockSpec((1, 8, rows), lambda i: (i, 0, 0)),
        ],
        out_shape=[
            jax.ShapeDtypeStruct((chips, HEAD, rows), BF),
            jax.ShapeDtypeStruct((chips * rows, tokens), BF),
            jax.ShapeDtypeStruct((chips, 8, rows), F32),
        ],
        scratch_shapes=[
            pltpu.VMEM((2 * HEAD + 16, tokens), BF),
            pltpu.VMEM((tokens, 2 * HEAD), BF),
        ],
        compiler_params=pltpu.CompilerParams(vmem_limit_bytes=48 * 2**20),
        cost_estimate=cost(14),
        name="attend",
    )(length, core, near, far)


def attend_back_kernel(chips, rows, near_ref, far_ref, e_ref, o_ref, l_ref, do_ref,
                       dq_ref, dk_ref, dv_ref, keys_ref, values_ref, dk_acc, dv_acc):
    step = pl.program_id(0)
    span = chips * rows

    @pl.when(step == 0)
    def _():
        row = lax.broadcasted_iota(jnp.int32, (16, rows), 0)
        ones = jnp.where(row < 3, 1.0, 0.0).astype(BF)
        for side in range(2):
            source = near_ref if side == 0 else far_ref
            base = HEAD if side == 0 else 0
            for chip in range(chips):
                cols = slice(side * span + chip * rows, side * span + (chip + 1) * rows)
                key = source[chip, base:base + HEAD, :].astype(F32)
                stacked = jnp.concatenate([key, jnp.zeros((HEAD, rows), F32)], 0)
                keys_ref[cols, :] = stacked.T.astype(BF)
                values_ref[0:HEAD, cols] = source[chip, base + HEAD:base + 2 * HEAD, :]
                values_ref[HEAD:HEAD + 16, cols] = ones
        dk_acc[...] = jnp.zeros_like(dk_acc)
        dv_acc[...] = jnp.zeros_like(dv_acc)

    inverse = l_ref[0, 0:1, :]
    grad = do_ref[0].astype(F32) * inverse
    total = -jnp.sum(grad * o_ref[0].astype(F32), 0, keepdims=True)
    high = total.astype(BF).astype(F32)
    mid = (total - high).astype(BF).astype(F32)
    low = total - high - mid
    grad_low = grad.astype(BF)
    row = lax.broadcasted_iota(jnp.int32, (16, rows), 0)
    extra = jnp.where(row == 0, high, jnp.where(row == 1, mid, jnp.where(row == 2, low, 0.0)))
    grads = jnp.concatenate([grad_low, extra.astype(BF)], 0)
    query = near_ref[step, 0:HEAD, :]
    block = 1024
    dq = jnp.zeros((rows, 2 * HEAD), F32)
    for start in range(0, 2 * span, block):
        cols = slice(start, start + block)
        expo = e_ref[:, cols]
        d_probs = contract(grads, values_ref[:, cols], 0, 0)
        d_scores = (expo.astype(F32) * d_probs).astype(BF)
        dq = dq + matmul(d_scores, keys_ref[cols, :])
        dk_acc[:, cols] += matmul(query, d_scores)
        dv_acc[:, cols] += matmul(grad_low, expo)
    dq_ref[0] = (dq.T[0:HEAD] * HEAD ** -0.5).astype(BF)

    @pl.when(step == chips - 1)
    def _():
        for side in range(2):
            for chip in range(chips):
                cols = slice(side * span + chip * rows, side * span + (chip + 1) * rows)
                dk_ref[side, chip] = (dk_acc[:, cols] * HEAD ** -0.5).astype(BF)
                dv_ref[side, chip] = dv_acc[:, cols].astype(BF)


def attend_back(near, far, expo, out, inverse, d_out):
    chips, _, rows = near.shape
    tokens = 2 * chips * rows
    whole = lambda i: (0, 0, 0)
    one = lambda i: (i, 0, 0)
    return pl.pallas_call(
        functools.partial(attend_back_kernel, chips, rows),
        grid=(chips,),
        in_specs=[
            pl.BlockSpec(near.shape, whole),
            pl.BlockSpec(far.shape, whole),
            pl.BlockSpec((rows, tokens), lambda i: (i, 0)),
            pl.BlockSpec((1, HEAD, rows), one),
            pl.BlockSpec((1, 8, rows), one),
            pl.BlockSpec((1, HEAD, rows), one),
        ],
        out_specs=[
            pl.BlockSpec((1, HEAD, rows), one),
            pl.BlockSpec((2, chips, HEAD, rows), lambda i: (0, 0, 0, 0)),
            pl.BlockSpec((2, chips, HEAD, rows), lambda i: (0, 0, 0, 0)),
        ],
        out_shape=[
            jax.ShapeDtypeStruct((chips, HEAD, rows), BF),
            jax.ShapeDtypeStruct((2, chips, HEAD, rows), BF),
            jax.ShapeDtypeStruct((2, chips, HEAD, rows), BF),
        ],
        scratch_shapes=[
            pltpu.VMEM((tokens, 2 * HEAD), BF),
            pltpu.VMEM((HEAD + 16, tokens), BF),
            pltpu.VMEM((HEAD, tokens), F32),
            pltpu.VMEM((HEAD, tokens), F32),
        ],
        compiler_params=pltpu.CompilerParams(vmem_limit_bytes=48 * 2**20),
        cost_estimate=cost(3),
        name="attend_back",
    )(near, far, expo, out, inverse, d_out)


VMEM = pl.BlockSpec(memory_space=pltpu.VMEM)
SMEM = pl.BlockSpec(memory_space=pltpu.SMEM)
ANY = pl.BlockSpec(memory_space=pl.ANY)
RIM = 8
EARLY = 144
SMALL = 320
LATE = 208


def call(kernel, outs, specs, scratch, name, micros, *args):
    return pl.pallas_call(
        kernel,
        in_specs=specs,
        out_specs=[VMEM] * len(outs),
        out_shape=[jax.ShapeDtypeStruct(shape, kind) for shape, kind in outs],
        scratch_shapes=scratch,
        compiler_params=pltpu.CompilerParams(vmem_limit_bytes=56 * 2**20),
        cost_estimate=cost(micros),
        name=name,
    )(*args)


def cost(micros):
    return pl.CostEstimate(
        flops=int(micros * 1.0e9), bytes_accessed=int(micros * 3.0e6), transcendentals=0
    )


def fetch(core, near_ref, far_ref, both_ref, sems):
    copies = [
        pltpu.make_async_copy(near_ref, both_ref.at[core], sems.at[0]),
        pltpu.make_async_copy(far_ref, both_ref.at[1 - core], sems.at[1]),
    ]
    for copy in copies:
        copy.start()
    return copies


def settle(copies):
    for copy in copies:
        copy.wait()


def gains_of(small_ref):
    total = small_ref[0, SMALL:SMALL + 16, :].astype(F32)
    for w in range(1, 8):
        total = total + small_ref[w, SMALL:SMALL + 16, :].astype(F32)
    return jnp.concatenate([total[0:8], total[8:16]], 1)


def taps_of(small_ref, index):
    small = small_ref[index, SMALL + 16:SMALL + 32, :].astype(F32)
    return small[0:9], small[9:10]


def normal_of(value):
    average = jnp.mean(value, -1, keepdims=True)
    centred = value - average
    scale = lax.rsqrt(jnp.mean(centred * centred, -1, keepdims=True) + EPSILON)
    return centred * scale, scale


def back_of(incoming, normal, scale, gain):
    scaled = incoming * gain
    return scale * (
        scaled
        - jnp.mean(scaled, -1, keepdims=True)
        - normal * jnp.mean(scaled * normal, -1, keepdims=True)
    )


def column_sum(value):
    return jnp.sum(value, 0, keepdims=True)


def mask_of(info_ref, count, before):
    place = info_ref[1] - before + lax.broadcasted_iota(jnp.int32, (count, 1), 0)
    return jnp.where((place >= 0) & (place < info_ref[2]), 1.0, 0.0)


def block_cols(index, size=256):
    return pl.ds(pl.multiple_of(index * size, size), size)


def upper_block(both_ref, index):
    rows = pl.ds(pl.multiple_of(lax.rem(index, 4) * 64, 64), 64)
    if len(both_ref.shape) == 5:
        return both_ref[lax.div(index, 4), :, :, rows, :].reshape(512, 256)
    return both_ref[lax.div(index, 4), :, rows, :].reshape(512, 256)


def narrow_block(both_ref, tap):
    return both_ref[0, :, :, 256 + 64 * tap:320 + 64 * tap, :].reshape(512, 256)


def point_block(both_ref, index):
    return both_ref[1, lax.div(index, 4), lax.rem(index, 4), 256:512, :]


def collect(info_ref, near_refs, far_refs, both_ref, sems):
    core, z = info_ref[0], info_ref[4]
    half = both_ref.shape[3] // 2
    copies = []
    for side, refs in ((core, near_refs), (1 - core, far_refs)):
        own, up, down, up2, down2 = refs
        for ref, step in ((own, 0), (up, 3), (down, 1)):
            copies.append((ref, both_ref.at[side, :, lax.rem(z + step, 4)]))
        opposite = lax.rem(z + 2, 4)
        copies.append((up2, both_ref.at[side, :, opposite, 0:half, :]))
        copies.append((down2, both_ref.at[side, :, opposite, half:2 * half, :]))
    copies = [
        pltpu.make_async_copy(source, target, sems.at[i]) for i, (source, target) in enumerate(copies)
    ]
    for copy in copies:
        copy.start()
    return copies


def glu_of(ref):
    return jnp.concatenate(
        [ref[:, 64 * i:64 * i + 64, :].reshape(512, 256) for i in range(2)], 1
    )


def queries_of(both_ref, side, part):
    return both_ref[side, :, 128 + 64 * part:192 + 64 * part, :].reshape(512, 256)


def glu_kernel(info_ref, low_ref, x_ref, high_ref, near_ref, far_ref, n1_ref, a_ref, sg_ref, h1_ref):
    rows = x_ref.shape[0]
    main = slice(RIM, RIM + rows)
    x = jnp.concatenate(
        [low_ref[...].astype(F32), x_ref[...].astype(F32), high_ref[...].astype(F32)], 0
    )
    normal, _ = normal_of(x)
    normed = normal * gains_of(near_ref)[0:1]
    n1 = normed.astype(BF)
    n1_ref[...] = normed[main].astype(BF)
    first = info_ref[0] == 0
    near = matmul(n1, glu_of(near_ref))
    far = matmul(n1, glu_of(far_ref))
    a = jnp.where(first, near, far)
    sg = jax.nn.sigmoid(jnp.where(first, far, near))
    a_ref[...] = a[main]
    sg_ref[...] = sg[main]
    h1_ref[...] = x + a * sg


def conv_kernel(info_ref, h1_ref, small_ref, *refs):
    near2, far2, rest = refs[0:5], refs[5:10], refs[10:]
    conv_body(info_ref, h1_ref, small_ref, near2, far2, *rest)


def conv_body(info_ref, h1_ref, small_ref, near2, far2, nearq_ref, farq_ref,
                n2_ref, wp_ref, np_ref, nm_ref, mean_ref, scale_ref, sp_ref, h2_ref, n3_ref,
                qkv_ref, w2_ref, wq_ref, mix_ref, sem2, semq):
    core = info_ref[0]
    rim_rows = h1_ref.shape[0]
    rows = rim_rows - 2 * RIM
    copies2 = collect(info_ref, near2, far2, w2_ref, sem2)
    copiesq = fetch(core, nearq_ref, farq_ref, wq_ref, semq)
    gains = gains_of(small_ref)
    valid = mask_of(info_ref, rim_rows, RIM)
    normal, _ = normal_of(h1_ref[...])
    n2f = normal * gains[1:2] * valid
    n2 = n2f.astype(BF)
    n2_ref[...] = n2
    n2f = n2.astype(F32)
    settle(copies2)
    narrow = jnp.zeros((rim_rows, 256), F32)
    for tap in range(3):
        if tap == 1:
            moved = n2
        else:
            moved = pltpu.roll(n2f, 1 if tap == 0 else rim_rows - 1, 0).astype(BF)
        narrow = narrow + matmul(moved, narrow_block(w2_ref, tap))
    np_ref[...] = narrow
    narrow = smooth_unit(narrow)

    def first_pass(index, total):
        cols = block_cols(index)
        wide = matmul(n2_ref[...], upper_block(w2_ref, index))
        wp_ref[:, cols] = wide
        mixed = smooth_unit(wide) + narrow * jnp.where(index == 0, 1.0, 0.0)
        mix_ref[:, cols] = mixed
        return total + jnp.sum(mixed, -1, keepdims=True)

    total = lax.fori_loop(0, 8, first_pass, jnp.zeros((rim_rows, 1), F32))
    mean = total * (1.0 / 2048)

    def second_pass(index, total):
        centred = mix_ref[:, block_cols(index)] - mean
        return total + jnp.sum(centred * centred, -1, keepdims=True)

    total = lax.fori_loop(0, 8, second_pass, jnp.zeros((rim_rows, 1), F32))
    scale = lax.rsqrt(total * (1.0 / 2048) + EPSILON)
    mean_ref[...] = jnp.broadcast_to(mean, mean_ref.shape)
    scale_ref[...] = jnp.broadcast_to(scale, scale_ref.shape)
    h2_ref[...] = h1_ref[RIM:RIM + rows, :]

    def third_pass(index, carry):
        cols = block_cols(index)
        taps, gain = taps_of(small_ref, index)
        nm = ((mix_ref[:, cols] - mean) * scale * gain * valid).astype(BF)
        nm_ref[:, cols] = nm
        mix_ref[:, cols] = nm.astype(F32)
        spread = jnp.zeros((rows, 256), F32)
        for tap in range(9):
            spread = spread + mix_ref[4 + tap:4 + tap + rows, cols] * taps[tap:tap + 1]
        spread = spread.astype(BF)
        sp_ref[:, cols] = spread
        h2_ref[:, 0:256] += matmul(spread, point_block(w2_ref, index))
        return carry

    lax.fori_loop(0, 8, third_pass, 0)
    normal, _ = normal_of(h2_ref[...])
    n3 = (normal * gains[2:3]).astype(BF)
    n3_ref[...] = n3
    settle(copiesq)
    for part in range(3):
        for side in range(2):
            block = matmul(n3, queries_of(wq_ref, side, part))
            qkv_ref[4 * side:4 * side + 4, 64 * part:64 * part + 64, :] = (
                block.T.astype(BF).reshape(4, 64, rows)
            )


def ffn_kernel(info_ref, h2_ref, o_ref, small_ref, cot_ref, near_ref, far_ref,
               out_ref, r_ref, du_ref, n4_ref, gy_ref, ga_ref, g3_ref, dob_ref, gain_ref,
               w_ref, y_ref, dn_ref, sem):
    rows = h2_ref.shape[0]
    copies = fetch(info_ref[0], near_ref, far_ref, w_ref, sem)
    gains = gains_of(small_ref)
    valid = mask_of(info_ref, rows, 0)
    heads = o_ref[...].reshape(512, rows)
    gy = (cot_ref[...].astype(F32) * valid).astype(BF)
    gy_ref[...] = gy
    settle(copies)
    outs = [w_ref[side, :, 512:576, :].reshape(512, 256) for side in range(2)]
    h3 = h2_ref[...] + jnp.concatenate([contract(heads, outs[side], 0, 0) for side in range(2)], 1)
    normal, scale = normal_of(h3)
    n4_ref[...] = (normal * gains[3:4]).astype(BF)
    y_ref[...] = h3
    dn_ref[...] = jnp.zeros_like(dn_ref)

    def step(index, carry):
        cols = block_cols(index)
        upper = upper_block(w_ref, index)
        lower = [w_ref[side, index, 256:512, :] for side in range(2)]
        u = matmul(n4_ref[...], upper)
        sigma = jax.nn.sigmoid(u)
        r = (u * sigma).astype(BF)
        r_ref[:, cols] = r
        y_ref[:, 0:256] += matmul(r, lower[0])
        y_ref[:, 256:512] += matmul(r, lower[1])
        dr = contract(gy_ref[:, 0:256], lower[0], 1, 1) + contract(gy_ref[:, 256:512], lower[1], 1, 1)
        du = (dr * (sigma * (1.0 + u * (1.0 - sigma)))).astype(BF)
        du_ref[:, cols] = du
        dn_ref[...] += contract(du, upper, 1, 1)
        return carry

    lax.fori_loop(0, 8, step, 0)
    out_ref[...] = (y_ref[...] * valid).astype(BF)
    dn = dn_ref[...]
    gain_ref[...] = column_sum(dn * normal)
    g3 = gy.astype(F32) + back_of(dn, normal, scale, gains[3:4])
    g3_ref[...] = g3
    ga = g3.astype(BF)
    ga_ref[...] = ga
    dob = contract(outs[0], ga[:, 0:256], 1, 1) + contract(outs[1], ga[:, 256:512], 1, 1)
    dob_ref[...] = dob.astype(BF).reshape(HEADS, HEAD, rows)


def pair_rows(value):
    split = value.reshape(8, 8, 8, 256)
    return jnp.concatenate([split[..., 0:128], split[..., 128:256]], 2)


def writer(out_ref, add_ref):
    def write(value, *where):
        if add_ref is not None:
            value = value + add_ref[where].astype(F32)
        out_ref[where] = value.astype(BF)
    return write


def early_kernel(keeps, info_ref, r_ref, du_ref, n4_ref, gy_ref, ga_ref, o_ref, *refs):
    rows = r_ref.shape[0]
    side = info_ref[0] if keeps else 1 - info_ref[0]
    write = writer(refs[-1], refs[0] if keeps else None)
    full = slice(None)
    for j in range(4):
        res = contract(n4_ref[...], du_ref[:, block_cols(side * 4 + j)], 0, 0)
        for i in range(2):
            write(res[:, 128 * i:128 * i + 128].reshape(8, 64, 128), full, 2 * j + i, slice(0, 64))
    gy = gy_ref[:, block_cols(side)]
    for w in range(8):
        res = contract(gy, r_ref[:, 256 * w:256 * w + 256], 0, 0).reshape(8, 32, 256)
        for i in range(2):
            write(res[:, :, 128 * i:128 * i + 128], w, full, slice(64 + 32 * i, 96 + 32 * i))
    res = matmul(o_ref[...].reshape(512, rows), ga_ref[:, block_cols(side)])
    write(pair_rows(res), full, full, slice(128, 144))


def attn_in_kernel(info_ref, d_ref, h2_ref, g3_ref, small_ref, near_ref, far_ref,
                   g2_ref, gs_ref, lo_ref, hi_ref, gain_ref, w_ref, sem):
    rows = h2_ref.shape[0]
    copies = fetch(info_ref[0], near_ref, far_ref, w_ref, sem)
    gains = gains_of(small_ref)
    normal, scale = normal_of(h2_ref[...])
    settle(copies)
    dn = jnp.zeros((rows, 512), F32)
    for part in range(3):
        for side in range(2):
            block = d_ref[4 * side:4 * side + 4, 64 * part:64 * part + 64, :].reshape(256, rows)
            dn = dn + contract(block, queries_of(w_ref, side, part), 0, 1)
    gain_ref[...] = column_sum(dn * normal)
    g2 = g3_ref[...] + back_of(dn, normal, scale, gains[2:3])
    g2_ref[...] = g2
    gs = g2[:, 0:256]
    gs_ref[...] = gs.astype(BF)
    lo_ref[...] = gs[0:RIM].astype(BF)
    hi_ref[...] = gs[rows - RIM:rows].astype(BF)


def conv_back_kernel(info_ref, lo_ref, gs_ref, hi_ref, nm_ref, wp_ref, np_ref, mean_ref,
                     scale_ref, small_ref, *refs):
    near2, far2, rest = refs[0:5], refs[5:10], refs[10:]
    conv_back_body(info_ref, lo_ref, gs_ref, hi_ref, nm_ref, wp_ref, np_ref, mean_ref,
                   scale_ref, small_ref, near2, far2, *rest)


def conv_back_body(info_ref, lo_ref, gs_ref, hi_ref, nm_ref, wp_ref, np_ref, mean_ref,
                   scale_ref, small_ref, near2, far2, dw_ref, dnar_ref, table_ref,
                   w2_ref, nmf_ref, dsp_ref, sc_ref, hat_ref, sem2):
    rim_rows = wp_ref.shape[0]
    rows = rim_rows - 2 * RIM
    main = slice(RIM, RIM + rows)
    copies = collect(info_ref, near2, far2, w2_ref, sem2)
    valid = mask_of(info_ref, rim_rows, RIM)
    gs = jnp.concatenate(
        [lo_ref[...].astype(F32), gs_ref[...].astype(F32), hi_ref[...].astype(F32)], 0
    ).astype(BF)
    mean = mean_ref[:, 0:1]
    scale = scale_ref[:, 0:1]
    table_ref[...] = jnp.zeros_like(table_ref)
    dsp_ref[0:RIM, :] = jnp.zeros((RIM, 256), F32)
    dsp_ref[RIM + rim_rows:, :] = jnp.zeros((RIM, 256), F32)
    settle(copies)

    def first_pass(index, carry):
        one, two = carry
        cols = block_cols(index)
        taps, gain = taps_of(small_ref, index)
        dsp = contract(gs, point_block(w2_ref, index), 1, 1).astype(BF).astype(F32)
        dsp_ref[RIM:RIM + rim_rows, :] = dsp
        nmf_ref[...] = nm_ref[:, cols].astype(F32)
        inner = dsp[main]
        dn = jnp.zeros((rim_rows, 256), F32)
        for tap in range(9):
            dn = dn + dsp_ref[12 - tap:12 - tap + rim_rows, :] * taps[tap:tap + 1]
            table_ref[tap:tap + 1, cols] = column_sum(nmf_ref[4 + tap:4 + tap + rows, :] * inner)
        dn = dn * valid
        mixed = smooth_unit(wp_ref[:, cols]) + smooth_unit(np_ref[...]) * jnp.where(index == 0, 1.0, 0.0)
        hat = (mixed - mean) * scale
        hat_ref[:, cols] = hat
        table_ref[9:10, cols] = column_sum((dn * hat)[main])
        scaled = dn * gain
        sc_ref[:, cols] = scaled
        return (one + jnp.sum(scaled, -1, keepdims=True),
                two + jnp.sum(scaled * hat, -1, keepdims=True))

    zero = jnp.zeros((rim_rows, 1), F32)
    one, two = lax.fori_loop(0, 8, first_pass, (zero, zero))
    one = one * (1.0 / 2048)
    two = two * (1.0 / 2048)
    back = scale * (sc_ref[:, 0:256] - one - hat_ref[:, 0:256] * two)
    dnar_ref[...] = (back * smooth_slope(np_ref[...])).astype(BF)

    def second_pass(index, carry):
        cols = block_cols(index)
        back = scale[main] * (
            sc_ref[main, cols] - one[main] - hat_ref[main, cols] * two[main]
        )
        dw_ref[:, cols] = (back * smooth_slope(wp_ref[main, cols])).astype(BF)
        return carry

    lax.fori_loop(0, 8, second_pass, 0)


def glu_back_kernel(info_ref, dw_ref, dnar_ref, h1_ref, small_ref, *refs):
    near2, far2, rest = refs[0:5], refs[5:10], refs[10:]
    glu_back_body(info_ref, dw_ref, dnar_ref, h1_ref, small_ref, near2, far2, *rest)


def glu_back_body(info_ref, dw_ref, dnar_ref, h1_ref, small_ref, near2, far2, far1_ref, g2_ref,
                  a_ref, sg_ref, x_ref, dx_ref, da_ref, db_ref, gconv_ref, gglu_ref,
                  w2_ref, dn_ref, nar_ref, sem2):
    rows = g2_ref.shape[0]
    main = slice(RIM, RIM + rows)
    copies = collect(info_ref, near2, far2, w2_ref, sem2)
    gains = gains_of(small_ref)
    valid = mask_of(info_ref, rows, 0)
    nar_ref[...] = dnar_ref[...].astype(F32)
    dn_ref[...] = jnp.zeros_like(dn_ref)
    normal, scale1 = normal_of(h1_ref[main, :])
    settle(copies)
    for tap in range(3):
        moved = nar_ref[9 - tap:9 - tap + rows, :].astype(BF)
        dn_ref[...] += contract(moved, narrow_block(w2_ref, tap), 1, 1)

    def step(index, carry):
        dn_ref[...] += contract(dw_ref[:, block_cols(index)], upper_block(w2_ref, index), 1, 1)
        return carry

    lax.fori_loop(0, 8, step, 0)
    dn = dn_ref[...] * valid
    gconv_ref[...] = column_sum(dn * normal)
    g1 = g2_ref[...] + back_of(dn, normal, scale1, gains[1:2])
    sg = sg_ref[...]
    da = g1 * sg
    db = g1 * a_ref[...] * sg * (1.0 - sg)
    da_ref[...] = da.astype(BF)
    db_ref[...] = db.astype(BF)
    first = info_ref[0] == 0
    dn = contract(jnp.where(first, da, db).astype(BF), glu_of(small_ref), 1, 1)
    dn = dn + contract(jnp.where(first, db, da).astype(BF), glu_of(far1_ref), 1, 1)
    normal, scale0 = normal_of(x_ref[...].astype(F32))
    gglu_ref[...] = column_sum(dn * normal)
    dx_ref[...] = g1 + back_of(dn, normal, scale0, gains[0:1])


FULL = slice(None)


def conv_grads(side, write, n2_ref, dw_ref, dnar_ref, sp_ref, gs_ref, n3_ref, d_ref, n2f_ref):
    rows = dw_ref.shape[0]
    n2f_ref[...] = n2_ref[...].astype(F32)
    shifted = [n2f_ref[7 + tap:7 + tap + rows, :].astype(BF) for tap in range(3)]
    for j in range(4):
        res = contract(shifted[1], dw_ref[:, block_cols(side * 4 + j)], 0, 0)
        for i in range(2):
            write(res[:, 128 * i:128 * i + 128].reshape(8, 64, 128), 2 * j + i, FULL, slice(0, 64))
    gs = gs_ref[:, block_cols(side, 128)]
    for w in range(8):
        res = contract(gs, sp_ref[:, 256 * w:256 * w + 256], 0, 0).reshape(8, 16, 256)
        for i in range(2):
            write(res[:, :, 128 * i:128 * i + 128], FULL, w, slice(64 + 16 * i, 80 + 16 * i))
    for part in range(3):
        d = d_ref[pl.ds(side * 4, 4), 64 * part:64 * part + 64, :].reshape(256, rows)
        packed = pair_rows(contract(n3_ref[...], d, 0, 1))
        for w in range(8):
            write(packed[w], FULL, w, slice(96 + 16 * part, 112 + 16 * part))
    return shifted


def main_rows(rows):
    return slice(RIM, RIM + rows)


def narrow_grads(side, shifted, dnar_ref, narf_ref):
    rows = shifted[0].shape[0]
    narf_ref[...] = dnar_ref[...].astype(F32)
    dnar = narf_ref[main_rows(rows), block_cols(side, 128)].astype(BF)
    return [contract(piece, dnar, 0, 0) for piece in shifted]


def narrow_rows(narrow, c, w):
    return [n[64 * w + 8 * c:64 * w + 8 * c + 8] for n in narrow]


def glu_grads(side, write, base, n1_ref, da_ref, db_ref):
    for place, d_ref in enumerate((da_ref, db_ref)):
        packed = pair_rows(contract(n1_ref[...], d_ref[:, block_cols(side)], 0, 0))
        for w in range(8):
            write(packed[w], FULL, w, slice(base + 16 * place, base + 16 * place + 16))


def small_rows(side, table_ref, gain_refs, w):
    lanes = pl.ds(pl.multiple_of(w * 256 + side * 128, 128), 128)
    pair = slice(128 * (w // 2), 128 * (w // 2) + 128)
    return jnp.concatenate(
        [table_ref[0:10, lanes]] + [ref[:, pair] for ref in gain_refs] + [table_ref[14:16, lanes]], 0
    )


def conv_give_kernel(info_ref, n2_ref, dw_ref, dnar_ref, sp_ref, gs_ref, n3_ref, d_ref, out_ref,
                     n2f_ref, narf_ref):
    side = 1 - info_ref[0]
    shifted = conv_grads(side, writer(out_ref, None), n2_ref, dw_ref, dnar_ref, sp_ref, gs_ref,
                         n3_ref, d_ref, n2f_ref)
    narrow = narrow_grads(side, shifted, dnar_ref, narf_ref)
    for w in range(8):
        for c in range(8):
            rows = jnp.concatenate(narrow_rows(narrow, c, w) + [jnp.zeros((8, 128), F32)], 0)
            out_ref[c, w, 144:176, :] = rows.astype(BF)


def glu_give_kernel(info_ref, n1_ref, da_ref, db_ref, table_ref, gglu_ref, gconv_ref, gattn_ref,
                    gffn_ref, out_ref):
    side = 1 - info_ref[0]
    glu_grads(side, writer(out_ref, None), 0, n1_ref, da_ref, db_ref)
    for w in range(8):
        table = small_rows(side, table_ref, (gglu_ref, gconv_ref, gattn_ref, gffn_ref), w)
        for c in range(8):
            rows = jnp.concatenate([table[2 * c:2 * c + 2], jnp.zeros((14, 128), F32)], 0)
            out_ref[c, w, 32:48, :] = rows.astype(BF)


def late_keep_kernel(info_ref, n2_ref, dw_ref, dnar_ref, sp_ref, gs_ref, n3_ref, d_ref, n1_ref,
                     da_ref, db_ref, table_ref, gglu_ref, gconv_ref, gattn_ref, gffn_ref,
                     conv_ref, glu_ref, out_ref, n2f_ref, narf_ref):
    side = info_ref[0]

    def write(value, *where):
        out_ref[where] = (value + conv_ref[where].astype(F32)).astype(BF)

    shifted = conv_grads(side, write, n2_ref, dw_ref, dnar_ref, sp_ref, gs_ref, n3_ref, d_ref, n2f_ref)
    narrow = narrow_grads(side, shifted, dnar_ref, narf_ref)

    def write_glu(value, *where):
        start = where[2].start
        added = value + glu_ref[where[0], where[1], start - 176:start - 160, :].astype(F32)
        out_ref[where] = added.astype(BF)

    glu_grads(side, write_glu, 176, n1_ref, da_ref, db_ref)
    for w in range(8):
        table = small_rows(side, table_ref, (gglu_ref, gconv_ref, gattn_ref, gffn_ref), w)
        for c in range(8):
            other = glu_ref[c, w, 32:48, :].astype(F32)
            small = jnp.concatenate([table[2 * c:2 * c + 2], jnp.zeros((6, 128), F32)], 0) + other[0:8]
            rows = jnp.concatenate(narrow_rows(narrow, c, w) + [jnp.zeros((8, 128), F32)], 0)
            rows = rows + conv_ref[c, w, 144:176, :].astype(F32)
            out_ref[c, w, 144:176, :] = jnp.concatenate([rows[0:24], small], 0).astype(BF)


def unpack_kernel(info_ref, near_ref, far_ref, gglu_ref, val_ref, gat_ref, gconv_ref, wid_ref, nar_ref,
                  gmid_ref, dep_ref, pnt_ref, gatt_ref, qry_ref, key_ref, vls_ref, outp_ref,
                  gffn_ref, upper_ref, lower_ref, fin_ref, low_ref, pt_ref, table_ref, sem):
    settle(fetch(info_ref[0], near_ref, far_ref, fin_ref, sem))
    for c in range(8):
        for k in range(2):
            fin = fin_ref[k, c].astype(F32)
            lanes = slice(k * 1024 + c * 128, k * 1024 + c * 128 + 128)
            upper_ref[:, lanes] = fin[0:64]
            wid_ref[:, lanes] = fin[EARLY:EARLY + 64]
            late = EARLY
            for i in range(2):
                low_ref[k * 256 + c * 32:k * 256 + c * 32 + 32, 128 * i:128 * i + 128] = (
                    fin[64 + 32 * i:96 + 32 * i]
                )
                pt_ref[k * 128 + c * 16:k * 128 + c * 16 + 16, 128 * i:128 * i + 128] = (
                    fin[late + 64 + 16 * i:late + 80 + 16 * i]
                )
            for tap in range(3):
                nar_ref[tap, 8 * c:8 * c + 8, 128 * k:128 * k + 128] = (
                    fin[late + 144 + 8 * tap:late + 152 + 8 * tap]
                )
            table_ref[2 * c:2 * c + 2, 128 * k:128 * k + 128] = fin[late + 168:late + 170]
            bases = [128] + [late + 96 + 16 * i for i in range(3)] + [late + 176, late + 192]
            targets = [outp_ref, qry_ref, key_ref, vls_ref, val_ref, gat_ref]
            for base, target in zip(bases, targets):
                for i in range(2):
                    target[8 * c:8 * c + 8, k * 256 + 128 * i:k * 256 + 128 * i + 128] = (
                        fin[base + 8 * i:base + 8 * i + 8]
                    )
    lower_ref[...] = low_ref[...].T
    pnt_ref[...] = pt_ref[...].T
    dep_ref[...] = table_ref[0:9, :]
    gmid_ref[...] = table_ref[9:10, :]
    even = info_ref[3] == 0
    gains = jnp.where(even, table_ref[10:14, 0:64], table_ref[10:14, 64:128])
    gglu_ref[...] = gains[0:1]
    gconv_ref[...] = gains[1:2]
    gatt_ref[...] = gains[2:3]
    gffn_ref[...] = gains[3:4]


def spread_out(own, axes, count):
    copies = jnp.broadcast_to(own[None], (count,) + own.shape)
    return lax.all_to_all(copies, axes, 0, 0, tiled=True)


def shards(
    inputs, lengths, cotangent, glu_gain, glu_value, glu_gate, conv_gain, wide_weight,
    narrow_weight, mid_gain, depth_weight, point_weight, attn_gain, query_weight, key_weight,
    value_weight, output_weight, ffn_gain, ffn_in, ffn_out,
):
    rows, width = inputs.shape[1], inputs.shape[2]
    units = wide_weight.shape[1]
    rim_rows = rows + 2 * RIM
    core = lax.axis_index("core")
    shard = lax.axis_index("xl") * 4 + lax.axis_index("z")
    first = (lax.axis_index("y") * 4 + lax.axis_index("xh") * 2 + core) * rows
    z = lax.axis_index("z")
    info = jnp.stack([core, first, lengths[0], shard % 2, z]).astype(jnp.int32)
    flip = shift(dc=1)

    def own_half(weight):
        cols = weight.shape[-1] // 2
        return lax.dynamic_slice_in_dim(weight, core * cols, cols, weight.ndim - 1)

    def blocks(weight):
        return [weight[:, 256 * i:256 * i + 256] for i in range(weight.shape[1] // 256)]

    narrow_rows = jnp.pad(narrow_weight.reshape(192, 256), ((0, 64), (0, 0)))
    pack2 = jnp.concatenate(
        blocks(own_half(wide_weight)) + [jnp.where(core == 0, narrow_rows, point_weight)], 0
    )
    half = pack2.shape[0] // 2
    other = send(pack2, shift(dxl=1))
    pair = jnp.where(shard < 4, jnp.stack([pack2, other]), jnp.stack([other, pack2]))
    up, down = send(pair, shift(dz=1)), send(pair, shift(dz=-1))
    up2, down2 = send(up[:, :half], shift(dz=1)), send(down[:, half:], shift(dz=-1))
    near2 = [pair, up, down, up2, down2]
    far2 = [send(piece, flip) for piece in near2]

    place = lax.broadcasted_iota(jnp.int32, (1, width), 1) // 64 == shard
    gains = jnp.stack([glu_gain, conv_gain, attn_gain, ffn_gain])
    gains = jnp.where(place, jnp.tile(gains, (1, 8)), jnp.zeros((), BF))
    gains = jnp.pad(gains, ((0, 4), (0, 0)))
    taps = jnp.pad(jnp.concatenate([depth_weight, mid_gain[None]], 0), ((0, 6), (0, 0)))
    pack1 = jnp.concatenate(
        blocks(jnp.where(core == 0, glu_value, glu_gate))
        + [own_half(w) for w in (query_weight, key_weight, value_weight)]
        + blocks(gains) + [taps], 0,
    )
    near1 = spread_out(pack1, WT, 8)
    near1, up, down = lax.optimization_barrier((near1, near2[1], near2[2]))
    far1 = send(near1[:, :SMALL], flip)
    x = inputs[0]
    low_x = send(x[rows - RIM:], along(1))
    high_x = send(x[:RIM], along(-1))
    pack3 = jnp.concatenate(
        blocks(own_half(ffn_in)) + [own_half(ffn_out), own_half(output_weight)], 0
    )
    pack3, _, _ = lax.optimization_barrier((pack3, near2[3], near2[4]))
    near3 = lax.all_gather(pack3, WT, axis=0)
    far3 = send(near3, flip)

    tall, wide, narrow = (rows, width), (rows, units), (rows, 256)
    dma = pltpu.SemaphoreType.DMA
    ring = pltpu.VMEM((2, 2, 4) + pack2.shape, BF)
    n1, a, sg, h1 = call(
        glu_kernel, [(tall, BF), (tall, F32), (tall, F32), ((rim_rows, width), F32)],
        [SMEM] + [VMEM] * 5, [], "glu", 3, info, low_x, x, high_x, near1, far1,
    )
    n2, wp, np_, nm, mean, scale, sp, h2, n3, qkv = call(
        conv_kernel,
        [((rim_rows, width), BF), ((rim_rows, units), F32), ((rim_rows, 256), F32),
         ((rim_rows, units), BF), ((rim_rows, 128), F32), ((rim_rows, 128), F32),
         (wide, BF), (tall, F32), (tall, BF), ((HEADS, 3 * HEAD, rows), BF)],
        [SMEM, VMEM, VMEM] + [ANY] * 12,
        [ring, pltpu.VMEM((2, 8, SMALL, 256), BF), pltpu.VMEM((rim_rows, units), F32),
         dma((10,)), dma((2,))],
        "conv", 15, info, h1, near1, *near2, *far2, near1[:, :SMALL], far1,
    )
    near = lax.all_to_all(qkv, CHIPS, 0, 0, tiled=True)
    far = send(near[:, HEAD:], flip)
    head_out, expo, inverse = attend(near, far, lengths, info[:1])
    heads_in = lax.all_to_all(head_out, CHIPS, 0, 0, tiled=True)
    output, r, du, n4, gy, ga, g3, dob, d_gffn = call(
        ffn_kernel,
        [(tall, BF), (wide, BF), (wide, BF), (tall, BF), (tall, BF), (tall, BF), (tall, F32),
         ((HEADS, HEAD, rows), BF), ((1, width), F32)],
        [SMEM, VMEM, VMEM, VMEM, VMEM, ANY, ANY],
        [pltpu.VMEM((2,) + near3.shape, BF), pltpu.VMEM(tall, F32), pltpu.VMEM(tall, F32), dma((2,))],
        "ffn", 11, info, h2, heads_in, near1, cotangent[0], near3, far3,
    )

    d_near = lax.all_to_all(dob, CHIPS, 0, 0, tiled=True)
    early = [((8, 8, EARLY, 128), BF)]
    given = (info, r, du, n4, gy, ga, heads_in)
    give = call(
        functools.partial(early_kernel, False), early, [SMEM] + [VMEM] * 6, [], "early_give", 0.3,
        *given,
    )[0]
    early = call(
        functools.partial(early_kernel, True), early, [SMEM] + [VMEM] * 7, [], "early_keep", 0.3,
        *given, send(give, flip),
    )[0]
    d_near, early = lax.optimization_barrier((d_near, early))
    early = lax.psum_scatter(early, WT, scatter_dimension=0, tiled=True)
    early = early[0]
    dq, dk, dv = attend_back(near, far, expo, head_out, inverse, d_near)
    d_far = send(jnp.concatenate([dk[1], dv[1]], 1), flip).astype(F32)
    d_own = jnp.concatenate([dk[0], dv[0]], 1).astype(F32)
    d_qkv = jnp.concatenate([dq, (d_own + d_far).astype(BF)], 1)
    d_qkv = lax.all_to_all(d_qkv, CHIPS, 0, 0, tiled=True)
    g2, gs, lo, hi, d_gatt = call(
        attn_in_kernel,
        [(tall, F32), (narrow, BF), ((RIM, 256), BF), ((RIM, 256), BF), ((1, width), F32)],
        [SMEM] + [VMEM] * 4 + [ANY] * 2,
        [pltpu.VMEM((2, 8, SMALL, 256), BF), dma((2,))],
        "attn_in", 0.5, info, d_qkv, h2, g3, near1, near1[:, :SMALL], far1,
    )
    low_gs = send(hi, along(1))
    high_gs = send(lo, along(-1))
    rim_narrow = ((rim_rows, 256), BF)
    dw, dnar, table = call(
        conv_back_kernel, [(wide, BF), rim_narrow, ((16, units), F32)],
        [SMEM] + [VMEM] * 9 + [ANY] * 10,
        [ring, pltpu.VMEM((rim_rows, 256), F32), pltpu.VMEM((rim_rows + 2 * RIM, 256), F32),
         pltpu.VMEM((rim_rows, units), F32), pltpu.VMEM((rim_rows, units), F32), dma((10,))],
        "conv_back", 2, info, low_gs, gs, high_gs, nm, wp, np_, mean, scale, near1, *near2, *far2,
    )
    shapes = [pltpu.VMEM((rim_rows, width), F32), pltpu.VMEM((rim_rows, 256), F32)]
    conv_given = (n2, dw, dnar, sp, gs, n3, d_qkv)
    give1 = call(
        conv_give_kernel, [((8, 8, 176, 128), BF)], [SMEM] + [VMEM] * 7, shapes, "conv_give", 0.5,
        info, *conv_given,
    )[0]
    take1 = send(give1, flip)
    g2, _, early = lax.optimization_barrier((g2, give1, early))
    early = lax.all_to_all(early, CHIPS, 0, 0, tiled=True)
    dx, da, db, d_gconv, d_gglu = call(
        glu_back_kernel,
        [(tall, F32), (tall, BF), (tall, BF), ((1, width), F32), ((1, width), F32)],
        [SMEM] + [VMEM] * 4 + [ANY] * 10 + [VMEM] * 5,
        [ring, pltpu.VMEM(tall, F32), pltpu.VMEM((rim_rows, 256), F32), dma((10,))],
        "glu_back", 1, info, dw, dnar, h1, near1, *near2, *far2, far1, g2, a, sg, x,
    )
    glu_given = (n1, da, db, table, d_gglu, d_gconv, d_gatt, d_gffn)
    give2 = call(
        glu_give_kernel, [((8, 8, 48, 128), BF)], [SMEM] + [VMEM] * 8, [], "glu_give", 0.3,
        info, *glu_given,
    )[0]
    late = call(
        late_keep_kernel, [((8, 8, LATE, 128), BF)], [SMEM] + [VMEM] * 17, shapes, "late_keep", 0.5,
        info, *conv_given, *glu_given, take1, send(give2, flip),
    )[0]
    late, early = lax.optimization_barrier((late, early))
    early = jnp.sum(early.astype(F32), 0).astype(BF)
    late = lax.all_to_all(late.reshape(64, LATE, 128), CHIPS + WT, 0, 0, tiled=True)
    late = jnp.sum(late.astype(F32), 0).astype(BF)
    final = spread_out(jnp.concatenate([early, late], 0), CHIPS, 8)
    square, broad = ((64, 512), F32), ((64, 2048), F32)
    line = ((1, 64), F32)
    grads = call(
        unpack_kernel,
        [line, square, square, line, broad, ((3, 64, 256), F32), ((1, 256), F32),
         ((9, 256), F32), ((256, 256), F32), line, square, square, square, square, line, broad,
         ((256, 512), F32)],
        [SMEM, ANY, ANY],
        [pltpu.VMEM((2, 8, EARLY + LATE, 128), BF), pltpu.VMEM((512, 256), F32),
         pltpu.VMEM((256, 256), F32), pltpu.VMEM((16, 256), F32), dma((2,))],
        "unpack", 3, info, final, send(final, flip),
    )
    grads = [g[0] if g.shape[0] == 1 else g for g in grads]
    return (output[None], dx[None]) + tuple(grads)


def solution(mesh):
    fine = Mesh(mesh.devices.reshape(SIZES), AXES)
    flat, row, mid = P(WT), P(WT, None), P(None, WT, None)
    col = P(None, WT)
    tokens = P(WT, CTX, None)
    weights = (
        flat, row, row, flat, row, mid, flat, col, row, flat, row, row, row, row, flat, row, row,
    )
    return jax.shard_map(
        shards, mesh=fine, in_specs=(tokens, flat, tokens) + weights,
        out_specs=(tokens, tokens) + weights, check_vma=False,
    )
```

time: 516 us -> 372 us (0.72); the launches traced: 506 us -> 370 us
  Pallas kernels: 32.3 us -> 121 us
  local copies, waits for them, and re-layouts: 113 us -> 25.4 us
  other arithmetic: 69.3 us -> 4.38 us
  starting transfers between devices: 116 us -> 64.4 us
  blocking collectives: 0 us -> 50.2 us
  waiting for transfers between devices: 136 us -> 89.5 us
  matrix products: 35 us -> 0 us
  between operations: 4.49 us -> 15.2 us
    pallas_call x0 -> x12, Pallas kernels: none -> 89 us  [call(): pl.pallas_call(kernel, in_specs=specs, out_specs=[VMEM] * len(outs), out_...]
    ppermute x54 -> x22, waiting for transfers between devices: 115 us -> 30.4 us  [send(): return lax.ppermute(value, AXES, pairs)]
    ppermute x54 -> x22, starting transfers between devices: 94.6 us -> 33.9 us  [send(): return lax.ppermute(value, AXES, pairs)]
    all_to_all x0 -> x3, blocking collectives: none -> 50.2 us  [the longest x1 22.2 us: shards(): d_qkv = lax.all_to_all(d_qkv, CHIPS, 0, 0, tiled=True)]
    all_to_all x3 -> x4, waiting for transfers between devices: 8.17 us -> 45.1 us  [the longest x1 41.6 us: shards(): lax.all_to_all(late.reshape(64, LATE, 128), CHIPS + WT, 0, 0, tiled=True)]
    dot_general x33 -> x0, matrix products: 35 us -> none  [the longest x26 25.2 us: contract(): lax.dot_general(left, right, (((ldim,), (rdim,)), ((), ())), preferred_el...]
    unnamed x303 -> x49, local copies, waits for them, and re-layouts: 38.4 us -> 17.8 us
    another operation x12 -> x3, local copies, waits for them, and re-layouts: 21.2 us -> 0.67 us  [the longest x1 0.57 us: shards(): info = jnp.stack([core, first, lengths[0], shard % 2, z]).astype(jnp.int32)]
  transfers between devices with their start and end apart: 58 -> 29, of which waited for: 28 -> 14; matrix products, arithmetic and copies ran while one was open for 35% -> 5% of each run, Pallas kernels for 0% -> 28%
where the time goes in v2:
time: 372 us; the launch traced here: 370 us
  Pallas kernels  121 us (33%)
  waiting for transfers between devices  89.5 us (24%)
  starting transfers between devices  64.4 us (17%)
  blocking collectives  50.2 us (13%)
  local copies, waits for them, and re-layouts  25.4 us (7%)
  between operations  15.2 us (4%)
  other arithmetic  4.38 us (1%)
    pallas_call x12, Pallas kernels, call(): pl.pallas_call(kernel, in_specs=specs, out_specs=[VMEM] * len(outs), out_...  89 us
    all_to_all x1, waiting for transfers between devices, shards(): lax.all_to_all(late.reshape(64, LATE, 128), CHIPS + WT, 0, 0, tiled=True)  41.6 us
    ppermute x22, starting transfers between devices, send(): return lax.ppermute(value, AXES, pairs)  33.9 us
    ppermute x22, waiting for transfers between devices, send(): return lax.ppermute(value, AXES, pairs)  30.4 us
    all_to_all x1, blocking collectives, shards(): d_qkv = lax.all_to_all(d_qkv, CHIPS, 0, 0, tiled=True)  22.2 us
    pallas_call x1, Pallas kernels, attend_back(): pl.pallas_call(functools.partial(attend_back_kernel, chips, rows), grid=(...  18.4 us
    unnamed x49, local copies, waits for them, and re-layouts  17.8 us
    all_to_all x1, blocking collectives, spread_out(): return lax.all_to_all(copies, axes, 0, 0, tiled=True)  16.4 us
  transfers between devices with their start and end apart: 29, of which 14 were waited for; matrix products, arithmetic and copies ran while one was open for 5% of the time, Pallas kernels for 28%

profile of v2, /device:TPU:1, one launch (start us, length us, event | category | flops | bytes accessed | tf_op | source)
XLA Modules:
  0.0 370.2 jit_solution(14089569962413866961)
XLA Ops:
  7.2 1.4 constant_dynamic-update-slice_fusion.11
  11.9 2.1 collective-permute-start.2
  19.7 4.3 %collective-permute-start.4 = (bf16[2,512,256]{2,1,0:T(8,128)(2,1)S(1)}, bf16[2,512,256]{2,1,0:T(8,128)(2,1)S(1)}, u32[]{:S(2)}, u32[]{:S(2)}) collective-permute-start(bf16[2,512,256]{2,1,0:T(8,128)(2,1)S(1)} %maximum_select_fusion.refs_0_), channel_id=1, source_target_pairs={{0,3},{1,0},{2,1},{3,2},{4,7},{5,4},{6,5},{7,6},{8,11},{9,8},{10,9... | collective-permute-start | bytes 1572872 | tf_op jit(solution)/shard_map/ppermute | solution.py:53
  25.2 4.9 %all-to-all-start = ((bf16[8,352,256]{2,1,0:T(8,128)(2,1)}), bf16[8,352,256]{2,1,0:T(8,128)(2,1)S(1)}, u32[]{:S(2)}, u32[]{:S(2)}) async-start(bf16[8,352,256]{2,1,0:T(8,128)(2,1)} %broadcast_in_dim.36), calls=%async_computation | async-start | bytes 2883584 | tf_op jit(solution)/shard_map/all_to_all | solution.py:821
  30.1 1.4 constant_dynamic-update-slice_fusion.15
  32.9 6.5 %collective-permute-done.4.refs_2_ = bf16[2,512,256]{2,1,0:T(8,128)(2,1)S(1)} collective-permute-done((bf16[2,512,256]{2,1,0:T(8,128)(2,1)S(1)}, bf16[2,512,256]{2,1,0:T(8,128)(2,1)S(1)}, u32[]{:S(2)}, u32[]{:S(2)}) %collective-permute-start.4) | collective-permute-done | bytes 524320 | tf_op jit(solution)/shard_map/ppermute | solution.py:53
  40.1 3.6 collective-permute-start.7
  44.4 1.4 constant_dynamic-update-slice_fusion.13
  45.8 1.6 dynamic-slice_dynamic-update-slice_fusion
  47.4 1.4 constant_dynamic-update-slice_fusion.12
  48.7 5.3 %collective-permute-done.7.refs_4_ = bf16[2,256,256]{2,1,0:T(8,128)(2,1)S(1)} collective-permute-done((bf16[2,256,256]{2,1,0:T(8,128)(2,1)}, bf16[2,256,256]{2,1,0:T(8,128)(2,1)S(1)}, u32[]{:S(2)}, u32[]{:S(2)}) %collective-permute-start.7) | collective-permute-done | bytes 262176 | tf_op jit(solution)/shard_map/ppermute | solution.py:53
  54.0 3.0 collective-permute-done.6.refs_3_
  59.0 4.9 %collective-permute-start.5 = (bf16[8,320,256]{2,1,0:T(8,128)(2,1)}, bf16[8,320,256]{2,1,0:T(8,128)(2,1)S(1)}, u32[]{:S(2)}, u32[]{:S(2)}) collective-permute-start(bf16[8,320,256]{2,1,0:T(8,128)(2,1)} %slice.86.refs_10_.near_ref), channel_id=1, source_target_pairs={{0,8},{1,9},{2,10},{3,11},{4,12},{5,13},{6,14},{7,15},{8,0},{9,1},... | collective-permute-start | bytes 3932168 | tf_op jit(solution)/shard_map/ppermute | solution.py:53
  65.2 2.4 collective-permute-start.1
  67.6 4.1 %collective-permute-done.1.high_ref = bf16[8,512]{1,0:T(8,128)(2,1)S(1)} collective-permute-done((bf16[8,512]{1,0:T(8,128)(2,1)S(1)}, bf16[8,512]{1,0:T(8,128)(2,1)S(1)}, u32[]{:S(2)}, u32[]{:S(2)}) %collective-permute-start.1) | collective-permute-done | bytes 8224 | tf_op jit(solution)/shard_map/ppermute | solution.py:53
  71.6 1.9 collective-permute-start
  76.9 3.8 %glu.1 = (bf16[256,512]{1,0:T(8,128)(2,1)}, f32[256,512]{1,0:T(8,128)}, f32[256,512]{1,0:T(8,128)}, f32[272,512]{1,0:T(8,128)}) custom-call(s32[5]{0:T(128)} %stack.48.info_ref, bf16[8,512]{1,0:T(8,128)(2,1)} %collective-permute-done.low_ref, bf16[256,512]{1,0:T(8,128)(2,1)} %bitcast.37, bf16[8,512]{1,0:T(8,128)(2,1)} %copy-done.16, ...), custom_call_target="tpu_custom_call" | custom-call | flops 3000000000 | bytes 9000000 | tf_op jit(solution)/shard_map/glu/pallas_call | solution.py:251
  81.5 15.9 %conv.1 = (bf16[272,512]{1,0:T(8,128)(2,1)}, f32[272,2048]{1,0:T(8,128)}, f32[272,256]{1,0:T(8,128)}, bf16[272,2048]{1,0:T(8,128)(2,1)}, f32[272,128]{1,0:T(8,12...) custom-call(s32[5]{0:T(128)} %stack.48.info_ref, ...), custom_call_target="tpu_custom_call" | custom-call | flops 15000000512 | bytes 45000000 | tf_op jit(solution)/shard_map/conv/pallas_call | solution.py:251
  97.4 7.4 %all-to-all-start.1 = ((bf16[8,192,256]{2,1,0:T(8,128)(2,1)}), bf16[8,192,256]{2,1,0:T(8,128)(2,1)S(1)}, u32[]{:S(2)}, u32[]{:S(2)}) async-start(bf16[8,192,256]{2,1,0:T(8,128)(2,1)} %get-tuple-element.89), calls=%async_computation.1 | async-start | bytes 1572864 | tf_op jit(solution)/shard_map/all_to_all | solution.py:898
  105.2 13.9 %all-to-all-done.1.near_ref = bf16[8,192,256]{2,1,0:T(8,128)(2,1)S(1)} async-done(((bf16[8,192,256]{2,1,0:T(8,128)(2,1)}), bf16[8,192,256]{2,1,0:T(8,128)(2,1)S(1)}, u32[]{:S(2)}, u32[]{:S(2)}) %all-to-all-start.1) | async-done | bytes 786464 | tf_op jit(solution)/shard_map/all_to_all | solution.py:898
  120.3 1.5 collective-permute-done.13.far_ref
  121.9 13.9 %attend.1 = (bf16[8,64,256]{2,1,0:T(8,128)(2,1)S(1)}, bf16[2048,4096]{1,0:T(8,128)(2,1)}, f32[8,8,256]{2,1,0:T(8,128)S(1)}) custom-call(s32[1]{0:T(128)S(6)} %copy.55.length_ref, s32[1]{0:T(128)} %bitcast.core_ref, bf16[8,192,256]{2,1,0:T(8,128)(2,1)S(1)} %all-to-all-done.1.near_ref, bf16[8,128,256]{2,1,0:T(8,128)(2,1)S(1)} %collective-permute-done.13.far_ref), custom_call_target="tpu_custom_call" | custom-call | flops 14000000000 | bytes 42000000 | tf_op jit(solution)/shard_map/attend/pallas_call | solution.py:120
  135.7 11.6 %all_to_all.40.o_ref = bf16[8,64,256]{2,1,0:T(8,128)(2,1)} all-to-all(bf16[8,64,256]{2,1,0:T(8,128)(2,1)S(1)} %get-tuple-element.90.o_ref), channel_id=1, replica_groups=mesh['y'=4,'xh'=2,'core'=2,'xl'=2,'z'=4] {'y','xh'}, dimensions={0} | all-to-all | bytes 524288 | tf_op jit(solution)/shard_map/all_to_all | solution.py:901
  147.3 11.2 %ffn.1 = (bf16[256,512]{1,0:T(8,128)(2,1)}, bf16[256,2048]{1,0:T(8,128)(2,1)}, bf16[256,2048]{1,0:T(8,128)(2,1)}, bf16[256,512]{1,0:T(8,128)(2,1)}, bf16[256,512...) custom-call(s32[5]{0:T(128)} %stack.48.info_ref, ...), custom_call_target="tpu_custom_call" | custom-call | flops 11000000512 | bytes 33000000 | tf_op jit(solution)/shard_map/ffn/pallas_call | solution.py:251
  158.5 4.0 %early_give.1 = bf16[8,8,144,128]{3,2,1,0:T(8,128)(2,1)} custom-call(s32[5]{0:T(128)} %stack.48.info_ref, bf16[256,2048]{1,0:T(8,128)(2,1)} %get-tuple-element.96.r_ref, bf16[256,2048]{1,0:T(8,128)(2,1)} %get-tuple-element.97.du_ref, bf16[256,512]{1,0:T(8,128)(2,1)} %get-tuple-element.98.n4_ref, bf16[256,512]{1,0:T(8,128)(2,1)} %get-tuple-element.99.gy_ref, ...), custom_call_target="tpu_custom_call" | custom-call | flops 300000000 | bytes 900000 | tf_op jit(solution)/shard_map/early_give/pallas_call | solution.py:251
  163.8 3.4 all-to-all-start.3
  168.3 4.9 %early_keep.1 = bf16[8,8,144,128]{3,2,1,0:T(8,128)(2,1)} custom-call(s32[5]{0:T(128)} %stack.48.info_ref, bf16[256,2048]{1,0:T(8,128)(2,1)} %get-tuple-element.96.r_ref, bf16[256,2048]{1,0:T(8,128)(2,1)} %get-tuple-element.97.du_ref, bf16[256,512]{1,0:T(8,128)(2,1)} %get-tuple-element.98.n4_ref, bf16[256,512]{1,0:T(8,128)(2,1)} %get-tuple-element.99.gy_ref, ...), custom_call_target="tpu_custom_call" | custom-call | flops 300000000 | bytes 900000 | tf_op jit(solution)/shard_map/early_keep/pallas_call | solution.py:251
  173.2 2.6 all-to-all-done.3.do_ref
  175.8 18.4 %attend_back.1 = (bf16[8,64,256]{2,1,0:T(8,128)(2,1)S(1)}, bf16[2,8,64,256]{3,2,1,0:T(8,128)(2,1)S(1)}, bf16[2,8,64,256]{3,2,1,0:T(8,128)(2,1)S(1)}) custom-call(bf16[8,192,256]{2,1,0:T(8,128)(2,1)S(1)} %all-to-all-done.1.near_ref, bf16[8,128,256]{2,1,0:T(8,128)(2,1)S(1)} %collective-permute-done.13.far_ref, bf16[2048,4096]{1,0:T(8,128)(2,1)} %get-tuple-element.93.e_ref, ...), custom_call_target="tpu_custom_call" | custom-call | flops 3000000000 | bytes 9000000 | tf_op jit(solution)/shard_map/attend_back/pallas_call | solution.py:208
  195.5 1.5 collective-permute-done.16
  197.2 22.2 %all_to_all.41.d_ref = bf16[8,192,256]{2,1,0:T(8,128)(2,1)} all-to-all(bf16[8,192,256]{2,1,0:T(8,128)(2,1)S(1)} %pad_maximum_fusion), channel_id=1, replica_groups=mesh['y'=4,'xh'=2,'core'=2,'xl'=2,'z'=4] {'y','xh'}, dimensions={0} | all-to-all | bytes 1572864 | tf_op jit(solution)/shard_map/all_to_all | solution.py:929
  219.4 5.2 %attn_in.1 = (f32[256,512]{1,0:T(8,128)}, bf16[256,256]{1,0:T(8,128)(2,1)}, bf16[8,256]{1,0:T(8,128)(2,1)}, bf16[8,256]{1,0:T(8,128)(2,1)}, f32[1,512]{1,0:T(1,128)}) custom-call(s32[5]{0:T(128)} %stack.48.info_ref, bf16[8,192,256]{2,1,0:T(8,128)(2,1)} %all_to_all.41.d_ref, f32[256,512]{1,0:T(8,128)} %get-tuple-element.88.h2_ref, ...), custom_call_target="tpu_custom_call" | custom-call | flops 500000000 | bytes 1500000 | tf_op jit(solution)/shard_map/attn_in/pallas_call | solution.py:251
  224.7 3.3 collective-permute-start.17
  227.9 1.9 collective-permute-start.18
  229.9 4.7 %collective-permute-done.18.hi_ref = bf16[8,256]{1,0:T(8,128)(2,1)S(1)} collective-permute-done((bf16[8,256]{1,0:T(8,128)(2,1)}, bf16[8,256]{1,0:T(8,128)(2,1)S(1)}, u32[]{:S(2)}, u32[]{:S(2)}) %collective-permute-start.18) | collective-permute-done | bytes 4128 | tf_op jit(solution)/shard_map/ppermute | solution.py:53
  235.2 17.5 %conv_back.1 = (bf16[256,2048]{1,0:T(8,128)(2,1)}, bf16[272,256]{1,0:T(8,128)(2,1)}, f32[16,2048]{1,0:T(8,128)}) custom-call(s32[5]{0:T(128)} %stack.48.info_ref, bf16[8,256]{1,0:T(8,128)(2,1)} %copy-done.13, bf16[256,256]{1,0:T(8,128)(2,1)} %get-tuple-element.107.gs_ref, bf16[8,256]{1,0:T(8,128)(2,1)} %copy-done.14, ...), custom_call_target="tpu_custom_call" | custom-call | flops 2000000000 | bytes 6000000 | tf_op jit(solution)/shard_map/conv_back/pallas_call | solution.py:251
  252.7 4.7 %conv_give.1 = bf16[8,8,176,128]{3,2,1,0:T(8,128)(2,1)} custom-call(s32[5]{0:T(128)} %stack.48.info_ref, bf16[272,512]{1,0:T(8,128)(2,1)} %get-tuple-element.117.n2_ref, bf16[256,2048]{1,0:T(8,128)(2,1)} %get-tuple-element.114.dw_ref, bf16[272,256]{1,0:T(8,128)(2,1)} %get-tuple-element.115.dnar_ref, bf16[256,2048]{1,0:T(8,128)(2,1)} %get-tuple-element.118.sp_ref, ...), custom_call_target="tpu_custom_call" | custom-call | flops 500000000 | bytes 1500000 | tf_op jit(solution)/shard_map/conv_give/pallas_call | solution.py:251
  257.4 9.2 %glu_back.1 = (f32[256,512]{1,0:T(8,128)}, bf16[256,512]{1,0:T(8,128)(2,1)}, bf16[256,512]{1,0:T(8,128)(2,1)}, f32[1,512]{1,0:T(1,128)}, f32[1,512]{1,0:T(1,128)}) custom-call(s32[5]{0:T(128)} %stack.48.info_ref, bf16[256,2048]{1,0:T(8,128)(2,1)} %get-tuple-element.114.dw_ref, bf16[272,256]{1,0:T(8,128)(2,1)} %get-tuple-element.115.dnar_ref, ...), custom_call_target="tpu_custom_call" | custom-call | flops 1000000000 | bytes 3000000 | tf_op jit(solution)/shard_map/glu_back/pallas_call | solution.py:251
  266.6 2.4 glu_give.1
  269.5 6.3 %all-to-all-start.5 = ((bf16[8,144,128]{2,1,0:T(8,128)(2,1)}), bf16[8,144,128]{2,1,0:T(8,128)(2,1)S(1)}, u32[]{:S(2)}, u32[]{:S(2)}) async-start(bf16[8,144,128]{2,1,0:T(8,128)(2,1)} %bitcast.21), calls=%async_computation.6 | async-start | bytes 589824 | tf_op jit(solution)/shard_map/all_to_all | solution.py:955
  275.8 1.6 copy-done.5
  277.4 6.4 %late_keep.1 = bf16[8,8,208,128]{3,2,1,0:T(8,128)(2,1)} custom-call(s32[5]{0:T(128)} %stack.48.info_ref, bf16[272,512]{1,0:T(8,128)(2,1)} %get-tuple-element.117.n2_ref, bf16[256,2048]{1,0:T(8,128)(2,1)} %get-tuple-element.114.dw_ref, bf16[272,256]{1,0:T(8,128)(2,1)} %get-tuple-element.115.dnar_ref, bf16[256,2048]{1,0:T(8,128)(2,1)} %get-tuple-element.118.sp_ref, ...), custom_call_target="tpu_custom_call" | custom-call | flops 500000000 | bytes 1500000 | tf_op jit(solution)/shard_map/late_keep/pallas_call | solution.py:251
  285.4 8.4 %all-to-all-start.6 = ((bf16[64,208,128]{2,1,0:T(8,128)(2,1)}), bf16[64,208,128]{2,1,0:T(8,128)(2,1)S(1)}, u32[]{:S(2)}, u32[]{:S(2)}) async-start(bf16[64,208,128]{2,1,0:T(8,128)(2,1)} %bitcast.35), calls=%async_computation.7 | async-start | bytes 6815744 | tf_op jit(solution)/shard_map/all_to_all | solution.py:974
  294.9 41.6 %all-to-all-done.6 = bf16[64,208,128]{2,1,0:T(8,128)(2,1)S(1)} async-done(((bf16[64,208,128]{2,1,0:T(8,128)(2,1)}), bf16[64,208,128]{2,1,0:T(8,128)(2,1)S(1)}, u32[]{:S(2)}, u32[]{:S(2)}) %all-to-all-start.6) | async-done | bytes 3407904 | tf_op jit(solution)/shard_map/all_to_all | solution.py:974
  337.0 16.4 %all_to_all.42.near_ref = bf16[8,352,128]{2,1,0:T(8,128)(2,1)S(1)} all-to-all(bf16[8,352,128]{2,1,0:T(8,128)(2,1)S(1)} %broadcast_in_dim.39), channel_id=1, replica_groups=mesh['y'=4,'xh'=2,'core'=2,'xl'=2,'z'=4] {'y','xh'}, dimensions={0} | all-to-all | bytes 1441792 | tf_op jit(solution)/shard_map/all_to_all | solution.py:821
  353.5 3.5 collective-permute-start.21
  356.9 1.8 collective-permute-done.21.far_ref
  359.7 3.7 %unpack.1 = (f32[1,64]{1,0:T(1,128)}, f32[64,512]{1,0:T(8,128)}, f32[64,512]{1,0:T(8,128)}, f32[1,64]{1,0:T(1,128)}, f32[64,2048]{1,0:T(8,128)}, /*index=5*/f32[...) custom-call(s32[5]{0:T(128)} %stack.48.info_ref, ...), custom_call_target="tpu_custom_call" | custom-call | flops 3000000000 | bytes 9000000 | tf_op jit(solution)/shard_map/unpack/pallas_call | solution.py:251
  (105 shorter events, 30.3 us)
Async XLA Ops:
  7.2 16.8 %copy-start.12 = (bf16[9,256]{1,0:T(8,128)(2,1)S(1)}, bf16[9,256]{1,0:T(8,128)(2,1)}, u32[]{:S(2)}) copy-start(bf16[9,256]{1,0:T(8,128)(2,1)} %param.30) | copy-start | bytes 13828
  11.9 7.7 %collective-permute-start.2 = (bf16[512,256]{1,0:T(8,128)(2,1)S(1)}, bf16[512,256]{1,0:T(8,128)(2,1)S(1)}, u32[]{:S(2)}, u32[]{:S(2)}) collective-permute-start(bf16[512,256]{1,0:T(8,128)(2,1)S(1)} %select_dynamic-update-slice_fusion), channel_id=1, source_target_pairs={{0,4},{1,5},{2,6},{3,7},{4,0},{5,1},{6,2},{7,3},{8,12},{9,13},{10,... | collective-permute-start | bytes 786440 | tf_op jit(solution)/shard_map/ppermute | solution.py:53
  19.7 61.0 %copy-start.2 = (bf16[2,512,256]{2,1,0:T(8,128)(2,1)}, bf16[2,512,256]{2,1,0:T(8,128)(2,1)S(1)}, u32[]{:S(2)}) copy-start(bf16[2,512,256]{2,1,0:T(8,128)(2,1)S(1)} %maximum_select_fusion.refs_0_) | copy-start | bytes 1572868
  19.7 19.7 %collective-permute-start.4 = (bf16[2,512,256]{2,1,0:T(8,128)(2,1)S(1)}, bf16[2,512,256]{2,1,0:T(8,128)(2,1)S(1)}, u32[]{:S(2)}, u32[]{:S(2)}) collective-permute-start(bf16[2,512,256]{2,1,0:T(8,128)(2,1)S(1)} %maximum_select_fusion.refs_0_), channel_id=1, source_target_pairs={{0,3},{1,0},{2,1},{3,2},{4,7},{5,4},{6,5},{7,6},{8,11},{9,8},{10,9... | collective-permute-start | bytes 1572872 | tf_op jit(solution)/shard_map/ppermute | solution.py:53
  23.9 19.7 %collective-permute-start.3 = (bf16[2,512,256]{2,1,0:T(8,128)(2,1)S(1)}, bf16[2,512,256]{2,1,0:T(8,128)(2,1)S(1)}, u32[]{:S(2)}, u32[]{:S(2)}) collective-permute-start(bf16[2,512,256]{2,1,0:T(8,128)(2,1)S(1)} %maximum_select_fusion.refs_0_), channel_id=1, source_target_pairs={{0,1},{1,2},{2,3},{3,0},{4,5},{5,6},{6,7},{7,4},{8,9},{9,10},{10,1... | collective-permute-start | bytes 1572872 | tf_op jit(solution)/shard_map/ppermute | solution.py:53
  25.2 31.9 %all-to-all-start = ((bf16[8,352,256]{2,1,0:T(8,128)(2,1)}), bf16[8,352,256]{2,1,0:T(8,128)(2,1)S(1)}, u32[]{:S(2)}, u32[]{:S(2)}) async-start(bf16[8,352,256]{2,1,0:T(8,128)(2,1)} %broadcast_in_dim.36), calls=%async_computation | async-start | bytes 2883584 | tf_op jit(solution)/shard_map/all_to_all | solution.py:821
  30.1 74.8 %all-gather.3.cloned.1.call-start = ((), (), s32[]{:S(2)}) async-start(), calls=%async_computation.10 | async-start | bytes 2654208 | tf_op jit(solution)/shard_map/all_gather | solution.py:878
  39.3 17.8 %copy-start.3 = (bf16[2,512,256]{2,1,0:T(8,128)(2,1)}, bf16[2,512,256]{2,1,0:T(8,128)(2,1)S(1)}, u32[]{:S(2)}) copy-start(bf16[2,512,256]{2,1,0:T(8,128)(2,1)S(1)} %collective-permute-done.4.refs_2_) | copy-start | bytes 1572868
  40.1 14.0 %collective-permute-start.7 = (bf16[2,256,256]{2,1,0:T(8,128)(2,1)}, bf16[2,256,256]{2,1,0:T(8,128)(2,1)S(1)}, u32[]{:S(2)}, u32[]{:S(2)}) collective-permute-start(bf16[2,256,256]{2,1,0:T(8,128)(2,1)} %slice.101), channel_id=1, source_target_pairs={{0,3},{1,0},{2,1},{3,2},{4,7},{5,4},{6,5},{7,6},{8,11},{9,8},{10,9... | collective-permute-start | bytes 786440 | tf_op jit(solution)/shard_map/ppermute | solution.py:53
  43.6 13.5 %copy-start.4 = (bf16[2,512,256]{2,1,0:T(8,128)(2,1)}, bf16[2,512,256]{2,1,0:T(8,128)(2,1)S(1)}, u32[]{:S(2)}) copy-start(bf16[2,512,256]{2,1,0:T(8,128)(2,1)S(1)} %collective-permute-done.3.refs_1_) | copy-start | bytes 1572868
  44.4 12.6 %collective-permute-start.6 = (bf16[2,256,256]{2,1,0:T(8,128)(2,1)}, bf16[2,256,256]{2,1,0:T(8,128)(2,1)S(1)}, u32[]{:S(2)}, u32[]{:S(2)}) collective-permute-start(bf16[2,256,256]{2,1,0:T(8,128)(2,1)} %slice.100), channel_id=1, source_target_pairs={{0,1},{1,2},{2,3},{3,0},{4,5},{5,6},{6,7},{7,4},{8,9},{9,10},{10,1... | collective-permute-start | bytes 786440 | tf_op jit(solution)/shard_map/ppermute | solution.py:53
  54.0 26.6 %copy-start.7 = (bf16[2,256,256]{2,1,0:T(8,128)(2,1)}, bf16[2,256,256]{2,1,0:T(8,128)(2,1)S(1)}, u32[]{:S(2)}) copy-start(bf16[2,256,256]{2,1,0:T(8,128)(2,1)S(1)} %collective-permute-done.7.refs_4_) | copy-start | bytes 786436
  57.1 0.7 copy-start.8
  57.8 18.2 %copy-start = (bf16[8,352,256]{2,1,0:T(8,128)(2,1)}, bf16[8,352,256]{2,1,0:T(8,128)(2,1)S(1)}, u32[]{:S(2)}) copy-start(bf16[8,352,256]{2,1,0:T(8,128)(2,1)S(1)} %all-to-all-done.near_ref.small_ref) | copy-start | bytes 4325380
  59.0 16.8 %collective-permute-start.5 = (bf16[8,320,256]{2,1,0:T(8,128)(2,1)}, bf16[8,320,256]{2,1,0:T(8,128)(2,1)S(1)}, u32[]{:S(2)}, u32[]{:S(2)}) collective-permute-start(bf16[8,320,256]{2,1,0:T(8,128)(2,1)} %slice.86.refs_10_.near_ref), channel_id=1, source_target_pairs={{0,8},{1,9},{2,10},{3,11},{4,12},{5,13},{6,14},{7,15},{8,0},{9,1},... | collective-permute-start | bytes 3932168 | tf_op jit(solution)/shard_map/ppermute | solution.py:53
  63.9 16.8 %collective-permute-start.8 = (bf16[2,512,256]{2,1,0:T(8,128)(2,1)S(1)}, bf16[2,512,256]{2,1,0:T(8,128)(2,1)}, u32[]{:S(2)}, u32[]{:S(2)}) collective-permute-start(bf16[2,512,256]{2,1,0:T(8,128)(2,1)S(1)} %maximum_select_fusion.refs_0_), channel_id=1, source_target_pairs={{0,8},{1,9},{2,10},{3,11},{4,12},{5,13},{6,14},{7,15},{8,0},{9,1},... | collective-permute-start | bytes 1572872 | tf_op jit(solution)/shard_map/ppermute | solution.py:53
  63.9 16.8 %collective-permute-start.10 = (bf16[2,512,256]{2,1,0:T(8,128)(2,1)}, bf16[2,512,256]{2,1,0:T(8,128)(2,1)}, u32[]{:S(2)}, u32[]{:S(2)}) collective-permute-start(bf16[2,512,256]{2,1,0:T(8,128)(2,1)} %copy-done.3), channel_id=1, source_target_pairs={{0,8},{1,9},{2,10},{3,11},{4,12},{5,13},{6,14},{7,15},{8,0},{9,1},... | collective-permute-start | bytes 1572872 | tf_op jit(solution)/shard_map/ppermute | solution.py:53
  64.4 16.3 %collective-permute-start.9 = (bf16[2,512,256]{2,1,0:T(8,128)(2,1)}, bf16[2,512,256]{2,1,0:T(8,128)(2,1)}, u32[]{:S(2)}, u32[]{:S(2)}) collective-permute-start(bf16[2,512,256]{2,1,0:T(8,128)(2,1)} %copy-done.4), channel_id=1, source_target_pairs={{0,8},{1,9},{2,10},{3,11},{4,12},{5,13},{6,14},{7,15},{8,0},{9,1},... | collective-permute-start | bytes 1572872 | tf_op jit(solution)/shard_map/ppermute | solution.py:53
  65.2 6.5 %collective-permute-start.1 = (bf16[8,512]{1,0:T(8,128)(2,1)S(1)}, bf16[8,512]{1,0:T(8,128)(2,1)S(1)}, u32[]{:S(2)}, u32[]{:S(2)}) collective-permute-start(bf16[8,512]{1,0:T(8,128)(2,1)S(1)} %get-tuple-element.157), channel_id=1, source_target_pairs={{8,0},{9,1},{10,2},{11,3},{12,4},{13,5},{14,6},{15,7},{16,8},{17,9... | collective-permute-start | bytes 24584 | tf_op jit(solution)/shard_map/ppermute | solution.py:53
  71.6 4.3 %copy-start.16 = (bf16[8,512]{1,0:T(8,128)(2,1)}, bf16[8,512]{1,0:T(8,128)(2,1)S(1)}, u32[]{:S(2)}) copy-start(bf16[8,512]{1,0:T(8,128)(2,1)S(1)} %collective-permute-done.1.high_ref) | copy-start | bytes 24580
  71.6 3.2 collective-permute-start
  74.8 5.9 %collective-permute-start.12 = (bf16[2,256,256]{2,1,0:T(8,128)(2,1)S(1)}, bf16[2,256,256]{2,1,0:T(8,128)(2,1)S(1)}, u32[]{:S(2)}, u32[]{:S(2)}) collective-permute-start(bf16[2,256,256]{2,1,0:T(8,128)(2,1)S(1)} %collective-permute-done.7.refs_4_), channel_id=1, source_target_pairs={{0,8},{1,9},{2,10},{3,11},{4,12},{5,13},{6,14},{7,15},{8,0},{9,1},... | collective-permute-start | bytes 786440 | tf_op jit(solution)/shard_map/ppermute | solution.py:53
  75.9 1.0 copy-start.1
  75.9 4.9 %collective-permute-start.11 = (bf16[2,256,256]{2,1,0:T(8,128)(2,1)}, bf16[2,256,256]{2,1,0:T(8,128)(2,1)S(1)}, u32[]{:S(2)}, u32[]{:S(2)}) collective-permute-start(bf16[2,256,256]{2,1,0:T(8,128)(2,1)} %copy-done.8), channel_id=1, source_target_pairs={{0,8},{1,9},{2,10},{3,11},{4,12},{5,13},{6,14},{7,15},{8,0},{9,1},... | collective-permute-start | bytes 786440 | tf_op jit(solution)/shard_map/ppermute | solution.py:53
  80.7 0.7 copy-start.9
  80.7 0.8 copy-start.10
  97.4 21.7 %all-to-all-start.1 = ((bf16[8,192,256]{2,1,0:T(8,128)(2,1)}), bf16[8,192,256]{2,1,0:T(8,128)(2,1)S(1)}, u32[]{:S(2)}, u32[]{:S(2)}) async-start(bf16[8,192,256]{2,1,0:T(8,128)(2,1)} %get-tuple-element.89), calls=%async_computation.1 | async-start | bytes 1572864 | tf_op jit(solution)/shard_map/all_to_all | solution.py:898
  104.9 42.4 %collective-permute-start.14 = (bf16[8,576,256]{2,1,0:T(8,128)(2,1)}, bf16[8,576,256]{2,1,0:T(8,128)(2,1)}, u32[]{:S(2)}, u32[]{:S(2)}) collective-permute-start(bf16[8,576,256]{2,1,0:T(8,128)(2,1)} %bitcast.45), channel_id=1, source_target_pairs={{0,8},{1,9},{2,10},{3,11},{4,12},{5,13},{6,14},{7,15},{8,0},{9,1},... | collective-permute-start | bytes 7077896 | tf_op jit(solution)/shard_map/ppermute | solution.py:53
  119.1 2.7 collective-permute-start.13
  162.6 5.7 %collective-permute-start.15 = (bf16[8,8,144,128]{3,2,1,0:T(8,128)(2,1)}, bf16[8,8,144,128]{3,2,1,0:T(8,128)(2,1)}, u32[]{:S(2)}, u32[]{:S(2)}) collective-permute-start(bf16[8,8,144,128]{3,2,1,0:T(8,128)(2,1)} %early_give.1), channel_id=1, source_target_pairs={{0,8},{1,9},{2,10},{3,11},{4,12},{5,13},{6,14},{7,15},{8,0},{9,1},... | collective-permute-start | bytes 7077896 | tf_op jit(solution)/shard_map/ppermute | solution.py:53
  163.8 12.0 %all-to-all-start.3 = ((bf16[8,64,256]{2,1,0:T(8,128)(2,1)}), bf16[8,64,256]{2,1,0:T(8,128)(2,1)S(1)}, u32[]{:S(2)}, u32[]{:S(2)}) async-start(bf16[8,64,256]{2,1,0:T(8,128)(2,1)} %get-tuple-element.95), calls=%async_computation.3 | async-start | bytes 524288 | tf_op jit(solution)/shard_map/all_to_all | solution.py:911
  167.2 90.2 %reduce-scatter.2.cloned.1.call-start = ((), (), s32[]{:S(2)}) async-start(), calls=%async_computation.9 | async-start | bytes 2654208 | tf_op jit(solution)/shard_map/reduce_scatter | solution.py:923
  194.3 2.7 collective-permute-start.16
  224.7 5.2 %collective-permute-start.17 = (bf16[8,256]{1,0:T(8,128)(2,1)}, bf16[8,256]{1,0:T(8,128)(2,1)S(1)}, u32[]{:S(2)}, u32[]{:S(2)}) collective-permute-start(bf16[8,256]{1,0:T(8,128)(2,1)} %get-tuple-element.106), channel_id=1, source_target_pairs={{0,8},{1,9},{2,10},{3,11},{4,12},{5,13},{6,14},{7,15},{8,16},{9,17... | collective-permute-start | bytes 12296 | tf_op jit(solution)/shard_map/ppermute | solution.py:53
  227.9 6.6 %collective-permute-start.18 = (bf16[8,256]{1,0:T(8,128)(2,1)}, bf16[8,256]{1,0:T(8,128)(2,1)S(1)}, u32[]{:S(2)}, u32[]{:S(2)}) collective-permute-start(bf16[8,256]{1,0:T(8,128)(2,1)} %get-tuple-element.108), channel_id=1, source_target_pairs={{8,0},{9,1},{10,2},{11,3},{12,4},{13,5},{14,6},{15,7},{16,8},{17,9... | collective-permute-start | bytes 12296 | tf_op jit(solution)/shard_map/ppermute | solution.py:53
  229.9 4.7 %copy-start.13 = (bf16[8,256]{1,0:T(8,128)(2,1)}, bf16[8,256]{1,0:T(8,128)(2,1)S(1)}, u32[]{:S(2)}) copy-start(bf16[8,256]{1,0:T(8,128)(2,1)S(1)} %collective-permute-done.17.lo_ref) | copy-start | bytes 12292
  234.6 0.6 copy-start.14
  257.4 18.4 %collective-permute-start.19 = (bf16[8,8,176,128]{3,2,1,0:T(8,128)(2,1)}, bf16[8,8,176,128]{3,2,1,0:T(8,128)(2,1)S(1)}, u32[]{:S(2)}, u32[]{:S(2)}) collective-permute-start(bf16[8,8,176,128]{3,2,1,0:T(8,128)(2,1)} %conv_give.1), channel_id=1, source_target_pairs={{0,8},{1,9},{2,10},{3,11},{4,12},{5,13},{6,14},{7,15},{8,0},{9,1},... | collective-permute-start | bytes 8650760 | tf_op jit(solution)/shard_map/ppermute | solution.py:53
  269.0 6.8 %collective-permute-start.20 = (bf16[8,8,48,128]{3,2,1,0:T(8,128)(2,1)}, bf16[8,8,48,128]{3,2,1,0:T(8,128)(2,1)}, u32[]{:S(2)}, u32[]{:S(2)}) collective-permute-start(bf16[8,8,48,128]{3,2,1,0:T(8,128)(2,1)} %glu_give.1), channel_id=1, source_target_pairs={{0,8},{1,9},{2,10},{3,11},{4,12},{5,13},{6,14},{7,15},{8,0},{9,1},... | collective-permute-start | bytes 2359304 | tf_op jit(solution)/shard_map/ppermute | solution.py:53
  269.5 15.2 %all-to-all-start.5 = ((bf16[8,144,128]{2,1,0:T(8,128)(2,1)}), bf16[8,144,128]{2,1,0:T(8,128)(2,1)S(1)}, u32[]{:S(2)}, u32[]{:S(2)}) async-start(bf16[8,144,128]{2,1,0:T(8,128)(2,1)} %bitcast.21), calls=%async_computation.6 | async-start | bytes 589824 | tf_op jit(solution)/shard_map/all_to_all | solution.py:955
  275.8 1.6 copy-start.5
  284.7 0.7 copy-start.6
  285.4 51.0 %all-to-all-start.6 = ((bf16[64,208,128]{2,1,0:T(8,128)(2,1)}), bf16[64,208,128]{2,1,0:T(8,128)(2,1)S(1)}, u32[]{:S(2)}, u32[]{:S(2)}) async-start(bf16[64,208,128]{2,1,0:T(8,128)(2,1)} %bitcast.35), calls=%async_computation.7 | async-start | bytes 6815744 | tf_op jit(solution)/shard_map/all_to_all | solution.py:974
  353.5 5.3 %copy-start.11 = (bf16[8,352,128]{2,1,0:T(8,128)(2,1)}, bf16[8,352,128]{2,1,0:T(8,128)(2,1)S(1)}, u32[]{:S(2)}) copy-start(bf16[8,352,128]{2,1,0:T(8,128)(2,1)S(1)} %all_to_all.42.near_ref) | copy-start | bytes 2162692
  353.5 5.3 %collective-permute-start.21 = (bf16[8,352,128]{2,1,0:T(8,128)(2,1)S(1)}, bf16[8,352,128]{2,1,0:T(8,128)(2,1)S(1)}, u32[]{:S(2)}, u32[]{:S(2)}) collective-permute-start(bf16[8,352,128]{2,1,0:T(8,128)(2,1)S(1)} %all_to_all.42.near_ref), channel_id=1, source_target_pairs={{0,8},{1,9},{2,10},{3,11},{4,12},{5,13},{6,14},{7,15},{8,0},{9,1},... | collective-permute-start | bytes 2162696 | tf_op jit(solution)/shard_map/ppermute | solution.py:53
  358.8 0.9 copy-start.15
Sparse Core Ops, SparseCore 0:
  57.2 40.6 all-gather.2
  176.0 40.6 reduce-scatter.1

commit v3 on v2

v3 whole, which is shorter than its diff:
```python
import functools

import jax
import jax.numpy as jnp
import numpy as np
from jax import lax
from jax.experimental import pallas as pl
from jax.experimental.pallas import tpu as pltpu
from jax.sharding import Mesh
from jax.sharding import PartitionSpec as P

HEADS = 8
HEAD = 64
EPSILON = 1e-06
AXES = ("y", "xh", "core", "xl", "z")
SIZES = (4, 2, 2, 2, 4)
CTX = ("y", "xh", "core")
CHIPS = ("y", "xh")
WT = ("xl", "z")
LOG2E = 1.4426950408889634
BF = jnp.bfloat16
F32 = jnp.float32


def moves(target):
    pairs = []
    for source in range(int(np.prod(SIZES))):
        place = [int(v) for v in np.unravel_index(source, SIZES)]
        goal = target(*place)
        if goal is not None:
            pairs.append((source, int(np.ravel_multi_index(tuple(goal), SIZES))))
    return pairs


def shift(dy=0, dxh=0, dc=0, dxl=0, dz=0):
    return moves(
        lambda y, xh, c, xl, z: (
            (y + dy) % 4, (xh + dxh) % 2, (c + dc) % 2, (xl + dxl) % 2, (z + dz) % 4,
        )
    )


def along(step):
    def target(y, xh, c, xl, z):
        place = y * 4 + xh * 2 + c + step
        if place < 0 or place > 15:
            return None
        return (place // 4, place // 2 % 2, place % 2, xl, z)
    return moves(target)


def send(value, pairs):
    return lax.ppermute(value, AXES, pairs)


def matmul(left, right):
    return jnp.dot(left, right, preferred_element_type=F32)


def contract(left, right, ldim, rdim):
    return lax.dot_general(
        left, right, (((ldim,), (rdim,)), ((), ())), preferred_element_type=F32
    )


def smooth_unit(value):
    return value * jax.nn.sigmoid(value)


def smooth_slope(value):
    sigma = jax.nn.sigmoid(value)
    return sigma * (1.0 + value * (1.0 - sigma))


VMEM = pl.BlockSpec(memory_space=pltpu.VMEM)
SMEM = pl.BlockSpec(memory_space=pltpu.SMEM)
HBM = pl.BlockSpec(memory_space=pltpu.HBM)
ANY = pl.BlockSpec(memory_space=pl.ANY)
FREE = "free"


def attend_kernel(chips, rows, length_ref, core_ref, near_ref, far_ref, o_ref, e_ref, l_ref,
                  near_out, far_out, keys_ref, values_ref, sem):
    step = pl.program_id(0)
    span = chips * rows
    aug = 2 * HEAD
    pairs = [(near_ref, near_out), (far_ref, far_out)]

    @pl.when(step == chips - 1)
    def _():
        for i, (source, target) in enumerate(pairs):
            pltpu.make_async_copy(source, target, sem.at[i]).wait()

    @pl.when(step == 0)
    def _():
        launch(pairs, sem)
        length = length_ref[0]
        core = core_ref[0]
        ones = jnp.ones((16, rows), F32)
        for side in range(2):
            source = near_ref if side == 0 else far_ref
            base = HEAD if side == 0 else 0
            owner = core if side == 0 else 1 - core
            for chip in range(chips):
                cols = slice(side * span + chip * rows, side * span + (chip + 1) * rows)
                key = source[chip, base:base + HEAD, :]
                keys_ref[0:HEAD, cols] = key
                keys_ref[HEAD:aug, cols] = key
                place = (chip * 2 + owner) * rows + lax.broadcasted_iota(jnp.int32, (16, rows), 1)
                row = lax.broadcasted_iota(jnp.int32, (16, rows), 0)
                bias = jnp.where((place < length) | (row > 0), 0.0, -1e30)
                keys_ref[aug:aug + 16, cols] = bias.astype(BF)
                value = source[chip, base + HEAD:base + 2 * HEAD, :].astype(F32)
                stacked = jnp.concatenate([value, ones, jnp.zeros((48, rows), F32)], 0)
                values_ref[cols, :] = stacked.T.astype(BF)

    query = near_ref[step, 0:HEAD, :].astype(F32) * (LOG2E * HEAD ** -0.5)
    high = query.astype(BF)
    low = (query - high.astype(F32)).astype(BF)
    query = jnp.concatenate([high, low, jnp.ones((16, rows), BF)], 0)
    scores = contract(query, keys_ref[...], 0, 0)
    top = jnp.max(scores, 1, keepdims=True)
    expo = jnp.exp2(scores - top).astype(BF)
    e_ref[...] = expo
    out = matmul(expo, values_ref[...]).T
    inverse = 1.0 / out[HEAD:HEAD + 8]
    o_ref[0] = (out[0:HEAD] * inverse[0:1]).astype(BF)
    l_ref[0] = inverse


def attend(near, far, length, core):
    chips, _, rows = near.shape
    tokens = 2 * chips * rows
    return pl.pallas_call(
        functools.partial(attend_kernel, chips, rows),
        grid=(chips,),
        in_specs=[
            pl.BlockSpec(memory_space=pltpu.SMEM),
            pl.BlockSpec(memory_space=pltpu.SMEM),
            pl.BlockSpec(near.shape, lambda i: (0, 0, 0)),
            pl.BlockSpec(far.shape, lambda i: (0, 0, 0)),
        ],
        out_specs=[
            pl.BlockSpec((1, HEAD, rows), lambda i: (i, 0, 0)),
            pl.BlockSpec((rows, tokens), lambda i: (i, 0)),
            pl.BlockSpec((1, 8, rows), lambda i: (i, 0, 0)),
            HBM,
            HBM,
        ],
        out_shape=[
            pltpu.HBM((chips, HEAD, rows), BF),
            pltpu.HBM((chips * rows, tokens), BF),
            pltpu.HBM((chips, 8, rows), F32),
            pltpu.HBM(near.shape, BF),
            pltpu.HBM(far.shape, BF),
        ],
        scratch_shapes=[
            pltpu.VMEM((2 * HEAD + 16, tokens), BF),
            pltpu.VMEM((tokens, 2 * HEAD), BF),
            pltpu.SemaphoreType.DMA((2,)),
        ],
        compiler_params=pltpu.CompilerParams(vmem_limit_bytes=32 * 2**20),
        cost_estimate=cost(14),
        name="attend",
    )(length, core, near, far)


def attend_back_kernel(chips, rows, near_ref, far_ref, e_ref, o_ref, l_ref, do_ref,
                       dq_ref, dk_ref, dv_ref, keys_ref, values_ref, dk_acc, dv_acc):
    step = pl.program_id(0)
    span = chips * rows

    @pl.when(step == 0)
    def _():
        row = lax.broadcasted_iota(jnp.int32, (16, rows), 0)
        ones = jnp.where(row < 3, 1.0, 0.0).astype(BF)
        for side in range(2):
            source = near_ref if side == 0 else far_ref
            base = HEAD if side == 0 else 0
            for chip in range(chips):
                cols = slice(side * span + chip * rows, side * span + (chip + 1) * rows)
                key = source[chip, base:base + HEAD, :].astype(F32)
                stacked = jnp.concatenate([key, jnp.zeros((HEAD, rows), F32)], 0)
                keys_ref[cols, :] = stacked.T.astype(BF)
                values_ref[0:HEAD, cols] = source[chip, base + HEAD:base + 2 * HEAD, :]
                values_ref[HEAD:HEAD + 16, cols] = ones
        dk_acc[...] = jnp.zeros_like(dk_acc)
        dv_acc[...] = jnp.zeros_like(dv_acc)

    inverse = l_ref[0, 0:1, :]
    grad = do_ref[0].astype(F32) * inverse
    total = -jnp.sum(grad * o_ref[0].astype(F32), 0, keepdims=True)
    high = total.astype(BF).astype(F32)
    mid = (total - high).astype(BF).astype(F32)
    low = total - high - mid
    grad_low = grad.astype(BF)
    row = lax.broadcasted_iota(jnp.int32, (16, rows), 0)
    extra = jnp.where(row == 0, high, jnp.where(row == 1, mid, jnp.where(row == 2, low, 0.0)))
    grads = jnp.concatenate([grad_low, extra.astype(BF)], 0)
    query = near_ref[step, 0:HEAD, :]
    block = 1024
    dq = jnp.zeros((rows, 2 * HEAD), F32)
    for start in range(0, 2 * span, block):
        cols = slice(start, start + block)
        expo = e_ref[:, cols]
        d_probs = contract(grads, values_ref[:, cols], 0, 0)
        d_scores = (expo.astype(F32) * d_probs).astype(BF)
        dq = dq + matmul(d_scores, keys_ref[cols, :])
        dk_acc[:, cols] += matmul(query, d_scores)
        dv_acc[:, cols] += matmul(grad_low, expo)
    dq_ref[0] = (dq.T[0:HEAD] * HEAD ** -0.5).astype(BF)

    @pl.when(step == chips - 1)
    def _():
        for side in range(2):
            for chip in range(chips):
                cols = slice(side * span + chip * rows, side * span + (chip + 1) * rows)
                dk_ref[side, chip] = (dk_acc[:, cols] * HEAD ** -0.5).astype(BF)
                dv_ref[side, chip] = dv_acc[:, cols].astype(BF)


def attend_back(near, far, expo, out, inverse, d_out):
    chips, _, rows = near.shape
    tokens = 2 * chips * rows
    whole = lambda i: (0, 0, 0)
    one = lambda i: (i, 0, 0)
    return pl.pallas_call(
        functools.partial(attend_back_kernel, chips, rows),
        grid=(chips,),
        in_specs=[
            pl.BlockSpec(near.shape, whole),
            pl.BlockSpec(far.shape, whole),
            pl.BlockSpec((rows, tokens), lambda i: (i, 0)),
            pl.BlockSpec((1, HEAD, rows), one),
            pl.BlockSpec((1, 8, rows), one),
            pl.BlockSpec((1, HEAD, rows), one),
        ],
        out_specs=[
            pl.BlockSpec((1, HEAD, rows), one),
            pl.BlockSpec((2, chips, HEAD, rows), lambda i: (0, 0, 0, 0)),
            pl.BlockSpec((2, chips, HEAD, rows), lambda i: (0, 0, 0, 0)),
        ],
        out_shape=[
            pltpu.HBM((chips, HEAD, rows), BF),
            jax.ShapeDtypeStruct((2, chips, HEAD, rows), BF),
            jax.ShapeDtypeStruct((2, chips, HEAD, rows), BF),
        ],
        scratch_shapes=[
            pltpu.VMEM((tokens, 2 * HEAD), BF),
            pltpu.VMEM((HEAD + 16, tokens), BF),
            pltpu.VMEM((HEAD, tokens), F32),
            pltpu.VMEM((HEAD, tokens), F32),
        ],
        compiler_params=pltpu.CompilerParams(vmem_limit_bytes=32 * 2**20),
        cost_estimate=cost(3),
        name="attend_back",
    )(in_hbm(near), in_hbm(far), in_hbm(expo), in_hbm(out), in_hbm(inverse), d_out)


RIM = 8
ACT_N4 = slice(4096, 4608)
ACT_GY = slice(4608, 5120)
ACT_GA = slice(5120, 5632)
EARLY = 144
SMALL = 320
MIDDLE = 80
LATE = 128


def call(kernel, outs, specs, scratch, name, micros, *args):
    args = [arg if spec in (SMEM, FREE, ANY) else in_hbm(arg) for arg, spec in zip(args, specs)]
    kinds = [out[2] if len(out) > 2 else VMEM for out in outs]
    return pl.pallas_call(
        kernel,
        in_specs=[VMEM if spec is FREE else spec for spec in specs],
        out_specs=[VMEM if kind is FREE else kind for kind in kinds],
        out_shape=[
            (jax.ShapeDtypeStruct if kind is FREE else pltpu.HBM)(out[0], out[1])
            for kind, out in zip(kinds, outs)
        ],
        scratch_shapes=scratch,
        compiler_params=pltpu.CompilerParams(vmem_limit_bytes=32 * 2**20),
        cost_estimate=cost(micros),
        name=name,
    )(*args)


def in_hbm(value):
    return pltpu.with_memory_space_constraint(value, pltpu.HBM)


def cost(micros):
    return pl.CostEstimate(
        flops=int(micros * 1.0e9), bytes_accessed=int(micros * 3.0e6), transcendentals=0
    )


def launch(pairs, sems):
    copies = [
        pltpu.make_async_copy(source, target, sems.at[i]) for i, (source, target) in enumerate(pairs)
    ]
    for copy in copies:
        copy.start()
    return copies


def fetch(core, near_ref, far_ref, both_ref, sems):
    return launch([(near_ref, both_ref.at[core]), (far_ref, both_ref.at[1 - core])], sems)


def settle(copies):
    for copy in copies:
        copy.wait()


def gains_of(small_ref):
    total = small_ref[0, 0:16, :].astype(F32)
    for w in range(1, 8):
        total = total + small_ref[w, 0:16, :].astype(F32)
    return jnp.concatenate([total[0:8], total[8:16]], 1)


def taps_of(small_ref, index):
    small = small_ref[index, 16:32, :].astype(F32)
    return small[0:9], small[9:10]


def normal_of(value):
    average = jnp.mean(value, -1, keepdims=True)
    centred = value - average
    scale = lax.rsqrt(jnp.mean(centred * centred, -1, keepdims=True) + EPSILON)
    return centred * scale, scale


def back_of(incoming, normal, scale, gain):
    scaled = incoming * gain
    return scale * (
        scaled
        - jnp.mean(scaled, -1, keepdims=True)
        - normal * jnp.mean(scaled * normal, -1, keepdims=True)
    )


def column_sum(value):
    return jnp.sum(value, 0, keepdims=True)


def mask_of(info_ref, count, before):
    place = info_ref[1] - before + lax.broadcasted_iota(jnp.int32, (count, 1), 0)
    return jnp.where((place >= 0) & (place < info_ref[2]), 1.0, 0.0)


def block_cols(index, size=256):
    return pl.ds(pl.multiple_of(index * size, size), size)


def upper_block(both_ref, index):
    rows = pl.ds(pl.multiple_of(lax.rem(index, 4) * 64, 64), 64)
    if len(both_ref.shape) == 5:
        return both_ref[lax.div(index, 4), :, :, rows, :].reshape(512, 256)
    return both_ref[lax.div(index, 4), :, rows, :].reshape(512, 256)


def narrow_block(both_ref, tap):
    return both_ref[0, :, :, 256 + 64 * tap:320 + 64 * tap, :].reshape(512, 256)


def point_block(both_ref, index):
    return both_ref[1, lax.div(index, 4), lax.rem(index, 4), 256:512, :]


def collect(info_ref, near_refs, far_refs, both_ref, sems, rows=slice(0, 512)):
    core, x, z = info_ref[0], info_ref[5], info_ref[4]
    copies = []
    for side, refs in ((core, near_refs), (1 - core, far_refs)):
        for i, ref in enumerate(refs):
            place = x if i < 4 else 1 - x
            target = both_ref.at[side, place, lax.rem(z + i % 4, 4), rows]
            copies.append((ref.at[rows], target))
    return launch(copies, sems)


def glu_of(both_ref, side):
    return jnp.concatenate(
        [both_ref[side, :, 64 * i:64 * i + 64, :].reshape(512, 256) for i in range(2)], 1
    )


def queries_of(both_ref, side, part):
    return both_ref[side, :, 64 * part:64 * part + 64, :].reshape(512, 256)


def small_pair(one_ref, small_ref):
    return (one_ref.at[0, :, SMALL:SMALL + 32, :], small_ref)


def glu_kernel(info_ref, low_ref, x_ref, high_ref, near_ref, far_ref, n1_ref, a_ref, sg_ref, h1_ref,
               main_ref, one_ref, w_ref, sem):
    rows = x_ref.shape[0]
    main = slice(RIM, RIM + rows)
    copies = fetch(info_ref[0], near_ref, far_ref, w_ref, sem)
    x = jnp.concatenate(
        [low_ref[...].astype(F32), x_ref[...].astype(F32), high_ref[...].astype(F32)], 0
    )
    normal, _ = normal_of(x)
    settle(copies)
    copies = launch([(w_ref, one_ref)], sem)
    normed = normal * gains_of(w_ref.at[0, :, SMALL:SMALL + 32, :])[0:1]
    n1 = normed.astype(BF)
    n1_ref[...] = normed[main].astype(BF)
    a = matmul(n1, glu_of(w_ref, 0))
    sg = jax.nn.sigmoid(matmul(n1, glu_of(w_ref, 1)))
    a_ref[...] = a[main]
    sg_ref[...] = sg[main]
    h1 = x + a * sg
    h1_ref[...] = h1
    main_ref[...] = h1[main]
    settle(copies)


def conv_kernel(info_ref, h1_ref, *refs):
    near2, far2, rest = refs[0:8], refs[8:16], refs[16:]
    conv_body(info_ref, h1_ref, near2, far2, *rest)


def conv_body(info_ref, h1_ref, near2, far2, one_ref,
              n2_ref, wp_out, np_ref, nm_out, mean_ref, scale_ref, sp_out, h2_ref, n3_ref,
              qkv_ref, two_ref, w2_ref, wq_ref, small_ref, mix_ref, wp_ref, nm_ref, sp_ref,
              sem2, semq, sems):
    core = info_ref[0]
    rim_rows = h1_ref.shape[0]
    rows = rim_rows - 2 * RIM
    copiesq = launch(
        [small_pair(one_ref, small_ref), (one_ref.at[:, :, 128:SMALL, :], wq_ref)], semq
    )
    copies2 = collect(info_ref, near2, far2, w2_ref, sem2)
    settle(copiesq[:1])

    def leaving(which, index):
        source, target = ((wp_ref, wp_out), (nm_ref, nm_out), (sp_ref, sp_out))[which]
        cols = block_cols(index)
        return pltpu.make_async_copy(source.at[:, cols], target.at[:, cols], sems.at[which, index])

    gains = gains_of(small_ref)
    valid = mask_of(info_ref, rim_rows, RIM)
    normal, _ = normal_of(h1_ref[...])
    n2f = normal * gains[1:2] * valid
    n2 = n2f.astype(BF)
    n2_ref[...] = n2
    n2f = n2.astype(F32)
    settle(copies2)
    copies2 = launch([(w2_ref, two_ref)], sem2)
    narrow = jnp.zeros((rim_rows, 256), F32)
    for tap in range(3):
        if tap == 1:
            moved = n2
        else:
            moved = pltpu.roll(n2f, 1 if tap == 0 else rim_rows - 1, 0).astype(BF)
        narrow = narrow + matmul(moved, narrow_block(w2_ref, tap))
    np_ref[...] = narrow
    narrow = smooth_unit(narrow)

    def first_pass(index, total):
        cols = block_cols(index)
        wide = matmul(n2_ref[...], upper_block(w2_ref, index))
        wp_ref[:, cols] = wide
        leaving(0, index).start()
        mixed = smooth_unit(wide) + narrow * jnp.where(index == 0, 1.0, 0.0)
        mix_ref[:, cols] = mixed
        return total + jnp.sum(mixed, -1, keepdims=True)

    total = lax.fori_loop(0, 8, first_pass, jnp.zeros((rim_rows, 1), F32))
    mean = total * (1.0 / 2048)

    def second_pass(index, total):
        centred = mix_ref[:, block_cols(index)] - mean
        return total + jnp.sum(centred * centred, -1, keepdims=True)

    total = lax.fori_loop(0, 8, second_pass, jnp.zeros((rim_rows, 1), F32))
    scale = lax.rsqrt(total * (1.0 / 2048) + EPSILON)
    mean_ref[...] = jnp.broadcast_to(mean, mean_ref.shape)
    scale_ref[...] = jnp.broadcast_to(scale, scale_ref.shape)
    h2_ref[...] = h1_ref[RIM:RIM + rows, :]

    def third_pass(index, carry):
        cols = block_cols(index)
        taps, gain = taps_of(small_ref, index)
        nm = ((mix_ref[:, cols] - mean) * scale * gain * valid).astype(BF)
        nm_ref[:, cols] = nm
        leaving(1, index).start()
        mix_ref[:, cols] = nm.astype(F32)
        spread = jnp.zeros((rows, 256), F32)
        for tap in range(9):
            spread = spread + mix_ref[4 + tap:4 + tap + rows, cols] * taps[tap:tap + 1]
        spread = spread.astype(BF)
        sp_ref[:, cols] = spread
        leaving(2, index).start()
        h2_ref[:, 0:256] += matmul(spread, point_block(w2_ref, index))
        return carry

    lax.fori_loop(0, 8, third_pass, 0)
    normal, _ = normal_of(h2_ref[...])
    n3 = (normal * gains[2:3]).astype(BF)
    n3_ref[...] = n3
    settle(copiesq[1:])
    for part in range(3):
        for side in range(2):
            block = matmul(n3, queries_of(wq_ref, side, part))
            qkv_ref[4 * side:4 * side + 4, 64 * part:64 * part + 64, :] = (
                block.T.astype(BF).reshape(4, 64, rows)
            )
    settle(copies2)
    for which in range(3):
        for index in range(8):
            leaving(which, index).wait()


def ffn_kernel(info_ref, h2_ref, o_ref, cot_ref, one_ref, near_ref, far_ref,
               out_ref, acts_ref, g3_ref, dob_ref, gain_ref, heads_ref,
               w_ref, small_ref, y_ref, dn_ref, sem):
    rows = h2_ref.shape[0]
    core = info_ref[0]
    x = info_ref[5]
    pairs = [small_pair(one_ref, small_ref)]
    for side, ref in ((core, near_ref), (1 - core, far_ref)):
        pairs += [(ref.at[:, 0], w_ref.at[side, x]), (ref.at[:, 1], w_ref.at[side, 1 - x])]
    copies = launch(pairs, sem)
    valid = mask_of(info_ref, rows, 0)
    heads_ref[...] = o_ref[...]
    heads = o_ref[...].reshape(512, rows)
    gy = (cot_ref[...].astype(F32) * valid).astype(BF)
    acts_ref[:, ACT_GY] = gy
    settle(copies)
    gains = gains_of(small_ref)
    outs = [w_ref[side, :, :, 512:576, :].reshape(512, 256) for side in range(2)]
    h3 = h2_ref[...] + jnp.concatenate([contract(heads, outs[side], 0, 0) for side in range(2)], 1)
    normal, scale = normal_of(h3)
    acts_ref[:, ACT_N4] = (normal * gains[3:4]).astype(BF)
    y_ref[...] = h3
    dn_ref[...] = jnp.zeros_like(dn_ref)

    def step(index, carry):
        cols = block_cols(index)
        upper = upper_block(w_ref, index)
        lower = [w_ref[side, lax.div(index, 4), lax.rem(index, 4), 256:512, :] for side in range(2)]
        u = matmul(acts_ref[:, ACT_N4], upper)
        sigma = jax.nn.sigmoid(u)
        r = (u * sigma).astype(BF)
        acts_ref[:, cols] = r
        y_ref[:, 0:256] += matmul(r, lower[0])
        y_ref[:, 256:512] += matmul(r, lower[1])
        dr = contract(acts_ref[:, 4608:4864], lower[0], 1, 1) + contract(acts_ref[:, 4864:5120], lower[1], 1, 1)
        du = (dr * (sigma * (1.0 + u * (1.0 - sigma)))).astype(BF)
        acts_ref[:, block_cols(index + 8)] = du
        dn_ref[...] += contract(du, upper, 1, 1)
        return carry

    lax.fori_loop(0, 8, step, 0)
    out_ref[...] = (y_ref[...] * valid).astype(BF)
    dn = dn_ref[...]
    gain_ref[...] = column_sum(dn * normal)
    g3 = gy.astype(F32) + back_of(dn, normal, scale, gains[3:4])
    g3_ref[...] = g3
    ga = g3.astype(BF)
    acts_ref[:, ACT_GA] = ga
    dob = contract(outs[0], ga[:, 0:256], 1, 1) + contract(outs[1], ga[:, 256:512], 1, 1)
    dob_ref[...] = dob.astype(BF).reshape(HEADS, HEAD, rows)


def pair_rows(value):
    split = value.reshape(8, 8, 8, 256)
    return jnp.concatenate([split[..., 0:128], split[..., 128:256]], 2)


FULL = slice(None)


def by_chip(out_ref, c, rows, value):
    out_ref[c % 2, :, :, c // 2, rows, :] = value.astype(BF).reshape((2, 4) + value.shape[1:])


def by_shard(out_ref, w, rows, value):
    value = value.astype(BF).reshape((4, 2) + value.shape[1:])
    for xh in range(2):
        out_ref[xh, w // 4, w % 4, :, rows, :] = value[:, xh]


def both(product, pairs):
    return sum((product(*pair) for pair in pairs[1:]), product(*pairs[0]))


def early_kernel(info_ref, acts_ref, heads_ref, acts2_ref, heads2_ref, out_ref):
    rows = acts_ref.shape[0]
    side = info_ref[0]
    refs = (acts_ref, acts2_ref)
    for j in range(4):
        cols = block_cols(side * 4 + j + 8)
        res = both(lambda n, d: contract(n, d, 0, 0), [(ref[:, ACT_N4], ref[:, cols]) for ref in refs])
        for i in range(2):
            by_chip(out_ref, 2 * j + i, slice(0, 64), res[:, 128 * i:128 * i + 128].reshape(8, 64, 128))
    gy = [ref[:, block_cols(side + 18)] for ref in refs]
    for w in range(8):
        cols = slice(256 * w, 256 * w + 256)
        res = both(lambda g, r: contract(g, r, 0, 0), [(g, ref[:, cols]) for g, ref in zip(gy, refs)])
        res = res.reshape(8, 32, 256)
        for i in range(2):
            by_shard(out_ref, w, slice(64 + 32 * i, 96 + 32 * i), res[:, :, 128 * i:128 * i + 128])
    ga = block_cols(side + 20)
    res = both(matmul, [(h[...].reshape(512, rows), ref[:, ga])
                        for h, ref in zip((heads_ref, heads2_ref), refs)])
    packed = pair_rows(res)
    for c in range(8):
        by_chip(out_ref, c, slice(128, 144), packed[:, c])


def attn_in_kernel(info_ref, d_ref, h2_ref, g3_ref, one_ref,
                   g2_ref, gs_ref, lo_ref, hi_ref, gain_ref, w_ref, small_ref, sem):
    rows = h2_ref.shape[0]
    copies = launch(
        [small_pair(one_ref, small_ref), (one_ref.at[:, :, 128:SMALL, :], w_ref)], sem
    )
    normal, scale = normal_of(h2_ref[...])
    settle(copies)
    gains = gains_of(small_ref)
    dn = jnp.zeros((rows, 512), F32)
    for part in range(3):
        for side in range(2):
            block = d_ref[4 * side:4 * side + 4, 64 * part:64 * part + 64, :].reshape(256, rows)
            dn = dn + contract(block, queries_of(w_ref, side, part), 0, 1)
    gain_ref[...] = column_sum(dn * normal)
    g2 = g3_ref[...] + back_of(dn, normal, scale, gains[2:3])
    g2_ref[...] = g2
    gs = g2[:, 0:256]
    gs_ref[...] = gs.astype(BF)
    lo_ref[...] = gs[0:RIM].astype(BF)
    hi_ref[...] = gs[rows - RIM:rows].astype(BF)


def conv_back_kernel(info_ref, lo_ref, gs_ref, hi_ref, nm_ref, wp_ref, np_ref, mean_ref,
                     scale_ref, two_ref, one_ref, dw_ref, dnar_ref, table_ref,
                     pt_ref, small_ref, nmf_ref, dsp_ref, sc_ref, hat_ref, sem):
    rim_rows = wp_ref.shape[0]
    rows = rim_rows - 2 * RIM
    main = slice(RIM, RIM + rows)
    copies = launch(
        [small_pair(one_ref, small_ref), (two_ref.at[1, :, :, 256:512, :], pt_ref)], sem
    )
    valid = mask_of(info_ref, rim_rows, RIM)
    gs = jnp.concatenate(
        [lo_ref[...].astype(F32), gs_ref[...].astype(F32), hi_ref[...].astype(F32)], 0
    ).astype(BF)
    mean = mean_ref[:, 0:1]
    scale = scale_ref[:, 0:1]
    table_ref[...] = jnp.zeros_like(table_ref)
    dsp_ref[0:RIM, :] = jnp.zeros((RIM, 256), F32)
    dsp_ref[RIM + rim_rows:, :] = jnp.zeros((RIM, 256), F32)
    settle(copies)

    def first_pass(index, carry):
        one, two = carry
        cols = block_cols(index)
        taps, gain = taps_of(small_ref, index)
        dsp = contract(gs, pt_ref[lax.div(index, 4), lax.rem(index, 4)], 1, 1).astype(BF).astype(F32)
        dsp_ref[RIM:RIM + rim_rows, :] = dsp
        nmf_ref[...] = nm_ref[:, cols].astype(F32)
        inner = dsp[main]
        dn = jnp.zeros((rim_rows, 256), F32)
        for tap in range(9):
            dn = dn + dsp_ref[12 - tap:12 - tap + rim_rows, :] * taps[tap:tap + 1]
            table_ref[tap:tap + 1, cols] = column_sum(nmf_ref[4 + tap:4 + tap + rows, :] * inner)
        dn = dn * valid
        mixed = smooth_unit(wp_ref[:, cols]) + smooth_unit(np_ref[...]) * jnp.where(index == 0, 1.0, 0.0)
        hat = (mixed - mean) * scale
        hat_ref[:, cols] = hat
        table_ref[9:10, cols] = column_sum((dn * hat)[main])
        scaled = dn * gain
        sc_ref[:, cols] = scaled
        return (one + jnp.sum(scaled, -1, keepdims=True),
                two + jnp.sum(scaled * hat, -1, keepdims=True))

    zero = jnp.zeros((rim_rows, 1), F32)
    one, two = lax.fori_loop(0, 8, first_pass, (zero, zero))
    one = one * (1.0 / 2048)
    two = two * (1.0 / 2048)
    back = scale * (sc_ref[:, 0:256] - one - hat_ref[:, 0:256] * two)
    dnar_ref[...] = (back * smooth_slope(np_ref[...])).astype(BF)

    def second_pass(index, carry):
        cols = block_cols(index)
        back = scale[main] * (
            sc_ref[main, cols] - one[main] - hat_ref[main, cols] * two[main]
        )
        dw_ref[:, cols] = (back * smooth_slope(wp_ref[main, cols])).astype(BF)
        return carry

    lax.fori_loop(0, 8, second_pass, 0)


def glu_back_kernel(info_ref, dw_ref, dnar_ref, h1_ref, two_ref, one_ref, g2_ref,
                    a_ref, sg_ref, x_ref, table_ref, gattn_ref, gffn_ref, dx_ref, dab_ref, sums_ref,
                    w2_ref, w1_ref, small_ref, dn_ref, nar_ref, sem):
    rows = g2_ref.shape[0]
    copies = launch([(two_ref, w2_ref)], sem)
    copies1 = launch(
        [small_pair(one_ref, small_ref), (one_ref.at[:, :, 0:128, :], w1_ref)], sem.at[1:3]
    )
    valid = mask_of(info_ref, rows, 0)
    nar_ref[...] = dnar_ref[...].astype(F32)
    dn_ref[...] = jnp.zeros_like(dn_ref)
    normal, scale1 = normal_of(h1_ref[...])
    settle(copies)
    for tap in range(3):
        moved = nar_ref[9 - tap:9 - tap + rows, :].astype(BF)
        dn_ref[...] += contract(moved, narrow_block(w2_ref, tap), 1, 1)

    def step(index, carry):
        dn_ref[...] += contract(dw_ref[:, block_cols(index)], upper_block(w2_ref, index), 1, 1)
        return carry

    lax.fori_loop(0, 8, step, 0)
    settle(copies1)
    gains = gains_of(small_ref)
    dn = dn_ref[...] * valid
    gconv = column_sum(dn * normal)
    g1 = g2_ref[...] + back_of(dn, normal, scale1, gains[1:2])
    sg = sg_ref[...]
    da = (g1 * sg).astype(BF)
    db = (g1 * a_ref[...] * sg * (1.0 - sg)).astype(BF)
    dab_ref[:, 0:512] = da
    dab_ref[:, 512:1024] = db
    sums_ref[0:16, :] = table_ref[...]
    sums_ref[16:24, :] = jnp.zeros((8, 2048), F32)
    sums_ref[17:18, 0:512] = gconv
    sums_ref[18:19, 0:512] = gattn_ref[...]
    sums_ref[19:20, 0:512] = gffn_ref[...]
    dn = contract(da, glu_of(w1_ref, 0), 1, 1) + contract(db, glu_of(w1_ref, 1), 1, 1)
    normal, scale0 = normal_of(x_ref[...].astype(F32))
    sums_ref[16:17, 0:512] = column_sum(dn * normal)
    dx_ref[...] = g1 + back_of(dn, normal, scale0, gains[0:1])


def middle_kernel(info_ref, sp_ref, gs_ref, n3_ref, d_ref, sp2_ref, gs2_ref, n32_ref, d2_ref, out_ref):
    rows = gs_ref.shape[0]
    side = info_ref[0]
    gs = [ref[:, block_cols(side, 128)] for ref in (gs_ref, gs2_ref)]
    for w in range(8):
        cols = slice(256 * w, 256 * w + 256)
        res = both(lambda g, s: contract(g, s, 0, 0),
                   [(g, ref[:, cols]) for g, ref in zip(gs, (sp_ref, sp2_ref))])
        res = res.reshape(8, 16, 256)
        for i in range(2):
            by_shard(out_ref, w, slice(16 * i, 16 * i + 16), res[:, :, 128 * i:128 * i + 128])
    for part in range(3):
        pairs = [(n[...], d[pl.ds(side * 4, 4), 64 * part:64 * part + 64, :].reshape(256, rows))
                 for n, d in ((n3_ref, d_ref), (n32_ref, d2_ref))]
        res = both(lambda n, d: contract(n, d, 0, 1), pairs)
        packed = pair_rows(res)
        for c in range(8):
            by_chip(out_ref, c, slice(32 + 16 * part, 48 + 16 * part), packed[:, c])


def late_kernel(info_ref, n2_ref, dw_ref, dnar_ref, n1_ref, dab_ref, small_ref, n22_ref, dw2_ref,
                dnar2_ref, n12_ref, dab2_ref, small2_ref, out_ref, n2f_ref, narf_ref):
    rows = dw_ref.shape[0]
    side = info_ref[0]
    shifted = []
    dnar = []
    for n_ref, d_ref in ((n2_ref, dnar_ref), (n22_ref, dnar2_ref)):
        n2f_ref[...] = n_ref[...].astype(F32)
        narf_ref[...] = d_ref[...].astype(F32)
        shifted.append([n2f_ref[7 + tap:7 + tap + rows, :].astype(BF) for tap in range(3)])
        dnar.append(narf_ref[RIM:RIM + rows, block_cols(side, 128)].astype(BF))
    for j in range(4):
        cols = block_cols(side * 4 + j)
        res = both(lambda n, d: contract(n, d, 0, 0),
                   [(n[1], ref[:, cols]) for n, ref in zip(shifted, (dw_ref, dw2_ref))])
        for i in range(2):
            part = res[:, 128 * i:128 * i + 128].reshape(8, 64, 128)
            out_ref[2 * j + i, :, 0:64, :] = part.astype(BF)
    narrow = [
        both(lambda n, d: contract(n, d, 0, 0), [(n[tap], d) for n, d in zip(shifted, dnar)])
        for tap in range(3)
    ]
    for w in range(8):
        lanes = pl.ds(pl.multiple_of(w * 256 + side * 128, 128), 128)
        pair = slice(128 * (w // 2), 128 * (w // 2) + 128)
        table = small_ref[0:16, lanes] + small2_ref[0:16, lanes]
        gains = small_ref[16:20, pair] + small2_ref[16:20, pair]
        table = jnp.concatenate([table[0:10], gains, table[14:16]], 0)
        for c in range(8):
            pieces = [n[64 * w + 8 * c:64 * w + 8 * c + 8] for n in narrow]
            pieces += [table[2 * c:2 * c + 2], jnp.zeros((6, 128), F32)]
            out_ref[c, w, 64:96, :] = jnp.concatenate(pieces, 0).astype(BF)
    for place in range(2):
        cols = block_cols(side + 2 * place)
        res = both(lambda n, d: contract(n, d, 0, 0),
                   [(n[...], d[:, cols]) for n, d in ((n1_ref, dab_ref), (n12_ref, dab2_ref))])
        packed = pair_rows(res).astype(BF)
        for w in range(8):
            out_ref[:, w, 96 + 16 * place:112 + 16 * place, :] = packed[w]


def unpack_kernel(info_ref, near_ref, far_ref, gglu_ref, val_ref, gat_ref, gconv_ref, wid_ref, nar_ref,
                  gmid_ref, dep_ref, pnt_ref, gatt_ref, qry_ref, key_ref, vls_ref, outp_ref,
                  gffn_ref, upper_ref, lower_ref, fin_ref, low_ref, pt_ref, table_ref, sem):
    settle(fetch(info_ref[0], near_ref, far_ref, fin_ref, sem))
    for c in range(8):
        for k in range(2):
            fin = fin_ref[k, c].astype(F32)
            lanes = slice(k * 1024 + c * 128, k * 1024 + c * 128 + 128)
            upper_ref[:, lanes] = fin[0:64]
            wid_ref[:, lanes] = fin[EARLY + MIDDLE:EARLY + MIDDLE + 64]
            middle = EARLY
            late = EARLY + MIDDLE
            for i in range(2):
                low_ref[k * 256 + c * 32:k * 256 + c * 32 + 32, 128 * i:128 * i + 128] = (
                    fin[64 + 32 * i:96 + 32 * i]
                )
                pt_ref[k * 128 + c * 16:k * 128 + c * 16 + 16, 128 * i:128 * i + 128] = (
                    fin[middle + 16 * i:middle + 16 * i + 16]
                )
            for tap in range(3):
                nar_ref[tap, 8 * c:8 * c + 8, 128 * k:128 * k + 128] = (
                    fin[late + 64 + 8 * tap:late + 72 + 8 * tap]
                )
            table_ref[2 * c:2 * c + 2, 128 * k:128 * k + 128] = fin[late + 88:late + 90]
            bases = [128] + [middle + 32 + 16 * i for i in range(3)] + [late + 96, late + 112]
            targets = [outp_ref, qry_ref, key_ref, vls_ref, val_ref, gat_ref]
            for base, target in zip(bases, targets):
                for i in range(2):
                    target[8 * c:8 * c + 8, k * 256 + 128 * i:k * 256 + 128 * i + 128] = (
                        fin[base + 8 * i:base + 8 * i + 8]
                    )
    lower_ref[...] = low_ref[...].T
    pnt_ref[...] = pt_ref[...].T
    dep_ref[...] = table_ref[0:9, :]
    gmid_ref[...] = table_ref[9:10, :]
    even = info_ref[3] == 0
    gains = jnp.where(even, table_ref[10:14, 0:64], table_ref[10:14, 64:128])
    gglu_ref[...] = gains[0:1]
    gconv_ref[...] = gains[1:2]
    gatt_ref[...] = gains[2:3]
    gffn_ref[...] = gains[3:4]


def pack_ring_kernel(info_ref, wide_ref, narrow_ref, point_ref, out_ref, sem):
    core = info_ref[0]
    pairs = [
        (wide_ref.at[:, block_cols(core * 4 + j)], out_ref.at[64 * j:64 * j + 64, :]) for j in range(4)
    ]
    copies = launch(pairs, sem)

    @pl.when(core == 0)
    def _():
        settle(launch([(narrow_ref, out_ref.at[256:448, :]),
                       (narrow_ref.at[0:64, :], out_ref.at[448:512, :])], sem.at[4:6]))

    @pl.when(core == 1)
    def _():
        settle(launch([(point_ref, out_ref.at[256:512, :])], sem.at[4:5]))

    settle(copies)


def pack_rest_kernel(info_ref, value_ref, gate_ref, query_ref, key_ref, values_ref, g0_ref, g1_ref,
                     g2_ref, g3_ref, depth_ref, mid_ref, in_ref, out_ref, outw_ref, one_ref,
                     three_ref, pack_ref, g0, g1, g2, g3, depth, mid, sem):
    core = info_ref[0]
    own = block_cols(core)
    small = [(g0_ref, g0), (g1_ref, g1), (g2_ref, g2), (g3_ref, g3), (depth_ref, depth), (mid_ref, mid)]
    small = launch(small, sem)
    weights = launch(
        [(ref.at[:, own], pack_ref.at[128 + 64 * i:192 + 64 * i, :])
         for i, ref in enumerate((query_ref, key_ref, values_ref))], sem.at[6:9],
    )
    later = [(in_ref.at[:, block_cols(core * 4 + j)], three_ref.at[64 * j:64 * j + 64, :]) for j in range(4)]
    later += [(out_ref.at[:, own], three_ref.at[256:512, :]), (outw_ref.at[:, own], three_ref.at[512:576, :])]
    later = launch(later, sem.at[9:15])
    for index, ref in ((0, value_ref), (1, gate_ref)):
        @pl.when(core == index)
        def _():
            settle(launch([(ref.at[:, 256 * i:256 * i + 256], pack_ref.at[64 * i:64 * i + 64, :])
                           for i in range(2)], sem.at[15:17]))
    settle(small)
    gains = jnp.concatenate(
        [ref[...].astype(F32) for ref in (g0, g1, g2, g3)] + [jnp.zeros((4, 64), F32)], 0
    )
    gains = jnp.concatenate([gains] * 8, 1)
    place = lax.broadcasted_iota(jnp.int32, (8, 512), 1)
    start = (info_ref[5] * 4 + info_ref[4]) * 64
    gains = jnp.where((place >= start) & (place < start + 64), gains, 0.0)
    gains = jnp.concatenate([gains[:, 0:256], gains[:, 256:512]], 0)
    pack_ref[SMALL:SMALL + 16, :] = gains.astype(BF)
    taps = jnp.concatenate([depth[...].astype(F32), mid[...].astype(F32), jnp.zeros((6, 256), F32)], 0)
    pack_ref[SMALL + 16:SMALL + 32, :] = taps.astype(BF)
    settle(weights)
    for w in range(8):
        one_ref[w] = pack_ref[...]
    settle(later)


def over_x(value):
    value = value.reshape((4,) + value.shape[2:])
    return lax.psum_scatter(value, ("xh", "xl"), scatter_dimension=0, tiled=True)[0]


def over_z(value):
    return lax.psum_scatter(value, "z", scatter_dimension=0, tiled=True)[0]


def spread_out(own, axes, count):
    copies = jnp.broadcast_to(own[None], (count,) + own.shape)
    return lax.all_to_all(copies, axes, 0, 0, tiled=True)


def shards(
    inputs, lengths, cotangent, glu_gain, glu_value, glu_gate, conv_gain, wide_weight,
    narrow_weight, mid_gain, depth_weight, point_weight, attn_gain, query_weight, key_weight,
    value_weight, output_weight, ffn_gain, ffn_in, ffn_out,
):
    rows, width = inputs.shape[1], inputs.shape[2]
    units = wide_weight.shape[1]
    rim_rows = rows + 2 * RIM
    core = lax.axis_index("core")
    shard = lax.axis_index("xl") * 4 + lax.axis_index("z")
    first = (lax.axis_index("y") * 4 + lax.axis_index("xh") * 2 + core) * rows
    xl, z = lax.axis_index("xl"), lax.axis_index("z")
    info = jnp.stack([core, first, lengths[0], shard % 2, z, xl]).astype(jnp.int32)
    flip = shift(dc=1)
    dma = pltpu.SemaphoreType.DMA

    pack2 = call(
        pack_ring_kernel, [((512, 256), BF, FREE)], [SMEM] + [HBM] * 3, [dma((6,))], "pack_ring", 1,
        info, wide_weight, narrow_weight.reshape(192, 256), point_weight,
    )[0]
    steps = [shift(dz=-1), shift(dz=2), shift(dz=1)]
    other = send(pack2, shift(dxl=1))
    own_pieces = [send(pack2, step) for step in steps]
    other_pieces = [send(other, step) for step in steps]

    line = lambda v: v.reshape(1, -1)
    pack1, pack3 = call(
        pack_rest_kernel, [((8, SMALL + 32, 256), BF, FREE), ((576, 256), BF, FREE)], [SMEM] + [HBM] * 14,
        [pltpu.VMEM((SMALL + 32, 256), BF)] + [pltpu.VMEM((1, 64), BF)] * 4
        + [pltpu.VMEM((9, 256), BF), pltpu.VMEM((1, 256), BF), dma((17,))],
        "pack_rest", 1, info, glu_value, glu_gate, query_weight, key_weight, value_weight,
        line(glu_gain), line(conv_gain), line(attn_gain), line(ffn_gain), depth_weight,
        line(mid_gain), ffn_in, ffn_out, output_weight,
    )

    pack1, *_ = lax.optimization_barrier((pack1, *own_pieces, other))
    near1 = lax.all_to_all(pack1, WT, 0, 0, tiled=True)
    x = inputs[0]
    low_x = send(x[rows - RIM:], along(1))
    high_x = send(x[:RIM], along(-1))
    other3 = send(pack3, shift(dxl=1))
    near1, pack3, other3, low_x, high_x, *ready = lax.optimization_barrier(
        (near1, pack3, other3, low_x, high_x, *own_pieces, *other_pieces)
    )
    near2 = [pack2] + ready[:3] + [other] + ready[3:]
    far2 = [send(piece, flip) for piece in near2]
    far1 = send(near1, flip)
    near3 = lax.all_gather(jnp.stack([pack3, other3]), "z", axis=0)

    tall, wide, narrow = (rows, width), (rows, units), (rows, 256)
    tiny = pltpu.VMEM((8, 32, 256), BF)
    ring = pltpu.VMEM((2, 2, 4) + pack2.shape, BF)
    n1, a, sg, h1, h1m, one = call(
        glu_kernel,
        [(tall, BF), (tall, F32), (tall, F32), ((rim_rows, width), F32, FREE), (tall, F32),
         ((2,) + near1.shape, BF, HBM)],
        [SMEM] + [FREE] * 3 + [ANY] * 2, [pltpu.VMEM((2,) + near1.shape, BF), dma((2,))], "glu", 3,
        info, low_x, x, high_x, near1, far1,
    )
    n2, wp, np_, nm, mean, scale, sp, h2, n3, qkv, two = call(
        conv_kernel,
        [((rim_rows, width), BF), ((rim_rows, units), F32, HBM), ((rim_rows, 256), F32),
         ((rim_rows, units), BF, HBM), ((rim_rows, 128), F32), ((rim_rows, 128), F32),
         (wide, BF, HBM), (tall, F32), (tall, BF), ((HEADS, 3 * HEAD, rows), BF, FREE),
         (ring.shape, BF, HBM)],
        [SMEM, FREE] + [ANY] * 16 + [HBM],
        [ring, pltpu.VMEM((2, 8, SMALL - 128, 256), BF), tiny, pltpu.VMEM((rim_rows, units), F32),
         pltpu.VMEM((rim_rows, units), F32), pltpu.VMEM((rim_rows, units), BF), pltpu.VMEM(wide, BF),
         dma((16,)), dma((2,)), dma((3, 8))],
        "conv", 15, info, h1, *near2, *far2, one,
    )
    near = lax.all_to_all(qkv, CHIPS, 0, 0, tiled=True)
    far = send(near[:, HEAD:], flip)
    head_out, expo, inverse, near, far = attend(near, far, lengths, info[:1])
    near3, _ = lax.optimization_barrier((near3, head_out))
    far3 = send(near3, flip)
    heads_in = lax.all_to_all(head_out, CHIPS, 0, 0, tiled=True)
    output, acts, g3, dob, d_gffn, heads_in = call(
        ffn_kernel,
        [(tall, BF), ((rows, 5632), BF), (tall, F32), ((HEADS, HEAD, rows), BF, FREE),
         ((1, width), F32), ((HEADS, HEAD, rows), BF)],
        [SMEM, VMEM, FREE, VMEM, HBM, HBM, ANY],
        [pltpu.VMEM((2, 2, 4) + pack3.shape, BF), tiny, pltpu.VMEM(tall, F32), pltpu.VMEM(tall, F32),
         dma((5,))],
        "ffn", 11, info, h2, heads_in, cotangent[0], one, near3, far3,
    )

    d_near = lax.all_to_all(dob, CHIPS, 0, 0, tiled=True)
    early = call(
        early_kernel, [((2, 2, 4, 4, EARLY, 128), BF)], [SMEM] + [VMEM] * 2 + [FREE] * 2, [], "early", 0.3,
        info, acts, heads_in, send(acts, flip), send(heads_in, flip),
    )[0]
    d_near, early = lax.optimization_barrier((d_near, early))
    early = over_x(early)
    dq, dk, dv = attend_back(near, far, expo, head_out, inverse, d_near)
    d_far = send(jnp.concatenate([dk[1], dv[1]], 1), flip).astype(F32)
    d_own = jnp.concatenate([dk[0], dv[0]], 1).astype(F32)
    d_qkv = jnp.concatenate([dq, (d_own + d_far).astype(BF)], 1)
    d_qkv = lax.all_to_all(d_qkv, CHIPS, 0, 0, tiled=True)
    early, _ = lax.optimization_barrier((early, d_qkv))
    early = over_z(early)
    g2, gs, lo, hi, d_gatt = call(
        attn_in_kernel,
        [(tall, F32), (narrow, BF), ((RIM, 256), BF), ((RIM, 256), BF), ((1, width), F32)],
        [SMEM, FREE] + [VMEM] * 2 + [HBM],
        [pltpu.VMEM((2, 8, SMALL - 128, 256), BF), tiny, dma((2,))],
        "attn_in", 0.5, info, d_qkv, h2, g3, one,
    )
    low_gs = send(hi, along(1))
    high_gs = send(lo, along(-1))
    middle = call(
        middle_kernel, [((2, 2, 4, 4, MIDDLE, 128), BF)], [SMEM] + [VMEM] * 3 + [FREE] * 5, [], "middle", 0.3,
        info, sp, gs, n3, d_qkv, *[send(v, flip) for v in (sp, gs, n3, d_qkv)],
    )[0]
    low_gs, high_gs, middle = lax.optimization_barrier((low_gs, high_gs, middle))
    middle = over_x(middle)
    rim_narrow = ((rim_rows, 256), BF)
    dw, dnar, table = call(
        conv_back_kernel, [(wide, BF), rim_narrow, ((16, units), F32)],
        [SMEM, FREE, VMEM, FREE] + [VMEM] * 5 + [HBM] * 2,
        [pltpu.VMEM((2, 4, 256, 256), BF), tiny, pltpu.VMEM((rim_rows, 256), F32), pltpu.VMEM((rim_rows + 2 * RIM, 256), F32),
         pltpu.VMEM((rim_rows, units), F32), pltpu.VMEM((rim_rows, units), F32), dma((2,))],
        "conv_back", 2, info, low_gs, gs, high_gs, nm, wp, np_, mean, scale, two, one,
    )
    dw2, dnar2 = send(dw, flip), send(dnar, flip)
    g2, early = lax.optimization_barrier((g2, early))
    dx, dab, sums = call(
        glu_back_kernel, [(tall, F32), ((rows, 2 * width), BF), ((24, units), F32)],
        [SMEM] + [VMEM] * 3 + [HBM] * 2 + [VMEM] * 7,
        [ring, pltpu.VMEM((2, 8, 128, 256), BF), tiny, pltpu.VMEM(tall, F32),
         pltpu.VMEM((rim_rows, 256), F32), dma((3,))],
        "glu_back", 1, info, dw, dnar, h1m, two, one, g2, a, sg, x, table, d_gatt, d_gffn,
    )
    dab2, sums2 = send(dab, flip), send(sums, flip)
    dab2, middle = lax.optimization_barrier((dab2, middle))
    middle = over_z(middle)
    late = call(
        late_kernel, [((8, 8, LATE, 128), BF)], [SMEM] + [VMEM] * 6 + [FREE] * 6,
        [pltpu.VMEM((rim_rows, width), F32), pltpu.VMEM((rim_rows, 256), F32)], "late", 0.5,
        info, n2, dw, dnar, n1, dab, sums, send(n2, flip), dw2, dnar2, send(n1, flip), dab2, sums2,
    )[0]
    _, early, middle = lax.optimization_barrier((late, early, middle))
    y = lax.axis_index("y")
    pieces = jnp.concatenate([early, middle], 1)
    pick = lambda index: lax.dynamic_index_in_dim(pieces, index % 4, 0, keepdims=False)
    parts = [send(pick(y + d), shift(dy=d)) for d in (1, 2, 3)]
    early = sum((part.astype(F32) for part in parts), pick(y).astype(F32)).astype(BF)
    late = lax.all_to_all(late.reshape(64, LATE, 128), CHIPS + WT, 0, 0, tiled=True)
    late = jnp.sum(late.astype(F32), 0).astype(BF)
    final = spread_out(jnp.concatenate([early, late], 0), CHIPS, 8)
    square, broad = ((64, 512), F32), ((64, 2048), F32)
    line = ((1, 64), F32)
    grads = call(
        unpack_kernel,
        [line, square, square, line, broad, ((3, 64, 256), F32), ((1, 256), F32),
         ((9, 256), F32), ((256, 256), F32), line, square, square, square, square, line, broad,
         ((256, 512), F32)],
        [SMEM, ANY, ANY],
        [pltpu.VMEM((2,) + final.shape, BF), pltpu.VMEM((512, 256), F32),
         pltpu.VMEM((256, 256), F32), pltpu.VMEM((16, 256), F32), dma((2,))],
        "unpack", 3, info, final, send(final, flip),
    )
    grads = [g[0] if g.shape[0] == 1 else g for g in grads]
    return (output[None], dx[None]) + tuple(grads)


def solution(mesh):
    fine = Mesh(mesh.devices.reshape(SIZES), AXES)
    flat, row, mid = P(WT), P(WT, None), P(None, WT, None)
    col = P(None, WT)
    tokens = P(WT, CTX, None)
    weights = (
        flat, row, row, flat, row, mid, flat, col, row, flat, row, row, row, row, flat, row, row,
    )
    return jax.shard_map(
        shards, mesh=fine, in_specs=(tokens, flat, tokens) + weights,
        out_specs=(tokens, tokens) + weights, check_vma=False,
    )
```

time: 372 us -> 335 us (0.901)
  local copies, waits for them, and re-layouts: 25.4 us -> 4.04 us
  waiting for transfers between devices: 89.5 us -> 73.2 us
  blocking collectives: 50.2 us -> 65.9 us
  Pallas kernels: 121 us -> 113 us
  starting transfers between devices: 64.4 us -> 59.8 us
    all_to_all x1, waiting for transfers between devices: 41.6 us -> 0.01 us  [shards(): lax.all_to_all(late.reshape(64, LATE, 128), CHIPS + WT, 0, 0, tiled=True)]
    reduce_scatter x1 -> x4, waiting for transfers between devices: 0.01 us -> 33.2 us  [the longest x2 32 us: over_z(): return lax.psum_scatter(value, 'z', scatter_dimension=0, tiled=True)[0]]
    all_to_all x0 -> x1, blocking collectives: none -> 21.1 us  [shards(): near = lax.all_to_all(qkv, CHIPS, 0, 0, tiled=True)]
    unnamed x49 -> x31, local copies, waits for them, and re-layouts: 17.8 us -> 2.24 us
    all_to_all x3 -> x1, starting transfers between devices: 18.6 us -> 3.58 us  [shards(): near1 = lax.all_to_all(pack1, WT, 0, 0, tiled=True)]
    all_to_all x3 -> x1, waiting for transfers between devices: 14.8 us -> 0.01 us  [shards(): near1 = lax.all_to_all(pack1, WT, 0, 0, tiled=True)]
    pallas_call x12, Pallas kernels: 89 us -> 79.1 us  [call(): pl.pallas_call(kernel, in_specs=[VMEM if spec is FREE else spec for spec...]
    ppermute x22 -> x40, starting transfers between devices: 33.9 us -> 43.6 us  [send(): return lax.ppermute(value, AXES, pairs)]
  transfers between devices with their start and end apart: 29 -> 48, of which waited for: 14 -> 17; matrix products, arithmetic and copies ran while one was open for 5% -> 1% of each run, Pallas kernels for 28% -> 28%
where the time goes in v3:
time: 335 us; the launch traced here: 334 us
  Pallas kernels  113 us (34%)
  waiting for transfers between devices  73.2 us (22%)
  blocking collectives  65.9 us (20%)
  starting transfers between devices  59.8 us (18%)
  between operations  15 us (4%)
  local copies, waits for them, and re-layouts  4.04 us (1%)
    pallas_call x12, Pallas kernels, call(): pl.pallas_call(kernel, in_specs=[VMEM if spec is FREE else spec for spec...  79.1 us
    ppermute x40, starting transfers between devices, send(): return lax.ppermute(value, AXES, pairs)  43.6 us
    ppermute x40, waiting for transfers between devices, send(): return lax.ppermute(value, AXES, pairs)  38.3 us
    reduce_scatter x2, waiting for transfers between devices, over_z(): return lax.psum_scatter(value, 'z', scatter_dimension=0, tiled=True)[0]  32 us
    all_to_all x1, blocking collectives, shards(): near = lax.all_to_all(qkv, CHIPS, 0, 0, tiled=True)  21.1 us
    pallas_call x1, Pallas kernels, attend_back(): pl.pallas_call(functools.partial(attend_back_kernel, chips, rows), grid=(...  20.1 us
    all_to_all x1, blocking collectives, spread_out(): return lax.all_to_all(copies, axes, 0, 0, tiled=True)  16.6 us
    all_to_all x1, blocking collectives, shards(): d_qkv = lax.all_to_all(d_qkv, CHIPS, 0, 0, tiled=True)  16.2 us
  transfers between devices with their start and end apart: 48, of which 17 were waited for; matrix products, arithmetic and copies ran while one was open for 1% of the time, Pallas kernels for 28%

profile of v3, /device:TPU:1, one launch (start us, length us, event | category | flops | bytes accessed | tf_op | source)
XLA Modules:
  0.0 333.6 jit_solution(6685622720323980985)
XLA Ops:
  8.0 1.6 pack_ring.1.refs_0_
  9.5 4.7 %collective-permute-start = (bf16[512,256]{1,0:T(8,128)(2,1)S(1)}, bf16[512,256]{1,0:T(8,128)(2,1)S(1)}, u32[]{:S(2)}, u32[]{:S(2)}) collective-permute-start(bf16[512,256]{1,0:T(8,128)(2,1)S(1)} %pack_ring.1.refs_0_), channel_id=1, source_target_pairs={{0,3},{1,0},{2,1},{3,2},{4,7},{5,4},{6,5},{7,6},{8,11},{9,8},{10,9... | collective-permute-start | bytes 786440 | tf_op jit(solution)/shard_map/ppermute | solution.py:53
  14.9 1.2 collective-permute-start.3
  16.7 3.1 pack_rest.1
  19.8 4.9 %collective-permute-done.refs_1_ = bf16[512,256]{1,0:T(8,128)(2,1)S(1)} collective-permute-done((bf16[512,256]{1,0:T(8,128)(2,1)S(1)}, bf16[512,256]{1,0:T(8,128)(2,1)S(1)}, u32[]{:S(2)}, u32[]{:S(2)}) %collective-permute-start) | collective-permute-done | bytes 262176 | tf_op jit(solution)/shard_map/ppermute | solution.py:53
  24.7 4.3 %collective-permute-done.2.refs_3_ = bf16[512,256]{1,0:T(8,128)(2,1)S(1)} collective-permute-done((bf16[512,256]{1,0:T(8,128)(2,1)S(1)}, bf16[512,256]{1,0:T(8,128)(2,1)S(1)}, u32[]{:S(2)}, u32[]{:S(2)}) %collective-permute-start.2) | collective-permute-done | bytes 262176 | tf_op jit(solution)/shard_map/ppermute | solution.py:53
  28.9 3.6 %all-to-all-start = ((bf16[8,352,256]{2,1,0:T(8,128)(2,1)}), bf16[8,352,256]{2,1,0:T(8,128)(2,1)S(1)}, u32[]{:S(2)}, u32[]{:S(2)}) async-start(bf16[8,352,256]{2,1,0:T(8,128)(2,1)} %get-tuple-element.106), calls=%async_computation | async-start | bytes 2883584 | tf_op jit(solution)/shard_map/all_to_all | solution.py:952
  32.6 1.3 collective-permute-start.4
  33.9 2.4 collective-permute-start.7
  37.5 6.8 %collective-permute-start.5 = (bf16[8,512]{1,0:T(8,128)(2,1)S(1)}, bf16[8,512]{1,0:T(8,128)(2,1)S(1)}, u32[]{:S(2)}, u32[]{:S(2)}) collective-permute-start(bf16[8,512]{1,0:T(8,128)(2,1)S(1)} %get-tuple-element.196), channel_id=1, source_target_pairs={{0,8},{1,9},{2,10},{3,11},{4,12},{5,13},{6,14},{7,15},{8,16},{9,17... | collective-permute-start | bytes 24584 | tf_op jit(solution)/shard_map/ppermute | solution.py:53
  44.2 10.0 %collective-permute-done.5.low_ref = bf16[8,512]{1,0:T(8,128)(2,1)S(1)} collective-permute-done((bf16[8,512]{1,0:T(8,128)(2,1)S(1)}, bf16[8,512]{1,0:T(8,128)(2,1)S(1)}, u32[]{:S(2)}, u32[]{:S(2)}) %collective-permute-start.5) | collective-permute-done | bytes 8224 | tf_op jit(solution)/shard_map/ppermute | solution.py:53
  54.2 1.9 collective-permute-start.6
  56.1 5.3 %collective-permute-done.6.high_ref = bf16[8,512]{1,0:T(8,128)(2,1)S(1)} collective-permute-done((bf16[8,512]{1,0:T(8,128)(2,1)S(1)}, bf16[8,512]{1,0:T(8,128)(2,1)S(1)}, u32[]{:S(2)}, u32[]{:S(2)}) %collective-permute-start.6) | collective-permute-done | bytes 8224 | tf_op jit(solution)/shard_map/ppermute | solution.py:53
  64.8 1.8 pad_maximum_fusion.1
  68.4 5.0 %glu.1 = (bf16[256,512]{1,0:T(8,128)(2,1)}, f32[256,512]{1,0:T(8,128)}, f32[256,512]{1,0:T(8,128)}, f32[272,512]{1,0:T(8,128)S(1)}, f32[256,512]{1,0:T(8,128)}, /*index=5*/bf16[2,8,352,256]{3,2,1,0:T(8,128)(2,1)}) custom-call(s32[6]{0:T(128)S(1)} %stack.32.info_ref, bf16[8,512]{1,0:T(8,128)(2,1)S(1)} %collective-permute-done.5.low_ref, ...), custom_call_target="tpu_custom_call" | custom-call | flops 3000000000 | bytes 9000000 | tf_op jit(solution)/shard_map/glu/pallas_call | solution.py:273
  73.4 13.3 %conv.1 = (bf16[272,512]{1,0:T(8,128)(2,1)}, f32[272,2048]{1,0:T(8,128)}, f32[272,256]{1,0:T(8,128)}, bf16[272,2048]{1,0:T(8,128)(2,1)}, f32[272,128]{1,0:T(8,12...) custom-call(s32[6]{0:T(128)S(1)} %stack.32.info_ref, ...), custom_call_target="tpu_custom_call" | custom-call | flops 15000000512 | bytes 45000000 | tf_op jit(solution)/shard_map/conv/pallas_call | solution.py:273
  86.8 21.1 %all_to_all.35.near_ref = bf16[8,192,256]{2,1,0:T(8,128)(2,1)S(1)} all-to-all(bf16[8,192,256]{2,1,0:T(8,128)(2,1)S(1)} %get-tuple-element.120), channel_id=1, replica_groups=mesh['y'=4,'xh'=2,'core'=2,'xl'=2,'z'=4] {'y','xh'}, dimensions={0} | all-to-all | bytes 1572864 | tf_op jit(solution)/shard_map/all_to_all | solution.py:987
  107.9 1.4 collective-permute-start.19
  109.2 1.5 collective-permute-done.19.far_ref
  110.8 14.0 %attend.1 = (bf16[8,64,256]{2,1,0:T(8,128)(2,1)}, bf16[2048,4096]{1,0:T(8,128)(2,1)}, f32[8,8,256]{2,1,0:T(8,128)}, bf16[8,192,256]{2,1,0:T(8,128)(2,1)}, bf16[8,128,256]{2,1,0:T(8,128)(2,1)}) custom-call(s32[1]{0:T(128)S(6)} %copy.40.length_ref, s32[1]{0:T(128)} %bitcast.core_ref, bf16[8,192,256]{2,1,0:T(8,128)(2,1)S(1)} %all_to_all.35.near_ref, ...), custom_call_target="tpu_custom_call" | custom-call | flops 14000000000 | bytes 42000000 | tf_op jit(solution)/shard_map/attend/pallas_call | solution.py:134
  125.3 12.1 %all_to_all.36.o_ref = bf16[8,64,256]{2,1,0:T(8,128)(2,1)S(1)} all-to-all(bf16[8,64,256]{2,1,0:T(8,128)(2,1)} %get-tuple-element.121.o_ref), channel_id=1, replica_groups=mesh['y'=4,'xh'=2,'core'=2,'xl'=2,'z'=4] {'y','xh'}, dimensions={0} | all-to-all | bytes 524288 | tf_op jit(solution)/shard_map/all_to_all | solution.py:992
  137.4 11.6 %ffn.1 = (bf16[256,512]{1,0:T(8,128)(2,1)}, bf16[256,5632]{1,0:T(8,128)(2,1)}, f32[256,512]{1,0:T(8,128)}, bf16[8,64,256]{2,1,0:T(8,128)(2,1)S(1)}, f32[1,512]{1,0:T(1,128)}, /*index=5*/bf16[8,64,256]{2,1,0:T(8,128)(2,1)}) custom-call(s32[6]{0:T(128)S(1)} %stack.32.info_ref, f32[256,512]{1,0:T(8,128)} %get-tuple-element.119.h2_ref, ...), custom_call_target="tpu_custom_call" | custom-call | flops 11000000512 | bytes 33000000 | tf_op jit(solution)/shard_map/ffn/pallas_call | solution.py:273
  150.6 3.4 %all-to-all-start.3 = ((bf16[8,64,256]{2,1,0:T(8,128)(2,1)}), bf16[8,64,256]{2,1,0:T(8,128)(2,1)S(1)}, u32[]{:S(2)}, u32[]{:S(2)}) async-start(bf16[8,64,256]{2,1,0:T(8,128)(2,1)} %copy-done.1), calls=%async_computation.3 | async-start | bytes 524288 | tf_op jit(solution)/shard_map/all_to_all | solution.py:1003
  154.1 2.0 collective-permute-done.22.heads2_ref
  156.1 4.8 %early.1 = bf16[2,2,4,4,144,128]{5,4,3,2,1,0:T(8,128)(2,1)} custom-call(s32[6]{0:T(128)S(1)} %stack.32.info_ref, bf16[256,5632]{1,0:T(8,128)(2,1)} %get-tuple-element.131.acts_ref, bf16[8,64,256]{2,1,0:T(8,128)(2,1)} %get-tuple-element.132.heads_ref, bf16[256,5632]{1,0:T(8,128)(2,1)S(1)} %collective-permute-done.21.acts2_ref, ...), custom_call_target="tpu_custom_call" | custom-call | flops 300000000 | bytes 900000 | tf_op jit(solution)/shard_map/early/pallas_call | solution.py:273
  162.1 20.1 %attend_back.1 = (bf16[8,64,256]{2,1,0:T(8,128)(2,1)}, bf16[2,8,64,256]{3,2,1,0:T(8,128)(2,1)S(1)}, bf16[2,8,64,256]{3,2,1,0:T(8,128)(2,1)S(1)}) custom-call(bf16[8,192,256]{2,1,0:T(8,128)(2,1)} %get-tuple-element.126.near_ref, bf16[8,128,256]{2,1,0:T(8,128)(2,1)} %get-tuple-element.127.far_ref, bf16[2048,4096]{1,0:T(8,128)(2,1)} %get-tuple-element.128.e_ref, ...), custom_call_target="tpu_custom_call" | custom-call | flops 3000000000 | bytes 9000000 | tf_op jit(solution)/shard_map/attend_back/pallas_call | solution.py:227
  182.4 1.8 collective-permute-start.23
  184.1 1.5 collective-permute-done.23
  185.9 16.2 %all_to_all.37.d_ref = bf16[8,192,256]{2,1,0:T(8,128)(2,1)S(1)} all-to-all(bf16[8,192,256]{2,1,0:T(8,128)(2,1)S(1)} %pad_maximum_fusion), channel_id=1, replica_groups=mesh['y'=4,'xh'=2,'core'=2,'xl'=2,'z'=4] {'y','xh'}, dimensions={0} | all-to-all | bytes 1572864 | tf_op jit(solution)/shard_map/all_to_all | solution.py:1014
  202.2 1.8 collective-permute-start.26
  204.5 4.3 %attn_in.1 = (f32[256,512]{1,0:T(8,128)}, bf16[256,256]{1,0:T(8,128)(2,1)}, bf16[8,256]{1,0:T(8,128)(2,1)}, bf16[8,256]{1,0:T(8,128)(2,1)}, f32[1,512]{1,0:T(1,128)}) custom-call(s32[6]{0:T(128)S(1)} %stack.32.info_ref, bf16[8,192,256]{2,1,0:T(8,128)(2,1)S(1)} %all_to_all.37.d_ref, f32[256,512]{1,0:T(8,128)} %get-tuple-element.119.h2_ref, ...), custom_call_target="tpu_custom_call" | custom-call | flops 500000000 | bytes 1500000 | tf_op jit(solution)/shard_map/attn_in/pallas_call | solution.py:273
  208.9 2.8 collective-permute-start.24
  211.7 1.9 collective-permute-start.25
  213.7 3.5 %middle.1 = bf16[2,2,4,4,80,128]{5,4,3,2,1,0:T(8,128)(2,1)} custom-call(s32[6]{0:T(128)S(1)} %stack.32.info_ref, bf16[256,2048]{1,0:T(8,128)(2,1)} %get-tuple-element.140.sp_ref, bf16[256,256]{1,0:T(8,128)(2,1)} %get-tuple-element.141.gs_ref, bf16[256,512]{1,0:T(8,128)(2,1)} %get-tuple-element.142.n3_ref, bf16[8,192,256]{2,1,0:T(8,128)(2,1)S(1)} %all_to_all.37.d_ref, ...), custom_call_target="tpu_custom_call" | custom-call | flops 300000000 | bytes 900000 | tf_op jit(solution)/shard_map/middle/pallas_call | solution.py:273
  217.2 1.2 collective-permute-done.25.hi_ref
  218.4 16.1 %conv_back.1 = (bf16[256,2048]{1,0:T(8,128)(2,1)}, bf16[272,256]{1,0:T(8,128)(2,1)}, f32[16,2048]{1,0:T(8,128)}) custom-call(s32[6]{0:T(128)S(1)} %stack.32.info_ref, bf16[8,256]{1,0:T(8,128)(2,1)S(1)} %collective-permute-done.24.lo_ref, bf16[256,256]{1,0:T(8,128)(2,1)} %get-tuple-element.141.gs_ref, bf16[8,256]{1,0:T(8,128)(2,1)S(1)} %collective-permute-done.25.hi_ref, ...), custom_call_target="tpu_custom_call" | custom-call | flops 2000000000 | bytes 6000000 | tf_op jit(solution)/shard_map/conv_back/pallas_call | solution.py:273
  234.9 8.5 %glu_back.1 = (f32[256,512]{1,0:T(8,128)}, bf16[256,1024]{1,0:T(8,128)(2,1)}, f32[24,2048]{1,0:T(8,128)}) custom-call(s32[6]{0:T(128)S(1)} %stack.32.info_ref, bf16[256,2048]{1,0:T(8,128)(2,1)} %get-tuple-element.151.dw_ref, bf16[272,256]{1,0:T(8,128)(2,1)} %get-tuple-element.152.dnar_ref, f32[256,512]{1,0:T(8,128)} %get-tuple-element.153.h1_ref, ...), custom_call_target="tpu_custom_call" | custom-call | flops 1000000000 | bytes 3000000 | tf_op jit(solution)/shard_map/glu_back/pallas_call | solution.py:273
  244.5 1.1 collective-permute-done.34.dab2_ref
  246.0 1.1 reduce-scatter.9.cloned.1.call-done
  247.2 4.5 %late.1 = bf16[8,8,128,128]{3,2,1,0:T(8,128)(2,1)} custom-call(s32[6]{0:T(128)S(1)} %stack.32.info_ref, bf16[272,512]{1,0:T(8,128)(2,1)} %get-tuple-element.164.n2_ref, bf16[256,2048]{1,0:T(8,128)(2,1)} %get-tuple-element.151.dw_ref, bf16[272,256]{1,0:T(8,128)(2,1)} %get-tuple-element.152.dnar_ref, bf16[256,512]{1,0:T(8,128)(2,1)} %get-tuple-element.165.n1_ref, ...), custom_call_target="tpu_custom_call" | custom-call | flops 500000000 | bytes 1500000 | tf_op jit(solution)/shard_map/late/pallas_call | solution.py:273
  251.6 9.0 %all-to-all-start.5 = ((bf16[64,128,128]{2,1,0:T(8,128)(2,1)}), bf16[64,128,128]{2,1,0:T(8,128)(2,1)S(1)}, u32[]{:S(2)}, u32[]{:S(2)}) async-start(bf16[64,128,128]{2,1,0:T(8,128)(2,1)} %bitcast.54), calls=%async_computation.9 | async-start | bytes 4194304 | tf_op jit(solution)/shard_map/all_to_all | solution.py:1063
  261.3 32.0 %reduce-scatter.11.cloned.1.call-done = bf16[1,4,80,128]{3,2,1,0:T(8,128)(2,1)} async-done(((bf16[4,4,80,128]{3,2,1,0:T(8,128)(2,1)}), bf16[1,4,80,128]{3,2,1,0:T(8,128)(2,1)}) %reduce-scatter.11.cloned.1.call-update) | async-done | bytes 81936 | tf_op jit(solution)/shard_map/reduce_scatter | solution.py:908
  294.3 1.5 collective-permute-start.38
  297.3 2.9 collective-permute-done.37
  301.4 16.6 %all_to_all.38.near_ref = bf16[8,352,128]{2,1,0:T(8,128)(2,1)S(1)} all-to-all(bf16[8,352,128]{2,1,0:T(8,128)(2,1)S(1)} %broadcast_in_dim.14), channel_id=1, replica_groups=mesh['y'=4,'xh'=2,'core'=2,'xl'=2,'z'=4] {'y','xh'}, dimensions={0} | all-to-all | bytes 1441792 | tf_op jit(solution)/shard_map/all_to_all | solution.py:913
  318.0 4.4 %collective-permute-start.39 = (bf16[8,352,128]{2,1,0:T(8,128)(2,1)S(1)}, bf16[8,352,128]{2,1,0:T(8,128)(2,1)S(1)}, u32[]{:S(2)}, u32[]{:S(2)}) collective-permute-start(bf16[8,352,128]{2,1,0:T(8,128)(2,1)S(1)} %all_to_all.38.near_ref), channel_id=1, source_target_pairs={{0,8},{1,9},{2,10},{3,11},{4,12},{5,13},{6,14},{7,15},{8,0},{9,1},... | collective-permute-start | bytes 2162696 | tf_op jit(solution)/shard_map/ppermute | solution.py:53
  322.3 1.8 collective-permute-done.39.far_ref
  324.2 2.9 unpack.1
  (117 shorter events, 18.2 us)
Async XLA Ops:
  9.5 15.1 %collective-permute-start = (bf16[512,256]{1,0:T(8,128)(2,1)S(1)}, bf16[512,256]{1,0:T(8,128)(2,1)S(1)}, u32[]{:S(2)}, u32[]{:S(2)}) collective-permute-start(bf16[512,256]{1,0:T(8,128)(2,1)S(1)} %pack_ring.1.refs_0_), channel_id=1, source_target_pairs={{0,3},{1,0},{2,1},{3,2},{4,7},{5,4},{6,5},{7,6},{8,11},{9,8},{10,9... | collective-permute-start | bytes 786440 | tf_op jit(solution)/shard_map/ppermute | solution.py:53
  14.2 10.5 %collective-permute-start.1 = (bf16[512,256]{1,0:T(8,128)(2,1)S(1)}, bf16[512,256]{1,0:T(8,128)(2,1)S(1)}, u32[]{:S(2)}, u32[]{:S(2)}) collective-permute-start(bf16[512,256]{1,0:T(8,128)(2,1)S(1)} %pack_ring.1.refs_0_), channel_id=1, source_target_pairs={{0,2},{1,3},{2,0},{3,1},{4,6},{5,7},{6,4},{7,5},{8,10},{9,11},{10,... | collective-permute-start | bytes 786440 | tf_op jit(solution)/shard_map/ppermute | solution.py:53
  14.2 14.7 %collective-permute-start.2 = (bf16[512,256]{1,0:T(8,128)(2,1)S(1)}, bf16[512,256]{1,0:T(8,128)(2,1)S(1)}, u32[]{:S(2)}, u32[]{:S(2)}) collective-permute-start(bf16[512,256]{1,0:T(8,128)(2,1)S(1)} %pack_ring.1.refs_0_), channel_id=1, source_target_pairs={{0,1},{1,2},{2,3},{3,0},{4,5},{5,6},{6,7},{7,4},{8,9},{9,10},{10,1... | collective-permute-start | bytes 786440 | tf_op jit(solution)/shard_map/ppermute | solution.py:53
  14.9 14.0 %collective-permute-start.3 = (bf16[512,256]{1,0:T(8,128)(2,1)S(1)}, bf16[512,256]{1,0:T(8,128)(2,1)S(1)}, u32[]{:S(2)}, u32[]{:S(2)}) collective-permute-start(bf16[512,256]{1,0:T(8,128)(2,1)S(1)} %pack_ring.1.refs_0_), channel_id=1, source_target_pairs={{0,4},{1,5},{2,6},{3,7},{4,0},{5,1},{6,2},{7,3},{8,12},{9,13},{10,... | collective-permute-start | bytes 786440 | tf_op jit(solution)/shard_map/ppermute | solution.py:53
  28.9 34.0 %all-to-all-start = ((bf16[8,352,256]{2,1,0:T(8,128)(2,1)}), bf16[8,352,256]{2,1,0:T(8,128)(2,1)S(1)}, u32[]{:S(2)}, u32[]{:S(2)}) async-start(bf16[8,352,256]{2,1,0:T(8,128)(2,1)} %get-tuple-element.106), calls=%async_computation | async-start | bytes 2883584 | tf_op jit(solution)/shard_map/all_to_all | solution.py:952
  32.5 92.3 %all-gather.3.cloned.1.call-start = ((), (), s32[]{:S(2)}) async-start(), calls=%async_computation.15 | async-start | bytes 2949120 | tf_op jit(solution)/shard_map/all_gather | solution.py:963
  32.6 28.8 %collective-permute-start.4 = (bf16[576,256]{1,0:T(8,128)(2,1)S(1)}, bf16[576,256]{1,0:T(8,128)(2,1)S(1)}, u32[]{:S(2)}, u32[]{:S(2)}) collective-permute-start(bf16[576,256]{1,0:T(8,128)(2,1)S(1)} %get-tuple-element.122), channel_id=1, source_target_pairs={{0,4},{1,5},{2,6},{3,7},{4,0},{5,1},{6,2},{7,3},{8,12},{9,13},{10,... | collective-permute-start | bytes 884744 | tf_op jit(solution)/shard_map/ppermute | solution.py:53
  33.9 27.5 %collective-permute-start.7 = (bf16[512,256]{1,0:T(8,128)(2,1)S(1)}, bf16[512,256]{1,0:T(8,128)(2,1)S(1)}, u32[]{:S(2)}, u32[]{:S(2)}) collective-permute-start(bf16[512,256]{1,0:T(8,128)(2,1)S(1)} %collective-permute-done.3.refs_4_), channel_id=1, source_target_pairs={{0,3},{1,0},{2,1},{3,2},{4,7},{5,4},{6,5},{7,6},{8,11},{9,8},{10,9... | collective-permute-start | bytes 786440 | tf_op jit(solution)/shard_map/ppermute | solution.py:53
  36.3 25.1 %collective-permute-start.8 = (bf16[512,256]{1,0:T(8,128)(2,1)S(1)}, bf16[512,256]{1,0:T(8,128)(2,1)S(1)}, u32[]{:S(2)}, u32[]{:S(2)}) collective-permute-start(bf16[512,256]{1,0:T(8,128)(2,1)S(1)} %collective-permute-done.3.refs_4_), channel_id=1, source_target_pairs={{0,2},{1,3},{2,0},{3,1},{4,6},{5,7},{6,4},{7,5},{8,10},{9,11},{10,... | collective-permute-start | bytes 786440 | tf_op jit(solution)/shard_map/ppermute | solution.py:53
  36.9 26.0 %collective-permute-start.9 = (bf16[512,256]{1,0:T(8,128)(2,1)S(1)}, bf16[512,256]{1,0:T(8,128)(2,1)}, u32[]{:S(2)}, u32[]{:S(2)}) collective-permute-start(bf16[512,256]{1,0:T(8,128)(2,1)S(1)} %collective-permute-done.3.refs_4_), channel_id=1, source_target_pairs={{0,1},{1,2},{2,3},{3,0},{4,5},{5,6},{6,7},{7,4},{8,9},{9,10},{10,1... | collective-permute-start | bytes 786440 | tf_op jit(solution)/shard_map/ppermute | solution.py:53
  37.5 16.7 %collective-permute-start.5 = (bf16[8,512]{1,0:T(8,128)(2,1)S(1)}, bf16[8,512]{1,0:T(8,128)(2,1)S(1)}, u32[]{:S(2)}, u32[]{:S(2)}) collective-permute-start(bf16[8,512]{1,0:T(8,128)(2,1)S(1)} %get-tuple-element.196), channel_id=1, source_target_pairs={{0,8},{1,9},{2,10},{3,11},{4,12},{5,13},{6,14},{7,15},{8,16},{9,17... | collective-permute-start | bytes 24584 | tf_op jit(solution)/shard_map/ppermute | solution.py:53
  54.2 7.2 %collective-permute-start.6 = (bf16[8,512]{1,0:T(8,128)(2,1)S(1)}, bf16[8,512]{1,0:T(8,128)(2,1)S(1)}, u32[]{:S(2)}, u32[]{:S(2)}) collective-permute-start(bf16[8,512]{1,0:T(8,128)(2,1)S(1)} %get-tuple-element.195), channel_id=1, source_target_pairs={{8,0},{9,1},{10,2},{11,3},{12,4},{13,5},{14,6},{15,7},{16,8},{17,9... | collective-permute-start | bytes 24584 | tf_op jit(solution)/shard_map/ppermute | solution.py:53
  62.9 5.3 %collective-permute-start.10 = (bf16[8,352,256]{2,1,0:T(8,128)(2,1)S(1)}, bf16[8,352,256]{2,1,0:T(8,128)(2,1)}, u32[]{:S(2)}, u32[]{:S(2)}) collective-permute-start(bf16[8,352,256]{2,1,0:T(8,128)(2,1)S(1)} %all-to-all-done.near_ref), channel_id=1, source_target_pairs={{0,8},{1,9},{2,10},{3,11},{4,12},{5,13},{6,14},{7,15},{8,0},{9,1},... | collective-permute-start | bytes 4325384 | tf_op jit(solution)/shard_map/ppermute | solution.py:53
  63.7 3.4 %collective-permute-start.11 = (bf16[512,256]{1,0:T(8,128)(2,1)S(1)}, bf16[512,256]{1,0:T(8,128)(2,1)}, u32[]{:S(2)}, u32[]{:S(2)}) collective-permute-start(bf16[512,256]{1,0:T(8,128)(2,1)S(1)} %pack_ring.1.refs_0_), channel_id=1, source_target_pairs={{0,8},{1,9},{2,10},{3,11},{4,12},{5,13},{6,14},{7,15},{8,0},{9,1},... | collective-permute-start | bytes 786440 | tf_op jit(solution)/shard_map/ppermute | solution.py:53
  63.7 3.7 %collective-permute-start.15 = (bf16[512,256]{1,0:T(8,128)(2,1)S(1)}, bf16[512,256]{1,0:T(8,128)(2,1)}, u32[]{:S(2)}, u32[]{:S(2)}) collective-permute-start(bf16[512,256]{1,0:T(8,128)(2,1)S(1)} %collective-permute-done.3.refs_4_), channel_id=1, source_target_pairs={{0,8},{1,9},{2,10},{3,11},{4,12},{5,13},{6,14},{7,15},{8,0},{9,1},... | collective-permute-start | bytes 786440 | tf_op jit(solution)/shard_map/ppermute | solution.py:53
  64.2 3.6 %collective-permute-start.12 = (bf16[512,256]{1,0:T(8,128)(2,1)S(1)}, bf16[512,256]{1,0:T(8,128)(2,1)}, u32[]{:S(2)}, u32[]{:S(2)}) collective-permute-start(bf16[512,256]{1,0:T(8,128)(2,1)S(1)} %collective-permute-done.refs_1_), channel_id=1, source_target_pairs={{0,8},{1,9},{2,10},{3,11},{4,12},{5,13},{6,14},{7,15},{8,0},{9,1},... | collective-permute-start | bytes 786440 | tf_op jit(solution)/shard_map/ppermute | solution.py:53
  64.2 9.1 %collective-permute-start.13 = (bf16[512,256]{1,0:T(8,128)(2,1)S(1)}, bf16[512,256]{1,0:T(8,128)(2,1)}, u32[]{:S(2)}, u32[]{:S(2)}) collective-permute-start(bf16[512,256]{1,0:T(8,128)(2,1)S(1)} %collective-permute-done.1.refs_2_), channel_id=1, source_target_pairs={{0,8},{1,9},{2,10},{3,11},{4,12},{5,13},{6,14},{7,15},{8,0},{9,1},... | collective-permute-start | bytes 786440 | tf_op jit(solution)/shard_map/ppermute | solution.py:53
  67.1 6.3 %collective-permute-start.14 = (bf16[512,256]{1,0:T(8,128)(2,1)S(1)}, bf16[512,256]{1,0:T(8,128)(2,1)S(1)}, u32[]{:S(2)}, u32[]{:S(2)}) collective-permute-start(bf16[512,256]{1,0:T(8,128)(2,1)S(1)} %collective-permute-done.2.refs_3_), channel_id=1, source_target_pairs={{0,8},{1,9},{2,10},{3,11},{4,12},{5,13},{6,14},{7,15},{8,0},{9,1},... | collective-permute-start | bytes 786440 | tf_op jit(solution)/shard_map/ppermute | solution.py:53
  67.5 5.9 %collective-permute-start.16 = (bf16[512,256]{1,0:T(8,128)(2,1)}, bf16[512,256]{1,0:T(8,128)(2,1)S(1)}, u32[]{:S(2)}, u32[]{:S(2)}) collective-permute-start(bf16[512,256]{1,0:T(8,128)(2,1)} %copy-done.2), channel_id=1, source_target_pairs={{0,8},{1,9},{2,10},{3,11},{4,12},{5,13},{6,14},{7,15},{8,0},{9,1},... | collective-permute-start | bytes 786440 | tf_op jit(solution)/shard_map/ppermute | solution.py:53
  67.8 5.6 %collective-permute-start.17 = (bf16[512,256]{1,0:T(8,128)(2,1)}, bf16[512,256]{1,0:T(8,128)(2,1)S(1)}, u32[]{:S(2)}, u32[]{:S(2)}) collective-permute-start(bf16[512,256]{1,0:T(8,128)(2,1)} %copy-done.4), channel_id=1, source_target_pairs={{0,8},{1,9},{2,10},{3,11},{4,12},{5,13},{6,14},{7,15},{8,0},{9,1},... | collective-permute-start | bytes 786440 | tf_op jit(solution)/shard_map/ppermute | solution.py:53
  68.2 5.2 %collective-permute-start.18 = (bf16[512,256]{1,0:T(8,128)(2,1)}, bf16[512,256]{1,0:T(8,128)(2,1)S(1)}, u32[]{:S(2)}, u32[]{:S(2)}) collective-permute-start(bf16[512,256]{1,0:T(8,128)(2,1)} %collective-permute-done.9.refs_7_), channel_id=1, source_target_pairs={{0,8},{1,9},{2,10},{3,11},{4,12},{5,13},{6,14},{7,15},{8,0},{9,1},... | collective-permute-start | bytes 786440 | tf_op jit(solution)/shard_map/ppermute | solution.py:53
  107.9 2.9 collective-permute-start.19
  124.8 12.6 %collective-permute-start.20 = (bf16[4,2,576,256]{3,2,1,0:T(8,128)(2,1)}, bf16[4,2,576,256]{3,2,1,0:T(8,128)(2,1)S(1)}, u32[]{:S(2)}, u32[]{:S(2)}) collective-permute-start(bf16[4,2,576,256]{3,2,1,0:T(8,128)(2,1)} %bitcast.61), channel_id=1, source_target_pairs={{0,8},{1,9},{2,10},{3,11},{4,12},{5,13},{6,14},{7,15},{8,0},{9,1},... | collective-permute-start | bytes 7077896 | tf_op jit(solution)/shard_map/ppermute | solution.py:53
  149.7 6.4 %collective-permute-start.21 = (bf16[256,5632]{1,0:T(8,128)(2,1)}, bf16[256,5632]{1,0:T(8,128)(2,1)S(1)}, u32[]{:S(2)}, u32[]{:S(2)}) collective-permute-start(bf16[256,5632]{1,0:T(8,128)(2,1)} %get-tuple-element.131.acts_ref), channel_id=1, source_target_pairs={{0,8},{1,9},{2,10},{3,11},{4,12},{5,13},{6,14},{7,15},{8,0},{9,1},... | collective-permute-start | bytes 8650760 | tf_op jit(solution)/shard_map/ppermute | solution.py:53
  150.6 5.5 %collective-permute-start.22 = (bf16[8,64,256]{2,1,0:T(8,128)(2,1)}, bf16[8,64,256]{2,1,0:T(8,128)(2,1)S(1)}, u32[]{:S(2)}, u32[]{:S(2)}) collective-permute-start(bf16[8,64,256]{2,1,0:T(8,128)(2,1)} %get-tuple-element.132.heads_ref), channel_id=1, source_target_pairs={{0,8},{1,9},{2,10},{3,11},{4,12},{5,13},{6,14},{7,15},{8,0},{9,1},... | collective-permute-start | bytes 786440 | tf_op jit(solution)/shard_map/ppermute | solution.py:53
  150.6 11.4 %all-to-all-start.3 = ((bf16[8,64,256]{2,1,0:T(8,128)(2,1)}), bf16[8,64,256]{2,1,0:T(8,128)(2,1)S(1)}, u32[]{:S(2)}, u32[]{:S(2)}) async-start(bf16[8,64,256]{2,1,0:T(8,128)(2,1)} %copy-done.1), calls=%async_computation.3 | async-start | bytes 524288 | tf_op jit(solution)/shard_map/all_to_all | solution.py:1003
  154.0 48.1 %reduce-scatter.5.cloned.1.call-start = ((), (), s32[]{:S(2)}) async-start(), calls=%async_computation.11 | async-start | bytes 2949120 | tf_op jit(solution)/shard_map/reduce_scatter | solution.py:904
  162.1 72.8 %reduce-scatter.7.cloned.1.call-start = ((), (), s32[]{:S(2)}) async-start(), calls=%async_computation.12 | async-start | bytes 737280 | tf_op jit(solution)/shard_map/reduce_scatter | solution.py:908
  182.4 3.3 collective-permute-start.23
  202.1 45.0 %reduce-scatter.9.cloned.1.call-start = ((), (), s32[]{:S(2)}) async-start(), calls=%async_computation.13 | async-start | bytes 1638400 | tf_op jit(solution)/shard_map/reduce_scatter | solution.py:904
  202.2 11.5 %collective-permute-start.26 = (bf16[256,2048]{1,0:T(8,128)(2,1)S(1)}, bf16[256,2048]{1,0:T(8,128)(2,1)S(1)}, u32[]{:S(2)}, u32[]{:S(2)}) collective-permute-start(bf16[256,2048]{1,0:T(8,128)(2,1)S(1)} %copy-done.6), channel_id=1, source_target_pairs={{0,8},{1,9},{2,10},{3,11},{4,12},{5,13},{6,14},{7,15},{8,0},{9,1},... | collective-permute-start | bytes 3145736 | tf_op jit(solution)/shard_map/ppermute | solution.py:53
  204.0 9.7 %collective-permute-start.29 = (bf16[8,192,256]{2,1,0:T(8,128)(2,1)S(1)}, bf16[8,192,256]{2,1,0:T(8,128)(2,1)S(1)}, u32[]{:S(2)}, u32[]{:S(2)}) collective-permute-start(bf16[8,192,256]{2,1,0:T(8,128)(2,1)S(1)} %all_to_all.37.d_ref), channel_id=1, source_target_pairs={{0,8},{1,9},{2,10},{3,11},{4,12},{5,13},{6,14},{7,15},{8,0},{9,1},... | collective-permute-start | bytes 2359304 | tf_op jit(solution)/shard_map/ppermute | solution.py:53
  204.0 7.7 %collective-permute-start.28 = (bf16[256,512]{1,0:T(8,128)(2,1)S(1)}, bf16[256,512]{1,0:T(8,128)(2,1)S(1)}, u32[]{:S(2)}, u32[]{:S(2)}) collective-permute-start(bf16[256,512]{1,0:T(8,128)(2,1)S(1)} %copy-done.11), channel_id=1, source_target_pairs={{0,8},{1,9},{2,10},{3,11},{4,12},{5,13},{6,14},{7,15},{8,0},{9,1},... | collective-permute-start | bytes 786440 | tf_op jit(solution)/shard_map/ppermute | solution.py:53
  208.8 4.9 %collective-permute-start.27 = (bf16[256,256]{1,0:T(8,128)(2,1)}, bf16[256,256]{1,0:T(8,128)(2,1)S(1)}, u32[]{:S(2)}, u32[]{:S(2)}) collective-permute-start(bf16[256,256]{1,0:T(8,128)(2,1)} %get-tuple-element.141.gs_ref), channel_id=1, source_target_pairs={{0,8},{1,9},{2,10},{3,11},{4,12},{5,13},{6,14},{7,15},{8,0},{9,1},... | collective-permute-start | bytes 393224 | tf_op jit(solution)/shard_map/ppermute | solution.py:53
  208.9 8.2 %collective-permute-start.24 = (bf16[8,256]{1,0:T(8,128)(2,1)}, bf16[8,256]{1,0:T(8,128)(2,1)S(1)}, u32[]{:S(2)}, u32[]{:S(2)}) collective-permute-start(bf16[8,256]{1,0:T(8,128)(2,1)} %get-tuple-element.138), channel_id=1, source_target_pairs={{0,8},{1,9},{2,10},{3,11},{4,12},{5,13},{6,14},{7,15},{8,16},{9,17... | collective-permute-start | bytes 12296 | tf_op jit(solution)/shard_map/ppermute | solution.py:53
  211.7 6.6 %collective-permute-start.25 = (bf16[8,256]{1,0:T(8,128)(2,1)}, bf16[8,256]{1,0:T(8,128)(2,1)S(1)}, u32[]{:S(2)}, u32[]{:S(2)}) collective-permute-start(bf16[8,256]{1,0:T(8,128)(2,1)} %get-tuple-element.139), channel_id=1, source_target_pairs={{8,0},{9,1},{10,2},{11,3},{12,4},{13,5},{14,6},{15,7},{16,8},{17,9... | collective-permute-start | bytes 12296 | tf_op jit(solution)/shard_map/ppermute | solution.py:53
  234.5 12.7 %collective-permute-start.31 = (bf16[256,2048]{1,0:T(8,128)(2,1)}, bf16[256,2048]{1,0:T(8,128)(2,1)S(1)}, u32[]{:S(2)}, u32[]{:S(2)}) collective-permute-start(bf16[256,2048]{1,0:T(8,128)(2,1)} %get-tuple-element.151.dw_ref), channel_id=1, source_target_pairs={{0,8},{1,9},{2,10},{3,11},{4,12},{5,13},{6,14},{7,15},{8,0},{9,1},... | collective-permute-start | bytes 3145736 | tf_op jit(solution)/shard_map/ppermute | solution.py:53
  243.3 2.3 collective-permute-start.34
  243.9 3.3 collective-permute-start.30
  244.0 3.2 collective-permute-start.33
  244.4 2.8 collective-permute-start.35
  245.6 1.5 collective-permute-start.32
  251.6 49.3 %all-to-all-start.5 = ((bf16[64,128,128]{2,1,0:T(8,128)(2,1)}), bf16[64,128,128]{2,1,0:T(8,128)(2,1)S(1)}, u32[]{:S(2)}, u32[]{:S(2)}) async-start(bf16[64,128,128]{2,1,0:T(8,128)(2,1)} %bitcast.54), calls=%async_computation.9 | async-start | bytes 4194304 | tf_op jit(solution)/shard_map/all_to_all | solution.py:1063
  260.7 32.6 %reduce-scatter.11.cloned.1.call-start = ((), (), s32[]{:S(2)}) async-start(), calls=%async_computation.14 | async-start | bytes 409600 | tf_op jit(solution)/shard_map/reduce_scatter | solution.py:908
  294.3 3.1 collective-permute-start.38
  295.7 4.6 %collective-permute-start.37 = (bf16[224,128]{1,0:T(8,128)(2,1)S(1)}, bf16[224,128]{1,0:T(8,128)(2,1)S(1)}, u32[]{:S(2)}, u32[]{:S(2)}) collective-permute-start(bf16[224,128]{1,0:T(8,128)(2,1)S(1)} %get-tuple-element.199), channel_id=1, source_target_pairs={{0,64},{1,65},{2,66},{3,67},{4,68},{5,69},{6,70},{7,71},{8,72},{9,... | collective-permute-start | bytes 172040 | tf_op jit(solution)/shard_map/ppermute | solution.py:53
  296.4 4.5 %collective-permute-start.36 = (bf16[224,128]{1,0:T(8,128)(2,1)S(1)}, bf16[224,128]{1,0:T(8,128)(2,1)S(1)}, u32[]{:S(2)}, u32[]{:S(2)}) collective-permute-start(bf16[224,128]{1,0:T(8,128)(2,1)S(1)} %get-tuple-element.197), channel_id=1, source_target_pairs={{0,32},{1,33},{2,34},{3,35},{4,36},{5,37},{6,38},{7,39},{8,40},{9,... | collective-permute-start | bytes 172040 | tf_op jit(solution)/shard_map/ppermute | solution.py:53
  318.0 6.2 %collective-permute-start.39 = (bf16[8,352,128]{2,1,0:T(8,128)(2,1)S(1)}, bf16[8,352,128]{2,1,0:T(8,128)(2,1)S(1)}, u32[]{:S(2)}, u32[]{:S(2)}) collective-permute-start(bf16[8,352,128]{2,1,0:T(8,128)(2,1)S(1)} %all_to_all.38.near_ref), channel_id=1, source_target_pairs={{0,8},{1,9},{2,10},{3,11},{4,12},{5,13},{6,14},{7,15},{8,0},{9,1},... | collective-permute-start | bytes 2162696 | tf_op jit(solution)/shard_map/ppermute | solution.py:53
  (15 other events, 148.5 us)
Sparse Core Ops, SparseCore 0:
  66.7 34.4 all-gather.2
  162.2 29.9 reduce-scatter.4
  202.2 18.0 reduce-scatter.6
  222.6 24.4 reduce-scatter.8
  263.6 29.6 reduce-scatter.10

commit v4 on v3

--- a/solution.py
+++ b/solution.py
@@ -17,6 +17,7 @@
 CTX = ("y", "xh", "core")
 CHIPS = ("y", "xh")
 WT = ("xl", "z")
+BLOCK = 1024
 LOG2E = 1.4426950408889634
 BF = jnp.bfloat16
 F32 = jnp.float32
@@ -198,13 +199,13 @@
     extra = jnp.where(row == 0, high, jnp.where(row == 1, mid, jnp.where(row == 2, low, 0.0)))
     grads = jnp.concatenate([grad_low, extra.astype(BF)], 0)
     query = near_ref[step, 0:HEAD, :]
-    block = 1024
+    grads = grads.T
+    block = BLOCK
     dq = jnp.zeros((rows, 2 * HEAD), F32)
     for start in range(0, 2 * span, block):
         cols = slice(start, start + block)
         expo = e_ref[:, cols]
-        d_probs = contract(grads, values_ref[:, cols], 0, 0)
-        d_scores = (expo.astype(F32) * d_probs).astype(BF)
+        d_scores = (expo.astype(F32) * matmul(grads, values_ref[:, cols])).astype(BF)
         dq = dq + matmul(d_scores, keys_ref[cols, :])
         dk_acc[:, cols] += matmul(query, d_scores)
         dv_acc[:, cols] += matmul(grad_low, expo)
@@ -258,6 +259,7 @@
 
 
 RIM = 8
+FOLD = 15
 ACT_N4 = slice(4096, 4608)
 ACT_GY = slice(4608, 5120)
 ACT_GA = slice(5120, 5632)
@@ -395,27 +397,29 @@
 
 
 def glu_kernel(info_ref, low_ref, x_ref, high_ref, near_ref, far_ref, n1_ref, a_ref, sg_ref, h1_ref,
-               main_ref, one_ref, w_ref, sem):
+               main_ref, w_ref, small_ref, sem):
     rows = x_ref.shape[0]
     main = slice(RIM, RIM + rows)
-    copies = fetch(info_ref[0], near_ref, far_ref, w_ref, sem)
+    core = info_ref[0]
+    copies = launch(
+        [(near_ref.at[:, SMALL:SMALL + 32, :], small_ref), (near_ref.at[:, 0:128, :], w_ref.at[core]),
+         (far_ref.at[:, 0:128, :], w_ref.at[1 - core])], sem
+    )
     x = jnp.concatenate(
         [low_ref[...].astype(F32), x_ref[...].astype(F32), high_ref[...].astype(F32)], 0
     )
     normal, _ = normal_of(x)
     settle(copies)
-    copies = launch([(w_ref, one_ref)], sem)
-    normed = normal * gains_of(w_ref.at[0, :, SMALL:SMALL + 32, :])[0:1]
+    normed = normal * gains_of(small_ref)[0:1]
     n1 = normed.astype(BF)
     n1_ref[...] = normed[main].astype(BF)
     a = matmul(n1, glu_of(w_ref, 0))
     sg = jax.nn.sigmoid(matmul(n1, glu_of(w_ref, 1)))
-    a_ref[...] = a[main]
-    sg_ref[...] = sg[main]
+    a_ref[...] = a[main].astype(BF)
+    sg_ref[...] = sg[main].astype(BF)
     h1 = x + a * sg
     h1_ref[...] = h1
     main_ref[...] = h1[main]
-    settle(copies)
 
 
 def conv_kernel(info_ref, h1_ref, *refs):
@@ -423,18 +427,18 @@
     conv_body(info_ref, h1_ref, near2, far2, *rest)
 
 
-def conv_body(info_ref, h1_ref, near2, far2, one_ref,
+def conv_body(info_ref, h1_ref, near2, far2, near1_ref, far1_ref,
               n2_ref, wp_out, np_ref, nm_out, mean_ref, scale_ref, sp_out, h2_ref, n3_ref,
-              qkv_ref, two_ref, w2_ref, wq_ref, small_ref, mix_ref, wp_ref, nm_ref, sp_ref,
+              qkv_ref, two_ref, one_ref, w2_ref, w1_ref, mix_ref, wp_ref, nm_ref, sp_ref, slab_ref,
               sem2, semq, sems):
     core = info_ref[0]
     rim_rows = h1_ref.shape[0]
     rows = rim_rows - 2 * RIM
-    copiesq = launch(
-        [small_pair(one_ref, small_ref), (one_ref.at[:, :, 128:SMALL, :], wq_ref)], semq
-    )
+    copiesq = fetch(core, near1_ref, far1_ref, w1_ref, semq)
     copies2 = collect(info_ref, near2, far2, w2_ref, sem2)
-    settle(copiesq[:1])
+    small_ref = w1_ref.at[0, :, SMALL:SMALL + 32, :]
+    settle(copiesq)
+    copiesq = launch([(w1_ref, one_ref)], semq)
 
     def leaving(which, index):
         source, target = ((wp_ref, wp_out), (nm_ref, nm_out), (sp_ref, sp_out))[which]
@@ -461,22 +465,24 @@
     narrow = smooth_unit(narrow)
 
     def first_pass(index, total):
-        cols = block_cols(index)
-        wide = matmul(n2_ref[...], upper_block(w2_ref, index))
-        wp_ref[:, cols] = wide
-        leaving(0, index).start()
-        mixed = smooth_unit(wide) + narrow * jnp.where(index == 0, 1.0, 0.0)
-        mix_ref[:, cols] = mixed
+        weights = jnp.concatenate([upper_block(w2_ref, 2 * index + i) for i in range(2)], 1)
+        wide = matmul(n2_ref[...], weights)
+        wp_ref[:, block_cols(index, 512)] = wide
+        for i in range(2):
+            leaving(0, 2 * index + i).start()
+        mixed = smooth_unit(wide)
+        head = mixed[:, 0:256] + narrow * jnp.where(index == 0, 1.0, 0.0)
+        mixed = jnp.concatenate([head, mixed[:, 256:512]], 1)
+        mix_ref[:, block_cols(index, 512)] = mixed
         return total + jnp.sum(mixed, -1, keepdims=True)
 
-    total = lax.fori_loop(0, 8, first_pass, jnp.zeros((rim_rows, 1), F32))
+    total = lax.fori_loop(0, 4, first_pass, jnp.zeros((rim_rows, 1), F32))
     mean = total * (1.0 / 2048)
 
-    def second_pass(index, total):
-        centred = mix_ref[:, block_cols(index)] - mean
-        return total + jnp.sum(centred * centred, -1, keepdims=True)
-
-    total = lax.fori_loop(0, 8, second_pass, jnp.zeros((rim_rows, 1), F32))
+    total = jnp.zeros((rim_rows, 1), F32)
+    for index in range(8):
+        centred = mix_ref[:, 256 * index:256 * index + 256] - mean
+        total = total + jnp.sum(centred * centred, -1, keepdims=True)
     scale = lax.rsqrt(total * (1.0 / 2048) + EPSILON)
     mean_ref[...] = jnp.broadcast_to(mean, mean_ref.shape)
     scale_ref[...] = jnp.broadcast_to(scale, scale_ref.shape)
@@ -488,28 +494,32 @@
         nm = ((mix_ref[:, cols] - mean) * scale * gain * valid).astype(BF)
         nm_ref[:, cols] = nm
         leaving(1, index).start()
-        mix_ref[:, cols] = nm.astype(F32)
-        spread = jnp.zeros((rows, 256), F32)
-        for tap in range(9):
-            spread = spread + mix_ref[4 + tap:4 + tap + rows, cols] * taps[tap:tap + 1]
-        spread = spread.astype(BF)
+        nm = nm.astype(F32)
+        halves = []
+        for half in range(2):
+            lanes = slice(128 * half, 128 * half + 128)
+            slab_ref[half] = nm[:, lanes]
+            spread = jnp.zeros((rows, 128), F32)
+            for tap in range(9):
+                spread = spread + slab_ref[half, 4 + tap:4 + tap + rows, :] * taps[tap:tap + 1, lanes]
+            halves.append(spread)
+        spread = jnp.concatenate(halves, 1).astype(BF)
         sp_ref[:, cols] = spread
         leaving(2, index).start()
         h2_ref[:, 0:256] += matmul(spread, point_block(w2_ref, index))
         return carry
 
-    lax.fori_loop(0, 8, third_pass, 0)
+    lax.fori_loop(0, 8, third_pass, 0, unroll=2)
     normal, _ = normal_of(h2_ref[...])
     n3 = (normal * gains[2:3]).astype(BF)
     n3_ref[...] = n3
-    settle(copiesq[1:])
     for part in range(3):
         for side in range(2):
-            block = matmul(n3, queries_of(wq_ref, side, part))
+            block = matmul(n3, w1_ref[side, :, 128 + 64 * part:192 + 64 * part, :].reshape(512, 256))
             qkv_ref[4 * side:4 * side + 4, 64 * part:64 * part + 64, :] = (
                 block.T.astype(BF).reshape(4, 64, rows)
             )
-    settle(copies2)
+    settle(copies2 + copiesq)
     for which in range(3):
         for index in range(8):
             leaving(which, index).wait()
@@ -539,23 +549,28 @@
     y_ref[...] = h3
     dn_ref[...] = jnp.zeros_like(dn_ref)
 
+    gy0, gy1 = acts_ref[:, 4608:4864], acts_ref[:, 4864:5120]
+
     def step(index, carry):
-        cols = block_cols(index)
-        upper = upper_block(w_ref, index)
-        lower = [w_ref[side, lax.div(index, 4), lax.rem(index, 4), 256:512, :] for side in range(2)]
+        upper = jnp.concatenate([upper_block(w_ref, 2 * index + i) for i in range(2)], 1)
+        lower = []
+        for side in range(2):
+            blocks = [2 * index + i for i in range(2)]
+            blocks = [w_ref[side, lax.div(k, 4), lax.rem(k, 4), 256:512, :] for k in blocks]
+            lower.append(jnp.concatenate(blocks, 0))
         u = matmul(acts_ref[:, ACT_N4], upper)
         sigma = jax.nn.sigmoid(u)
         r = (u * sigma).astype(BF)
-        acts_ref[:, cols] = r
+        acts_ref[:, block_cols(index, 512)] = r
+        dr = contract(gy0, lower[0], 1, 1) + contract(gy1, lower[1], 1, 1)
+        du = (dr * (sigma * (1.0 + u * (1.0 - sigma)))).astype(BF)
+        acts_ref[:, block_cols(index + 4, 512)] = du
         y_ref[:, 0:256] += matmul(r, lower[0])
         y_ref[:, 256:512] += matmul(r, lower[1])
-        dr = contract(acts_ref[:, 4608:4864], lower[0], 1, 1) + contract(acts_ref[:, 4864:5120], lower[1], 1, 1)
-        du = (dr * (sigma * (1.0 + u * (1.0 - sigma)))).astype(BF)
-        acts_ref[:, block_cols(index + 8)] = du
         dn_ref[...] += contract(du, upper, 1, 1)
         return carry
 
-    lax.fori_loop(0, 8, step, 0)
+    lax.fori_loop(0, 4, step, 0)
     out_ref[...] = (y_ref[...] * valid).astype(BF)
     dn = dn_ref[...]
     gain_ref[...] = column_sum(dn * normal)
@@ -585,48 +600,50 @@
         out_ref[xh, w // 4, w % 4, :, rows, :] = value[:, xh]
 
 
-def both(product, pairs):
-    return sum((product(*pair) for pair in pairs[1:]), product(*pairs[0]))
+def stack_rows(*pieces):
+    return jnp.concatenate(pieces, 0)
 
 
 def early_kernel(info_ref, acts_ref, heads_ref, acts2_ref, heads2_ref, out_ref):
     rows = acts_ref.shape[0]
     side = info_ref[0]
-    refs = (acts_ref, acts2_ref)
+
+    def tokens(cols):
+        return stack_rows(acts_ref[:, cols], acts2_ref[:, cols])
+
+    n4 = tokens(ACT_N4).T
     for j in range(4):
-        cols = block_cols(side * 4 + j + 8)
-        res = both(lambda n, d: contract(n, d, 0, 0), [(ref[:, ACT_N4], ref[:, cols]) for ref in refs])
+        res = matmul(n4, tokens(block_cols(side * 4 + j + 8)))
         for i in range(2):
             by_chip(out_ref, 2 * j + i, slice(0, 64), res[:, 128 * i:128 * i + 128].reshape(8, 64, 128))
-    gy = [ref[:, block_cols(side + 18)] for ref in refs]
+    gy = tokens(block_cols(side + 18)).T
     for w in range(8):
-        cols = slice(256 * w, 256 * w + 256)
-        res = both(lambda g, r: contract(g, r, 0, 0), [(g, ref[:, cols]) for g, ref in zip(gy, refs)])
-        res = res.reshape(8, 32, 256)
+        res = matmul(gy, tokens(slice(256 * w, 256 * w + 256))).reshape(8, 32, 256)
         for i in range(2):
             by_shard(out_ref, w, slice(64 + 32 * i, 96 + 32 * i), res[:, :, 128 * i:128 * i + 128])
-    ga = block_cols(side + 20)
-    res = both(matmul, [(h[...].reshape(512, rows), ref[:, ga])
-                        for h, ref in zip((heads_ref, heads2_ref), refs)])
-    packed = pair_rows(res)
+    heads = jnp.concatenate([heads_ref[...].reshape(512, rows), heads2_ref[...].reshape(512, rows)], 1)
+    packed = pair_rows(matmul(heads, tokens(block_cols(side + 20))))
     for c in range(8):
         by_chip(out_ref, c, slice(128, 144), packed[:, c])
 
 
-def attn_in_kernel(info_ref, d_ref, h2_ref, g3_ref, one_ref,
-                   g2_ref, gs_ref, lo_ref, hi_ref, gain_ref, w_ref, small_ref, sem):
+def attn_in_kernel(info_ref, d_ref, h2_in, g3_in, one_ref,
+                   g2_ref, gs_ref, lo_ref, hi_ref, gain_ref, w_ref, small_ref, h2_ref, g3_ref, sem):
     rows = h2_ref.shape[0]
     copies = launch(
-        [small_pair(one_ref, small_ref), (one_ref.at[:, :, 128:SMALL, :], w_ref)], sem
-    )
+        [(h2_in, h2_ref), small_pair(one_ref, small_ref), (one_ref.at[:, :, 128:SMALL, :], w_ref),
+         (g3_in, g3_ref)], sem
+    )
+    settle(copies[:1])
     normal, scale = normal_of(h2_ref[...])
-    settle(copies)
+    settle(copies[1:])
     gains = gains_of(small_ref)
-    dn = jnp.zeros((rows, 512), F32)
-    for part in range(3):
-        for side in range(2):
-            block = d_ref[4 * side:4 * side + 4, 64 * part:64 * part + 64, :].reshape(256, rows)
-            dn = dn + contract(block, queries_of(w_ref, side, part), 0, 1)
+    parts = [(part, side) for part in range(3) for side in range(2)]
+    blocks = [
+        d_ref[4 * side:4 * side + 4, 64 * part:64 * part + 64, :].reshape(256, rows) for part, side in parts
+    ]
+    weights = [queries_of(w_ref, side, part) for part, side in parts]
+    dn = contract(stack_rows(*blocks).T, jnp.concatenate(weights, 1), 1, 1)
     gain_ref[...] = column_sum(dn * normal)
     g2 = g3_ref[...] + back_of(dn, normal, scale, gains[2:3])
     g2_ref[...] = g2
@@ -636,15 +653,24 @@
     hi_ref[...] = gs[rows - RIM:rows].astype(BF)
 
 
-def conv_back_kernel(info_ref, lo_ref, gs_ref, hi_ref, nm_ref, wp_ref, np_ref, mean_ref,
-                     scale_ref, two_ref, one_ref, dw_ref, dnar_ref, table_ref,
-                     pt_ref, small_ref, nmf_ref, dsp_ref, sc_ref, hat_ref, sem):
+def conv_back_kernel(info_ref, lo_ref, gs_ref, hi_ref, np_ref, mean_ref, scale_ref, nm_in, wp_in,
+                     two_ref, one_ref, dw_ref, dnar_ref, table_ref, pt_ref, small_ref, nmf_ref,
+                     dsp_ref, sc_ref, hat_ref, nm_ref, wp_ref, sem, sems):
     rim_rows = wp_ref.shape[0]
     rows = rim_rows - 2 * RIM
     main = slice(RIM, RIM + rows)
     copies = launch(
         [small_pair(one_ref, small_ref), (two_ref.at[1, :, :, 256:512, :], pt_ref)], sem
     )
+
+    def arriving(which, index):
+        source, target = ((nm_in, nm_ref), (wp_in, wp_ref))[which]
+        cols = block_cols(index)
+        return pltpu.make_async_copy(source.at[:, cols], target.at[:, cols], sems.at[which, index])
+
+    for index in range(8):
+        for which in range(2):
+            arriving(which, index).start()
     valid = mask_of(info_ref, rim_rows, RIM)
     gs = jnp.concatenate(
         [lo_ref[...].astype(F32), gs_ref[...].astype(F32), hi_ref[...].astype(F32)], 0
@@ -652,23 +678,34 @@
     mean = mean_ref[:, 0:1]
     scale = scale_ref[:, 0:1]
     table_ref[...] = jnp.zeros_like(table_ref)
-    dsp_ref[0:RIM, :] = jnp.zeros((RIM, 256), F32)
-    dsp_ref[RIM + rim_rows:, :] = jnp.zeros((RIM, 256), F32)
+    dsp_ref[:, 0:RIM, :] = jnp.zeros((2, RIM, 128), F32)
+    dsp_ref[:, RIM + rim_rows:, :] = jnp.zeros((2, RIM, 128), F32)
     settle(copies)
 
     def first_pass(index, carry):
         one, two = carry
         cols = block_cols(index)
         taps, gain = taps_of(small_ref, index)
+        arriving(0, index).wait()
+        arriving(1, index).wait()
         dsp = contract(gs, pt_ref[lax.div(index, 4), lax.rem(index, 4)], 1, 1).astype(BF).astype(F32)
-        dsp_ref[RIM:RIM + rim_rows, :] = dsp
-        nmf_ref[...] = nm_ref[:, cols].astype(F32)
-        inner = dsp[main]
-        dn = jnp.zeros((rim_rows, 256), F32)
-        for tap in range(9):
-            dn = dn + dsp_ref[12 - tap:12 - tap + rim_rows, :] * taps[tap:tap + 1]
-            table_ref[tap:tap + 1, cols] = column_sum(nmf_ref[4 + tap:4 + tap + rows, :] * inner)
-        dn = dn * valid
+        nm = nm_ref[:, cols].astype(F32)
+        halves = []
+        sums = []
+        for half in range(2):
+            lanes = slice(128 * half, 128 * half + 128)
+            dsp_ref[half, RIM:RIM + rim_rows, :] = dsp[:, lanes]
+            nmf_ref[half] = nm[:, lanes]
+            inner = dsp[main, lanes]
+            dn = jnp.zeros((rim_rows, 128), F32)
+            parts = []
+            for tap in range(9):
+                dn = dn + dsp_ref[half, 12 - tap:12 - tap + rim_rows, :] * taps[tap:tap + 1, lanes]
+                parts.append(column_sum(nmf_ref[half, 4 + tap:4 + tap + rows, :] * inner))
+            halves.append(dn)
+            sums.append(jnp.concatenate(parts, 0))
+        table_ref[0:9, cols] = jnp.concatenate(sums, 1)
+        dn = jnp.concatenate(halves, 1) * valid
         mixed = smooth_unit(wp_ref[:, cols]) + smooth_unit(np_ref[...]) * jnp.where(index == 0, 1.0, 0.0)
         hat = (mixed - mean) * scale
         hat_ref[:, cols] = hat
@@ -696,36 +733,40 @@
     lax.fori_loop(0, 8, second_pass, 0)
 
 
-def glu_back_kernel(info_ref, dw_ref, dnar_ref, h1_ref, two_ref, one_ref, g2_ref,
-                    a_ref, sg_ref, x_ref, table_ref, gattn_ref, gffn_ref, dx_ref, dab_ref, sums_ref,
-                    w2_ref, w1_ref, small_ref, dn_ref, nar_ref, sem):
+def glu_back_kernel(info_ref, dw_ref, dnar_ref, h1_in, two_ref, one_ref, g2_ref,
+                    a_in, sg_in, x_in, table_ref, gattn_ref, gffn_ref, dx_ref, dab_ref, sums_ref,
+                    w2_ref, w1_ref, small_ref, nar_ref, h1_ref, a_ref, sg_ref, x_ref, sem):
     rows = g2_ref.shape[0]
-    copies = launch([(two_ref, w2_ref)], sem)
+    first = launch([(h1_in, h1_ref)], sem)
+    copies = launch(
+        [(two_ref.at[0, :, :, 0:448, :], w2_ref.at[0]),
+         (two_ref.at[1, :, :, 0:256, :], w2_ref.at[1, :, :, 0:256, :])], sem.at[1:3]
+    )
     copies1 = launch(
-        [small_pair(one_ref, small_ref), (one_ref.at[:, :, 0:128, :], w1_ref)], sem.at[1:3]
+        [small_pair(one_ref, small_ref), (one_ref.at[:, :, 0:128, :], w1_ref), (a_in, a_ref),
+         (sg_in, sg_ref), (x_in, x_ref)], sem.at[3:8]
     )
     valid = mask_of(info_ref, rows, 0)
     nar_ref[...] = dnar_ref[...].astype(F32)
-    dn_ref[...] = jnp.zeros_like(dn_ref)
+    settle(first)
     normal, scale1 = normal_of(h1_ref[...])
-    settle(copies)
-    for tap in range(3):
-        moved = nar_ref[9 - tap:9 - tap + rows, :].astype(BF)
-        dn_ref[...] += contract(moved, narrow_block(w2_ref, tap), 1, 1)
-
-    def step(index, carry):
-        dn_ref[...] += contract(dw_ref[:, block_cols(index)], upper_block(w2_ref, index), 1, 1)
-        return carry
-
-    lax.fori_loop(0, 8, step, 0)
+    moved = jnp.concatenate([nar_ref[9 - tap:9 - tap + rows, :].astype(BF) for tap in range(3)], 1)
+    dn = jnp.zeros((rows, 512), F32)
+    for side in range(2):
+        copies[side].wait()
+        weights = [w2_ref[side, :, :, 64 * j:64 * j + 64, :].reshape(512, 256) for j in range(4)]
+        dn = dn + contract(dw_ref[:, 1024 * side:1024 * side + 1024], jnp.concatenate(weights, 1), 1, 1)
+        if side == 0:
+            weights = jnp.concatenate([narrow_block(w2_ref, tap) for tap in range(3)], 1)
+            dn = dn + contract(moved, weights, 1, 1)
     settle(copies1)
     gains = gains_of(small_ref)
-    dn = dn_ref[...] * valid
+    dn = dn * valid
     gconv = column_sum(dn * normal)
     g1 = g2_ref[...] + back_of(dn, normal, scale1, gains[1:2])
-    sg = sg_ref[...]
+    sg = sg_ref[...].astype(F32)
     da = (g1 * sg).astype(BF)
-    db = (g1 * a_ref[...] * sg * (1.0 - sg)).astype(BF)
+    db = (g1 * a_ref[...].astype(F32) * sg * (1.0 - sg)).astype(BF)
     dab_ref[:, 0:512] = da
     dab_ref[:, 512:1024] = db
     sums_ref[0:16, :] = table_ref[...]
@@ -742,19 +783,16 @@
 def middle_kernel(info_ref, sp_ref, gs_ref, n3_ref, d_ref, sp2_ref, gs2_ref, n32_ref, d2_ref, out_ref):
     rows = gs_ref.shape[0]
     side = info_ref[0]
-    gs = [ref[:, block_cols(side, 128)] for ref in (gs_ref, gs2_ref)]
+    gs = stack_rows(gs_ref[:, block_cols(side, 128)], gs2_ref[:, block_cols(side, 128)]).T
     for w in range(8):
         cols = slice(256 * w, 256 * w + 256)
-        res = both(lambda g, s: contract(g, s, 0, 0),
-                   [(g, ref[:, cols]) for g, ref in zip(gs, (sp_ref, sp2_ref))])
-        res = res.reshape(8, 16, 256)
+        res = matmul(gs, stack_rows(sp_ref[:, cols], sp2_ref[:, cols])).reshape(8, 16, 256)
         for i in range(2):
             by_shard(out_ref, w, slice(16 * i, 16 * i + 16), res[:, :, 128 * i:128 * i + 128])
+    n3 = stack_rows(n3_ref[...], n32_ref[...]).T
     for part in range(3):
-        pairs = [(n[...], d[pl.ds(side * 4, 4), 64 * part:64 * part + 64, :].reshape(256, rows))
-                 for n, d in ((n3_ref, d_ref), (n32_ref, d2_ref))]
-        res = both(lambda n, d: contract(n, d, 0, 1), pairs)
-        packed = pair_rows(res)
+        d = [ref[pl.ds(side * 4, 4), 64 * part:64 * part + 64, :].reshape(256, rows) for ref in (d_ref, d2_ref)]
+        packed = pair_rows(contract(n3, jnp.concatenate(d, 1), 1, 1))
         for c in range(8):
             by_chip(out_ref, c, slice(32 + 16 * part, 48 + 16 * part), packed[:, c])
 
@@ -770,17 +808,15 @@
         narf_ref[...] = d_ref[...].astype(F32)
         shifted.append([n2f_ref[7 + tap:7 + tap + rows, :].astype(BF) for tap in range(3)])
         dnar.append(narf_ref[RIM:RIM + rows, block_cols(side, 128)].astype(BF))
+    shifted = [stack_rows(*pair).T for pair in zip(*shifted)]
+    dnar = stack_rows(*dnar)
     for j in range(4):
         cols = block_cols(side * 4 + j)
-        res = both(lambda n, d: contract(n, d, 0, 0),
-                   [(n[1], ref[:, cols]) for n, ref in zip(shifted, (dw_ref, dw2_ref))])
+        res = matmul(shifted[1], stack_rows(dw_ref[:, cols], dw2_ref[:, cols]))
         for i in range(2):
             part = res[:, 128 * i:128 * i + 128].reshape(8, 64, 128)
             out_ref[2 * j + i, :, 0:64, :] = part.astype(BF)
-    narrow = [
-        both(lambda n, d: contract(n, d, 0, 0), [(n[tap], d) for n, d in zip(shifted, dnar)])
-        for tap in range(3)
-    ]
+    narrow = [matmul(piece, dnar) for piece in shifted]
     for w in range(8):
         lanes = pl.ds(pl.multiple_of(w * 256 + side * 128, 128), 128)
         pair = slice(128 * (w // 2), 128 * (w // 2) + 128)
@@ -791,11 +827,10 @@
             pieces = [n[64 * w + 8 * c:64 * w + 8 * c + 8] for n in narrow]
             pieces += [table[2 * c:2 * c + 2], jnp.zeros((6, 128), F32)]
             out_ref[c, w, 64:96, :] = jnp.concatenate(pieces, 0).astype(BF)
+    n1 = stack_rows(n1_ref[...], n12_ref[...]).T
     for place in range(2):
         cols = block_cols(side + 2 * place)
-        res = both(lambda n, d: contract(n, d, 0, 0),
-                   [(n[...], d[:, cols]) for n, d in ((n1_ref, dab_ref), (n12_ref, dab2_ref))])
-        packed = pair_rows(res).astype(BF)
+        packed = pair_rows(matmul(n1, stack_rows(dab_ref[:, cols], dab2_ref[:, cols]))).astype(BF)
         for w in range(8):
             out_ref[:, w, 96 + 16 * place:112 + 16 * place, :] = packed[w]
 
@@ -899,6 +934,13 @@
     settle(later)
 
 
+def fold_kernel(*refs):
+    total = refs[0][...].astype(F32)
+    for ref in refs[1:4]:
+        total = total + ref[...].astype(F32)
+    refs[4][...] = total.astype(BF)
+
+
 def over_x(value):
     value = value.reshape((4,) + value.shape[2:])
     return lax.psum_scatter(value, ("xh", "xl"), scatter_dimension=0, tiled=True)[0]
@@ -965,24 +1007,23 @@
     tall, wide, narrow = (rows, width), (rows, units), (rows, 256)
     tiny = pltpu.VMEM((8, 32, 256), BF)
     ring = pltpu.VMEM((2, 2, 4) + pack2.shape, BF)
-    n1, a, sg, h1, h1m, one = call(
+    n1, a, sg, h1, h1m = call(
         glu_kernel,
-        [(tall, BF), (tall, F32), (tall, F32), ((rim_rows, width), F32, FREE), (tall, F32),
-         ((2,) + near1.shape, BF, HBM)],
-        [SMEM] + [FREE] * 3 + [ANY] * 2, [pltpu.VMEM((2,) + near1.shape, BF), dma((2,))], "glu", 3,
+        [(tall, BF), (tall, BF), (tall, BF), ((rim_rows, width), F32, FREE), (tall, F32)],
+        [SMEM] + [FREE] * 3 + [ANY] * 2, [pltpu.VMEM((2, 8, 128, 256), BF), tiny, dma((3,))], "glu", 3,
         info, low_x, x, high_x, near1, far1,
     )
-    n2, wp, np_, nm, mean, scale, sp, h2, n3, qkv, two = call(
+    n2, wp, np_, nm, mean, scale, sp, h2, n3, qkv, two, one = call(
         conv_kernel,
         [((rim_rows, width), BF), ((rim_rows, units), F32, HBM), ((rim_rows, 256), F32),
          ((rim_rows, units), BF, HBM), ((rim_rows, 128), F32), ((rim_rows, 128), F32),
          (wide, BF, HBM), (tall, F32), (tall, BF), ((HEADS, 3 * HEAD, rows), BF, FREE),
-         (ring.shape, BF, HBM)],
-        [SMEM, FREE] + [ANY] * 16 + [HBM],
-        [ring, pltpu.VMEM((2, 8, SMALL - 128, 256), BF), tiny, pltpu.VMEM((rim_rows, units), F32),
+         (ring.shape, BF, HBM), ((2,) + near1.shape, BF, HBM)],
+        [SMEM, FREE] + [ANY] * 18,
+        [ring, pltpu.VMEM((2,) + near1.shape, BF), pltpu.VMEM((rim_rows, units), F32),
          pltpu.VMEM((rim_rows, units), F32), pltpu.VMEM((rim_rows, units), BF), pltpu.VMEM(wide, BF),
-         dma((16,)), dma((2,)), dma((3, 8))],
-        "conv", 15, info, h1, *near2, *far2, one,
+         pltpu.VMEM((2, rim_rows, 128), F32), dma((16,)), dma((2,)), dma((3, 8))],
+        "conv", 15, info, h1, *near2, *far2, near1, far1,
     )
     near = lax.all_to_all(qkv, CHIPS, 0, 0, tiled=True)
     far = send(near[:, HEAD:], flip)
@@ -992,8 +1033,8 @@
     heads_in = lax.all_to_all(head_out, CHIPS, 0, 0, tiled=True)
     output, acts, g3, dob, d_gffn, heads_in = call(
         ffn_kernel,
-        [(tall, BF), ((rows, 5632), BF), (tall, F32), ((HEADS, HEAD, rows), BF, FREE),
-         ((1, width), F32), ((HEADS, HEAD, rows), BF)],
+        [(tall, BF), ((rows, 5632), BF, FREE), (tall, F32), ((HEADS, HEAD, rows), BF),
+         ((1, width), F32), ((HEADS, HEAD, rows), BF, FREE)],
         [SMEM, VMEM, FREE, VMEM, HBM, HBM, ANY],
         [pltpu.VMEM((2, 2, 4) + pack3.shape, BF), tiny, pltpu.VMEM(tall, F32), pltpu.VMEM(tall, F32),
          dma((5,))],
@@ -1002,7 +1043,7 @@
 
     d_near = lax.all_to_all(dob, CHIPS, 0, 0, tiled=True)
     early = call(
-        early_kernel, [((2, 2, 4, 4, EARLY, 128), BF)], [SMEM] + [VMEM] * 2 + [FREE] * 2, [], "early", 0.3,
+        early_kernel, [((2, 2, 4, 4, EARLY, 128), BF)], [SMEM] + [FREE] * 4, [], "early", 0.3,
         info, acts, heads_in, send(acts, flip), send(heads_in, flip),
     )[0]
     d_near, early = lax.optimization_barrier((d_near, early))
@@ -1012,54 +1053,61 @@
     d_own = jnp.concatenate([dk[0], dv[0]], 1).astype(F32)
     d_qkv = jnp.concatenate([dq, (d_own + d_far).astype(BF)], 1)
     d_qkv = lax.all_to_all(d_qkv, CHIPS, 0, 0, tiled=True)
-    early, _ = lax.optimization_barrier((early, d_qkv))
     early = over_z(early)
     g2, gs, lo, hi, d_gatt = call(
         attn_in_kernel,
-        [(tall, F32), (narrow, BF), ((RIM, 256), BF), ((RIM, 256), BF), ((1, width), F32)],
-        [SMEM, FREE] + [VMEM] * 2 + [HBM],
-        [pltpu.VMEM((2, 8, SMALL - 128, 256), BF), tiny, dma((2,))],
+        [(tall, F32), (narrow, BF, FREE), ((RIM, 256), BF), ((RIM, 256), BF), ((1, width), F32)],
+        [SMEM, FREE] + [HBM] * 3,
+        [pltpu.VMEM((2, 8, SMALL - 128, 256), BF), tiny, pltpu.VMEM(tall, F32), pltpu.VMEM(tall, F32),
+         dma((4,))],
         "attn_in", 0.5, info, d_qkv, h2, g3, one,
     )
     low_gs = send(hi, along(1))
     high_gs = send(lo, along(-1))
+    info_mid, _, _ = lax.optimization_barrier((info, low_gs, high_gs))
     middle = call(
-        middle_kernel, [((2, 2, 4, 4, MIDDLE, 128), BF)], [SMEM] + [VMEM] * 3 + [FREE] * 5, [], "middle", 0.3,
-        info, sp, gs, n3, d_qkv, *[send(v, flip) for v in (sp, gs, n3, d_qkv)],
+        middle_kernel, [((2, 2, 4, 4, MIDDLE, 128), BF)], [SMEM, VMEM, FREE, VMEM, FREE] + [FREE] * 4, [], "middle", 0.3,
+        info_mid, sp, gs, n3, d_qkv, *[send(v, flip) for v in (sp, gs, n3, d_qkv)],
     )[0]
-    low_gs, high_gs, middle = lax.optimization_barrier((low_gs, high_gs, middle))
+    info_conv, middle = lax.optimization_barrier((info, middle))
     middle = over_x(middle)
     rim_narrow = ((rim_rows, 256), BF)
     dw, dnar, table = call(
-        conv_back_kernel, [(wide, BF), rim_narrow, ((16, units), F32)],
-        [SMEM, FREE, VMEM, FREE] + [VMEM] * 5 + [HBM] * 2,
-        [pltpu.VMEM((2, 4, 256, 256), BF), tiny, pltpu.VMEM((rim_rows, 256), F32), pltpu.VMEM((rim_rows + 2 * RIM, 256), F32),
-         pltpu.VMEM((rim_rows, units), F32), pltpu.VMEM((rim_rows, units), F32), dma((2,))],
-        "conv_back", 2, info, low_gs, gs, high_gs, nm, wp, np_, mean, scale, two, one,
+        conv_back_kernel, [(wide, BF, FREE), ((rim_rows, 256), BF, FREE), ((16, units), F32, FREE)],
+        [SMEM, FREE, FREE, FREE] + [VMEM] * 3 + [HBM] * 4,
+        [pltpu.VMEM((2, 4, 256, 256), BF), tiny, pltpu.VMEM((2, rim_rows, 128), F32),
+         pltpu.VMEM((2, rim_rows + 2 * RIM, 128), F32), pltpu.VMEM((rim_rows, units), F32),
+         pltpu.VMEM((rim_rows, units), F32), pltpu.VMEM((rim_rows, units), BF),
+         pltpu.VMEM((rim_rows, units), F32), dma((2,)), dma((2, 8))],
+        "conv_back", 2, info_conv, low_gs, gs, high_gs, np_, mean, scale, nm, wp, two, one,
     )
     dw2, dnar2 = send(dw, flip), send(dnar, flip)
-    g2, early = lax.optimization_barrier((g2, early))
+    info_glu, early = lax.optimization_barrier((info, early))
     dx, dab, sums = call(
-        glu_back_kernel, [(tall, F32), ((rows, 2 * width), BF), ((24, units), F32)],
-        [SMEM] + [VMEM] * 3 + [HBM] * 2 + [VMEM] * 7,
-        [ring, pltpu.VMEM((2, 8, 128, 256), BF), tiny, pltpu.VMEM(tall, F32),
-         pltpu.VMEM((rim_rows, 256), F32), dma((3,))],
-        "glu_back", 1, info, dw, dnar, h1m, two, one, g2, a, sg, x, table, d_gatt, d_gffn,
+        glu_back_kernel,
+        [(tall, F32), ((rows, 2 * width), BF, FREE), ((24, units), F32, FREE)],
+        [SMEM, FREE, FREE, HBM, HBM, HBM, VMEM, HBM, HBM, HBM, FREE, VMEM, VMEM],
+        [pltpu.VMEM((2, 2, 4, 448, 256), BF), pltpu.VMEM((2, 8, 128, 256), BF), tiny,
+         pltpu.VMEM((rim_rows, 256), F32), pltpu.VMEM(tall, F32), pltpu.VMEM(tall, BF),
+         pltpu.VMEM(tall, BF), pltpu.VMEM(tall, BF), dma((8,))],
+        "glu_back", 1, info_glu, dw, dnar, h1m, two, one, g2, a, sg, x, table, d_gatt, d_gffn,
     )
     dab2, sums2 = send(dab, flip), send(sums, flip)
-    dab2, middle = lax.optimization_barrier((dab2, middle))
+    info_late, middle = lax.optimization_barrier((info, middle))
     middle = over_z(middle)
     late = call(
-        late_kernel, [((8, 8, LATE, 128), BF)], [SMEM] + [VMEM] * 6 + [FREE] * 6,
-        [pltpu.VMEM((rim_rows, width), F32), pltpu.VMEM((rim_rows, 256), F32)], "late", 0.5,
-        info, n2, dw, dnar, n1, dab, sums, send(n2, flip), dw2, dnar2, send(n1, flip), dab2, sums2,
+        late_kernel, [((8, 8, LATE, 128), BF)], [SMEM, VMEM, FREE, FREE, VMEM, FREE, FREE] + [FREE] * 6,
+        [pltpu.VMEM((rim_rows, width), F32), pltpu.VMEM((rim_rows, 256), F32)], "late", 40,
+        info_late, n2, dw, dnar, n1, dab, sums, send(n2, flip), dw2, dnar2, send(n1, flip), dab2, sums2,
     )[0]
     _, early, middle = lax.optimization_barrier((late, early, middle))
     y = lax.axis_index("y")
     pieces = jnp.concatenate([early, middle], 1)
     pick = lambda index: lax.dynamic_index_in_dim(pieces, index % 4, 0, keepdims=False)
     parts = [send(pick(y + d), shift(dy=d)) for d in (1, 2, 3)]
-    early = sum((part.astype(F32) for part in parts), pick(y).astype(F32)).astype(BF)
+    early = call(
+        fold_kernel, [((EARLY + MIDDLE, 128), BF, FREE)], [FREE] * 4, [], "fold", FOLD, pick(y), *parts
+    )[0]
     late = lax.all_to_all(late.reshape(64, LATE, 128), CHIPS + WT, 0, 0, tiled=True)
     late = jnp.sum(late.astype(F32), 0).astype(BF)
     final = spread_out(jnp.concatenate([early, late], 0), CHIPS, 8)

time: 335 us -> 322 us (0.961)
  Pallas kernels: 113 us -> 95.9 us
  blocking collectives: 65.9 us -> 49.6 us
  waiting for transfers between devices: 73.2 us -> 86.3 us
  starting transfers between devices: 59.8 us -> 67.6 us
    pallas_call x12 -> x13, Pallas kernels: 79.1 us -> 61.8 us  [call(): pl.pallas_call(kernel, in_specs=[VMEM if spec is FREE else spec for spec...]
    all_to_all x1 -> x0, blocking collectives: 16.2 us -> none  [shards(): d_qkv = lax.all_to_all(d_qkv, CHIPS, 0, 0, tiled=True)]
    all_to_all x0 -> x1, waiting for transfers between devices: none -> 11.6 us  [shards(): d_qkv = lax.all_to_all(d_qkv, CHIPS, 0, 0, tiled=True)]
    reduce_scatter x2, waiting for transfers between devices: 32 us -> 25.6 us  [over_z(): return lax.psum_scatter(value, 'z', scatter_dimension=0, tiled=True)[0]]
    ppermute x40, waiting for transfers between devices: 38.3 us -> 43 us  [send(): return lax.ppermute(value, AXES, pairs)]
    ppermute x40, starting transfers between devices: 43.6 us -> 47.8 us  [send(): return lax.ppermute(value, AXES, pairs)]
    all_to_all x0 -> x1, starting transfers between devices: none -> 3.55 us  [shards(): d_qkv = lax.all_to_all(d_qkv, CHIPS, 0, 0, tiled=True)]
  transfers between devices with their start and end apart: 48 -> 49, of which waited for: 17 -> 20; matrix products, arithmetic and copies ran while one was open for 1% -> 1% of each run, Pallas kernels for 28% -> 26%
where the time goes in v4:
time: 322 us; the launch traced here: 321 us
  Pallas kernels  95.9 us (30%)
  waiting for transfers between devices  86.3 us (27%)
  starting transfers between devices  67.6 us (21%)
  blocking collectives  49.6 us (15%)
  between operations  15 us (5%)
  other arithmetic  3.35 us (1%)
  local copies, waits for them, and re-layouts  3.34 us (1%)
    pallas_call x13, Pallas kernels, call(): pl.pallas_call(kernel, in_specs=[VMEM if spec is FREE else spec for spec...  61.8 us
    ppermute x40, starting transfers between devices, send(): return lax.ppermute(value, AXES, pairs)  47.8 us
    ppermute x40, waiting for transfers between devices, send(): return lax.ppermute(value, AXES, pairs)  43 us
    reduce_scatter x2, waiting for transfers between devices, over_z(): return lax.psum_scatter(value, 'z', scatter_dimension=0, tiled=True)[0]  25.6 us
    all_to_all x1, blocking collectives, shards(): near = lax.all_to_all(qkv, CHIPS, 0, 0, tiled=True)  21.1 us
    pallas_call x1, Pallas kernels, attend_back(): pl.pallas_call(functools.partial(attend_back_kernel, chips, rows), grid=(...  20.1 us
    all_to_all x1, blocking collectives, spread_out(): return lax.all_to_all(copies, axes, 0, 0, tiled=True)  16.4 us
    pallas_call x1, Pallas kernels, attend(): pl.pallas_call(functools.partial(attend_kernel, chips, rows), grid=(chips...  14 us
  transfers between devices with their start and end apart: 49, of which 20 were waited for; matrix products, arithmetic and copies ran while one was open for 1% of the time, Pallas kernels for 26%

profile of v4, /device:TPU:1, one launch (start us, length us, event | category | flops | bytes accessed | tf_op | source)
XLA Modules:
  0.0 321.0 jit_solution(9511772075305303351)
XLA Ops:
  7.9 1.6 pack_ring.1.refs_0_
  9.5 4.7 %collective-permute-start = (bf16[512,256]{1,0:T(8,128)(2,1)S(1)}, bf16[512,256]{1,0:T(8,128)(2,1)S(1)}, u32[]{:S(2)}, u32[]{:S(2)}) collective-permute-start(bf16[512,256]{1,0:T(8,128)(2,1)S(1)} %pack_ring.1.refs_0_), channel_id=1, source_target_pairs={{0,3},{1,0},{2,1},{3,2},{4,7},{5,4},{6,5},{7,6},{8,11},{9,8},{10,9... | collective-permute-start | bytes 786440 | tf_op jit(solution)/shard_map/ppermute | solution.py:54
  16.7 3.1 pack_rest.1
  19.8 4.9 %collective-permute-done.refs_1_ = bf16[512,256]{1,0:T(8,128)(2,1)S(1)} collective-permute-done((bf16[512,256]{1,0:T(8,128)(2,1)S(1)}, bf16[512,256]{1,0:T(8,128)(2,1)S(1)}, u32[]{:S(2)}, u32[]{:S(2)}) %collective-permute-start) | collective-permute-done | bytes 262176 | tf_op jit(solution)/shard_map/ppermute | solution.py:54
  24.7 4.3 %collective-permute-done.2.refs_3_ = bf16[512,256]{1,0:T(8,128)(2,1)S(1)} collective-permute-done((bf16[512,256]{1,0:T(8,128)(2,1)S(1)}, bf16[512,256]{1,0:T(8,128)(2,1)S(1)}, u32[]{:S(2)}, u32[]{:S(2)}) %collective-permute-start.2) | collective-permute-done | bytes 262176 | tf_op jit(solution)/shard_map/ppermute | solution.py:54
  28.9 3.6 %all-to-all-start = ((bf16[8,352,256]{2,1,0:T(8,128)(2,1)}), bf16[8,352,256]{2,1,0:T(8,128)(2,1)S(1)}, u32[]{:S(2)}, u32[]{:S(2)}) async-start(bf16[8,352,256]{2,1,0:T(8,128)(2,1)} %get-tuple-element.105), calls=%async_computation | async-start | bytes 2883584 | tf_op jit(solution)/shard_map/all_to_all | solution.py:994
  33.9 2.4 collective-permute-start.7
  37.5 6.8 %collective-permute-start.5 = (bf16[8,512]{1,0:T(8,128)(2,1)S(1)}, bf16[8,512]{1,0:T(8,128)(2,1)S(1)}, u32[]{:S(2)}, u32[]{:S(2)}) collective-permute-start(bf16[8,512]{1,0:T(8,128)(2,1)S(1)} %get-tuple-element.194), channel_id=1, source_target_pairs={{0,8},{1,9},{2,10},{3,11},{4,12},{5,13},{6,14},{7,15},{8,16},{9,17... | collective-permute-start | bytes 24584 | tf_op jit(solution)/shard_map/ppermute | solution.py:54
  44.2 10.0 %collective-permute-done.5.low_ref = bf16[8,512]{1,0:T(8,128)(2,1)S(1)} collective-permute-done((bf16[8,512]{1,0:T(8,128)(2,1)S(1)}, bf16[8,512]{1,0:T(8,128)(2,1)S(1)}, u32[]{:S(2)}, u32[]{:S(2)}) %collective-permute-start.5) | collective-permute-done | bytes 8224 | tf_op jit(solution)/shard_map/ppermute | solution.py:54
  54.2 1.9 collective-permute-start.6
  56.1 5.3 %collective-permute-done.6.high_ref = bf16[8,512]{1,0:T(8,128)(2,1)S(1)} collective-permute-done((bf16[8,512]{1,0:T(8,128)(2,1)S(1)}, bf16[8,512]{1,0:T(8,128)(2,1)S(1)}, u32[]{:S(2)}, u32[]{:S(2)}) %collective-permute-start.6) | collective-permute-done | bytes 8224 | tf_op jit(solution)/shard_map/ppermute | solution.py:54
  64.8 1.8 pad_maximum_fusion.1
  68.4 3.1 glu.1
  71.5 10.3 %conv.1 = (bf16[272,512]{1,0:T(8,128)(2,1)}, f32[272,2048]{1,0:T(8,128)}, f32[272,256]{1,0:T(8,128)}, bf16[272,2048]{1,0:T(8,128)(2,1)}, f32[272,128]{1,0:T(8,12...) custom-call(s32[6]{0:T(128)S(1)} %stack.32.info_ref, ...), custom_call_target="tpu_custom_call" | custom-call | flops 15000000512 | bytes 45000000 | tf_op jit(solution)/shard_map/conv/pallas_call | solution.py:275
  81.8 21.1 %all_to_all.35.near_ref = bf16[8,192,256]{2,1,0:T(8,128)(2,1)S(1)} all-to-all(bf16[8,192,256]{2,1,0:T(8,128)(2,1)S(1)} %get-tuple-element.118), channel_id=1, replica_groups=mesh['y'=4,'xh'=2,'core'=2,'xl'=2,'z'=4] {'y','xh'}, dimensions={0} | all-to-all | bytes 1572864 | tf_op jit(solution)/shard_map/all_to_all | solution.py:1028
  102.9 1.5 collective-permute-start.19
  104.5 1.5 collective-permute-done.19.far_ref
  106.0 14.0 %attend.1 = (bf16[8,64,256]{2,1,0:T(8,128)(2,1)}, bf16[2048,4096]{1,0:T(8,128)(2,1)}, f32[8,8,256]{2,1,0:T(8,128)}, bf16[8,192,256]{2,1,0:T(8,128)(2,1)}, bf16[8,128,256]{2,1,0:T(8,128)(2,1)}) custom-call(s32[1]{0:T(128)S(6)} %copy.40.length_ref, s32[1]{0:T(128)} %bitcast.core_ref, bf16[8,192,256]{2,1,0:T(8,128)(2,1)S(1)} %all_to_all.35.near_ref, ...), custom_call_target="tpu_custom_call" | custom-call | flops 14000000000 | bytes 42000000 | tf_op jit(solution)/shard_map/attend/pallas_call | solution.py:135
  120.5 12.1 %all_to_all.36.o_ref = bf16[8,64,256]{2,1,0:T(8,128)(2,1)S(1)} all-to-all(bf16[8,64,256]{2,1,0:T(8,128)(2,1)} %get-tuple-element.119.o_ref), channel_id=1, replica_groups=mesh['y'=4,'xh'=2,'core'=2,'xl'=2,'z'=4] {'y','xh'}, dimensions={0} | all-to-all | bytes 524288 | tf_op jit(solution)/shard_map/all_to_all | solution.py:1033
  132.6 8.0 %ffn.1 = (bf16[256,512]{1,0:T(8,128)(2,1)}, bf16[256,5632]{1,0:T(8,128)(2,1)S(1)}, f32[256,512]{1,0:T(8,128)}, bf16[8,64,256]{2,1,0:T(8,128)(2,1)}, f32[1,512]{1,0:T(1,128)}, /*index=5*/bf16[8,64,256]{2,1,0:T(8,128)(2,1)S(1)}) custom-call(s32[6]{0:T(128)S(1)} %stack.32.info_ref, f32[256,512]{1,0:T(8,128)} %get-tuple-element.117.h2_ref.h2_in, ...), custom_call_target="tpu_custom_call" | custom-call | flops 11000000512 | bytes 33000000 | tf_op jit(solution)/shard_map/ffn/pallas_call | solution.py:275
  141.7 3.4 %all-to-all-start.3 = ((bf16[8,64,256]{2,1,0:T(8,128)(2,1)}), bf16[8,64,256]{2,1,0:T(8,128)(2,1)S(1)}, u32[]{:S(2)}, u32[]{:S(2)}) async-start(bf16[8,64,256]{2,1,0:T(8,128)(2,1)} %get-tuple-element.125), calls=%async_computation.3 | async-start | bytes 524288 | tf_op jit(solution)/shard_map/all_to_all | solution.py:1044
  145.2 1.9 collective-permute-done.22.heads2_ref
  147.0 4.8 %early.1 = bf16[2,2,4,4,144,128]{5,4,3,2,1,0:T(8,128)(2,1)} custom-call(s32[6]{0:T(128)S(1)} %stack.32.info_ref, bf16[256,5632]{1,0:T(8,128)(2,1)S(1)} %get-tuple-element.126.acts_ref, bf16[8,64,256]{2,1,0:T(8,128)(2,1)S(1)} %get-tuple-element.127.heads_ref, bf16[256,5632]{1,0:T(8,128)(2,1)} %collective-permute-done.21.acts2_ref, ...), custom_call_target="tpu_custom_call" | custom-call | flops 300000000 | bytes 900000 | tf_op jit(solution)/shard_map/early/pallas_call | solution.py:275
  151.8 1.7 all-to-all-done.3.do_ref
  153.5 20.1 %attend_back.1 = (bf16[8,64,256]{2,1,0:T(8,128)(2,1)}, bf16[2,8,64,256]{3,2,1,0:T(8,128)(2,1)S(1)}, bf16[2,8,64,256]{3,2,1,0:T(8,128)(2,1)S(1)}) custom-call(bf16[8,192,256]{2,1,0:T(8,128)(2,1)} %get-tuple-element.130.near_ref, bf16[8,128,256]{2,1,0:T(8,128)(2,1)} %get-tuple-element.131.far_ref, bf16[2048,4096]{1,0:T(8,128)(2,1)} %get-tuple-element.132.e_ref, ...), custom_call_target="tpu_custom_call" | custom-call | flops 3000000000 | bytes 9000000 | tf_op jit(solution)/shard_map/attend_back/pallas_call | solution.py:228
  175.1 1.5 collective-permute-done.23
  177.8 3.5 %all-to-all-start.4 = ((bf16[8,192,256]{2,1,0:T(8,128)(2,1)}), bf16[8,192,256]{2,1,0:T(8,128)(2,1)S(1)}, u32[]{:S(2)}, u32[]{:S(2)}) async-start(bf16[8,192,256]{2,1,0:T(8,128)(2,1)} %pad_maximum_fusion), calls=%async_computation.6 | async-start | bytes 1572864 | tf_op jit(solution)/shard_map/all_to_all | solution.py:1055
  181.4 1.7 reduce-scatter.5.cloned.1.call-done
  183.9 11.6 %all-to-all-done.4.d_ref = bf16[8,192,256]{2,1,0:T(8,128)(2,1)S(1)} async-done(((bf16[8,192,256]{2,1,0:T(8,128)(2,1)}), bf16[8,192,256]{2,1,0:T(8,128)(2,1)S(1)}, u32[]{:S(2)}, u32[]{:S(2)}) %all-to-all-start.4) | async-done | bytes 786464 | tf_op jit(solution)/shard_map/all_to_all | solution.py:1055
  196.7 3.8 %attn_in.1 = (f32[256,512]{1,0:T(8,128)}, bf16[256,256]{1,0:T(8,128)(2,1)S(1)}, bf16[8,256]{1,0:T(8,128)(2,1)}, bf16[8,256]{1,0:T(8,128)(2,1)}, f32[1,512]{1,0:T(1,128)}) custom-call(s32[6]{0:T(128)S(1)} %stack.32.info_ref, bf16[8,192,256]{2,1,0:T(8,128)(2,1)S(1)} %all-to-all-done.4.d_ref, f32[256,512]{1,0:T(8,128)} %get-tuple-element.117.h2_ref.h2_in, ...), custom_call_target="tpu_custom_call" | custom-call | flops 500000000 | bytes 1500000 | tf_op jit(solution)/shard_map/attn_in/pallas_call | solution.py:275
  201.1 2.4 collective-permute-start.24
  204.4 2.0 collective-permute-start.25
  206.4 5.2 %collective-permute-done.25.hi_ref = bf16[8,256]{1,0:T(8,128)(2,1)S(1)} collective-permute-done((bf16[8,256]{1,0:T(8,128)(2,1)}, bf16[8,256]{1,0:T(8,128)(2,1)S(1)}, u32[]{:S(2)}, u32[]{:S(2)}) %collective-permute-start.25) | collective-permute-done | bytes 4128 | tf_op jit(solution)/shard_map/ppermute | solution.py:54
  211.6 3.4 %middle.1 = bf16[2,2,4,4,80,128]{5,4,3,2,1,0:T(8,128)(2,1)} custom-call(s32[6]{0:T(128)S(1)} %stack.32.info_ref, bf16[256,2048]{1,0:T(8,128)(2,1)} %get-tuple-element.142.sp_ref, bf16[256,256]{1,0:T(8,128)(2,1)S(1)} %get-tuple-element.143.gs_ref, bf16[256,512]{1,0:T(8,128)(2,1)} %get-tuple-element.144.n3_ref, bf16[8,192,256]{2,1,0:T(8,128)(2,1)S(1)} %all-to-all-done.4.d_ref, ...), custom_call_target="tpu_custom_call" | custom-call | flops 300000000 | bytes 900000 | tf_op jit(solution)/shard_map/middle/pallas_call | solution.py:275
  215.3 11.2 %conv_back.1 = (bf16[256,2048]{1,0:T(8,128)(2,1)S(1)}, bf16[272,256]{1,0:T(8,128)(2,1)S(1)}, f32[16,2048]{1,0:T(8,128)S(1)}) custom-call(s32[6]{0:T(128)S(1)} %stack.32.info_ref, bf16[8,256]{1,0:T(8,128)(2,1)S(1)} %collective-permute-done.24.lo_ref, bf16[256,256]{1,0:T(8,128)(2,1)S(1)} %get-tuple-element.143.gs_ref, ...), custom_call_target="tpu_custom_call" | custom-call | flops 2000000000 | bytes 6000000 | tf_op jit(solution)/shard_map/conv_back/pallas_call | solution.py:275
  226.6 5.5 %glu_back.1 = (f32[256,512]{1,0:T(8,128)}, bf16[256,1024]{1,0:T(8,128)(2,1)S(1)}, f32[24,2048]{1,0:T(8,128)S(1)}) custom-call(s32[6]{0:T(128)S(1)} %stack.32.info_ref, bf16[256,2048]{1,0:T(8,128)(2,1)S(1)} %get-tuple-element.152.dw_ref, bf16[272,256]{1,0:T(8,128)(2,1)S(1)} %get-tuple-element.153.dnar_ref, f32[256,512]{1,0:T(8,128)} %get-tuple-element.154.h1_in, ...), custom_call_target="tpu_custom_call" | custom-call | flops 1000000000 | bytes 3000000 | tf_op jit(solution)/shard_map/glu_back/pallas_call | solution.py:275
  233.3 2.0 collective-permute-done.33.n12_ref
  235.6 2.6 reduce-scatter.9.cloned.1.call-done
  238.3 4.1 %late.1 = bf16[8,8,128,128]{3,2,1,0:T(8,128)(2,1)} custom-call(s32[6]{0:T(128)S(1)} %stack.32.info_ref, bf16[272,512]{1,0:T(8,128)(2,1)} %get-tuple-element.164.n2_ref, bf16[256,2048]{1,0:T(8,128)(2,1)S(1)} %get-tuple-element.152.dw_ref, bf16[272,256]{1,0:T(8,128)(2,1)S(1)} %get-tuple-element.153.dnar_ref, bf16[256,512]{1,0:T(8,128)(2,1)} %get-tuple-element.165.n1_ref, ...), custom_call_target="tpu_custom_call" | custom-call | flops 40000000000 | bytes 120000000 | tf_op jit(solution)/shard_map/late/pallas_call | solution.py:275
  242.4 8.8 %all-to-all-start.5 = ((bf16[64,128,128]{2,1,0:T(8,128)(2,1)}), bf16[64,128,128]{2,1,0:T(8,128)(2,1)S(1)}, u32[]{:S(2)}, u32[]{:S(2)}) async-start(bf16[64,128,128]{2,1,0:T(8,128)(2,1)} %bitcast.54), calls=%async_computation.9 | async-start | bytes 4194304 | tf_op jit(solution)/shard_map/all_to_all | solution.py:1111
  251.3 25.6 %reduce-scatter.11.cloned.1.call-done = bf16[1,4,80,128]{3,2,1,0:T(8,128)(2,1)} async-done(((bf16[4,4,80,128]{3,2,1,0:T(8,128)(2,1)}), bf16[1,4,80,128]{3,2,1,0:T(8,128)(2,1)}) %reduce-scatter.11.cloned.1.call-update) | async-done | bytes 81936 | tf_op jit(solution)/shard_map/reduce_scatter | solution.py:950
  277.8 4.5 %collective-permute-start.36 = (bf16[224,128]{1,0:T(8,128)(2,1)S(1)}, bf16[224,128]{1,0:T(8,128)(2,1)S(1)}, u32[]{:S(2)}, u32[]{:S(2)}) collective-permute-start(bf16[224,128]{1,0:T(8,128)(2,1)S(1)} %get-tuple-element.197), channel_id=1, source_target_pairs={{0,32},{1,33},{2,34},{3,35},{4,36},{5,37},{6,38},{7,39},{8,40},{9,... | collective-permute-start | bytes 172040 | tf_op jit(solution)/shard_map/ppermute | solution.py:54
  282.3 2.8 collective-permute-start.37
  285.5 1.9 collective-permute-done.37.refs_2_
  288.9 16.4 %all_to_all.37.near_ref = bf16[8,352,128]{2,1,0:T(8,128)(2,1)S(1)} all-to-all(bf16[8,352,128]{2,1,0:T(8,128)(2,1)S(1)} %broadcast_in_dim.14), channel_id=1, replica_groups=mesh['y'=4,'xh'=2,'core'=2,'xl'=2,'z'=4] {'y','xh'}, dimensions={0} | all-to-all | bytes 1441792 | tf_op jit(solution)/shard_map/all_to_all | solution.py:955
  305.3 4.3 %collective-permute-start.39 = (bf16[8,352,128]{2,1,0:T(8,128)(2,1)S(1)}, bf16[8,352,128]{2,1,0:T(8,128)(2,1)S(1)}, u32[]{:S(2)}, u32[]{:S(2)}) collective-permute-start(bf16[8,352,128]{2,1,0:T(8,128)(2,1)S(1)} %all_to_all.37.near_ref), channel_id=1, source_target_pairs={{0,8},{1,9},{2,10},{3,11},{4,12},{5,13},{6,14},{7,15},{8,0},{9,1},... | collective-permute-start | bytes 2162696 | tf_op jit(solution)/shard_map/ppermute | solution.py:54
  309.7 1.8 collective-permute-done.39.far_ref
  311.5 2.9 unpack.1
  (112 shorter events, 22.8 us)
Async XLA Ops:
  9.5 15.1 %collective-permute-start = (bf16[512,256]{1,0:T(8,128)(2,1)S(1)}, bf16[512,256]{1,0:T(8,128)(2,1)S(1)}, u32[]{:S(2)}, u32[]{:S(2)}) collective-permute-start(bf16[512,256]{1,0:T(8,128)(2,1)S(1)} %pack_ring.1.refs_0_), channel_id=1, source_target_pairs={{0,3},{1,0},{2,1},{3,2},{4,7},{5,4},{6,5},{7,6},{8,11},{9,8},{10,9... | collective-permute-start | bytes 786440 | tf_op jit(solution)/shard_map/ppermute | solution.py:54
  14.2 10.5 %collective-permute-start.1 = (bf16[512,256]{1,0:T(8,128)(2,1)S(1)}, bf16[512,256]{1,0:T(8,128)(2,1)S(1)}, u32[]{:S(2)}, u32[]{:S(2)}) collective-permute-start(bf16[512,256]{1,0:T(8,128)(2,1)S(1)} %pack_ring.1.refs_0_), channel_id=1, source_target_pairs={{0,2},{1,3},{2,0},{3,1},{4,6},{5,7},{6,4},{7,5},{8,10},{9,11},{10,... | collective-permute-start | bytes 786440 | tf_op jit(solution)/shard_map/ppermute | solution.py:54
  14.2 14.7 %collective-permute-start.2 = (bf16[512,256]{1,0:T(8,128)(2,1)S(1)}, bf16[512,256]{1,0:T(8,128)(2,1)S(1)}, u32[]{:S(2)}, u32[]{:S(2)}) collective-permute-start(bf16[512,256]{1,0:T(8,128)(2,1)S(1)} %pack_ring.1.refs_0_), channel_id=1, source_target_pairs={{0,1},{1,2},{2,3},{3,0},{4,5},{5,6},{6,7},{7,4},{8,9},{9,10},{10,1... | collective-permute-start | bytes 786440 | tf_op jit(solution)/shard_map/ppermute | solution.py:54
  14.9 14.0 %collective-permute-start.3 = (bf16[512,256]{1,0:T(8,128)(2,1)S(1)}, bf16[512,256]{1,0:T(8,128)(2,1)S(1)}, u32[]{:S(2)}, u32[]{:S(2)}) collective-permute-start(bf16[512,256]{1,0:T(8,128)(2,1)S(1)} %pack_ring.1.refs_0_), channel_id=1, source_target_pairs={{0,4},{1,5},{2,6},{3,7},{4,0},{5,1},{6,2},{7,3},{8,12},{9,13},{10,... | collective-permute-start | bytes 786440 | tf_op jit(solution)/shard_map/ppermute | solution.py:54
  28.9 34.0 %all-to-all-start = ((bf16[8,352,256]{2,1,0:T(8,128)(2,1)}), bf16[8,352,256]{2,1,0:T(8,128)(2,1)S(1)}, u32[]{:S(2)}, u32[]{:S(2)}) async-start(bf16[8,352,256]{2,1,0:T(8,128)(2,1)} %get-tuple-element.105), calls=%async_computation | async-start | bytes 2883584 | tf_op jit(solution)/shard_map/all_to_all | solution.py:994
  32.5 87.5 %all-gather.3.cloned.1.call-start = ((), (), s32[]{:S(2)}) async-start(), calls=%async_computation.15 | async-start | bytes 2949120 | tf_op jit(solution)/shard_map/all_gather | solution.py:1005
  32.6 28.8 %collective-permute-start.4 = (bf16[576,256]{1,0:T(8,128)(2,1)S(1)}, bf16[576,256]{1,0:T(8,128)(2,1)S(1)}, u32[]{:S(2)}, u32[]{:S(2)}) collective-permute-start(bf16[576,256]{1,0:T(8,128)(2,1)S(1)} %get-tuple-element.121), channel_id=1, source_target_pairs={{0,4},{1,5},{2,6},{3,7},{4,0},{5,1},{6,2},{7,3},{8,12},{9,13},{10,... | collective-permute-start | bytes 884744 | tf_op jit(solution)/shard_map/ppermute | solution.py:54
  33.9 27.5 %collective-permute-start.7 = (bf16[512,256]{1,0:T(8,128)(2,1)S(1)}, bf16[512,256]{1,0:T(8,128)(2,1)S(1)}, u32[]{:S(2)}, u32[]{:S(2)}) collective-permute-start(bf16[512,256]{1,0:T(8,128)(2,1)S(1)} %collective-permute-done.3.refs_4_), channel_id=1, source_target_pairs={{0,3},{1,0},{2,1},{3,2},{4,7},{5,4},{6,5},{7,6},{8,11},{9,8},{10,9... | collective-permute-start | bytes 786440 | tf_op jit(solution)/shard_map/ppermute | solution.py:54
  36.3 25.1 %collective-permute-start.8 = (bf16[512,256]{1,0:T(8,128)(2,1)S(1)}, bf16[512,256]{1,0:T(8,128)(2,1)S(1)}, u32[]{:S(2)}, u32[]{:S(2)}) collective-permute-start(bf16[512,256]{1,0:T(8,128)(2,1)S(1)} %collective-permute-done.3.refs_4_), channel_id=1, source_target_pairs={{0,2},{1,3},{2,0},{3,1},{4,6},{5,7},{6,4},{7,5},{8,10},{9,11},{10,... | collective-permute-start | bytes 786440 | tf_op jit(solution)/shard_map/ppermute | solution.py:54
  36.9 26.0 %collective-permute-start.9 = (bf16[512,256]{1,0:T(8,128)(2,1)S(1)}, bf16[512,256]{1,0:T(8,128)(2,1)}, u32[]{:S(2)}, u32[]{:S(2)}) collective-permute-start(bf16[512,256]{1,0:T(8,128)(2,1)S(1)} %collective-permute-done.3.refs_4_), channel_id=1, source_target_pairs={{0,1},{1,2},{2,3},{3,0},{4,5},{5,6},{6,7},{7,4},{8,9},{9,10},{10,1... | collective-permute-start | bytes 786440 | tf_op jit(solution)/shard_map/ppermute | solution.py:54
  37.5 16.7 %collective-permute-start.5 = (bf16[8,512]{1,0:T(8,128)(2,1)S(1)}, bf16[8,512]{1,0:T(8,128)(2,1)S(1)}, u32[]{:S(2)}, u32[]{:S(2)}) collective-permute-start(bf16[8,512]{1,0:T(8,128)(2,1)S(1)} %get-tuple-element.194), channel_id=1, source_target_pairs={{0,8},{1,9},{2,10},{3,11},{4,12},{5,13},{6,14},{7,15},{8,16},{9,17... | collective-permute-start | bytes 24584 | tf_op jit(solution)/shard_map/ppermute | solution.py:54
  54.2 7.2 %collective-permute-start.6 = (bf16[8,512]{1,0:T(8,128)(2,1)S(1)}, bf16[8,512]{1,0:T(8,128)(2,1)S(1)}, u32[]{:S(2)}, u32[]{:S(2)}) collective-permute-start(bf16[8,512]{1,0:T(8,128)(2,1)S(1)} %get-tuple-element.193), channel_id=1, source_target_pairs={{8,0},{9,1},{10,2},{11,3},{12,4},{13,5},{14,6},{15,7},{16,8},{17,9... | collective-permute-start | bytes 24584 | tf_op jit(solution)/shard_map/ppermute | solution.py:54
  62.9 5.3 %collective-permute-start.10 = (bf16[8,352,256]{2,1,0:T(8,128)(2,1)S(1)}, bf16[8,352,256]{2,1,0:T(8,128)(2,1)}, u32[]{:S(2)}, u32[]{:S(2)}) collective-permute-start(bf16[8,352,256]{2,1,0:T(8,128)(2,1)S(1)} %all-to-all-done.near_ref.refs_16_), channel_id=1, source_target_pairs={{0,8},{1,9},{2,10},{3,11},{4,12},{5,13},{6,14},{7,15},{8,0},{9,1},... | collective-permute-start | bytes 4325384 | tf_op jit(solution)/shard_map/ppermute | solution.py:54
  63.7 3.4 %collective-permute-start.11 = (bf16[512,256]{1,0:T(8,128)(2,1)S(1)}, bf16[512,256]{1,0:T(8,128)(2,1)}, u32[]{:S(2)}, u32[]{:S(2)}) collective-permute-start(bf16[512,256]{1,0:T(8,128)(2,1)S(1)} %pack_ring.1.refs_0_), channel_id=1, source_target_pairs={{0,8},{1,9},{2,10},{3,11},{4,12},{5,13},{6,14},{7,15},{8,0},{9,1},... | collective-permute-start | bytes 786440 | tf_op jit(solution)/shard_map/ppermute | solution.py:54
  63.7 3.7 %collective-permute-start.15 = (bf16[512,256]{1,0:T(8,128)(2,1)S(1)}, bf16[512,256]{1,0:T(8,128)(2,1)}, u32[]{:S(2)}, u32[]{:S(2)}) collective-permute-start(bf16[512,256]{1,0:T(8,128)(2,1)S(1)} %collective-permute-done.3.refs_4_), channel_id=1, source_target_pairs={{0,8},{1,9},{2,10},{3,11},{4,12},{5,13},{6,14},{7,15},{8,0},{9,1},... | collective-permute-start | bytes 786440 | tf_op jit(solution)/shard_map/ppermute | solution.py:54
  64.2 3.6 %collective-permute-start.12 = (bf16[512,256]{1,0:T(8,128)(2,1)S(1)}, bf16[512,256]{1,0:T(8,128)(2,1)}, u32[]{:S(2)}, u32[]{:S(2)}) collective-permute-start(bf16[512,256]{1,0:T(8,128)(2,1)S(1)} %collective-permute-done.refs_1_), channel_id=1, source_target_pairs={{0,8},{1,9},{2,10},{3,11},{4,12},{5,13},{6,14},{7,15},{8,0},{9,1},... | collective-permute-start | bytes 786440 | tf_op jit(solution)/shard_map/ppermute | solution.py:54
  64.2 7.2 %collective-permute-start.13 = (bf16[512,256]{1,0:T(8,128)(2,1)S(1)}, bf16[512,256]{1,0:T(8,128)(2,1)}, u32[]{:S(2)}, u32[]{:S(2)}) collective-permute-start(bf16[512,256]{1,0:T(8,128)(2,1)S(1)} %collective-permute-done.1.refs_2_), channel_id=1, source_target_pairs={{0,8},{1,9},{2,10},{3,11},{4,12},{5,13},{6,14},{7,15},{8,0},{9,1},... | collective-permute-start | bytes 786440 | tf_op jit(solution)/shard_map/ppermute | solution.py:54
  67.1 4.4 %collective-permute-start.14 = (bf16[512,256]{1,0:T(8,128)(2,1)S(1)}, bf16[512,256]{1,0:T(8,128)(2,1)S(1)}, u32[]{:S(2)}, u32[]{:S(2)}) collective-permute-start(bf16[512,256]{1,0:T(8,128)(2,1)S(1)} %collective-permute-done.2.refs_3_), channel_id=1, source_target_pairs={{0,8},{1,9},{2,10},{3,11},{4,12},{5,13},{6,14},{7,15},{8,0},{9,1},... | collective-permute-start | bytes 786440 | tf_op jit(solution)/shard_map/ppermute | solution.py:54
  67.5 4.0 %collective-permute-start.16 = (bf16[512,256]{1,0:T(8,128)(2,1)}, bf16[512,256]{1,0:T(8,128)(2,1)S(1)}, u32[]{:S(2)}, u32[]{:S(2)}) collective-permute-start(bf16[512,256]{1,0:T(8,128)(2,1)} %copy-done.1), channel_id=1, source_target_pairs={{0,8},{1,9},{2,10},{3,11},{4,12},{5,13},{6,14},{7,15},{8,0},{9,1},... | collective-permute-start | bytes 786440 | tf_op jit(solution)/shard_map/ppermute | solution.py:54
  67.8 3.6 %collective-permute-start.17 = (bf16[512,256]{1,0:T(8,128)(2,1)}, bf16[512,256]{1,0:T(8,128)(2,1)S(1)}, u32[]{:S(2)}, u32[]{:S(2)}) collective-permute-start(bf16[512,256]{1,0:T(8,128)(2,1)} %copy-done.3), channel_id=1, source_target_pairs={{0,8},{1,9},{2,10},{3,11},{4,12},{5,13},{6,14},{7,15},{8,0},{9,1},... | collective-permute-start | bytes 786440 | tf_op jit(solution)/shard_map/ppermute | solution.py:54
  68.2 3.3 %collective-permute-start.18 = (bf16[512,256]{1,0:T(8,128)(2,1)}, bf16[512,256]{1,0:T(8,128)(2,1)S(1)}, u32[]{:S(2)}, u32[]{:S(2)}) collective-permute-start(bf16[512,256]{1,0:T(8,128)(2,1)} %collective-permute-done.9.refs_7_), channel_id=1, source_target_pairs={{0,8},{1,9},{2,10},{3,11},{4,12},{5,13},{6,14},{7,15},{8,0},{9,1},... | collective-permute-start | bytes 786440 | tf_op jit(solution)/shard_map/ppermute | solution.py:54
  102.9 3.1 collective-permute-start.19
  120.1 12.5 %collective-permute-start.20 = (bf16[4,2,576,256]{3,2,1,0:T(8,128)(2,1)}, bf16[4,2,576,256]{3,2,1,0:T(8,128)(2,1)S(1)}, u32[]{:S(2)}, u32[]{:S(2)}) collective-permute-start(bf16[4,2,576,256]{3,2,1,0:T(8,128)(2,1)} %bitcast.60), channel_id=1, source_target_pairs={{0,8},{1,9},{2,10},{3,11},{4,12},{5,13},{6,14},{7,15},{8,0},{9,1},... | collective-permute-start | bytes 7077896 | tf_op jit(solution)/shard_map/ppermute | solution.py:54
  140.6 6.4 %collective-permute-start.21 = (bf16[256,5632]{1,0:T(8,128)(2,1)S(1)}, bf16[256,5632]{1,0:T(8,128)(2,1)}, u32[]{:S(2)}, u32[]{:S(2)}) collective-permute-start(bf16[256,5632]{1,0:T(8,128)(2,1)S(1)} %get-tuple-element.126.acts_ref), channel_id=1, source_target_pairs={{0,8},{1,9},{2,10},{3,11},{4,12},{5,13},{6,14},{7,15},{8,0},{9,1},... | collective-permute-start | bytes 8650760 | tf_op jit(solution)/shard_map/ppermute | solution.py:54
  141.6 5.4 %collective-permute-start.22 = (bf16[8,64,256]{2,1,0:T(8,128)(2,1)S(1)}, bf16[8,64,256]{2,1,0:T(8,128)(2,1)}, u32[]{:S(2)}, u32[]{:S(2)}) collective-permute-start(bf16[8,64,256]{2,1,0:T(8,128)(2,1)S(1)} %get-tuple-element.127.heads_ref), channel_id=1, source_target_pairs={{0,8},{1,9},{2,10},{3,11},{4,12},{5,13},{6,14},{7,15},{8,0},{9,1},... | collective-permute-start | bytes 786440 | tf_op jit(solution)/shard_map/ppermute | solution.py:54
  141.7 11.8 %all-to-all-start.3 = ((bf16[8,64,256]{2,1,0:T(8,128)(2,1)}), bf16[8,64,256]{2,1,0:T(8,128)(2,1)S(1)}, u32[]{:S(2)}, u32[]{:S(2)}) async-start(bf16[8,64,256]{2,1,0:T(8,128)(2,1)} %get-tuple-element.125), calls=%async_computation.3 | async-start | bytes 524288 | tf_op jit(solution)/shard_map/all_to_all | solution.py:1044
  145.1 38.0 %reduce-scatter.5.cloned.1.call-start = ((), (), s32[]{:S(2)}) async-start(), calls=%async_computation.11 | async-start | bytes 2949120 | tf_op jit(solution)/shard_map/reduce_scatter | solution.py:946
  173.8 2.9 collective-permute-start.23
  177.8 17.6 %all-to-all-start.4 = ((bf16[8,192,256]{2,1,0:T(8,128)(2,1)}), bf16[8,192,256]{2,1,0:T(8,128)(2,1)S(1)}, u32[]{:S(2)}, u32[]{:S(2)}) async-start(bf16[8,192,256]{2,1,0:T(8,128)(2,1)} %pad_maximum_fusion), calls=%async_computation.6 | async-start | bytes 1572864 | tf_op jit(solution)/shard_map/all_to_all | solution.py:1055
  181.4 45.2 %reduce-scatter.7.cloned.1.call-start = ((), (), s32[]{:S(2)}) async-start(), calls=%async_computation.12 | async-start | bytes 737280 | tf_op jit(solution)/shard_map/reduce_scatter | solution.py:950
  183.1 55.1 %reduce-scatter.9.cloned.1.call-start = ((), (), s32[]{:S(2)}) async-start(), calls=%async_computation.13 | async-start | bytes 1638400 | tf_op jit(solution)/shard_map/reduce_scatter | solution.py:946
  183.2 28.4 %collective-permute-start.26 = (bf16[256,2048]{1,0:T(8,128)(2,1)S(1)}, bf16[256,2048]{1,0:T(8,128)(2,1)S(1)}, u32[]{:S(2)}, u32[]{:S(2)}) collective-permute-start(bf16[256,2048]{1,0:T(8,128)(2,1)S(1)} %copy-done.5), channel_id=1, source_target_pairs={{0,8},{1,9},{2,10},{3,11},{4,12},{5,13},{6,14},{7,15},{8,0},{9,1},... | collective-permute-start | bytes 3145736 | tf_op jit(solution)/shard_map/ppermute | solution.py:54
  195.5 16.1 %collective-permute-start.29 = (bf16[8,192,256]{2,1,0:T(8,128)(2,1)S(1)}, bf16[8,192,256]{2,1,0:T(8,128)(2,1)S(1)}, u32[]{:S(2)}, u32[]{:S(2)}) collective-permute-start(bf16[8,192,256]{2,1,0:T(8,128)(2,1)S(1)} %all-to-all-done.4.d_ref), channel_id=1, source_target_pairs={{0,8},{1,9},{2,10},{3,11},{4,12},{5,13},{6,14},{7,15},{8,0},{9,1},... | collective-permute-start | bytes 2359304 | tf_op jit(solution)/shard_map/ppermute | solution.py:54
  196.7 14.9 %collective-permute-start.28 = (bf16[256,512]{1,0:T(8,128)(2,1)S(1)}, bf16[256,512]{1,0:T(8,128)(2,1)S(1)}, u32[]{:S(2)}, u32[]{:S(2)}) collective-permute-start(bf16[256,512]{1,0:T(8,128)(2,1)S(1)} %copy-done.7), channel_id=1, source_target_pairs={{0,8},{1,9},{2,10},{3,11},{4,12},{5,13},{6,14},{7,15},{8,0},{9,1},... | collective-permute-start | bytes 786440 | tf_op jit(solution)/shard_map/ppermute | solution.py:54
  200.5 11.1 %collective-permute-start.27 = (bf16[256,256]{1,0:T(8,128)(2,1)S(1)}, bf16[256,256]{1,0:T(8,128)(2,1)S(1)}, u32[]{:S(2)}, u32[]{:S(2)}) collective-permute-start(bf16[256,256]{1,0:T(8,128)(2,1)S(1)} %get-tuple-element.143.gs_ref), channel_id=1, source_target_pairs={{0,8},{1,9},{2,10},{3,11},{4,12},{5,13},{6,14},{7,15},{8,0},{9,1},... | collective-permute-start | bytes 393224 | tf_op jit(solution)/shard_map/ppermute | solution.py:54
  201.1 3.3 %collective-permute-start.24 = (bf16[8,256]{1,0:T(8,128)(2,1)}, bf16[8,256]{1,0:T(8,128)(2,1)S(1)}, u32[]{:S(2)}, u32[]{:S(2)}) collective-permute-start(bf16[8,256]{1,0:T(8,128)(2,1)} %get-tuple-element.139), channel_id=1, source_target_pairs={{0,8},{1,9},{2,10},{3,11},{4,12},{5,13},{6,14},{7,15},{8,16},{9,17... | collective-permute-start | bytes 12296 | tf_op jit(solution)/shard_map/ppermute | solution.py:54
  204.4 7.2 %collective-permute-start.25 = (bf16[8,256]{1,0:T(8,128)(2,1)}, bf16[8,256]{1,0:T(8,128)(2,1)S(1)}, u32[]{:S(2)}, u32[]{:S(2)}) collective-permute-start(bf16[8,256]{1,0:T(8,128)(2,1)} %get-tuple-element.140), channel_id=1, source_target_pairs={{8,0},{9,1},{10,2},{11,3},{12,4},{13,5},{14,6},{15,7},{16,8},{17,9... | collective-permute-start | bytes 12296 | tf_op jit(solution)/shard_map/ppermute | solution.py:54
  215.1 61.8 %reduce-scatter.11.cloned.1.call-start = ((), (), s32[]{:S(2)}) async-start(), calls=%async_computation.14 | async-start | bytes 409600 | tf_op jit(solution)/shard_map/reduce_scatter | solution.py:950
  226.5 11.8 %collective-permute-start.31 = (bf16[256,2048]{1,0:T(8,128)(2,1)S(1)}, bf16[256,2048]{1,0:T(8,128)(2,1)S(1)}, u32[]{:S(2)}, u32[]{:S(2)}) collective-permute-start(bf16[256,2048]{1,0:T(8,128)(2,1)S(1)} %get-tuple-element.152.dw_ref), channel_id=1, source_target_pairs={{0,8},{1,9},{2,10},{3,11},{4,12},{5,13},{6,14},{7,15},{8,0},{9,1},... | collective-permute-start | bytes 3145736 | tf_op jit(solution)/shard_map/ppermute | solution.py:54
  232.2 6.1 %collective-permute-start.34 = (bf16[256,1024]{1,0:T(8,128)(2,1)S(1)}, bf16[256,1024]{1,0:T(8,128)(2,1)}, u32[]{:S(2)}, u32[]{:S(2)}) collective-permute-start(bf16[256,1024]{1,0:T(8,128)(2,1)S(1)} %get-tuple-element.166.dab_ref), channel_id=1, source_target_pairs={{0,8},{1,9},{2,10},{3,11},{4,12},{5,13},{6,14},{7,15},{8,0},{9,1},... | collective-permute-start | bytes 1572872 | tf_op jit(solution)/shard_map/ppermute | solution.py:54
  232.8 5.5 %collective-permute-start.30 = (bf16[272,512]{1,0:T(8,128)(2,1)}, bf16[272,512]{1,0:T(8,128)(2,1)S(1)}, u32[]{:S(2)}, u32[]{:S(2)}) collective-permute-start(bf16[272,512]{1,0:T(8,128)(2,1)} %get-tuple-element.164.n2_ref), channel_id=1, source_target_pairs={{0,8},{1,9},{2,10},{3,11},{4,12},{5,13},{6,14},{7,15},{8,0},{9,1},... | collective-permute-start | bytes 835592 | tf_op jit(solution)/shard_map/ppermute | solution.py:54
  233.2 5.1 %collective-permute-start.35 = (f32[24,2048]{1,0:T(8,128)S(1)}, f32[24,2048]{1,0:T(8,128)}, u32[]{:S(2)}, u32[]{:S(2)}) collective-permute-start(f32[24,2048]{1,0:T(8,128)S(1)} %get-tuple-element.167.small_ref), channel_id=1, source_target_pairs={{0,8},{1,9},{2,10},{3,11},{4,12},{5,13},{6,14},{7,15},{8,0},{9,1},... | collective-permute-start | bytes 589832 | tf_op jit(solution)/shard_map/ppermute | solution.py:54
  235.3 3.0 collective-permute-start.32
  242.4 46.1 %all-to-all-start.5 = ((bf16[64,128,128]{2,1,0:T(8,128)(2,1)}), bf16[64,128,128]{2,1,0:T(8,128)(2,1)S(1)}, u32[]{:S(2)}, u32[]{:S(2)}) async-start(bf16[64,128,128]{2,1,0:T(8,128)(2,1)} %bitcast.54), calls=%async_computation.9 | async-start | bytes 4194304 | tf_op jit(solution)/shard_map/all_to_all | solution.py:1111
  277.8 7.7 %collective-permute-start.36 = (bf16[224,128]{1,0:T(8,128)(2,1)S(1)}, bf16[224,128]{1,0:T(8,128)(2,1)S(1)}, u32[]{:S(2)}, u32[]{:S(2)}) collective-permute-start(bf16[224,128]{1,0:T(8,128)(2,1)S(1)} %get-tuple-element.197), channel_id=1, source_target_pairs={{0,32},{1,33},{2,34},{3,35},{4,36},{5,37},{6,38},{7,39},{8,40},{9,... | collective-permute-start | bytes 172040 | tf_op jit(solution)/shard_map/ppermute | solution.py:54
  282.3 5.1 %collective-permute-start.37 = (bf16[224,128]{1,0:T(8,128)(2,1)S(1)}, bf16[224,128]{1,0:T(8,128)(2,1)S(1)}, u32[]{:S(2)}, u32[]{:S(2)}) collective-permute-start(bf16[224,128]{1,0:T(8,128)(2,1)S(1)} %get-tuple-element.196), channel_id=1, source_target_pairs={{0,64},{1,65},{2,66},{3,67},{4,68},{5,69},{6,70},{7,71},{8,72},{9,... | collective-permute-start | bytes 172040 | tf_op jit(solution)/shard_map/ppermute | solution.py:54
  285.1 3.3 %collective-permute-start.38 = (bf16[224,128]{1,0:T(8,128)(2,1)S(1)}, bf16[224,128]{1,0:T(8,128)(2,1)S(1)}, u32[]{:S(2)}, u32[]{:S(2)}) collective-permute-start(bf16[224,128]{1,0:T(8,128)(2,1)S(1)} %get-tuple-element.195), channel_id=1, source_target_pairs={{0,96},{1,97},{2,98},{3,99},{4,100},{5,101},{6,102},{7,103},{8,104... | collective-permute-start | bytes 172040 | tf_op jit(solution)/shard_map/ppermute | solution.py:54
  305.3 6.2 %collective-permute-start.39 = (bf16[8,352,128]{2,1,0:T(8,128)(2,1)S(1)}, bf16[8,352,128]{2,1,0:T(8,128)(2,1)S(1)}, u32[]{:S(2)}, u32[]{:S(2)}) collective-permute-start(bf16[8,352,128]{2,1,0:T(8,128)(2,1)S(1)} %all_to_all.37.near_ref), channel_id=1, source_target_pairs={{0,8},{1,9},{2,10},{3,11},{4,12},{5,13},{6,14},{7,15},{8,0},{9,1},... | collective-permute-start | bytes 2162696 | tf_op jit(solution)/shard_map/ppermute | solution.py:54
  (13 other events, 107.6 us)
Sparse Core Ops, SparseCore 0:
  66.7 34.4 all-gather.2
  153.7 29.4 reduce-scatter.4
  185.5 20.2 reduce-scatter.6
  215.2 23.0 reduce-scatter.8
  240.5 36.3 reduce-scatter.10

commit v5 on v4

--- a/solution.py
+++ b/solution.py
@@ -167,7 +167,7 @@
 
 
 def attend_back_kernel(chips, rows, near_ref, far_ref, e_ref, o_ref, l_ref, do_ref,
-                       dq_ref, dk_ref, dv_ref, keys_ref, values_ref, dk_acc, dv_acc):
+                       keep_ref, give_ref, keys_ref, values_ref, dk_acc, dv_acc):
     step = pl.program_id(0)
     span = chips * rows
 
@@ -209,15 +209,16 @@
         dq = dq + matmul(d_scores, keys_ref[cols, :])
         dk_acc[:, cols] += matmul(query, d_scores)
         dv_acc[:, cols] += matmul(grad_low, expo)
-    dq_ref[0] = (dq.T[0:HEAD] * HEAD ** -0.5).astype(BF)
+    keep_ref[step, 0:HEAD, :] = (dq.T[0:HEAD] * HEAD ** -0.5).astype(BF)
 
     @pl.when(step == chips - 1)
     def _():
         for side in range(2):
             for chip in range(chips):
                 cols = slice(side * span + chip * rows, side * span + (chip + 1) * rows)
-                dk_ref[side, chip] = (dk_acc[:, cols] * HEAD ** -0.5).astype(BF)
-                dv_ref[side, chip] = dv_acc[:, cols].astype(BF)
+                out_ref, base = (keep_ref, HEAD) if side == 0 else (give_ref, 0)
+                out_ref[chip, base:base + HEAD, :] = (dk_acc[:, cols] * HEAD ** -0.5).astype(BF)
+                out_ref[chip, base + HEAD:base + 2 * HEAD, :] = dv_acc[:, cols].astype(BF)
 
 
 def attend_back(near, far, expo, out, inverse, d_out):
@@ -236,15 +237,10 @@
             pl.BlockSpec((1, 8, rows), one),
             pl.BlockSpec((1, HEAD, rows), one),
         ],
-        out_specs=[
-            pl.BlockSpec((1, HEAD, rows), one),
-            pl.BlockSpec((2, chips, HEAD, rows), lambda i: (0, 0, 0, 0)),
-            pl.BlockSpec((2, chips, HEAD, rows), lambda i: (0, 0, 0, 0)),
-        ],
+        out_specs=[pl.BlockSpec((chips, 3 * HEAD, rows), whole), pl.BlockSpec((chips, 2 * HEAD, rows), whole)],
         out_shape=[
-            pltpu.HBM((chips, HEAD, rows), BF),
-            jax.ShapeDtypeStruct((2, chips, HEAD, rows), BF),
-            jax.ShapeDtypeStruct((2, chips, HEAD, rows), BF),
+            jax.ShapeDtypeStruct((chips, 3 * HEAD, rows), BF),
+            jax.ShapeDtypeStruct((chips, 2 * HEAD, rows), BF),
         ],
         scratch_shapes=[
             pltpu.VMEM((tokens, 2 * HEAD), BF),
@@ -259,7 +255,7 @@
 
 
 RIM = 8
-FOLD = 15
+FOLD = 0.3
 ACT_N4 = slice(4096, 4608)
 ACT_GY = slice(4608, 5120)
 ACT_GA = slice(5120, 5632)
@@ -788,13 +784,13 @@
         cols = slice(256 * w, 256 * w + 256)
         res = matmul(gs, stack_rows(sp_ref[:, cols], sp2_ref[:, cols])).reshape(8, 16, 256)
         for i in range(2):
-            by_shard(out_ref, w, slice(16 * i, 16 * i + 16), res[:, :, 128 * i:128 * i + 128])
+            out_ref[:, w, 16 * i:16 * i + 16, :] = res[:, :, 128 * i:128 * i + 128].astype(BF)
     n3 = stack_rows(n3_ref[...], n32_ref[...]).T
     for part in range(3):
         d = [ref[pl.ds(side * 4, 4), 64 * part:64 * part + 64, :].reshape(256, rows) for ref in (d_ref, d2_ref)]
-        packed = pair_rows(contract(n3, jnp.concatenate(d, 1), 1, 1))
-        for c in range(8):
-            by_chip(out_ref, c, slice(32 + 16 * part, 48 + 16 * part), packed[:, c])
+        packed = pair_rows(contract(n3, jnp.concatenate(d, 1), 1, 1)).astype(BF)
+        for w in range(8):
+            out_ref[:, w, 32 + 16 * part:48 + 16 * part, :] = packed[w]
 
 
 def late_kernel(info_ref, n2_ref, dw_ref, dnar_ref, n1_ref, dab_ref, small_ref, n22_ref, dw2_ref,
@@ -1048,29 +1044,30 @@
     )[0]
     d_near, early = lax.optimization_barrier((d_near, early))
     early = over_x(early)
-    dq, dk, dv = attend_back(near, far, expo, head_out, inverse, d_near)
-    d_far = send(jnp.concatenate([dk[1], dv[1]], 1), flip).astype(F32)
-    d_own = jnp.concatenate([dk[0], dv[0]], 1).astype(F32)
-    d_qkv = jnp.concatenate([dq, (d_own + d_far).astype(BF)], 1)
+    keep, give = attend_back(near, far, expo, head_out, inverse, d_near)
+    take = jnp.pad(send(give, flip), ((0, 0), (HEAD, 0), (0, 0)))
+    d_qkv = (keep.astype(F32) + take.astype(F32)).astype(BF)
     d_qkv = lax.all_to_all(d_qkv, CHIPS, 0, 0, tiled=True)
     early = over_z(early)
+    sp2, n32 = send(sp, flip), send(n3, flip)
+    info_attn, _ = lax.optimization_barrier((info, sp2))
     g2, gs, lo, hi, d_gatt = call(
         attn_in_kernel,
         [(tall, F32), (narrow, BF, FREE), ((RIM, 256), BF), ((RIM, 256), BF), ((1, width), F32)],
         [SMEM, FREE] + [HBM] * 3,
         [pltpu.VMEM((2, 8, SMALL - 128, 256), BF), tiny, pltpu.VMEM(tall, F32), pltpu.VMEM(tall, F32),
          dma((4,))],
-        "attn_in", 0.5, info, d_qkv, h2, g3, one,
+        "attn_in", 0.5, info_attn, d_qkv, h2, g3, one,
     )
     low_gs = send(hi, along(1))
     high_gs = send(lo, along(-1))
     info_mid, _, _ = lax.optimization_barrier((info, low_gs, high_gs))
     middle = call(
-        middle_kernel, [((2, 2, 4, 4, MIDDLE, 128), BF)], [SMEM, VMEM, FREE, VMEM, FREE] + [FREE] * 4, [], "middle", 0.3,
-        info_mid, sp, gs, n3, d_qkv, *[send(v, flip) for v in (sp, gs, n3, d_qkv)],
+        middle_kernel, [((8, 8, MIDDLE, 128), BF)], [SMEM, VMEM, FREE, VMEM, FREE] + [FREE] * 4, [], "middle", 0.3,
+        info_mid, sp, gs, n3, d_qkv, sp2, send(gs, flip), n32, send(d_qkv, flip),
     )[0]
     info_conv, middle = lax.optimization_barrier((info, middle))
-    middle = over_x(middle)
+    middle = lax.all_to_all(middle.reshape(64, MIDDLE, 128), CHIPS + WT, 0, 0, tiled=True)
     rim_narrow = ((rim_rows, 256), BF)
     dw, dnar, table = call(
         conv_back_kernel, [(wide, BF, FREE), ((rim_rows, 256), BF, FREE), ((16, units), F32, FREE)],
@@ -1093,24 +1090,22 @@
         "glu_back", 1, info_glu, dw, dnar, h1m, two, one, g2, a, sg, x, table, d_gatt, d_gffn,
     )
     dab2, sums2 = send(dab, flip), send(sums, flip)
-    info_late, middle = lax.optimization_barrier((info, middle))
-    middle = over_z(middle)
+    middle = jnp.sum(middle.astype(F32), 0).astype(BF)
     late = call(
         late_kernel, [((8, 8, LATE, 128), BF)], [SMEM, VMEM, FREE, FREE, VMEM, FREE, FREE] + [FREE] * 6,
-        [pltpu.VMEM((rim_rows, width), F32), pltpu.VMEM((rim_rows, 256), F32)], "late", 40,
-        info_late, n2, dw, dnar, n1, dab, sums, send(n2, flip), dw2, dnar2, send(n1, flip), dab2, sums2,
+        [pltpu.VMEM((rim_rows, width), F32), pltpu.VMEM((rim_rows, 256), F32)], "late", 0.5,
+        info, n2, dw, dnar, n1, dab, sums, send(n2, flip), dw2, dnar2, send(n1, flip), dab2, sums2,
     )[0]
-    _, early, middle = lax.optimization_barrier((late, early, middle))
+    _, early = lax.optimization_barrier((late, early))
     y = lax.axis_index("y")
-    pieces = jnp.concatenate([early, middle], 1)
-    pick = lambda index: lax.dynamic_index_in_dim(pieces, index % 4, 0, keepdims=False)
+    pick = lambda index: lax.dynamic_index_in_dim(early, index % 4, 0, keepdims=False)
     parts = [send(pick(y + d), shift(dy=d)) for d in (1, 2, 3)]
     early = call(
-        fold_kernel, [((EARLY + MIDDLE, 128), BF, FREE)], [FREE] * 4, [], "fold", FOLD, pick(y), *parts
+        fold_kernel, [((EARLY, 128), BF, FREE)], [FREE] * 4, [], "fold", FOLD, pick(y), *parts
     )[0]
     late = lax.all_to_all(late.reshape(64, LATE, 128), CHIPS + WT, 0, 0, tiled=True)
     late = jnp.sum(late.astype(F32), 0).astype(BF)
-    final = spread_out(jnp.concatenate([early, late], 0), CHIPS, 8)
+    final = spread_out(jnp.concatenate([early, middle, late], 0), CHIPS, 8)
     square, broad = ((64, 512), F32), ((64, 2048), F32)
     line = ((1, 64), F32)
     grads = call(

time: 322 us -> 317 us (0.984)
  waiting for transfers between devices: 86.3 us -> 75.9 us
  starting transfers between devices: 67.6 us -> 72.8 us
    reduce_scatter x2 -> x1, waiting for transfers between devices: 25.6 us -> 0.02 us  [over_z(): return lax.psum_scatter(value, 'z', scatter_dimension=0, tiled=True)[0]]
    ppermute x40, waiting for transfers between devices: 43 us -> 59.4 us  [send(): return lax.ppermute(value, AXES, pairs)]
    all_to_all x0 -> x1, starting transfers between devices: none -> 9.32 us  [shards(): lax.all_to_all(middle.reshape(64, MIDDLE, 128), CHIPS + WT, 0, 0, tiled=T...]
    ppermute x40, starting transfers between devices: 47.8 us -> 42.9 us  [send(): return lax.ppermute(value, AXES, pairs)]
    reduce_scatter x2 -> x1, waiting for transfers between devices: 4.27 us -> 0.01 us  [over_x(): lax.psum_scatter(value, ('xh', 'xl'), scatter_dimension=0, tiled=True)[0]]
  transfers between devices with their start and end apart: 49 -> 48, of which waited for: 20 -> 16; matrix products, arithmetic and copies ran while one was open for 1% -> 2% of each run, Pallas kernels for 26% -> 26%
where the time goes in v5:
time: 317 us; the launch traced here: 316 us
  Pallas kernels  95 us (30%)
  waiting for transfers between devices  75.9 us (24%)
  starting transfers between devices  72.8 us (23%)
  blocking collectives  50.1 us (16%)
  between operations  14.9 us (5%)
  other arithmetic  4.78 us (2%)
    pallas_call x13, Pallas kernels, call(): pl.pallas_call(kernel, in_specs=[VMEM if spec is FREE else spec for spec...  61.5 us
    ppermute x40, waiting for transfers between devices, send(): return lax.ppermute(value, AXES, pairs)  59.4 us
    ppermute x40, starting transfers between devices, send(): return lax.ppermute(value, AXES, pairs)  42.9 us
    all_to_all x1, blocking collectives, shards(): near = lax.all_to_all(qkv, CHIPS, 0, 0, tiled=True)  21.1 us
    pallas_call x1, Pallas kernels, attend_back(): pl.pallas_call(functools.partial(attend_back_kernel, chips, rows), grid=(...  19.4 us
    all_to_all x1, blocking collectives, spread_out(): return lax.all_to_all(copies, axes, 0, 0, tiled=True)  17 us
    pallas_call x1, Pallas kernels, attend(): pl.pallas_call(functools.partial(attend_kernel, chips, rows), grid=(chips...  14 us
    all_to_all x1, waiting for transfers between devices, shards(): d_qkv = lax.all_to_all(d_qkv, CHIPS, 0, 0, tiled=True)  13.6 us
  transfers between devices with their start and end apart: 48, of which 16 were waited for; matrix products, arithmetic and copies ran while one was open for 2% of the time, Pallas kernels for 26%

profile of v5, /device:TPU:1, one launch (start us, length us, event | category | flops | bytes accessed | tf_op | source)
XLA Modules:
  0.0 315.8 jit_solution(15186279007422226705)
XLA Ops:
  7.9 1.6 pack_ring.1.refs_0_
  9.5 4.7 %collective-permute-start = (bf16[512,256]{1,0:T(8,128)(2,1)S(1)}, bf16[512,256]{1,0:T(8,128)(2,1)S(1)}, u32[]{:S(2)}, u32[]{:S(2)}) collective-permute-start(bf16[512,256]{1,0:T(8,128)(2,1)S(1)} %pack_ring.1.refs_0_), channel_id=1, source_target_pairs={{0,3},{1,0},{2,1},{3,2},{4,7},{5,4},{6,5},{7,6},{8,11},{9,8},{10,9... | collective-permute-start | bytes 786440 | tf_op jit(solution)/shard_map/ppermute | solution.py:54
  16.7 3.1 pack_rest.1
  19.8 4.9 %collective-permute-done.refs_1_ = bf16[512,256]{1,0:T(8,128)(2,1)S(1)} collective-permute-done((bf16[512,256]{1,0:T(8,128)(2,1)S(1)}, bf16[512,256]{1,0:T(8,128)(2,1)S(1)}, u32[]{:S(2)}, u32[]{:S(2)}) %collective-permute-start) | collective-permute-done | bytes 262176 | tf_op jit(solution)/shard_map/ppermute | solution.py:54
  24.7 4.3 %collective-permute-done.2.refs_3_ = bf16[512,256]{1,0:T(8,128)(2,1)S(1)} collective-permute-done((bf16[512,256]{1,0:T(8,128)(2,1)S(1)}, bf16[512,256]{1,0:T(8,128)(2,1)S(1)}, u32[]{:S(2)}, u32[]{:S(2)}) %collective-permute-start.2) | collective-permute-done | bytes 262176 | tf_op jit(solution)/shard_map/ppermute | solution.py:54
  28.9 3.6 %all-to-all-start = ((bf16[8,352,256]{2,1,0:T(8,128)(2,1)}), bf16[8,352,256]{2,1,0:T(8,128)(2,1)S(1)}, u32[]{:S(2)}, u32[]{:S(2)}) async-start(bf16[8,352,256]{2,1,0:T(8,128)(2,1)} %get-tuple-element.102), calls=%async_computation | async-start | bytes 2883584 | tf_op jit(solution)/shard_map/all_to_all | solution.py:990
  32.6 1.3 collective-permute-start.4
  33.9 2.4 collective-permute-start.7
  37.5 6.8 %collective-permute-start.5 = (bf16[8,512]{1,0:T(8,128)(2,1)S(1)}, bf16[8,512]{1,0:T(8,128)(2,1)S(1)}, u32[]{:S(2)}, u32[]{:S(2)}) collective-permute-start(bf16[8,512]{1,0:T(8,128)(2,1)S(1)} %get-tuple-element.184), channel_id=1, source_target_pairs={{0,8},{1,9},{2,10},{3,11},{4,12},{5,13},{6,14},{7,15},{8,16},{9,17... | collective-permute-start | bytes 24584 | tf_op jit(solution)/shard_map/ppermute | solution.py:54
  44.2 10.0 %collective-permute-done.5.low_ref = bf16[8,512]{1,0:T(8,128)(2,1)S(1)} collective-permute-done((bf16[8,512]{1,0:T(8,128)(2,1)S(1)}, bf16[8,512]{1,0:T(8,128)(2,1)S(1)}, u32[]{:S(2)}, u32[]{:S(2)}) %collective-permute-start.5) | collective-permute-done | bytes 8224 | tf_op jit(solution)/shard_map/ppermute | solution.py:54
  54.2 1.9 collective-permute-start.6
  56.1 5.3 %collective-permute-done.6.high_ref = bf16[8,512]{1,0:T(8,128)(2,1)S(1)} collective-permute-done((bf16[8,512]{1,0:T(8,128)(2,1)S(1)}, bf16[8,512]{1,0:T(8,128)(2,1)S(1)}, u32[]{:S(2)}, u32[]{:S(2)}) %collective-permute-start.6) | collective-permute-done | bytes 8224 | tf_op jit(solution)/shard_map/ppermute | solution.py:54
  64.8 1.8 pad_maximum_fusion
  68.4 3.1 glu.1
  71.5 10.3 %conv.1 = (bf16[272,512]{1,0:T(8,128)(2,1)}, f32[272,2048]{1,0:T(8,128)}, f32[272,256]{1,0:T(8,128)}, bf16[272,2048]{1,0:T(8,128)(2,1)}, f32[272,128]{1,0:T(8,12...) custom-call(s32[6]{0:T(128)S(1)} %stack.32.info_ref, ...), custom_call_target="tpu_custom_call" | custom-call | flops 15000000512 | bytes 45000000 | tf_op jit(solution)/shard_map/conv/pallas_call | solution.py:271
  81.8 21.1 %all_to_all.40.near_ref = bf16[8,192,256]{2,1,0:T(8,128)(2,1)S(1)} all-to-all(bf16[8,192,256]{2,1,0:T(8,128)(2,1)S(1)} %get-tuple-element.115), channel_id=1, replica_groups=mesh['y'=4,'xh'=2,'core'=2,'xl'=2,'z'=4] {'y','xh'}, dimensions={0} | all-to-all | bytes 1572864 | tf_op jit(solution)/shard_map/all_to_all | solution.py:1024
  102.9 1.5 collective-permute-start.19
  104.5 1.5 collective-permute-done.19.far_ref
  106.0 14.0 %attend.1 = (bf16[8,64,256]{2,1,0:T(8,128)(2,1)}, bf16[2048,4096]{1,0:T(8,128)(2,1)}, f32[8,8,256]{2,1,0:T(8,128)}, bf16[8,192,256]{2,1,0:T(8,128)(2,1)}, bf16[8,128,256]{2,1,0:T(8,128)(2,1)}) custom-call(s32[1]{0:T(128)S(6)} %copy.39.length_ref, s32[1]{0:T(128)} %bitcast.core_ref, bf16[8,192,256]{2,1,0:T(8,128)(2,1)S(1)} %all_to_all.40.near_ref, ...), custom_call_target="tpu_custom_call" | custom-call | flops 14000000000 | bytes 42000000 | tf_op jit(solution)/shard_map/attend/pallas_call | solution.py:135
  120.5 12.1 %all_to_all.41.o_ref = bf16[8,64,256]{2,1,0:T(8,128)(2,1)S(1)} all-to-all(bf16[8,64,256]{2,1,0:T(8,128)(2,1)} %get-tuple-element.116.o_ref), channel_id=1, replica_groups=mesh['y'=4,'xh'=2,'core'=2,'xl'=2,'z'=4] {'y','xh'}, dimensions={0} | all-to-all | bytes 524288 | tf_op jit(solution)/shard_map/all_to_all | solution.py:1029
  132.6 7.9 %ffn.1 = (bf16[256,512]{1,0:T(8,128)(2,1)}, bf16[256,5632]{1,0:T(8,128)(2,1)S(1)}, f32[256,512]{1,0:T(8,128)}, bf16[8,64,256]{2,1,0:T(8,128)(2,1)}, f32[1,512]{1,0:T(1,128)}, /*index=5*/bf16[8,64,256]{2,1,0:T(8,128)(2,1)S(1)}) custom-call(s32[6]{0:T(128)S(1)} %stack.32.info_ref, f32[256,512]{1,0:T(8,128)} %get-tuple-element.114.h2_ref.h2_in, ...), custom_call_target="tpu_custom_call" | custom-call | flops 11000000512 | bytes 33000000 | tf_op jit(solution)/shard_map/ffn/pallas_call | solution.py:271
  141.7 3.4 %all-to-all-start.3 = ((bf16[8,64,256]{2,1,0:T(8,128)(2,1)}), bf16[8,64,256]{2,1,0:T(8,128)(2,1)S(1)}, u32[]{:S(2)}, u32[]{:S(2)}) async-start(bf16[8,64,256]{2,1,0:T(8,128)(2,1)} %get-tuple-element.122), calls=%async_computation.3 | async-start | bytes 524288 | tf_op jit(solution)/shard_map/all_to_all | solution.py:1040
  145.2 1.9 collective-permute-done.22.heads2_ref
  147.0 4.8 %early.1 = bf16[2,2,4,4,144,128]{5,4,3,2,1,0:T(8,128)(2,1)} custom-call(s32[6]{0:T(128)S(1)} %stack.32.info_ref, bf16[256,5632]{1,0:T(8,128)(2,1)S(1)} %get-tuple-element.123.acts_ref, bf16[8,64,256]{2,1,0:T(8,128)(2,1)S(1)} %get-tuple-element.124.heads_ref, bf16[256,5632]{1,0:T(8,128)(2,1)} %collective-permute-done.21.acts2_ref, ...), custom_call_target="tpu_custom_call" | custom-call | flops 300000000 | bytes 900000 | tf_op jit(solution)/shard_map/early/pallas_call | solution.py:271
  151.8 1.7 all-to-all-done.3.do_ref
  153.6 19.4 %attend_back.1 = (bf16[8,192,256]{2,1,0:T(8,128)(2,1)S(1)}, bf16[8,128,256]{2,1,0:T(8,128)(2,1)S(1)}) custom-call(bf16[8,192,256]{2,1,0:T(8,128)(2,1)} %get-tuple-element.129.near_ref, bf16[8,128,256]{2,1,0:T(8,128)(2,1)} %get-tuple-element.130.far_ref, bf16[2048,4096]{1,0:T(8,128)(2,1)} %get-tuple-element.131.e_ref, ...), custom_call_target="tpu_custom_call" | custom-call | flops 3000000000 | bytes 9000000 | tf_op jit(solution)/shard_map/attend_back/pallas_call | solution.py:229
  173.0 1.3 collective-permute-start.24
  174.3 1.5 collective-permute-done.24
  177.0 3.5 %all-to-all-start.4 = ((bf16[8,192,256]{2,1,0:T(8,128)(2,1)}), bf16[8,192,256]{2,1,0:T(8,128)(2,1)S(1)}, u32[]{:S(2)}, u32[]{:S(2)}) async-start(bf16[8,192,256]{2,1,0:T(8,128)(2,1)} %add_convert_fusion), calls=%async_computation.6 | async-start | bytes 1572864 | tf_op jit(solution)/shard_map/all_to_all | solution.py:1050
  181.0 13.6 %all-to-all-done.4.d_ref = bf16[8,192,256]{2,1,0:T(8,128)(2,1)S(1)} async-done(((bf16[8,192,256]{2,1,0:T(8,128)(2,1)}), bf16[8,192,256]{2,1,0:T(8,128)(2,1)S(1)}, u32[]{:S(2)}, u32[]{:S(2)}) %all-to-all-start.4) | async-done | bytes 786464 | tf_op jit(solution)/shard_map/all_to_all | solution.py:1050
  196.0 3.8 %attn_in.1 = (f32[256,512]{1,0:T(8,128)}, bf16[256,256]{1,0:T(8,128)(2,1)S(1)}, bf16[8,256]{1,0:T(8,128)(2,1)}, bf16[8,256]{1,0:T(8,128)(2,1)}, f32[1,512]{1,0:T(1,128)}) custom-call(s32[6]{0:T(128)S(1)} %stack.32.info_ref, bf16[8,192,256]{2,1,0:T(8,128)(2,1)S(1)} %all-to-all-done.4.d_ref, f32[256,512]{1,0:T(8,128)} %get-tuple-element.114.h2_ref.h2_in, ...), custom_call_target="tpu_custom_call" | custom-call | flops 500000000 | bytes 1500000 | tf_op jit(solution)/shard_map/attn_in/pallas_call | solution.py:271
  200.4 2.4 collective-permute-start.25
  202.8 1.9 collective-permute-start.26
  204.7 4.7 %collective-permute-done.26.hi_ref = bf16[8,256]{1,0:T(8,128)(2,1)S(1)} collective-permute-done((bf16[8,256]{1,0:T(8,128)(2,1)}, bf16[8,256]{1,0:T(8,128)(2,1)S(1)}, u32[]{:S(2)}, u32[]{:S(2)}) %collective-permute-start.26) | collective-permute-done | bytes 4128 | tf_op jit(solution)/shard_map/ppermute | solution.py:54
  209.4 3.4 %middle.1 = bf16[8,8,80,128]{3,2,1,0:T(8,128)(2,1)} custom-call(s32[6]{0:T(128)S(1)} %stack.32.info_ref, bf16[256,2048]{1,0:T(8,128)(2,1)} %get-tuple-element.127.sp_ref, bf16[256,256]{1,0:T(8,128)(2,1)S(1)} %get-tuple-element.140.gs_ref, bf16[256,512]{1,0:T(8,128)(2,1)} %get-tuple-element.141.n3_ref, bf16[8,192,256]{2,1,0:T(8,128)(2,1)S(1)} %all-to-all-done.4.d_ref, ...), custom_call_target="tpu_custom_call" | custom-call | flops 300000000 | bytes 900000 | tf_op jit(solution)/shard_map/middle/pallas_call | solution.py:271
  212.8 9.3 %all-to-all-start.5 = ((bf16[64,80,128]{2,1,0:T(8,128)(2,1)}), bf16[64,80,128]{2,1,0:T(8,128)(2,1)}, u32[]{:S(2)}, u32[]{:S(2)}) async-start(bf16[64,80,128]{2,1,0:T(8,128)(2,1)} %bitcast.44), calls=%async_computation.7 | async-start | bytes 2621440 | tf_op jit(solution)/shard_map/all_to_all | solution.py:1070
  222.2 11.2 %conv_back.1 = (bf16[256,2048]{1,0:T(8,128)(2,1)S(1)}, bf16[272,256]{1,0:T(8,128)(2,1)S(1)}, f32[16,2048]{1,0:T(8,128)S(1)}) custom-call(s32[6]{0:T(128)S(1)} %stack.32.info_ref, bf16[8,256]{1,0:T(8,128)(2,1)S(1)} %collective-permute-done.25.lo_ref, bf16[256,256]{1,0:T(8,128)(2,1)S(1)} %get-tuple-element.140.gs_ref, ...), custom_call_target="tpu_custom_call" | custom-call | flops 2000000000 | bytes 6000000 | tf_op jit(solution)/shard_map/conv_back/pallas_call | solution.py:271
  233.5 5.5 %glu_back.1 = (f32[256,512]{1,0:T(8,128)}, bf16[256,1024]{1,0:T(8,128)(2,1)S(1)}, f32[24,2048]{1,0:T(8,128)S(1)}) custom-call(s32[6]{0:T(128)S(1)} %stack.32.info_ref, bf16[256,2048]{1,0:T(8,128)(2,1)S(1)} %get-tuple-element.149.dw_ref, bf16[272,256]{1,0:T(8,128)(2,1)S(1)} %get-tuple-element.150.dnar_ref, f32[256,512]{1,0:T(8,128)} %get-tuple-element.151.h1_in, ...), custom_call_target="tpu_custom_call" | custom-call | flops 1000000000 | bytes 3000000 | tf_op jit(solution)/shard_map/glu_back/pallas_call | solution.py:271
  240.1 1.3 collective-permute-done.33.n12_ref
  242.8 3.9 %late.1 = bf16[8,8,128,128]{3,2,1,0:T(8,128)(2,1)} custom-call(s32[6]{0:T(128)S(1)} %stack.32.info_ref, bf16[272,512]{1,0:T(8,128)(2,1)} %get-tuple-element.159.n2_ref, bf16[256,2048]{1,0:T(8,128)(2,1)S(1)} %get-tuple-element.149.dw_ref, bf16[272,256]{1,0:T(8,128)(2,1)S(1)} %get-tuple-element.150.dnar_ref, bf16[256,512]{1,0:T(8,128)(2,1)} %get-tuple-element.160.n1_ref, ...), custom_call_target="tpu_custom_call" | custom-call | flops 500000000 | bytes 1500000 | tf_op jit(solution)/shard_map/late/pallas_call | solution.py:271
  246.7 9.8 %all-to-all-start.6 = ((bf16[64,128,128]{2,1,0:T(8,128)(2,1)}), bf16[64,128,128]{2,1,0:T(8,128)(2,1)S(1)}, u32[]{:S(2)}, u32[]{:S(2)}) async-start(bf16[64,128,128]{2,1,0:T(8,128)(2,1)} %bitcast.43), calls=%async_computation.8 | async-start | bytes 4194304 | tf_op jit(solution)/shard_map/all_to_all | solution.py:1106
  257.7 2.6 collective-permute-start.37
  261.4 1.5 reduce_sum.24
  262.9 20.8 %collective-permute-done.36.refs_1_ = bf16[144,128]{1,0:T(8,128)(2,1)S(1)} collective-permute-done((bf16[144,128]{1,0:T(8,128)(2,1)S(1)}, bf16[144,128]{1,0:T(8,128)(2,1)S(1)}, u32[]{:S(2)}, u32[]{:S(2)}) %collective-permute-start.36) | collective-permute-done | bytes 36896 | tf_op jit(solution)/shard_map/ppermute | solution.py:54
  285.3 17.0 %all_to_all.42.near_ref = bf16[8,352,128]{2,1,0:T(8,128)(2,1)S(1)} all-to-all(bf16[8,352,128]{2,1,0:T(8,128)(2,1)S(1)} %broadcast_in_dim.14), channel_id=1, replica_groups=mesh['y'=4,'xh'=2,'core'=2,'xl'=2,'z'=4] {'y','xh'}, dimensions={0} | all-to-all | bytes 1441792 | tf_op jit(solution)/shard_map/all_to_all | solution.py:951
  302.2 2.3 collective-permute-start.39
  304.5 1.8 collective-permute-done.39.far_ref
  306.3 2.9 unpack.1
  (102 shorter events, 20.4 us)
Async XLA Ops:
  9.5 15.1 %collective-permute-start = (bf16[512,256]{1,0:T(8,128)(2,1)S(1)}, bf16[512,256]{1,0:T(8,128)(2,1)S(1)}, u32[]{:S(2)}, u32[]{:S(2)}) collective-permute-start(bf16[512,256]{1,0:T(8,128)(2,1)S(1)} %pack_ring.1.refs_0_), channel_id=1, source_target_pairs={{0,3},{1,0},{2,1},{3,2},{4,7},{5,4},{6,5},{7,6},{8,11},{9,8},{10,9... | collective-permute-start | bytes 786440 | tf_op jit(solution)/shard_map/ppermute | solution.py:54
  14.2 10.5 %collective-permute-start.1 = (bf16[512,256]{1,0:T(8,128)(2,1)S(1)}, bf16[512,256]{1,0:T(8,128)(2,1)S(1)}, u32[]{:S(2)}, u32[]{:S(2)}) collective-permute-start(bf16[512,256]{1,0:T(8,128)(2,1)S(1)} %pack_ring.1.refs_0_), channel_id=1, source_target_pairs={{0,2},{1,3},{2,0},{3,1},{4,6},{5,7},{6,4},{7,5},{8,10},{9,11},{10,... | collective-permute-start | bytes 786440 | tf_op jit(solution)/shard_map/ppermute | solution.py:54
  14.2 14.7 %collective-permute-start.2 = (bf16[512,256]{1,0:T(8,128)(2,1)S(1)}, bf16[512,256]{1,0:T(8,128)(2,1)S(1)}, u32[]{:S(2)}, u32[]{:S(2)}) collective-permute-start(bf16[512,256]{1,0:T(8,128)(2,1)S(1)} %pack_ring.1.refs_0_), channel_id=1, source_target_pairs={{0,1},{1,2},{2,3},{3,0},{4,5},{5,6},{6,7},{7,4},{8,9},{9,10},{10,1... | collective-permute-start | bytes 786440 | tf_op jit(solution)/shard_map/ppermute | solution.py:54
  14.9 14.0 %collective-permute-start.3 = (bf16[512,256]{1,0:T(8,128)(2,1)S(1)}, bf16[512,256]{1,0:T(8,128)(2,1)S(1)}, u32[]{:S(2)}, u32[]{:S(2)}) collective-permute-start(bf16[512,256]{1,0:T(8,128)(2,1)S(1)} %pack_ring.1.refs_0_), channel_id=1, source_target_pairs={{0,4},{1,5},{2,6},{3,7},{4,0},{5,1},{6,2},{7,3},{8,12},{9,13},{10,... | collective-permute-start | bytes 786440 | tf_op jit(solution)/shard_map/ppermute | solution.py:54
  28.9 34.0 %all-to-all-start = ((bf16[8,352,256]{2,1,0:T(8,128)(2,1)}), bf16[8,352,256]{2,1,0:T(8,128)(2,1)S(1)}, u32[]{:S(2)}, u32[]{:S(2)}) async-start(bf16[8,352,256]{2,1,0:T(8,128)(2,1)} %get-tuple-element.102), calls=%async_computation | async-start | bytes 2883584 | tf_op jit(solution)/shard_map/all_to_all | solution.py:990
  32.5 87.6 %all-gather.3.cloned.1.call-start = ((), (), s32[]{:S(2)}) async-start(), calls=%async_computation.12 | async-start | bytes 2949120 | tf_op jit(solution)/shard_map/all_gather | solution.py:1001
  32.6 28.8 %collective-permute-start.4 = (bf16[576,256]{1,0:T(8,128)(2,1)S(1)}, bf16[576,256]{1,0:T(8,128)(2,1)S(1)}, u32[]{:S(2)}, u32[]{:S(2)}) collective-permute-start(bf16[576,256]{1,0:T(8,128)(2,1)S(1)} %get-tuple-element.118), channel_id=1, source_target_pairs={{0,4},{1,5},{2,6},{3,7},{4,0},{5,1},{6,2},{7,3},{8,12},{9,13},{10,... | collective-permute-start | bytes 884744 | tf_op jit(solution)/shard_map/ppermute | solution.py:54
  33.9 27.5 %collective-permute-start.7 = (bf16[512,256]{1,0:T(8,128)(2,1)S(1)}, bf16[512,256]{1,0:T(8,128)(2,1)S(1)}, u32[]{:S(2)}, u32[]{:S(2)}) collective-permute-start(bf16[512,256]{1,0:T(8,128)(2,1)S(1)} %collective-permute-done.3.refs_4_), channel_id=1, source_target_pairs={{0,3},{1,0},{2,1},{3,2},{4,7},{5,4},{6,5},{7,6},{8,11},{9,8},{10,9... | collective-permute-start | bytes 786440 | tf_op jit(solution)/shard_map/ppermute | solution.py:54
  36.3 25.1 %collective-permute-start.8 = (bf16[512,256]{1,0:T(8,128)(2,1)S(1)}, bf16[512,256]{1,0:T(8,128)(2,1)S(1)}, u32[]{:S(2)}, u32[]{:S(2)}) collective-permute-start(bf16[512,256]{1,0:T(8,128)(2,1)S(1)} %collective-permute-done.3.refs_4_), channel_id=1, source_target_pairs={{0,2},{1,3},{2,0},{3,1},{4,6},{5,7},{6,4},{7,5},{8,10},{9,11},{10,... | collective-permute-start | bytes 786440 | tf_op jit(solution)/shard_map/ppermute | solution.py:54
  36.9 26.0 %collective-permute-start.9 = (bf16[512,256]{1,0:T(8,128)(2,1)S(1)}, bf16[512,256]{1,0:T(8,128)(2,1)}, u32[]{:S(2)}, u32[]{:S(2)}) collective-permute-start(bf16[512,256]{1,0:T(8,128)(2,1)S(1)} %collective-permute-done.3.refs_4_), channel_id=1, source_target_pairs={{0,1},{1,2},{2,3},{3,0},{4,5},{5,6},{6,7},{7,4},{8,9},{9,10},{10,1... | collective-permute-start | bytes 786440 | tf_op jit(solution)/shard_map/ppermute | solution.py:54
  37.5 16.7 %collective-permute-start.5 = (bf16[8,512]{1,0:T(8,128)(2,1)S(1)}, bf16[8,512]{1,0:T(8,128)(2,1)S(1)}, u32[]{:S(2)}, u32[]{:S(2)}) collective-permute-start(bf16[8,512]{1,0:T(8,128)(2,1)S(1)} %get-tuple-element.184), channel_id=1, source_target_pairs={{0,8},{1,9},{2,10},{3,11},{4,12},{5,13},{6,14},{7,15},{8,16},{9,17... | collective-permute-start | bytes 24584 | tf_op jit(solution)/shard_map/ppermute | solution.py:54
  54.2 7.2 %collective-permute-start.6 = (bf16[8,512]{1,0:T(8,128)(2,1)S(1)}, bf16[8,512]{1,0:T(8,128)(2,1)S(1)}, u32[]{:S(2)}, u32[]{:S(2)}) collective-permute-start(bf16[8,512]{1,0:T(8,128)(2,1)S(1)} %get-tuple-element.183), channel_id=1, source_target_pairs={{8,0},{9,1},{10,2},{11,3},{12,4},{13,5},{14,6},{15,7},{16,8},{17,9... | collective-permute-start | bytes 24584 | tf_op jit(solution)/shard_map/ppermute | solution.py:54
  62.9 5.3 %collective-permute-start.10 = (bf16[8,352,256]{2,1,0:T(8,128)(2,1)S(1)}, bf16[8,352,256]{2,1,0:T(8,128)(2,1)}, u32[]{:S(2)}, u32[]{:S(2)}) collective-permute-start(bf16[8,352,256]{2,1,0:T(8,128)(2,1)S(1)} %all-to-all-done.near_ref.refs_16_), channel_id=1, source_target_pairs={{0,8},{1,9},{2,10},{3,11},{4,12},{5,13},{6,14},{7,15},{8,0},{9,1},... | collective-permute-start | bytes 4325384 | tf_op jit(solution)/shard_map/ppermute | solution.py:54
  63.7 3.4 %collective-permute-start.11 = (bf16[512,256]{1,0:T(8,128)(2,1)S(1)}, bf16[512,256]{1,0:T(8,128)(2,1)}, u32[]{:S(2)}, u32[]{:S(2)}) collective-permute-start(bf16[512,256]{1,0:T(8,128)(2,1)S(1)} %pack_ring.1.refs_0_), channel_id=1, source_target_pairs={{0,8},{1,9},{2,10},{3,11},{4,12},{5,13},{6,14},{7,15},{8,0},{9,1},... | collective-permute-start | bytes 786440 | tf_op jit(solution)/shard_map/ppermute | solution.py:54
  63.7 3.7 %collective-permute-start.15 = (bf16[512,256]{1,0:T(8,128)(2,1)S(1)}, bf16[512,256]{1,0:T(8,128)(2,1)}, u32[]{:S(2)}, u32[]{:S(2)}) collective-permute-start(bf16[512,256]{1,0:T(8,128)(2,1)S(1)} %collective-permute-done.3.refs_4_), channel_id=1, source_target_pairs={{0,8},{1,9},{2,10},{3,11},{4,12},{5,13},{6,14},{7,15},{8,0},{9,1},... | collective-permute-start | bytes 786440 | tf_op jit(solution)/shard_map/ppermute | solution.py:54
  64.2 3.6 %collective-permute-start.12 = (bf16[512,256]{1,0:T(8,128)(2,1)S(1)}, bf16[512,256]{1,0:T(8,128)(2,1)}, u32[]{:S(2)}, u32[]{:S(2)}) collective-permute-start(bf16[512,256]{1,0:T(8,128)(2,1)S(1)} %collective-permute-done.refs_1_), channel_id=1, source_target_pairs={{0,8},{1,9},{2,10},{3,11},{4,12},{5,13},{6,14},{7,15},{8,0},{9,1},... | collective-permute-start | bytes 786440 | tf_op jit(solution)/shard_map/ppermute | solution.py:54
  64.2 7.2 %collective-permute-start.13 = (bf16[512,256]{1,0:T(8,128)(2,1)S(1)}, bf16[512,256]{1,0:T(8,128)(2,1)}, u32[]{:S(2)}, u32[]{:S(2)}) collective-permute-start(bf16[512,256]{1,0:T(8,128)(2,1)S(1)} %collective-permute-done.1.refs_2_), channel_id=1, source_target_pairs={{0,8},{1,9},{2,10},{3,11},{4,12},{5,13},{6,14},{7,15},{8,0},{9,1},... | collective-permute-start | bytes 786440 | tf_op jit(solution)/shard_map/ppermute | solution.py:54
  67.1 4.4 %collective-permute-start.14 = (bf16[512,256]{1,0:T(8,128)(2,1)S(1)}, bf16[512,256]{1,0:T(8,128)(2,1)S(1)}, u32[]{:S(2)}, u32[]{:S(2)}) collective-permute-start(bf16[512,256]{1,0:T(8,128)(2,1)S(1)} %collective-permute-done.2.refs_3_), channel_id=1, source_target_pairs={{0,8},{1,9},{2,10},{3,11},{4,12},{5,13},{6,14},{7,15},{8,0},{9,1},... | collective-permute-start | bytes 786440 | tf_op jit(solution)/shard_map/ppermute | solution.py:54
  67.5 4.0 %collective-permute-start.16 = (bf16[512,256]{1,0:T(8,128)(2,1)}, bf16[512,256]{1,0:T(8,128)(2,1)S(1)}, u32[]{:S(2)}, u32[]{:S(2)}) collective-permute-start(bf16[512,256]{1,0:T(8,128)(2,1)} %copy-done.1), channel_id=1, source_target_pairs={{0,8},{1,9},{2,10},{3,11},{4,12},{5,13},{6,14},{7,15},{8,0},{9,1},... | collective-permute-start | bytes 786440 | tf_op jit(solution)/shard_map/ppermute | solution.py:54
  67.8 3.6 %collective-permute-start.17 = (bf16[512,256]{1,0:T(8,128)(2,1)}, bf16[512,256]{1,0:T(8,128)(2,1)S(1)}, u32[]{:S(2)}, u32[]{:S(2)}) collective-permute-start(bf16[512,256]{1,0:T(8,128)(2,1)} %copy-done.3), channel_id=1, source_target_pairs={{0,8},{1,9},{2,10},{3,11},{4,12},{5,13},{6,14},{7,15},{8,0},{9,1},... | collective-permute-start | bytes 786440 | tf_op jit(solution)/shard_map/ppermute | solution.py:54
  68.2 3.3 %collective-permute-start.18 = (bf16[512,256]{1,0:T(8,128)(2,1)}, bf16[512,256]{1,0:T(8,128)(2,1)S(1)}, u32[]{:S(2)}, u32[]{:S(2)}) collective-permute-start(bf16[512,256]{1,0:T(8,128)(2,1)} %collective-permute-done.9.refs_7_), channel_id=1, source_target_pairs={{0,8},{1,9},{2,10},{3,11},{4,12},{5,13},{6,14},{7,15},{8,0},{9,1},... | collective-permute-start | bytes 786440 | tf_op jit(solution)/shard_map/ppermute | solution.py:54
  102.9 3.1 collective-permute-start.19
  120.1 12.6 %collective-permute-start.20 = (bf16[4,2,576,256]{3,2,1,0:T(8,128)(2,1)}, bf16[4,2,576,256]{3,2,1,0:T(8,128)(2,1)S(1)}, u32[]{:S(2)}, u32[]{:S(2)}) collective-permute-start(bf16[4,2,576,256]{3,2,1,0:T(8,128)(2,1)} %bitcast.48), channel_id=1, source_target_pairs={{0,8},{1,9},{2,10},{3,11},{4,12},{5,13},{6,14},{7,15},{8,0},{9,1},... | collective-permute-start | bytes 7077896 | tf_op jit(solution)/shard_map/ppermute | solution.py:54
  140.6 6.5 %collective-permute-start.21 = (bf16[256,5632]{1,0:T(8,128)(2,1)S(1)}, bf16[256,5632]{1,0:T(8,128)(2,1)}, u32[]{:S(2)}, u32[]{:S(2)}) collective-permute-start(bf16[256,5632]{1,0:T(8,128)(2,1)S(1)} %get-tuple-element.123.acts_ref), channel_id=1, source_target_pairs={{0,8},{1,9},{2,10},{3,11},{4,12},{5,13},{6,14},{7,15},{8,0},{9,1},... | collective-permute-start | bytes 8650760 | tf_op jit(solution)/shard_map/ppermute | solution.py:54
  141.6 5.4 %collective-permute-start.22 = (bf16[8,64,256]{2,1,0:T(8,128)(2,1)S(1)}, bf16[8,64,256]{2,1,0:T(8,128)(2,1)}, u32[]{:S(2)}, u32[]{:S(2)}) collective-permute-start(bf16[8,64,256]{2,1,0:T(8,128)(2,1)S(1)} %get-tuple-element.124.heads_ref), channel_id=1, source_target_pairs={{0,8},{1,9},{2,10},{3,11},{4,12},{5,13},{6,14},{7,15},{8,0},{9,1},... | collective-permute-start | bytes 786440 | tf_op jit(solution)/shard_map/ppermute | solution.py:54
  141.7 11.8 %all-to-all-start.3 = ((bf16[8,64,256]{2,1,0:T(8,128)(2,1)}), bf16[8,64,256]{2,1,0:T(8,128)(2,1)S(1)}, u32[]{:S(2)}, u32[]{:S(2)}) async-start(bf16[8,64,256]{2,1,0:T(8,128)(2,1)} %get-tuple-element.122), calls=%async_computation.3 | async-start | bytes 524288 | tf_op jit(solution)/shard_map/all_to_all | solution.py:1040
  145.1 50.7 %reduce-scatter.3.cloned.1.call-start = ((), (), s32[]{:S(2)}) async-start(), calls=%async_computation.10 | async-start | bytes 2949120 | tf_op jit(solution)/shard_map/reduce_scatter | solution.py:942
  173.0 2.9 collective-permute-start.24
  177.0 17.6 %all-to-all-start.4 = ((bf16[8,192,256]{2,1,0:T(8,128)(2,1)}), bf16[8,192,256]{2,1,0:T(8,128)(2,1)S(1)}, u32[]{:S(2)}, u32[]{:S(2)}) async-start(bf16[8,192,256]{2,1,0:T(8,128)(2,1)} %add_convert_fusion), calls=%async_computation.6 | async-start | bytes 1572864 | tf_op jit(solution)/shard_map/all_to_all | solution.py:1050
  180.5 52.9 %reduce-scatter.5.cloned.1.call-start = ((), (), s32[]{:S(2)}) async-start(), calls=%async_computation.11 | async-start | bytes 737280 | tf_op jit(solution)/shard_map/reduce_scatter | solution.py:946
  180.6 15.4 %collective-permute-start.23 = (bf16[256,2048]{1,0:T(8,128)(2,1)}, bf16[256,2048]{1,0:T(8,128)(2,1)S(1)}, u32[]{:S(2)}, u32[]{:S(2)}) collective-permute-start(bf16[256,2048]{1,0:T(8,128)(2,1)} %get-tuple-element.127.sp_ref), channel_id=1, source_target_pairs={{0,8},{1,9},{2,10},{3,11},{4,12},{5,13},{6,14},{7,15},{8,0},{9,1},... | collective-permute-start | bytes 3145736 | tf_op jit(solution)/shard_map/ppermute | solution.py:54
  194.6 14.8 %collective-permute-start.29 = (bf16[8,192,256]{2,1,0:T(8,128)(2,1)S(1)}, bf16[8,192,256]{2,1,0:T(8,128)(2,1)S(1)}, u32[]{:S(2)}, u32[]{:S(2)}) collective-permute-start(bf16[8,192,256]{2,1,0:T(8,128)(2,1)S(1)} %all-to-all-done.4.d_ref), channel_id=1, source_target_pairs={{0,8},{1,9},{2,10},{3,11},{4,12},{5,13},{6,14},{7,15},{8,0},{9,1},... | collective-permute-start | bytes 2359304 | tf_op jit(solution)/shard_map/ppermute | solution.py:54
  195.9 13.5 %collective-permute-start.28 = (bf16[256,512]{1,0:T(8,128)(2,1)S(1)}, bf16[256,512]{1,0:T(8,128)(2,1)S(1)}, u32[]{:S(2)}, u32[]{:S(2)}) collective-permute-start(bf16[256,512]{1,0:T(8,128)(2,1)S(1)} %copy-done.8), channel_id=1, source_target_pairs={{0,8},{1,9},{2,10},{3,11},{4,12},{5,13},{6,14},{7,15},{8,0},{9,1},... | collective-permute-start | bytes 786440 | tf_op jit(solution)/shard_map/ppermute | solution.py:54
  199.8 9.6 %collective-permute-start.27 = (bf16[256,256]{1,0:T(8,128)(2,1)S(1)}, bf16[256,256]{1,0:T(8,128)(2,1)S(1)}, u32[]{:S(2)}, u32[]{:S(2)}) collective-permute-start(bf16[256,256]{1,0:T(8,128)(2,1)S(1)} %get-tuple-element.140.gs_ref), channel_id=1, source_target_pairs={{0,8},{1,9},{2,10},{3,11},{4,12},{5,13},{6,14},{7,15},{8,0},{9,1},... | collective-permute-start | bytes 393224 | tf_op jit(solution)/shard_map/ppermute | solution.py:54
  200.4 4.3 %collective-permute-start.25 = (bf16[8,256]{1,0:T(8,128)(2,1)}, bf16[8,256]{1,0:T(8,128)(2,1)S(1)}, u32[]{:S(2)}, u32[]{:S(2)}) collective-permute-start(bf16[8,256]{1,0:T(8,128)(2,1)} %get-tuple-element.137), channel_id=1, source_target_pairs={{0,8},{1,9},{2,10},{3,11},{4,12},{5,13},{6,14},{7,15},{8,16},{9,17... | collective-permute-start | bytes 12296 | tf_op jit(solution)/shard_map/ppermute | solution.py:54
  202.8 6.6 %collective-permute-start.26 = (bf16[8,256]{1,0:T(8,128)(2,1)}, bf16[8,256]{1,0:T(8,128)(2,1)S(1)}, u32[]{:S(2)}, u32[]{:S(2)}) collective-permute-start(bf16[8,256]{1,0:T(8,128)(2,1)} %get-tuple-element.138), channel_id=1, source_target_pairs={{8,0},{9,1},{10,2},{11,3},{12,4},{13,5},{14,6},{15,7},{16,8},{17,9... | collective-permute-start | bytes 12296 | tf_op jit(solution)/shard_map/ppermute | solution.py:54
  212.8 33.9 %all-to-all-start.5 = ((bf16[64,80,128]{2,1,0:T(8,128)(2,1)}), bf16[64,80,128]{2,1,0:T(8,128)(2,1)}, u32[]{:S(2)}, u32[]{:S(2)}) async-start(bf16[64,80,128]{2,1,0:T(8,128)(2,1)} %bitcast.44), calls=%async_computation.7 | async-start | bytes 2621440 | tf_op jit(solution)/shard_map/all_to_all | solution.py:1070
  233.3 9.5 %collective-permute-start.31 = (bf16[256,2048]{1,0:T(8,128)(2,1)S(1)}, bf16[256,2048]{1,0:T(8,128)(2,1)S(1)}, u32[]{:S(2)}, u32[]{:S(2)}) collective-permute-start(bf16[256,2048]{1,0:T(8,128)(2,1)S(1)} %get-tuple-element.149.dw_ref), channel_id=1, source_target_pairs={{0,8},{1,9},{2,10},{3,11},{4,12},{5,13},{6,14},{7,15},{8,0},{9,1},... | collective-permute-start | bytes 3145736 | tf_op jit(solution)/shard_map/ppermute | solution.py:54
  239.0 3.8 %collective-permute-start.34 = (bf16[256,1024]{1,0:T(8,128)(2,1)S(1)}, bf16[256,1024]{1,0:T(8,128)(2,1)S(1)}, u32[]{:S(2)}, u32[]{:S(2)}) collective-permute-start(bf16[256,1024]{1,0:T(8,128)(2,1)S(1)} %get-tuple-element.161.dab_ref), channel_id=1, source_target_pairs={{0,8},{1,9},{2,10},{3,11},{4,12},{5,13},{6,14},{7,15},{8,0},{9,1},... | collective-permute-start | bytes 1572872 | tf_op jit(solution)/shard_map/ppermute | solution.py:54
  239.5 1.9 collective-permute-start.33
  239.6 2.2 collective-permute-start.30
  240.0 2.8 collective-permute-start.35
  241.4 1.4 collective-permute-start.32
  246.7 38.1 %all-to-all-start.6 = ((bf16[64,128,128]{2,1,0:T(8,128)(2,1)}), bf16[64,128,128]{2,1,0:T(8,128)(2,1)S(1)}, u32[]{:S(2)}, u32[]{:S(2)}) async-start(bf16[64,128,128]{2,1,0:T(8,128)(2,1)} %bitcast.43), calls=%async_computation.8 | async-start | bytes 4194304 | tf_op jit(solution)/shard_map/all_to_all | solution.py:1106
  256.6 27.1 %collective-permute-start.36 = (bf16[144,128]{1,0:T(8,128)(2,1)S(1)}, bf16[144,128]{1,0:T(8,128)(2,1)S(1)}, u32[]{:S(2)}, u32[]{:S(2)}) collective-permute-start(bf16[144,128]{1,0:T(8,128)(2,1)S(1)} %get-tuple-element.187), channel_id=1, source_target_pairs={{0,32},{1,33},{2,34},{3,35},{4,36},{5,37},{6,38},{7,39},{8,40},{9,... | collective-permute-start | bytes 110600 | tf_op jit(solution)/shard_map/ppermute | solution.py:54
  257.7 26.0 %collective-permute-start.37 = (bf16[144,128]{1,0:T(8,128)(2,1)S(1)}, bf16[144,128]{1,0:T(8,128)(2,1)S(1)}, u32[]{:S(2)}, u32[]{:S(2)}) collective-permute-start(bf16[144,128]{1,0:T(8,128)(2,1)S(1)} %get-tuple-element.186), channel_id=1, source_target_pairs={{0,64},{1,65},{2,66},{3,67},{4,68},{5,69},{6,70},{7,71},{8,72},{9,... | collective-permute-start | bytes 110600 | tf_op jit(solution)/shard_map/ppermute | solution.py:54
  260.3 23.4 %collective-permute-start.38 = (bf16[144,128]{1,0:T(8,128)(2,1)S(1)}, bf16[144,128]{1,0:T(8,128)(2,1)S(1)}, u32[]{:S(2)}, u32[]{:S(2)}) collective-permute-start(bf16[144,128]{1,0:T(8,128)(2,1)S(1)} %get-tuple-element.185), channel_id=1, source_target_pairs={{0,96},{1,97},{2,98},{3,99},{4,100},{5,101},{6,102},{7,103},{8,104... | collective-permute-start | bytes 110600 | tf_op jit(solution)/shard_map/ppermute | solution.py:54
  302.2 4.1 %collective-permute-start.39 = (bf16[8,352,128]{2,1,0:T(8,128)(2,1)S(1)}, bf16[8,352,128]{2,1,0:T(8,128)(2,1)S(1)}, u32[]{:S(2)}, u32[]{:S(2)}) collective-permute-start(bf16[8,352,128]{2,1,0:T(8,128)(2,1)S(1)} %all_to_all.42.near_ref), channel_id=1, source_target_pairs={{0,8},{1,9},{2,10},{3,11},{4,12},{5,13},{6,14},{7,15},{8,0},{9,1},... | collective-permute-start | bytes 2162696 | tf_op jit(solution)/shard_map/ppermute | solution.py:54
  (11 other events, 77.2 us)
Sparse Core Ops, SparseCore 0:
  66.7 34.4 all-gather.2
  153.7 29.3 reduce-scatter.2
  196.0 16.5 reduce-scatter.4

commit v6 on v5

--- a/solution.py
+++ b/solution.py
@@ -260,7 +260,7 @@
 ACT_GY = slice(4608, 5120)
 ACT_GA = slice(5120, 5632)
 EARLY = 144
-SMALL = 320
+SMALL = 128
 MIDDLE = 80
 LATE = 128
 
@@ -425,7 +425,7 @@
 
 def conv_body(info_ref, h1_ref, near2, far2, near1_ref, far1_ref,
               n2_ref, wp_out, np_ref, nm_out, mean_ref, scale_ref, sp_out, h2_ref, n3_ref,
-              qkv_ref, two_ref, one_ref, w2_ref, w1_ref, mix_ref, wp_ref, nm_ref, sp_ref, slab_ref,
+              two_ref, one_ref, w2_ref, w1_ref, mix_ref, wp_ref, nm_ref, sp_ref, slab_ref,
               sem2, semq, sems):
     core = info_ref[0]
     rim_rows = h1_ref.shape[0]
@@ -509,28 +509,38 @@
     normal, _ = normal_of(h2_ref[...])
     n3 = (normal * gains[2:3]).astype(BF)
     n3_ref[...] = n3
-    for part in range(3):
-        for side in range(2):
-            block = matmul(n3, w1_ref[side, :, 128 + 64 * part:192 + 64 * part, :].reshape(512, 256))
-            qkv_ref[4 * side:4 * side + 4, 64 * part:64 * part + 64, :] = (
-                block.T.astype(BF).reshape(4, 64, rows)
-            )
     settle(copies2 + copiesq)
     for which in range(3):
         for index in range(8):
             leaving(which, index).wait()
 
 
+def queries_kernel(info_ref, n3_ref, near_ref, far_ref, qkv_ref, wq_out, w_ref, sem):
+    rows = n3_ref.shape[0]
+    settle(fetch(info_ref[0], near_ref, far_ref, w_ref, sem))
+    copies = launch([(w_ref, wq_out)], sem)
+    for part in range(3):
+        for side in range(2):
+            block = matmul(n3_ref[...], queries_of(w_ref, side, part))
+            qkv_ref[4 * side:4 * side + 4, 64 * part:64 * part + 64, :] = (
+                block.T.astype(BF).reshape(4, 64, rows)
+            )
+    settle(copies)
+
+
 def ffn_kernel(info_ref, h2_ref, o_ref, cot_ref, one_ref, near_ref, far_ref,
                out_ref, acts_ref, g3_ref, dob_ref, gain_ref, heads_ref,
-               w_ref, small_ref, y_ref, dn_ref, sem):
+               w_ref, small_ref, y_ref, dn_ref, sem, sem_later):
     rows = h2_ref.shape[0]
     core = info_ref[0]
     x = info_ref[5]
-    pairs = [small_pair(one_ref, small_ref)]
+    pairs, later = [small_pair(one_ref, small_ref)], []
     for side, ref in ((core, near_ref), (1 - core, far_ref)):
-        pairs += [(ref.at[:, 0], w_ref.at[side, x]), (ref.at[:, 1], w_ref.at[side, 1 - x])]
+        for rel, place in ((0, x), (1, 1 - x)):
+            pairs.append((ref.at[:, rel, 512:576, :], w_ref.at[side, place, :, 512:576, :]))
+            later.append((ref.at[:, rel, 0:512, :], w_ref.at[side, place, :, 0:512, :]))
     copies = launch(pairs, sem)
+    later = launch(later, sem_later)
     valid = mask_of(info_ref, rows, 0)
     heads_ref[...] = o_ref[...]
     heads = o_ref[...].reshape(512, rows)
@@ -545,6 +555,7 @@
     y_ref[...] = h3
     dn_ref[...] = jnp.zeros_like(dn_ref)
 
+    settle(later)
     gy0, gy1 = acts_ref[:, 4608:4864], acts_ref[:, 4864:5120]
 
     def step(index, carry):
@@ -623,11 +634,11 @@
         by_chip(out_ref, c, slice(128, 144), packed[:, c])
 
 
-def attn_in_kernel(info_ref, d_ref, h2_in, g3_in, one_ref,
+def attn_in_kernel(info_ref, d_ref, h2_in, g3_in, one_ref, wq_ref,
                    g2_ref, gs_ref, lo_ref, hi_ref, gain_ref, w_ref, small_ref, h2_ref, g3_ref, sem):
     rows = h2_ref.shape[0]
     copies = launch(
-        [(h2_in, h2_ref), small_pair(one_ref, small_ref), (one_ref.at[:, :, 128:SMALL, :], w_ref),
+        [(h2_in, h2_ref), small_pair(one_ref, small_ref), (wq_ref, w_ref),
          (g3_in, g3_ref)], sem
     )
     settle(copies[:1])
@@ -895,13 +906,13 @@
 
 def pack_rest_kernel(info_ref, value_ref, gate_ref, query_ref, key_ref, values_ref, g0_ref, g1_ref,
                      g2_ref, g3_ref, depth_ref, mid_ref, in_ref, out_ref, outw_ref, one_ref,
-                     three_ref, pack_ref, g0, g1, g2, g3, depth, mid, sem):
+                     q_ref, three_ref, pack_ref, packq_ref, g0, g1, g2, g3, depth, mid, sem):
     core = info_ref[0]
     own = block_cols(core)
     small = [(g0_ref, g0), (g1_ref, g1), (g2_ref, g2), (g3_ref, g3), (depth_ref, depth), (mid_ref, mid)]
     small = launch(small, sem)
     weights = launch(
-        [(ref.at[:, own], pack_ref.at[128 + 64 * i:192 + 64 * i, :])
+        [(ref.at[:, own], packq_ref.at[64 * i:64 * i + 64, :])
          for i, ref in enumerate((query_ref, key_ref, values_ref))], sem.at[6:9],
     )
     later = [(in_ref.at[:, block_cols(core * 4 + j)], three_ref.at[64 * j:64 * j + 64, :]) for j in range(4)]
@@ -927,6 +938,7 @@
     settle(weights)
     for w in range(8):
         one_ref[w] = pack_ref[...]
+        q_ref[w] = packq_ref[...]
     settle(later)
 
 
@@ -977,9 +989,10 @@
     other_pieces = [send(other, step) for step in steps]
 
     line = lambda v: v.reshape(1, -1)
-    pack1, pack3 = call(
-        pack_rest_kernel, [((8, SMALL + 32, 256), BF, FREE), ((576, 256), BF, FREE)], [SMEM] + [HBM] * 14,
-        [pltpu.VMEM((SMALL + 32, 256), BF)] + [pltpu.VMEM((1, 64), BF)] * 4
+    pack1, packq, pack3 = call(
+        pack_rest_kernel,
+        [((8, SMALL + 32, 256), BF, FREE), ((8, 192, 256), BF, FREE), ((576, 256), BF, FREE)], [SMEM] + [HBM] * 14,
+        [pltpu.VMEM((SMALL + 32, 256), BF), pltpu.VMEM((192, 256), BF)] + [pltpu.VMEM((1, 64), BF)] * 4
         + [pltpu.VMEM((9, 256), BF), pltpu.VMEM((1, 256), BF), dma((17,))],
         "pack_rest", 1, info, glu_value, glu_gate, query_weight, key_weight, value_weight,
         line(glu_gain), line(conv_gain), line(attn_gain), line(ffn_gain), depth_weight,
@@ -988,6 +1001,8 @@
 
     pack1, *_ = lax.optimization_barrier((pack1, *own_pieces, other))
     near1 = lax.all_to_all(pack1, WT, 0, 0, tiled=True)
+    packq, _ = lax.optimization_barrier((packq, near1))
+    nearq = lax.all_to_all(packq, WT, 0, 0, tiled=True)
     x = inputs[0]
     low_x = send(x[rows - RIM:], along(1))
     high_x = send(x[:RIM], along(-1))
@@ -1009,17 +1024,23 @@
         [SMEM] + [FREE] * 3 + [ANY] * 2, [pltpu.VMEM((2, 8, 128, 256), BF), tiny, dma((3,))], "glu", 3,
         info, low_x, x, high_x, near1, far1,
     )
-    n2, wp, np_, nm, mean, scale, sp, h2, n3, qkv, two, one = call(
+    n2, wp, np_, nm, mean, scale, sp, h2, n3, two, one = call(
         conv_kernel,
         [((rim_rows, width), BF), ((rim_rows, units), F32, HBM), ((rim_rows, 256), F32),
          ((rim_rows, units), BF, HBM), ((rim_rows, 128), F32), ((rim_rows, 128), F32),
-         (wide, BF, HBM), (tall, F32), (tall, BF), ((HEADS, 3 * HEAD, rows), BF, FREE),
+         (wide, BF, HBM), (tall, F32), (tall, BF),
          (ring.shape, BF, HBM), ((2,) + near1.shape, BF, HBM)],
         [SMEM, FREE] + [ANY] * 18,
         [ring, pltpu.VMEM((2,) + near1.shape, BF), pltpu.VMEM((rim_rows, units), F32),
          pltpu.VMEM((rim_rows, units), F32), pltpu.VMEM((rim_rows, units), BF), pltpu.VMEM(wide, BF),
          pltpu.VMEM((2, rim_rows, 128), F32), dma((16,)), dma((2,)), dma((3, 8))],
         "conv", 15, info, h1, *near2, *far2, near1, far1,
+    )
+    nearq, _ = lax.optimization_barrier((nearq, n3))
+    qkv, wq = call(
+        queries_kernel, [((HEADS, 3 * HEAD, rows), BF, FREE), ((2, 8, 192, 256), BF, HBM)],
+        [SMEM, VMEM, ANY, ANY], [pltpu.VMEM((2, 8, 192, 256), BF), dma((2,))], "queries", 1,
+        info, n3, nearq, send(nearq, flip),
     )
     near = lax.all_to_all(qkv, CHIPS, 0, 0, tiled=True)
     far = send(near[:, HEAD:], flip)
@@ -1033,7 +1054,7 @@
          ((1, width), F32), ((HEADS, HEAD, rows), BF, FREE)],
         [SMEM, VMEM, FREE, VMEM, HBM, HBM, ANY],
         [pltpu.VMEM((2, 2, 4) + pack3.shape, BF), tiny, pltpu.VMEM(tall, F32), pltpu.VMEM(tall, F32),
-         dma((5,))],
+         dma((5,)), dma((4,))],
         "ffn", 11, info, h2, heads_in, cotangent[0], one, near3, far3,
     )
 
@@ -1054,10 +1075,10 @@
     g2, gs, lo, hi, d_gatt = call(
         attn_in_kernel,
         [(tall, F32), (narrow, BF, FREE), ((RIM, 256), BF), ((RIM, 256), BF), ((1, width), F32)],
-        [SMEM, FREE] + [HBM] * 3,
-        [pltpu.VMEM((2, 8, SMALL - 128, 256), BF), tiny, pltpu.VMEM(tall, F32), pltpu.VMEM(tall, F32),
+        [SMEM, FREE] + [HBM] * 4,
+        [pltpu.VMEM((2, 8, 192, 256), BF), tiny, pltpu.VMEM(tall, F32), pltpu.VMEM(tall, F32),
          dma((4,))],
-        "attn_in", 0.5, info_attn, d_qkv, h2, g3, one,
+        "attn_in", 0.5, info_attn, d_qkv, h2, g3, one, wq,
     )
     low_gs = send(hi, along(1))
     high_gs = send(lo, along(-1))

time: 317 us -> 317 us (level)
  waiting for transfers between devices: 75.9 us -> 69.7 us
  starting transfers between devices: 72.8 us -> 78.6 us
    ppermute x40 -> x41, waiting for transfers between devices: 59.4 us -> 53.2 us  [send(): return lax.ppermute(value, AXES, pairs)]
    all_to_all x0 -> x1, starting transfers between devices: none -> 3.86 us  [shards(): nearq = lax.all_to_all(packq, WT, 0, 0, tiled=True)]
    ppermute x40 -> x41, starting transfers between devices: 42.9 us -> 44.3 us  [send(): return lax.ppermute(value, AXES, pairs)]
    pallas_call x13 -> x14, Pallas kernels: 61.5 us -> 62.6 us  [call(): pl.pallas_call(kernel, in_specs=[VMEM if spec is FREE else spec for spec...]
  transfers between devices with their start and end apart: 48 -> 50, of which waited for: 16 -> 17; matrix products, arithmetic and copies ran while one was open for 2% -> 2% of each run, Pallas kernels for 26% -> 27%
where the time goes in v6:
time: 317 us; the launch traced here: 315 us
  Pallas kernels  96.1 us (30%)
  starting transfers between devices  78.6 us (25%)
  waiting for transfers between devices  69.7 us (22%)
  blocking collectives  49.8 us (16%)
  between operations  14.9 us (5%)
  other arithmetic  4.76 us (2%)
    pallas_call x14, Pallas kernels, call(): pl.pallas_call(kernel, in_specs=[VMEM if spec is FREE else spec for spec...  62.6 us
    ppermute x41, waiting for transfers between devices, send(): return lax.ppermute(value, AXES, pairs)  53.2 us
    ppermute x41, starting transfers between devices, send(): return lax.ppermute(value, AXES, pairs)  44.3 us
    all_to_all x1, blocking collectives, shards(): near = lax.all_to_all(qkv, CHIPS, 0, 0, tiled=True)  20.8 us
    pallas_call x1, Pallas kernels, attend_back(): pl.pallas_call(functools.partial(attend_back_kernel, chips, rows), grid=(...  19.5 us
    all_to_all x1, blocking collectives, spread_out(): return lax.all_to_all(copies, axes, 0, 0, tiled=True)  17 us
    pallas_call x1, Pallas kernels, attend(): pl.pallas_call(functools.partial(attend_kernel, chips, rows), grid=(chips...  14 us
    all_to_all x1, waiting for transfers between devices, shards(): d_qkv = lax.all_to_all(d_qkv, CHIPS, 0, 0, tiled=True)  13.6 us
  transfers between devices with their start and end apart: 50, of which 17 were waited for; matrix products, arithmetic and copies ran while one was open for 2% of the time, Pallas kernels for 27%

profile of v6, /device:TPU:1, one launch (start us, length us, event | category | flops | bytes accessed | tf_op | source)
XLA Modules:
  0.0 315.4 jit_solution(8018590950384904309)
XLA Ops:
  8.0 1.6 pack_ring.1.refs_0_
  9.5 4.7 %collective-permute-start = (bf16[512,256]{1,0:T(8,128)(2,1)S(1)}, bf16[512,256]{1,0:T(8,128)(2,1)S(1)}, u32[]{:S(2)}, u32[]{:S(2)}) collective-permute-start(bf16[512,256]{1,0:T(8,128)(2,1)S(1)} %pack_ring.1.refs_0_), channel_id=1, source_target_pairs={{0,3},{1,0},{2,1},{3,2},{4,7},{5,4},{6,5},{7,6},{8,11},{9,8},{10,9... | collective-permute-start | bytes 786440 | tf_op jit(solution)/shard_map/ppermute | solution.py:54
  16.7 3.1 pack_rest.1
  19.8 4.9 %collective-permute-done.refs_1_ = bf16[512,256]{1,0:T(8,128)(2,1)S(1)} collective-permute-done((bf16[512,256]{1,0:T(8,128)(2,1)S(1)}, bf16[512,256]{1,0:T(8,128)(2,1)S(1)}, u32[]{:S(2)}, u32[]{:S(2)}) %collective-permute-start) | collective-permute-done | bytes 262176 | tf_op jit(solution)/shard_map/ppermute | solution.py:54
  24.7 4.3 %collective-permute-done.2.refs_3_ = bf16[512,256]{1,0:T(8,128)(2,1)S(1)} collective-permute-done((bf16[512,256]{1,0:T(8,128)(2,1)S(1)}, bf16[512,256]{1,0:T(8,128)(2,1)S(1)}, u32[]{:S(2)}, u32[]{:S(2)}) %collective-permute-start.2) | collective-permute-done | bytes 262176 | tf_op jit(solution)/shard_map/ppermute | solution.py:54
  28.9 3.5 %all-to-all-start = ((bf16[8,160,256]{2,1,0:T(8,128)(2,1)}), bf16[8,160,256]{2,1,0:T(8,128)(2,1)S(1)}, u32[]{:S(2)}, u32[]{:S(2)}) async-start(bf16[8,160,256]{2,1,0:T(8,128)(2,1)} %get-tuple-element.106), calls=%async_computation | async-start | bytes 1310720 | tf_op jit(solution)/shard_map/all_to_all | solution.py:1003
  33.9 2.4 collective-permute-start.7
  37.4 6.8 %collective-permute-start.5 = (bf16[8,512]{1,0:T(8,128)(2,1)S(1)}, bf16[8,512]{1,0:T(8,128)(2,1)S(1)}, u32[]{:S(2)}, u32[]{:S(2)}) collective-permute-start(bf16[8,512]{1,0:T(8,128)(2,1)S(1)} %get-tuple-element.192), channel_id=1, source_target_pairs={{0,8},{1,9},{2,10},{3,11},{4,12},{5,13},{6,14},{7,15},{8,16},{9,17... | collective-permute-start | bytes 24584 | tf_op jit(solution)/shard_map/ppermute | solution.py:54
  44.2 1.4 collective-permute-done.5.low_ref
  45.6 1.9 collective-permute-start.6
  47.5 5.3 %collective-permute-done.6.high_ref = bf16[8,512]{1,0:T(8,128)(2,1)S(1)} collective-permute-done((bf16[8,512]{1,0:T(8,128)(2,1)S(1)}, bf16[8,512]{1,0:T(8,128)(2,1)S(1)}, u32[]{:S(2)}, u32[]{:S(2)}) %collective-permute-start.6) | collective-permute-done | bytes 8224 | tf_op jit(solution)/shard_map/ppermute | solution.py:54
  56.4 3.9 %all-to-all-start.1 = ((bf16[8,192,256]{2,1,0:T(8,128)(2,1)}), bf16[8,192,256]{2,1,0:T(8,128)(2,1)S(1)}, u32[]{:S(2)}, u32[]{:S(2)}) async-start(bf16[8,192,256]{2,1,0:T(8,128)(2,1)} %get-tuple-element.121), calls=%async_computation.1 | async-start | bytes 1572864 | tf_op jit(solution)/shard_map/all_to_all | solution.py:1005
  60.3 1.9 pad_maximum_fusion
  63.6 2.3 glu.1
  66.0 10.4 %conv.1 = (bf16[272,512]{1,0:T(8,128)(2,1)}, f32[272,2048]{1,0:T(8,128)}, f32[272,256]{1,0:T(8,128)}, bf16[272,2048]{1,0:T(8,128)(2,1)}, f32[272,128]{1,0:T(8,12...) custom-call(s32[6]{0:T(128)S(1)} %stack.32.info_ref, ...), custom_call_target="tpu_custom_call" | custom-call | flops 15000000512 | bytes 45000000 | tf_op jit(solution)/shard_map/conv/pallas_call | solution.py:271
  76.9 1.9 collective-permute-done.19.far_ref
  78.8 2.3 queries.1
  81.1 20.8 %all_to_all.45.near_ref = bf16[8,192,256]{2,1,0:T(8,128)(2,1)S(1)} all-to-all(bf16[8,192,256]{2,1,0:T(8,128)(2,1)S(1)} %get-tuple-element.123), channel_id=1, replica_groups=mesh['y'=4,'xh'=2,'core'=2,'xl'=2,'z'=4] {'y','xh'}, dimensions={0} | all-to-all | bytes 1572864 | tf_op jit(solution)/shard_map/all_to_all | solution.py:1045
  101.9 2.1 collective-permute-start.20
  104.0 1.5 collective-permute-done.20.far_ref
  105.6 14.0 %attend.1 = (bf16[8,64,256]{2,1,0:T(8,128)(2,1)}, bf16[2048,4096]{1,0:T(8,128)(2,1)}, f32[8,8,256]{2,1,0:T(8,128)}, bf16[8,192,256]{2,1,0:T(8,128)(2,1)}, bf16[8,128,256]{2,1,0:T(8,128)(2,1)}) custom-call(s32[1]{0:T(128)S(6)} %copy.39.length_ref, s32[1]{0:T(128)} %bitcast.core_ref, bf16[8,192,256]{2,1,0:T(8,128)(2,1)S(1)} %all_to_all.45.near_ref, ...), custom_call_target="tpu_custom_call" | custom-call | flops 14000000000 | bytes 42000000 | tf_op jit(solution)/shard_map/attend/pallas_call | solution.py:135
  120.1 12.1 %all_to_all.46.o_ref = bf16[8,64,256]{2,1,0:T(8,128)(2,1)S(1)} all-to-all(bf16[8,64,256]{2,1,0:T(8,128)(2,1)} %get-tuple-element.124.o_ref), channel_id=1, replica_groups=mesh['y'=4,'xh'=2,'core'=2,'xl'=2,'z'=4] {'y','xh'}, dimensions={0} | all-to-all | bytes 524288 | tf_op jit(solution)/shard_map/all_to_all | solution.py:1050
  132.2 7.5 %ffn.1 = (bf16[256,512]{1,0:T(8,128)(2,1)}, bf16[256,5632]{1,0:T(8,128)(2,1)S(1)}, f32[256,512]{1,0:T(8,128)}, bf16[8,64,256]{2,1,0:T(8,128)(2,1)}, f32[1,512]{1,0:T(1,128)}, /*index=5*/bf16[8,64,256]{2,1,0:T(8,128)(2,1)S(1)}) custom-call(s32[6]{0:T(128)S(1)} %stack.32.info_ref, f32[256,512]{1,0:T(8,128)} %get-tuple-element.118.h2_ref.h2_in, ...), custom_call_target="tpu_custom_call" | custom-call | flops 11000000512 | bytes 33000000 | tf_op jit(solution)/shard_map/ffn/pallas_call | solution.py:271
  140.8 3.4 %all-to-all-start.4 = ((bf16[8,64,256]{2,1,0:T(8,128)(2,1)}), bf16[8,64,256]{2,1,0:T(8,128)(2,1)S(1)}, u32[]{:S(2)}, u32[]{:S(2)}) async-start(bf16[8,64,256]{2,1,0:T(8,128)(2,1)} %get-tuple-element.130), calls=%async_computation.4 | async-start | bytes 524288 | tf_op jit(solution)/shard_map/all_to_all | solution.py:1061
  144.3 1.9 collective-permute-done.23.heads2_ref
  146.1 4.8 %early.1 = bf16[2,2,4,4,144,128]{5,4,3,2,1,0:T(8,128)(2,1)} custom-call(s32[6]{0:T(128)S(1)} %stack.32.info_ref, bf16[256,5632]{1,0:T(8,128)(2,1)S(1)} %get-tuple-element.131.acts_ref, bf16[8,64,256]{2,1,0:T(8,128)(2,1)S(1)} %get-tuple-element.132.heads_ref, bf16[256,5632]{1,0:T(8,128)(2,1)} %collective-permute-done.22.acts2_ref, ...), custom_call_target="tpu_custom_call" | custom-call | flops 300000000 | bytes 900000 | tf_op jit(solution)/shard_map/early/pallas_call | solution.py:271
  150.9 1.8 all-to-all-done.4.do_ref
  152.7 19.5 %attend_back.1 = (bf16[8,192,256]{2,1,0:T(8,128)(2,1)S(1)}, bf16[8,128,256]{2,1,0:T(8,128)(2,1)S(1)}) custom-call(bf16[8,192,256]{2,1,0:T(8,128)(2,1)} %get-tuple-element.137.near_ref, bf16[8,128,256]{2,1,0:T(8,128)(2,1)} %get-tuple-element.138.far_ref, bf16[2048,4096]{1,0:T(8,128)(2,1)} %get-tuple-element.139.e_ref, ...), custom_call_target="tpu_custom_call" | custom-call | flops 3000000000 | bytes 9000000 | tf_op jit(solution)/shard_map/attend_back/pallas_call | solution.py:229
  173.5 1.5 collective-permute-done.25
  176.1 3.5 %all-to-all-start.5 = ((bf16[8,192,256]{2,1,0:T(8,128)(2,1)}), bf16[8,192,256]{2,1,0:T(8,128)(2,1)S(1)}, u32[]{:S(2)}, u32[]{:S(2)}) async-start(bf16[8,192,256]{2,1,0:T(8,128)(2,1)} %add_convert_fusion), calls=%async_computation.7 | async-start | bytes 1572864 | tf_op jit(solution)/shard_map/all_to_all | solution.py:1071
  180.1 13.6 %all-to-all-done.5.d_ref = bf16[8,192,256]{2,1,0:T(8,128)(2,1)S(1)} async-done(((bf16[8,192,256]{2,1,0:T(8,128)(2,1)}), bf16[8,192,256]{2,1,0:T(8,128)(2,1)S(1)}, u32[]{:S(2)}, u32[]{:S(2)}) %all-to-all-start.5) | async-done | bytes 786464 | tf_op jit(solution)/shard_map/all_to_all | solution.py:1071
  195.0 3.8 %attn_in.1 = (f32[256,512]{1,0:T(8,128)}, bf16[256,256]{1,0:T(8,128)(2,1)S(1)}, bf16[8,256]{1,0:T(8,128)(2,1)}, bf16[8,256]{1,0:T(8,128)(2,1)}, f32[1,512]{1,0:T(1,128)}) custom-call(s32[6]{0:T(128)S(1)} %stack.32.info_ref, bf16[8,192,256]{2,1,0:T(8,128)(2,1)S(1)} %all-to-all-done.5.d_ref, f32[256,512]{1,0:T(8,128)} %get-tuple-element.118.h2_ref.h2_in, ...), custom_call_target="tpu_custom_call" | custom-call | flops 500000000 | bytes 1500000 | tf_op jit(solution)/shard_map/attn_in/pallas_call | solution.py:271
  199.5 2.4 collective-permute-start.26
  201.8 1.9 collective-permute-start.27
  203.8 4.7 %collective-permute-done.27.hi_ref = bf16[8,256]{1,0:T(8,128)(2,1)S(1)} collective-permute-done((bf16[8,256]{1,0:T(8,128)(2,1)}, bf16[8,256]{1,0:T(8,128)(2,1)S(1)}, u32[]{:S(2)}, u32[]{:S(2)}) %collective-permute-start.27) | collective-permute-done | bytes 4128 | tf_op jit(solution)/shard_map/ppermute | solution.py:54
  208.5 3.4 %middle.1 = bf16[8,8,80,128]{3,2,1,0:T(8,128)(2,1)} custom-call(s32[6]{0:T(128)S(1)} %stack.32.info_ref, bf16[256,2048]{1,0:T(8,128)(2,1)} %get-tuple-element.135.sp_ref, bf16[256,256]{1,0:T(8,128)(2,1)S(1)} %get-tuple-element.149.gs_ref, bf16[256,512]{1,0:T(8,128)(2,1)} %get-tuple-element.119.n3_ref, bf16[8,192,256]{2,1,0:T(8,128)(2,1)S(1)} %all-to-all-done.5.d_ref, ...), custom_call_target="tpu_custom_call" | custom-call | flops 300000000 | bytes 900000 | tf_op jit(solution)/shard_map/middle/pallas_call | solution.py:271
  211.9 9.9 %all-to-all-start.6 = ((bf16[64,80,128]{2,1,0:T(8,128)(2,1)}), bf16[64,80,128]{2,1,0:T(8,128)(2,1)}, u32[]{:S(2)}, u32[]{:S(2)}) async-start(bf16[64,80,128]{2,1,0:T(8,128)(2,1)} %bitcast.44), calls=%async_computation.8 | async-start | bytes 2621440 | tf_op jit(solution)/shard_map/all_to_all | solution.py:1091
  221.8 11.2 %conv_back.1 = (bf16[256,2048]{1,0:T(8,128)(2,1)S(1)}, bf16[272,256]{1,0:T(8,128)(2,1)S(1)}, f32[16,2048]{1,0:T(8,128)S(1)}) custom-call(s32[6]{0:T(128)S(1)} %stack.32.info_ref, bf16[8,256]{1,0:T(8,128)(2,1)S(1)} %collective-permute-done.26.lo_ref, bf16[256,256]{1,0:T(8,128)(2,1)S(1)} %get-tuple-element.149.gs_ref, ...), custom_call_target="tpu_custom_call" | custom-call | flops 2000000000 | bytes 6000000 | tf_op jit(solution)/shard_map/conv_back/pallas_call | solution.py:271
  233.1 5.5 %glu_back.1 = (f32[256,512]{1,0:T(8,128)}, bf16[256,1024]{1,0:T(8,128)(2,1)S(1)}, f32[24,2048]{1,0:T(8,128)S(1)}) custom-call(s32[6]{0:T(128)S(1)} %stack.32.info_ref, bf16[256,2048]{1,0:T(8,128)(2,1)S(1)} %get-tuple-element.157.dw_ref, bf16[272,256]{1,0:T(8,128)(2,1)S(1)} %get-tuple-element.158.dnar_ref, f32[256,512]{1,0:T(8,128)} %get-tuple-element.159.h1_in, ...), custom_call_target="tpu_custom_call" | custom-call | flops 1000000000 | bytes 3000000 | tf_op jit(solution)/shard_map/glu_back/pallas_call | solution.py:271
  242.5 3.8 %late.1 = bf16[8,8,128,128]{3,2,1,0:T(8,128)(2,1)} custom-call(s32[6]{0:T(128)S(1)} %stack.32.info_ref, bf16[272,512]{1,0:T(8,128)(2,1)} %get-tuple-element.167.n2_ref, bf16[256,2048]{1,0:T(8,128)(2,1)S(1)} %get-tuple-element.157.dw_ref, bf16[272,256]{1,0:T(8,128)(2,1)S(1)} %get-tuple-element.158.dnar_ref, bf16[256,512]{1,0:T(8,128)(2,1)} %get-tuple-element.168.n1_ref, ...), custom_call_target="tpu_custom_call" | custom-call | flops 500000000 | bytes 1500000 | tf_op jit(solution)/shard_map/late/pallas_call | solution.py:271
  246.3 9.8 %all-to-all-start.7 = ((bf16[64,128,128]{2,1,0:T(8,128)(2,1)}), bf16[64,128,128]{2,1,0:T(8,128)(2,1)S(1)}, u32[]{:S(2)}, u32[]{:S(2)}) async-start(bf16[64,128,128]{2,1,0:T(8,128)(2,1)} %bitcast.43), calls=%async_computation.9 | async-start | bytes 4194304 | tf_op jit(solution)/shard_map/all_to_all | solution.py:1127
  257.4 2.6 collective-permute-start.38
  261.0 1.5 reduce_sum.24
  262.6 20.8 %collective-permute-done.37.refs_1_ = bf16[144,128]{1,0:T(8,128)(2,1)S(1)} collective-permute-done((bf16[144,128]{1,0:T(8,128)(2,1)S(1)}, bf16[144,128]{1,0:T(8,128)(2,1)S(1)}, u32[]{:S(2)}, u32[]{:S(2)}) %collective-permute-start.37) | collective-permute-done | bytes 36896 | tf_op jit(solution)/shard_map/ppermute | solution.py:54
  284.9 17.0 %all_to_all.47.near_ref = bf16[8,352,128]{2,1,0:T(8,128)(2,1)S(1)} all-to-all(bf16[8,352,128]{2,1,0:T(8,128)(2,1)S(1)} %broadcast_in_dim.14), channel_id=1, replica_groups=mesh['y'=4,'xh'=2,'core'=2,'xl'=2,'z'=4] {'y','xh'}, dimensions={0} | all-to-all | bytes 1441792 | tf_op jit(solution)/shard_map/all_to_all | solution.py:963
  301.9 2.3 collective-permute-start.40
  304.1 1.8 collective-permute-done.40.far_ref
  306.0 2.9 unpack.1
  (107 shorter events, 24.8 us)
Async XLA Ops:
  9.5 15.1 %collective-permute-start = (bf16[512,256]{1,0:T(8,128)(2,1)S(1)}, bf16[512,256]{1,0:T(8,128)(2,1)S(1)}, u32[]{:S(2)}, u32[]{:S(2)}) collective-permute-start(bf16[512,256]{1,0:T(8,128)(2,1)S(1)} %pack_ring.1.refs_0_), channel_id=1, source_target_pairs={{0,3},{1,0},{2,1},{3,2},{4,7},{5,4},{6,5},{7,6},{8,11},{9,8},{10,9... | collective-permute-start | bytes 786440 | tf_op jit(solution)/shard_map/ppermute | solution.py:54
  14.2 10.5 %collective-permute-start.1 = (bf16[512,256]{1,0:T(8,128)(2,1)S(1)}, bf16[512,256]{1,0:T(8,128)(2,1)}, u32[]{:S(2)}, u32[]{:S(2)}) collective-permute-start(bf16[512,256]{1,0:T(8,128)(2,1)S(1)} %pack_ring.1.refs_0_), channel_id=1, source_target_pairs={{0,2},{1,3},{2,0},{3,1},{4,6},{5,7},{6,4},{7,5},{8,10},{9,11},{10,... | collective-permute-start | bytes 786440 | tf_op jit(solution)/shard_map/ppermute | solution.py:54
  14.2 14.7 %collective-permute-start.2 = (bf16[512,256]{1,0:T(8,128)(2,1)S(1)}, bf16[512,256]{1,0:T(8,128)(2,1)S(1)}, u32[]{:S(2)}, u32[]{:S(2)}) collective-permute-start(bf16[512,256]{1,0:T(8,128)(2,1)S(1)} %pack_ring.1.refs_0_), channel_id=1, source_target_pairs={{0,1},{1,2},{2,3},{3,0},{4,5},{5,6},{6,7},{7,4},{8,9},{9,10},{10,1... | collective-permute-start | bytes 786440 | tf_op jit(solution)/shard_map/ppermute | solution.py:54
  14.9 14.0 %collective-permute-start.3 = (bf16[512,256]{1,0:T(8,128)(2,1)S(1)}, bf16[512,256]{1,0:T(8,128)(2,1)}, u32[]{:S(2)}, u32[]{:S(2)}) collective-permute-start(bf16[512,256]{1,0:T(8,128)(2,1)S(1)} %pack_ring.1.refs_0_), channel_id=1, source_target_pairs={{0,4},{1,5},{2,6},{3,7},{4,0},{5,1},{6,2},{7,3},{8,12},{9,13},{10,... | collective-permute-start | bytes 786440 | tf_op jit(solution)/shard_map/ppermute | solution.py:54
  28.9 25.5 %all-to-all-start = ((bf16[8,160,256]{2,1,0:T(8,128)(2,1)}), bf16[8,160,256]{2,1,0:T(8,128)(2,1)S(1)}, u32[]{:S(2)}, u32[]{:S(2)}) async-start(bf16[8,160,256]{2,1,0:T(8,128)(2,1)} %get-tuple-element.106), calls=%async_computation | async-start | bytes 1310720 | tf_op jit(solution)/shard_map/all_to_all | solution.py:1003
  32.5 20.4 %collective-permute-start.4 = (bf16[576,256]{1,0:T(8,128)(2,1)S(1)}, bf16[576,256]{1,0:T(8,128)(2,1)S(1)}, u32[]{:S(2)}, u32[]{:S(2)}) collective-permute-start(bf16[576,256]{1,0:T(8,128)(2,1)S(1)} %get-tuple-element.126), channel_id=1, source_target_pairs={{0,4},{1,5},{2,6},{3,7},{4,0},{5,1},{6,2},{7,3},{8,12},{9,13},{10,... | collective-permute-start | bytes 884744 | tf_op jit(solution)/shard_map/ppermute | solution.py:54
  33.9 19.0 %collective-permute-start.7 = (bf16[512,256]{1,0:T(8,128)(2,1)}, bf16[512,256]{1,0:T(8,128)(2,1)S(1)}, u32[]{:S(2)}, u32[]{:S(2)}) collective-permute-start(bf16[512,256]{1,0:T(8,128)(2,1)} %collective-permute-done.3.refs_4_), channel_id=1, source_target_pairs={{0,3},{1,0},{2,1},{3,2},{4,7},{5,4},{6,5},{7,6},{8,11},{9,8},{10,9... | collective-permute-start | bytes 786440 | tf_op jit(solution)/shard_map/ppermute | solution.py:54
  36.3 16.6 %collective-permute-start.8 = (bf16[512,256]{1,0:T(8,128)(2,1)}, bf16[512,256]{1,0:T(8,128)(2,1)S(1)}, u32[]{:S(2)}, u32[]{:S(2)}) collective-permute-start(bf16[512,256]{1,0:T(8,128)(2,1)} %collective-permute-done.3.refs_4_), channel_id=1, source_target_pairs={{0,2},{1,3},{2,0},{3,1},{4,6},{5,7},{6,4},{7,5},{8,10},{9,11},{10,... | collective-permute-start | bytes 786440 | tf_op jit(solution)/shard_map/ppermute | solution.py:54
  36.8 17.6 %collective-permute-start.9 = (bf16[512,256]{1,0:T(8,128)(2,1)}, bf16[512,256]{1,0:T(8,128)(2,1)}, u32[]{:S(2)}, u32[]{:S(2)}) collective-permute-start(bf16[512,256]{1,0:T(8,128)(2,1)} %collective-permute-done.3.refs_4_), channel_id=1, source_target_pairs={{0,1},{1,2},{2,3},{3,0},{4,5},{5,6},{6,7},{7,4},{8,9},{9,10},{10,1... | collective-permute-start | bytes 786440 | tf_op jit(solution)/shard_map/ppermute | solution.py:54
  37.4 8.2 %collective-permute-start.5 = (bf16[8,512]{1,0:T(8,128)(2,1)S(1)}, bf16[8,512]{1,0:T(8,128)(2,1)S(1)}, u32[]{:S(2)}, u32[]{:S(2)}) collective-permute-start(bf16[8,512]{1,0:T(8,128)(2,1)S(1)} %get-tuple-element.192), channel_id=1, source_target_pairs={{0,8},{1,9},{2,10},{3,11},{4,12},{5,13},{6,14},{7,15},{8,16},{9,17... | collective-permute-start | bytes 24584 | tf_op jit(solution)/shard_map/ppermute | solution.py:54
  45.6 7.2 %collective-permute-start.6 = (bf16[8,512]{1,0:T(8,128)(2,1)S(1)}, bf16[8,512]{1,0:T(8,128)(2,1)S(1)}, u32[]{:S(2)}, u32[]{:S(2)}) collective-permute-start(bf16[8,512]{1,0:T(8,128)(2,1)S(1)} %get-tuple-element.191), channel_id=1, source_target_pairs={{8,0},{9,1},{10,2},{11,3},{12,4},{13,5},{14,6},{15,7},{16,8},{17,9... | collective-permute-start | bytes 24584 | tf_op jit(solution)/shard_map/ppermute | solution.py:54
  54.4 9.1 %collective-permute-start.10 = (bf16[8,160,256]{2,1,0:T(8,128)(2,1)S(1)}, bf16[8,160,256]{2,1,0:T(8,128)(2,1)S(1)}, u32[]{:S(2)}, u32[]{:S(2)}) collective-permute-start(bf16[8,160,256]{2,1,0:T(8,128)(2,1)S(1)} %all-to-all-done.near_ref.refs_16_), channel_id=1, source_target_pairs={{0,8},{1,9},{2,10},{3,11},{4,12},{5,13},{6,14},{7,15},{8,0},{9,1},... | collective-permute-start | bytes 1966088 | tf_op jit(solution)/shard_map/ppermute | solution.py:54
  55.4 6.8 %collective-permute-start.11 = (bf16[512,256]{1,0:T(8,128)(2,1)S(1)}, bf16[512,256]{1,0:T(8,128)(2,1)}, u32[]{:S(2)}, u32[]{:S(2)}) collective-permute-start(bf16[512,256]{1,0:T(8,128)(2,1)S(1)} %pack_ring.1.refs_0_), channel_id=1, source_target_pairs={{0,8},{1,9},{2,10},{3,11},{4,12},{5,13},{6,14},{7,15},{8,0},{9,1},... | collective-permute-start | bytes 786440 | tf_op jit(solution)/shard_map/ppermute | solution.py:54
  55.4 7.5 %collective-permute-start.15 = (bf16[512,256]{1,0:T(8,128)(2,1)}, bf16[512,256]{1,0:T(8,128)(2,1)}, u32[]{:S(2)}, u32[]{:S(2)}) collective-permute-start(bf16[512,256]{1,0:T(8,128)(2,1)} %collective-permute-done.3.refs_4_), channel_id=1, source_target_pairs={{0,8},{1,9},{2,10},{3,11},{4,12},{5,13},{6,14},{7,15},{8,0},{9,1},... | collective-permute-start | bytes 786440 | tf_op jit(solution)/shard_map/ppermute | solution.py:54
  55.9 7.2 %collective-permute-start.12 = (bf16[512,256]{1,0:T(8,128)(2,1)S(1)}, bf16[512,256]{1,0:T(8,128)(2,1)}, u32[]{:S(2)}, u32[]{:S(2)}) collective-permute-start(bf16[512,256]{1,0:T(8,128)(2,1)S(1)} %collective-permute-done.refs_1_), channel_id=1, source_target_pairs={{0,8},{1,9},{2,10},{3,11},{4,12},{5,13},{6,14},{7,15},{8,0},{9,1},... | collective-permute-start | bytes 786440 | tf_op jit(solution)/shard_map/ppermute | solution.py:54
  56.0 9.9 %collective-permute-start.13 = (bf16[512,256]{1,0:T(8,128)(2,1)}, bf16[512,256]{1,0:T(8,128)(2,1)}, u32[]{:S(2)}, u32[]{:S(2)}) collective-permute-start(bf16[512,256]{1,0:T(8,128)(2,1)} %collective-permute-done.1.refs_2_), channel_id=1, source_target_pairs={{0,8},{1,9},{2,10},{3,11},{4,12},{5,13},{6,14},{7,15},{8,0},{9,1},... | collective-permute-start | bytes 786440 | tf_op jit(solution)/shard_map/ppermute | solution.py:54
  56.4 20.0 %all-to-all-start.1 = ((bf16[8,192,256]{2,1,0:T(8,128)(2,1)}), bf16[8,192,256]{2,1,0:T(8,128)(2,1)S(1)}, u32[]{:S(2)}, u32[]{:S(2)}) async-start(bf16[8,192,256]{2,1,0:T(8,128)(2,1)} %get-tuple-element.121), calls=%async_computation.1 | async-start | bytes 1572864 | tf_op jit(solution)/shard_map/all_to_all | solution.py:1005
  60.2 59.4 %all-gather.3.cloned.1.call-start = ((), (), s32[]{:S(2)}) async-start(), calls=%async_computation.13 | async-start | bytes 2949120 | tf_op jit(solution)/shard_map/all_gather | solution.py:1016
  62.2 3.7 %collective-permute-start.14 = (bf16[512,256]{1,0:T(8,128)(2,1)S(1)}, bf16[512,256]{1,0:T(8,128)(2,1)S(1)}, u32[]{:S(2)}, u32[]{:S(2)}) collective-permute-start(bf16[512,256]{1,0:T(8,128)(2,1)S(1)} %collective-permute-done.2.refs_3_), channel_id=1, source_target_pairs={{0,8},{1,9},{2,10},{3,11},{4,12},{5,13},{6,14},{7,15},{8,0},{9,1},... | collective-permute-start | bytes 786440 | tf_op jit(solution)/shard_map/ppermute | solution.py:54
  63.0 2.9 collective-permute-start.16
  63.1 2.8 collective-permute-start.17
  63.5 2.4 collective-permute-start.18
  76.4 2.4 collective-permute-start.19
  101.9 3.6 %collective-permute-start.20 = (bf16[8,128,256]{2,1,0:T(8,128)(2,1)S(1)}, bf16[8,128,256]{2,1,0:T(8,128)(2,1)S(1)}, u32[]{:S(2)}, u32[]{:S(2)}) collective-permute-start(bf16[8,128,256]{2,1,0:T(8,128)(2,1)S(1)} %slice.20), channel_id=1, source_target_pairs={{0,8},{1,9},{2,10},{3,11},{4,12},{5,13},{6,14},{7,15},{8,0},{9,1},... | collective-permute-start | bytes 1572872 | tf_op jit(solution)/shard_map/ppermute | solution.py:54
  119.6 12.5 %collective-permute-start.21 = (bf16[4,2,576,256]{3,2,1,0:T(8,128)(2,1)}, bf16[4,2,576,256]{3,2,1,0:T(8,128)(2,1)S(1)}, u32[]{:S(2)}, u32[]{:S(2)}) collective-permute-start(bf16[4,2,576,256]{3,2,1,0:T(8,128)(2,1)} %bitcast.48), channel_id=1, source_target_pairs={{0,8},{1,9},{2,10},{3,11},{4,12},{5,13},{6,14},{7,15},{8,0},{9,1},... | collective-permute-start | bytes 7077896 | tf_op jit(solution)/shard_map/ppermute | solution.py:54
  139.7 6.5 %collective-permute-start.22 = (bf16[256,5632]{1,0:T(8,128)(2,1)S(1)}, bf16[256,5632]{1,0:T(8,128)(2,1)}, u32[]{:S(2)}, u32[]{:S(2)}) collective-permute-start(bf16[256,5632]{1,0:T(8,128)(2,1)S(1)} %get-tuple-element.131.acts_ref), channel_id=1, source_target_pairs={{0,8},{1,9},{2,10},{3,11},{4,12},{5,13},{6,14},{7,15},{8,0},{9,1},... | collective-permute-start | bytes 8650760 | tf_op jit(solution)/shard_map/ppermute | solution.py:54
  140.7 5.4 %collective-permute-start.23 = (bf16[8,64,256]{2,1,0:T(8,128)(2,1)S(1)}, bf16[8,64,256]{2,1,0:T(8,128)(2,1)}, u32[]{:S(2)}, u32[]{:S(2)}) collective-permute-start(bf16[8,64,256]{2,1,0:T(8,128)(2,1)S(1)} %get-tuple-element.132.heads_ref), channel_id=1, source_target_pairs={{0,8},{1,9},{2,10},{3,11},{4,12},{5,13},{6,14},{7,15},{8,0},{9,1},... | collective-permute-start | bytes 786440 | tf_op jit(solution)/shard_map/ppermute | solution.py:54
  140.8 11.8 %all-to-all-start.4 = ((bf16[8,64,256]{2,1,0:T(8,128)(2,1)}), bf16[8,64,256]{2,1,0:T(8,128)(2,1)S(1)}, u32[]{:S(2)}, u32[]{:S(2)}) async-start(bf16[8,64,256]{2,1,0:T(8,128)(2,1)} %get-tuple-element.130), calls=%async_computation.4 | async-start | bytes 524288 | tf_op jit(solution)/shard_map/all_to_all | solution.py:1061
  144.2 50.7 %reduce-scatter.3.cloned.1.call-start = ((), (), s32[]{:S(2)}) async-start(), calls=%async_computation.11 | async-start | bytes 2949120 | tf_op jit(solution)/shard_map/reduce_scatter | solution.py:954
  172.1 2.9 collective-permute-start.25
  176.1 17.6 %all-to-all-start.5 = ((bf16[8,192,256]{2,1,0:T(8,128)(2,1)}), bf16[8,192,256]{2,1,0:T(8,128)(2,1)S(1)}, u32[]{:S(2)}, u32[]{:S(2)}) async-start(bf16[8,192,256]{2,1,0:T(8,128)(2,1)} %add_convert_fusion), calls=%async_computation.7 | async-start | bytes 1572864 | tf_op jit(solution)/shard_map/all_to_all | solution.py:1071
  179.6 53.5 %reduce-scatter.5.cloned.1.call-start = ((), (), s32[]{:S(2)}) async-start(), calls=%async_computation.12 | async-start | bytes 737280 | tf_op jit(solution)/shard_map/reduce_scatter | solution.py:958
  179.7 15.4 %collective-permute-start.24 = (bf16[256,2048]{1,0:T(8,128)(2,1)}, bf16[256,2048]{1,0:T(8,128)(2,1)S(1)}, u32[]{:S(2)}, u32[]{:S(2)}) collective-permute-start(bf16[256,2048]{1,0:T(8,128)(2,1)} %get-tuple-element.135.sp_ref), channel_id=1, source_target_pairs={{0,8},{1,9},{2,10},{3,11},{4,12},{5,13},{6,14},{7,15},{8,0},{9,1},... | collective-permute-start | bytes 3145736 | tf_op jit(solution)/shard_map/ppermute | solution.py:54
  193.7 14.8 %collective-permute-start.30 = (bf16[8,192,256]{2,1,0:T(8,128)(2,1)S(1)}, bf16[8,192,256]{2,1,0:T(8,128)(2,1)S(1)}, u32[]{:S(2)}, u32[]{:S(2)}) collective-permute-start(bf16[8,192,256]{2,1,0:T(8,128)(2,1)S(1)} %all-to-all-done.5.d_ref), channel_id=1, source_target_pairs={{0,8},{1,9},{2,10},{3,11},{4,12},{5,13},{6,14},{7,15},{8,0},{9,1},... | collective-permute-start | bytes 2359304 | tf_op jit(solution)/shard_map/ppermute | solution.py:54
  194.9 13.5 %collective-permute-start.29 = (bf16[256,512]{1,0:T(8,128)(2,1)S(1)}, bf16[256,512]{1,0:T(8,128)(2,1)S(1)}, u32[]{:S(2)}, u32[]{:S(2)}) collective-permute-start(bf16[256,512]{1,0:T(8,128)(2,1)S(1)} %copy-done.8), channel_id=1, source_target_pairs={{0,8},{1,9},{2,10},{3,11},{4,12},{5,13},{6,14},{7,15},{8,0},{9,1},... | collective-permute-start | bytes 786440 | tf_op jit(solution)/shard_map/ppermute | solution.py:54
  198.9 9.6 %collective-permute-start.28 = (bf16[256,256]{1,0:T(8,128)(2,1)S(1)}, bf16[256,256]{1,0:T(8,128)(2,1)S(1)}, u32[]{:S(2)}, u32[]{:S(2)}) collective-permute-start(bf16[256,256]{1,0:T(8,128)(2,1)S(1)} %get-tuple-element.149.gs_ref), channel_id=1, source_target_pairs={{0,8},{1,9},{2,10},{3,11},{4,12},{5,13},{6,14},{7,15},{8,0},{9,1},... | collective-permute-start | bytes 393224 | tf_op jit(solution)/shard_map/ppermute | solution.py:54
  199.5 4.3 %collective-permute-start.26 = (bf16[8,256]{1,0:T(8,128)(2,1)}, bf16[8,256]{1,0:T(8,128)(2,1)S(1)}, u32[]{:S(2)}, u32[]{:S(2)}) collective-permute-start(bf16[8,256]{1,0:T(8,128)(2,1)} %get-tuple-element.146), channel_id=1, source_target_pairs={{0,8},{1,9},{2,10},{3,11},{4,12},{5,13},{6,14},{7,15},{8,16},{9,17... | collective-permute-start | bytes 12296 | tf_op jit(solution)/shard_map/ppermute | solution.py:54
  201.8 6.6 %collective-permute-start.27 = (bf16[8,256]{1,0:T(8,128)(2,1)}, bf16[8,256]{1,0:T(8,128)(2,1)S(1)}, u32[]{:S(2)}, u32[]{:S(2)}) collective-permute-start(bf16[8,256]{1,0:T(8,128)(2,1)} %get-tuple-element.147), channel_id=1, source_target_pairs={{8,0},{9,1},{10,2},{11,3},{12,4},{13,5},{14,6},{15,7},{16,8},{17,9... | collective-permute-start | bytes 12296 | tf_op jit(solution)/shard_map/ppermute | solution.py:54
  211.9 34.5 %all-to-all-start.6 = ((bf16[64,80,128]{2,1,0:T(8,128)(2,1)}), bf16[64,80,128]{2,1,0:T(8,128)(2,1)}, u32[]{:S(2)}, u32[]{:S(2)}) async-start(bf16[64,80,128]{2,1,0:T(8,128)(2,1)} %bitcast.44), calls=%async_computation.8 | async-start | bytes 2621440 | tf_op jit(solution)/shard_map/all_to_all | solution.py:1091
  233.0 9.5 %collective-permute-start.32 = (bf16[256,2048]{1,0:T(8,128)(2,1)S(1)}, bf16[256,2048]{1,0:T(8,128)(2,1)S(1)}, u32[]{:S(2)}, u32[]{:S(2)}) collective-permute-start(bf16[256,2048]{1,0:T(8,128)(2,1)S(1)} %get-tuple-element.157.dw_ref), channel_id=1, source_target_pairs={{0,8},{1,9},{2,10},{3,11},{4,12},{5,13},{6,14},{7,15},{8,0},{9,1},... | collective-permute-start | bytes 3145736 | tf_op jit(solution)/shard_map/ppermute | solution.py:54
  238.7 3.8 %collective-permute-start.35 = (bf16[256,1024]{1,0:T(8,128)(2,1)S(1)}, bf16[256,1024]{1,0:T(8,128)(2,1)S(1)}, u32[]{:S(2)}, u32[]{:S(2)}) collective-permute-start(bf16[256,1024]{1,0:T(8,128)(2,1)S(1)} %get-tuple-element.169.dab_ref), channel_id=1, source_target_pairs={{0,8},{1,9},{2,10},{3,11},{4,12},{5,13},{6,14},{7,15},{8,0},{9,1},... | collective-permute-start | bytes 1572872 | tf_op jit(solution)/shard_map/ppermute | solution.py:54
  239.3 2.2 collective-permute-start.31
  239.7 2.8 collective-permute-start.36
  246.3 38.1 %all-to-all-start.7 = ((bf16[64,128,128]{2,1,0:T(8,128)(2,1)}), bf16[64,128,128]{2,1,0:T(8,128)(2,1)S(1)}, u32[]{:S(2)}, u32[]{:S(2)}) async-start(bf16[64,128,128]{2,1,0:T(8,128)(2,1)} %bitcast.43), calls=%async_computation.9 | async-start | bytes 4194304 | tf_op jit(solution)/shard_map/all_to_all | solution.py:1127
  256.3 27.1 %collective-permute-start.37 = (bf16[144,128]{1,0:T(8,128)(2,1)S(1)}, bf16[144,128]{1,0:T(8,128)(2,1)S(1)}, u32[]{:S(2)}, u32[]{:S(2)}) collective-permute-start(bf16[144,128]{1,0:T(8,128)(2,1)S(1)} %get-tuple-element.195), channel_id=1, source_target_pairs={{0,32},{1,33},{2,34},{3,35},{4,36},{5,37},{6,38},{7,39},{8,40},{9,... | collective-permute-start | bytes 110600 | tf_op jit(solution)/shard_map/ppermute | solution.py:54
  257.4 26.0 %collective-permute-start.38 = (bf16[144,128]{1,0:T(8,128)(2,1)S(1)}, bf16[144,128]{1,0:T(8,128)(2,1)S(1)}, u32[]{:S(2)}, u32[]{:S(2)}) collective-permute-start(bf16[144,128]{1,0:T(8,128)(2,1)S(1)} %get-tuple-element.194), channel_id=1, source_target_pairs={{0,64},{1,65},{2,66},{3,67},{4,68},{5,69},{6,70},{7,71},{8,72},{9,... | collective-permute-start | bytes 110600 | tf_op jit(solution)/shard_map/ppermute | solution.py:54
  260.0 23.4 %collective-permute-start.39 = (bf16[144,128]{1,0:T(8,128)(2,1)S(1)}, bf16[144,128]{1,0:T(8,128)(2,1)S(1)}, u32[]{:S(2)}, u32[]{:S(2)}) collective-permute-start(bf16[144,128]{1,0:T(8,128)(2,1)S(1)} %get-tuple-element.193), channel_id=1, source_target_pairs={{0,96},{1,97},{2,98},{3,99},{4,100},{5,101},{6,102},{7,103},{8,104... | collective-permute-start | bytes 110600 | tf_op jit(solution)/shard_map/ppermute | solution.py:54
  301.9 4.1 %collective-permute-start.40 = (bf16[8,352,128]{2,1,0:T(8,128)(2,1)S(1)}, bf16[8,352,128]{2,1,0:T(8,128)(2,1)S(1)}, u32[]{:S(2)}, u32[]{:S(2)}) collective-permute-start(bf16[8,352,128]{2,1,0:T(8,128)(2,1)S(1)} %all_to_all.47.near_ref), channel_id=1, source_target_pairs={{0,8},{1,9},{2,10},{3,11},{4,12},{5,13},{6,14},{7,15},{8,0},{9,1},... | collective-permute-start | bytes 2162696 | tf_op jit(solution)/shard_map/ppermute | solution.py:54
  (13 other events, 82.8 us)
Sparse Core Ops, SparseCore 0:
  62.7 35.9 all-gather.2
  152.8 29.9 reduce-scatter.2
  195.1 17.1 reduce-scatter.4

commit v7 on v6

--- a/solution.py
+++ b/solution.py
@@ -1007,13 +1007,13 @@
     low_x = send(x[rows - RIM:], along(1))
     high_x = send(x[:RIM], along(-1))
     other3 = send(pack3, shift(dxl=1))
-    near1, pack3, other3, low_x, high_x, *ready = lax.optimization_barrier(
-        (near1, pack3, other3, low_x, high_x, *own_pieces, *other_pieces)
+    near1, shards3, low_x, high_x, *ready = lax.optimization_barrier(
+        (near1, jnp.stack([pack3, other3]), low_x, high_x, *own_pieces, *other_pieces)
     )
     near2 = [pack2] + ready[:3] + [other] + ready[3:]
     far2 = [send(piece, flip) for piece in near2]
     far1 = send(near1, flip)
-    near3 = lax.all_gather(jnp.stack([pack3, other3]), "z", axis=0)
+    near3 = lax.all_gather(shards3, "z", axis=0)
 
     tall, wide, narrow = (rows, width), (rows, units), (rows, 256)
     tiny = pltpu.VMEM((8, 32, 256), BF)

time: 317 us -> 315 us (level)
  transfers between devices with their start and end apart: 50 -> 50, of which waited for: 17 -> 16; matrix products, arithmetic and copies ran while one was open for 2% -> 1% of each run, Pallas kernels for 27% -> 27%
where the time goes in v7:
time: 315 us; the launch traced here: 314 us
  Pallas kernels  96 us (30%)
  starting transfers between devices  79.6 us (25%)
  waiting for transfers between devices  69 us (22%)
  blocking collectives  48.7 us (15%)
  between operations  14.9 us (5%)
  other arithmetic  3.8 us (1%)
    pallas_call x14, Pallas kernels, call(): pl.pallas_call(kernel, in_specs=[VMEM if spec is FREE else spec for spec...  62.5 us
    ppermute x41, waiting for transfers between devices, send(): return lax.ppermute(value, AXES, pairs)  51.8 us
    ppermute x41, starting transfers between devices, send(): return lax.ppermute(value, AXES, pairs)  45.2 us
    all_to_all x1, blocking collectives, shards(): near = lax.all_to_all(qkv, CHIPS, 0, 0, tiled=True)  19.7 us
    pallas_call x1, Pallas kernels, attend_back(): pl.pallas_call(functools.partial(attend_back_kernel, chips, rows), grid=(...  19.5 us
    all_to_all x1, blocking collectives, spread_out(): return lax.all_to_all(copies, axes, 0, 0, tiled=True)  17 us
    pallas_call x1, Pallas kernels, attend(): pl.pallas_call(functools.partial(attend_kernel, chips, rows), grid=(chips...  14 us
    all_to_all x1, waiting for transfers between devices, shards(): d_qkv = lax.all_to_all(d_qkv, CHIPS, 0, 0, tiled=True)  13.6 us
  transfers between devices with their start and end apart: 50, of which 16 were waited for; matrix products, arithmetic and copies ran while one was open for 1% of the time, Pallas kernels for 27%

profile of v7, /device:TPU:1, one launch (start us, length us, event | category | flops | bytes accessed | tf_op | source)
XLA Modules:
  0.0 313.6 jit_solution(9054904215770019839)
XLA Ops:
  7.9 1.6 pack_ring.1.refs_0_
  9.5 4.7 %collective-permute-start = (bf16[512,256]{1,0:T(8,128)(2,1)S(1)}, bf16[512,256]{1,0:T(8,128)(2,1)S(1)}, u32[]{:S(2)}, u32[]{:S(2)}) collective-permute-start(bf16[512,256]{1,0:T(8,128)(2,1)S(1)} %pack_ring.1.refs_0_), channel_id=1, source_target_pairs={{0,3},{1,0},{2,1},{3,2},{4,7},{5,4},{6,5},{7,6},{8,11},{9,8},{10,9... | collective-permute-start | bytes 786440 | tf_op jit(solution)/shard_map/ppermute | solution.py:54
  16.7 3.1 pack_rest.1
  19.8 4.9 %collective-permute-done.refs_1_ = bf16[512,256]{1,0:T(8,128)(2,1)S(1)} collective-permute-done((bf16[512,256]{1,0:T(8,128)(2,1)S(1)}, bf16[512,256]{1,0:T(8,128)(2,1)S(1)}, u32[]{:S(2)}, u32[]{:S(2)}) %collective-permute-start) | collective-permute-done | bytes 262176 | tf_op jit(solution)/shard_map/ppermute | solution.py:54
  24.7 4.3 %collective-permute-done.2.refs_3_ = bf16[512,256]{1,0:T(8,128)(2,1)S(1)} collective-permute-done((bf16[512,256]{1,0:T(8,128)(2,1)S(1)}, bf16[512,256]{1,0:T(8,128)(2,1)S(1)}, u32[]{:S(2)}, u32[]{:S(2)}) %collective-permute-start.2) | collective-permute-done | bytes 262176 | tf_op jit(solution)/shard_map/ppermute | solution.py:54
  28.9 3.5 %all-to-all-start = ((bf16[8,160,256]{2,1,0:T(8,128)(2,1)}), bf16[8,160,256]{2,1,0:T(8,128)(2,1)S(1)}, u32[]{:S(2)}, u32[]{:S(2)}) async-start(bf16[8,160,256]{2,1,0:T(8,128)(2,1)} %get-tuple-element.105), calls=%async_computation | async-start | bytes 1310720 | tf_op jit(solution)/shard_map/all_to_all | solution.py:1003
  32.5 1.4 collective-permute-start.4
  33.8 2.4 collective-permute-start.7
  37.4 6.8 %collective-permute-start.5 = (bf16[8,512]{1,0:T(8,128)(2,1)S(1)}, bf16[8,512]{1,0:T(8,128)(2,1)S(1)}, u32[]{:S(2)}, u32[]{:S(2)}) collective-permute-start(bf16[8,512]{1,0:T(8,128)(2,1)S(1)} %get-tuple-element.190), channel_id=1, source_target_pairs={{0,8},{1,9},{2,10},{3,11},{4,12},{5,13},{6,14},{7,15},{8,16},{9,17... | collective-permute-start | bytes 24584 | tf_op jit(solution)/shard_map/ppermute | solution.py:54
  44.2 3.1 collective-permute-done.4
  47.3 3.7 %collective-permute-start.6 = (bf16[8,512]{1,0:T(8,128)(2,1)S(1)}, bf16[8,512]{1,0:T(8,128)(2,1)S(1)}, u32[]{:S(2)}, u32[]{:S(2)}) collective-permute-start(bf16[8,512]{1,0:T(8,128)(2,1)S(1)} %get-tuple-element.189), channel_id=1, source_target_pairs={{8,0},{9,1},{10,2},{11,3},{12,4},{13,5},{14,6},{15,7},{16,8},{17,9... | collective-permute-start | bytes 24584 | tf_op jit(solution)/shard_map/ppermute | solution.py:54
  51.9 3.1 collective-permute-done.6.high_ref
  56.9 4.0 %all-to-all-start.1 = ((bf16[8,192,256]{2,1,0:T(8,128)(2,1)}), bf16[8,192,256]{2,1,0:T(8,128)(2,1)S(1)}, u32[]{:S(2)}, u32[]{:S(2)}) async-start(bf16[8,192,256]{2,1,0:T(8,128)(2,1)} %get-tuple-element.120), calls=%async_computation.1 | async-start | bytes 1572864 | tf_op jit(solution)/shard_map/all_to_all | solution.py:1005
  63.0 2.3 glu.1
  65.4 10.3 %conv.1 = (bf16[272,512]{1,0:T(8,128)(2,1)}, f32[272,2048]{1,0:T(8,128)}, f32[272,256]{1,0:T(8,128)}, bf16[272,2048]{1,0:T(8,128)(2,1)}, f32[272,128]{1,0:T(8,12...) custom-call(s32[6]{0:T(128)S(1)} %stack.32.info_ref, ...), custom_call_target="tpu_custom_call" | custom-call | flops 15000000512 | bytes 45000000 | tf_op jit(solution)/shard_map/conv/pallas_call | solution.py:271
  76.2 1.9 collective-permute-done.19.far_ref
  78.1 2.3 queries.1
  80.4 19.7 %all_to_all.45.near_ref = bf16[8,192,256]{2,1,0:T(8,128)(2,1)S(1)} all-to-all(bf16[8,192,256]{2,1,0:T(8,128)(2,1)S(1)} %get-tuple-element.122), channel_id=1, replica_groups=mesh['y'=4,'xh'=2,'core'=2,'xl'=2,'z'=4] {'y','xh'}, dimensions={0} | all-to-all | bytes 1572864 | tf_op jit(solution)/shard_map/all_to_all | solution.py:1045
  100.1 2.1 collective-permute-start.20
  102.2 1.5 collective-permute-done.20.far_ref
  103.7 14.0 %attend.1 = (bf16[8,64,256]{2,1,0:T(8,128)(2,1)}, bf16[2048,4096]{1,0:T(8,128)(2,1)}, f32[8,8,256]{2,1,0:T(8,128)}, bf16[8,192,256]{2,1,0:T(8,128)(2,1)}, bf16[8,128,256]{2,1,0:T(8,128)(2,1)}) custom-call(s32[1]{0:T(128)S(6)} %copy.39.length_ref, s32[1]{0:T(128)} %bitcast.core_ref, bf16[8,192,256]{2,1,0:T(8,128)(2,1)S(1)} %all_to_all.45.near_ref, ...), custom_call_target="tpu_custom_call" | custom-call | flops 14000000000 | bytes 42000000 | tf_op jit(solution)/shard_map/attend/pallas_call | solution.py:135
  118.2 12.1 %all_to_all.46.o_ref = bf16[8,64,256]{2,1,0:T(8,128)(2,1)S(1)} all-to-all(bf16[8,64,256]{2,1,0:T(8,128)(2,1)} %get-tuple-element.123.o_ref), channel_id=1, replica_groups=mesh['y'=4,'xh'=2,'core'=2,'xl'=2,'z'=4] {'y','xh'}, dimensions={0} | all-to-all | bytes 524288 | tf_op jit(solution)/shard_map/all_to_all | solution.py:1050
  130.3 7.5 %ffn.1 = (bf16[256,512]{1,0:T(8,128)(2,1)}, bf16[256,5632]{1,0:T(8,128)(2,1)S(1)}, f32[256,512]{1,0:T(8,128)}, bf16[8,64,256]{2,1,0:T(8,128)(2,1)}, f32[1,512]{1,0:T(1,128)}, /*index=5*/bf16[8,64,256]{2,1,0:T(8,128)(2,1)S(1)}) custom-call(s32[6]{0:T(128)S(1)} %stack.32.info_ref, f32[256,512]{1,0:T(8,128)} %get-tuple-element.117.h2_ref.h2_in, ...), custom_call_target="tpu_custom_call" | custom-call | flops 11000000512 | bytes 33000000 | tf_op jit(solution)/shard_map/ffn/pallas_call | solution.py:271
  139.0 3.4 %all-to-all-start.4 = ((bf16[8,64,256]{2,1,0:T(8,128)(2,1)}), bf16[8,64,256]{2,1,0:T(8,128)(2,1)S(1)}, u32[]{:S(2)}, u32[]{:S(2)}) async-start(bf16[8,64,256]{2,1,0:T(8,128)(2,1)} %get-tuple-element.128), calls=%async_computation.4 | async-start | bytes 524288 | tf_op jit(solution)/shard_map/all_to_all | solution.py:1061
  142.4 1.9 collective-permute-done.23.heads2_ref
  144.3 4.8 %early.1 = bf16[2,2,4,4,144,128]{5,4,3,2,1,0:T(8,128)(2,1)} custom-call(s32[6]{0:T(128)S(1)} %stack.32.info_ref, bf16[256,5632]{1,0:T(8,128)(2,1)S(1)} %get-tuple-element.129.acts_ref, bf16[8,64,256]{2,1,0:T(8,128)(2,1)S(1)} %get-tuple-element.130.heads_ref, bf16[256,5632]{1,0:T(8,128)(2,1)} %collective-permute-done.22.acts2_ref, ...), custom_call_target="tpu_custom_call" | custom-call | flops 300000000 | bytes 900000 | tf_op jit(solution)/shard_map/early/pallas_call | solution.py:271
  149.0 1.7 all-to-all-done.4.do_ref
  150.8 19.5 %attend_back.1 = (bf16[8,192,256]{2,1,0:T(8,128)(2,1)S(1)}, bf16[8,128,256]{2,1,0:T(8,128)(2,1)S(1)}) custom-call(bf16[8,192,256]{2,1,0:T(8,128)(2,1)} %get-tuple-element.135.near_ref, bf16[8,128,256]{2,1,0:T(8,128)(2,1)} %get-tuple-element.136.far_ref, bf16[2048,4096]{1,0:T(8,128)(2,1)} %get-tuple-element.137.e_ref, ...), custom_call_target="tpu_custom_call" | custom-call | flops 3000000000 | bytes 9000000 | tf_op jit(solution)/shard_map/attend_back/pallas_call | solution.py:229
  171.6 1.5 collective-permute-done.25
  174.2 3.5 %all-to-all-start.5 = ((bf16[8,192,256]{2,1,0:T(8,128)(2,1)}), bf16[8,192,256]{2,1,0:T(8,128)(2,1)S(1)}, u32[]{:S(2)}, u32[]{:S(2)}) async-start(bf16[8,192,256]{2,1,0:T(8,128)(2,1)} %add_convert_fusion), calls=%async_computation.7 | async-start | bytes 1572864 | tf_op jit(solution)/shard_map/all_to_all | solution.py:1071
  178.3 13.6 %all-to-all-done.5.d_ref = bf16[8,192,256]{2,1,0:T(8,128)(2,1)S(1)} async-done(((bf16[8,192,256]{2,1,0:T(8,128)(2,1)}), bf16[8,192,256]{2,1,0:T(8,128)(2,1)S(1)}, u32[]{:S(2)}, u32[]{:S(2)}) %all-to-all-start.5) | async-done | bytes 786464 | tf_op jit(solution)/shard_map/all_to_all | solution.py:1071
  193.2 3.8 %attn_in.1 = (f32[256,512]{1,0:T(8,128)}, bf16[256,256]{1,0:T(8,128)(2,1)S(1)}, bf16[8,256]{1,0:T(8,128)(2,1)}, bf16[8,256]{1,0:T(8,128)(2,1)}, f32[1,512]{1,0:T(1,128)}) custom-call(s32[6]{0:T(128)S(1)} %stack.32.info_ref, bf16[8,192,256]{2,1,0:T(8,128)(2,1)S(1)} %all-to-all-done.5.d_ref, f32[256,512]{1,0:T(8,128)} %get-tuple-element.117.h2_ref.h2_in, ...), custom_call_target="tpu_custom_call" | custom-call | flops 500000000 | bytes 1500000 | tf_op jit(solution)/shard_map/attn_in/pallas_call | solution.py:271
  197.6 2.4 collective-permute-start.26
  200.0 1.9 collective-permute-start.27
  201.9 4.7 %collective-permute-done.27.hi_ref = bf16[8,256]{1,0:T(8,128)(2,1)S(1)} collective-permute-done((bf16[8,256]{1,0:T(8,128)(2,1)}, bf16[8,256]{1,0:T(8,128)(2,1)S(1)}, u32[]{:S(2)}, u32[]{:S(2)}) %collective-permute-start.27) | collective-permute-done | bytes 4128 | tf_op jit(solution)/shard_map/ppermute | solution.py:54
  206.6 3.4 %middle.1 = bf16[8,8,80,128]{3,2,1,0:T(8,128)(2,1)} custom-call(s32[6]{0:T(128)S(1)} %stack.32.info_ref, bf16[256,2048]{1,0:T(8,128)(2,1)} %get-tuple-element.133.sp_ref, bf16[256,256]{1,0:T(8,128)(2,1)S(1)} %get-tuple-element.147.gs_ref, bf16[256,512]{1,0:T(8,128)(2,1)} %get-tuple-element.118.n3_ref, bf16[8,192,256]{2,1,0:T(8,128)(2,1)S(1)} %all-to-all-done.5.d_ref, ...), custom_call_target="tpu_custom_call" | custom-call | flops 300000000 | bytes 900000 | tf_op jit(solution)/shard_map/middle/pallas_call | solution.py:271
  210.0 10.0 %all-to-all-start.6 = ((bf16[64,80,128]{2,1,0:T(8,128)(2,1)}), bf16[64,80,128]{2,1,0:T(8,128)(2,1)}, u32[]{:S(2)}, u32[]{:S(2)}) async-start(bf16[64,80,128]{2,1,0:T(8,128)(2,1)} %bitcast.44), calls=%async_computation.8 | async-start | bytes 2621440 | tf_op jit(solution)/shard_map/all_to_all | solution.py:1091
  220.0 11.2 %conv_back.1 = (bf16[256,2048]{1,0:T(8,128)(2,1)S(1)}, bf16[272,256]{1,0:T(8,128)(2,1)S(1)}, f32[16,2048]{1,0:T(8,128)S(1)}) custom-call(s32[6]{0:T(128)S(1)} %stack.32.info_ref, bf16[8,256]{1,0:T(8,128)(2,1)S(1)} %collective-permute-done.26.lo_ref, bf16[256,256]{1,0:T(8,128)(2,1)S(1)} %get-tuple-element.147.gs_ref, ...), custom_call_target="tpu_custom_call" | custom-call | flops 2000000000 | bytes 6000000 | tf_op jit(solution)/shard_map/conv_back/pallas_call | solution.py:271
  231.3 5.5 %glu_back.1 = (f32[256,512]{1,0:T(8,128)}, bf16[256,1024]{1,0:T(8,128)(2,1)S(1)}, f32[24,2048]{1,0:T(8,128)S(1)}) custom-call(s32[6]{0:T(128)S(1)} %stack.32.info_ref, bf16[256,2048]{1,0:T(8,128)(2,1)S(1)} %get-tuple-element.155.dw_ref, bf16[272,256]{1,0:T(8,128)(2,1)S(1)} %get-tuple-element.156.dnar_ref, f32[256,512]{1,0:T(8,128)} %get-tuple-element.157.h1_in, ...), custom_call_target="tpu_custom_call" | custom-call | flops 1000000000 | bytes 3000000 | tf_op jit(solution)/shard_map/glu_back/pallas_call | solution.py:271
  240.7 3.8 %late.1 = bf16[8,8,128,128]{3,2,1,0:T(8,128)(2,1)} custom-call(s32[6]{0:T(128)S(1)} %stack.32.info_ref, bf16[272,512]{1,0:T(8,128)(2,1)} %get-tuple-element.165.n2_ref, bf16[256,2048]{1,0:T(8,128)(2,1)S(1)} %get-tuple-element.155.dw_ref, bf16[272,256]{1,0:T(8,128)(2,1)S(1)} %get-tuple-element.156.dnar_ref, bf16[256,512]{1,0:T(8,128)(2,1)} %get-tuple-element.166.n1_ref, ...), custom_call_target="tpu_custom_call" | custom-call | flops 500000000 | bytes 1500000 | tf_op jit(solution)/shard_map/late/pallas_call | solution.py:271
  244.5 9.8 %all-to-all-start.7 = ((bf16[64,128,128]{2,1,0:T(8,128)(2,1)}), bf16[64,128,128]{2,1,0:T(8,128)(2,1)S(1)}, u32[]{:S(2)}, u32[]{:S(2)}) async-start(bf16[64,128,128]{2,1,0:T(8,128)(2,1)} %bitcast.43), calls=%async_computation.9 | async-start | bytes 4194304 | tf_op jit(solution)/shard_map/all_to_all | solution.py:1127
  255.5 2.6 collective-permute-start.38
  259.2 1.5 reduce_sum.24
  260.7 20.8 %collective-permute-done.37.refs_1_ = bf16[144,128]{1,0:T(8,128)(2,1)S(1)} collective-permute-done((bf16[144,128]{1,0:T(8,128)(2,1)S(1)}, bf16[144,128]{1,0:T(8,128)(2,1)S(1)}, u32[]{:S(2)}, u32[]{:S(2)}) %collective-permute-start.37) | collective-permute-done | bytes 36896 | tf_op jit(solution)/shard_map/ppermute | solution.py:54
  283.1 17.0 %all_to_all.47.near_ref = bf16[8,352,128]{2,1,0:T(8,128)(2,1)S(1)} all-to-all(bf16[8,352,128]{2,1,0:T(8,128)(2,1)S(1)} %broadcast_in_dim.14), channel_id=1, replica_groups=mesh['y'=4,'xh'=2,'core'=2,'xl'=2,'z'=4] {'y','xh'}, dimensions={0} | all-to-all | bytes 1441792 | tf_op jit(solution)/shard_map/all_to_all | solution.py:963
  300.0 2.3 collective-permute-start.40
  302.3 1.8 collective-permute-done.40.far_ref
  304.1 2.9 unpack.1
  (109 shorter events, 23.2 us)
Async XLA Ops:
  9.5 15.1 %collective-permute-start = (bf16[512,256]{1,0:T(8,128)(2,1)S(1)}, bf16[512,256]{1,0:T(8,128)(2,1)S(1)}, u32[]{:S(2)}, u32[]{:S(2)}) collective-permute-start(bf16[512,256]{1,0:T(8,128)(2,1)S(1)} %pack_ring.1.refs_0_), channel_id=1, source_target_pairs={{0,3},{1,0},{2,1},{3,2},{4,7},{5,4},{6,5},{7,6},{8,11},{9,8},{10,9... | collective-permute-start | bytes 786440 | tf_op jit(solution)/shard_map/ppermute | solution.py:54
  14.2 10.5 %collective-permute-start.1 = (bf16[512,256]{1,0:T(8,128)(2,1)S(1)}, bf16[512,256]{1,0:T(8,128)(2,1)S(1)}, u32[]{:S(2)}, u32[]{:S(2)}) collective-permute-start(bf16[512,256]{1,0:T(8,128)(2,1)S(1)} %pack_ring.1.refs_0_), channel_id=1, source_target_pairs={{0,2},{1,3},{2,0},{3,1},{4,6},{5,7},{6,4},{7,5},{8,10},{9,11},{10,... | collective-permute-start | bytes 786440 | tf_op jit(solution)/shard_map/ppermute | solution.py:54
  14.2 14.7 %collective-permute-start.2 = (bf16[512,256]{1,0:T(8,128)(2,1)S(1)}, bf16[512,256]{1,0:T(8,128)(2,1)S(1)}, u32[]{:S(2)}, u32[]{:S(2)}) collective-permute-start(bf16[512,256]{1,0:T(8,128)(2,1)S(1)} %pack_ring.1.refs_0_), channel_id=1, source_target_pairs={{0,1},{1,2},{2,3},{3,0},{4,5},{5,6},{6,7},{7,4},{8,9},{9,10},{10,1... | collective-permute-start | bytes 786440 | tf_op jit(solution)/shard_map/ppermute | solution.py:54
  14.9 14.0 %collective-permute-start.3 = (bf16[512,256]{1,0:T(8,128)(2,1)S(1)}, bf16[512,256]{1,0:T(8,128)(2,1)}, u32[]{:S(2)}, u32[]{:S(2)}) collective-permute-start(bf16[512,256]{1,0:T(8,128)(2,1)S(1)} %pack_ring.1.refs_0_), channel_id=1, source_target_pairs={{0,4},{1,5},{2,6},{3,7},{4,0},{5,1},{6,2},{7,3},{8,12},{9,13},{10,... | collective-permute-start | bytes 786440 | tf_op jit(solution)/shard_map/ppermute | solution.py:54
  28.9 26.9 %all-to-all-start = ((bf16[8,160,256]{2,1,0:T(8,128)(2,1)}), bf16[8,160,256]{2,1,0:T(8,128)(2,1)S(1)}, u32[]{:S(2)}, u32[]{:S(2)}) async-start(bf16[8,160,256]{2,1,0:T(8,128)(2,1)} %get-tuple-element.105), calls=%async_computation | async-start | bytes 1310720 | tf_op jit(solution)/shard_map/all_to_all | solution.py:1003
  32.5 14.8 %collective-permute-start.4 = (bf16[576,256]{1,0:T(8,128)(2,1)S(1)}, bf16[576,256]{1,0:T(8,128)(2,1)S(1)}, u32[]{:S(2)}, u32[]{:S(2)}) collective-permute-start(bf16[576,256]{1,0:T(8,128)(2,1)S(1)} %get-tuple-element.106), channel_id=1, source_target_pairs={{0,4},{1,5},{2,6},{3,7},{4,0},{5,1},{6,2},{7,3},{8,12},{9,13},{10,... | collective-permute-start | bytes 884744 | tf_op jit(solution)/shard_map/ppermute | solution.py:54
  33.8 21.1 %collective-permute-start.7 = (bf16[512,256]{1,0:T(8,128)(2,1)}, bf16[512,256]{1,0:T(8,128)(2,1)S(1)}, u32[]{:S(2)}, u32[]{:S(2)}) collective-permute-start(bf16[512,256]{1,0:T(8,128)(2,1)} %collective-permute-done.3.refs_4_), channel_id=1, source_target_pairs={{0,3},{1,0},{2,1},{3,2},{4,7},{5,4},{6,5},{7,6},{8,11},{9,8},{10,9... | collective-permute-start | bytes 786440 | tf_op jit(solution)/shard_map/ppermute | solution.py:54
  36.3 18.7 %collective-permute-start.8 = (bf16[512,256]{1,0:T(8,128)(2,1)}, bf16[512,256]{1,0:T(8,128)(2,1)S(1)}, u32[]{:S(2)}, u32[]{:S(2)}) collective-permute-start(bf16[512,256]{1,0:T(8,128)(2,1)} %collective-permute-done.3.refs_4_), channel_id=1, source_target_pairs={{0,2},{1,3},{2,0},{3,1},{4,6},{5,7},{6,4},{7,5},{8,10},{9,11},{10,... | collective-permute-start | bytes 786440 | tf_op jit(solution)/shard_map/ppermute | solution.py:54
  36.8 18.2 %collective-permute-start.9 = (bf16[512,256]{1,0:T(8,128)(2,1)}, bf16[512,256]{1,0:T(8,128)(2,1)S(1)}, u32[]{:S(2)}, u32[]{:S(2)}) collective-permute-start(bf16[512,256]{1,0:T(8,128)(2,1)} %collective-permute-done.3.refs_4_), channel_id=1, source_target_pairs={{0,1},{1,2},{2,3},{3,0},{4,5},{5,6},{6,7},{7,4},{8,9},{9,10},{10,1... | collective-permute-start | bytes 786440 | tf_op jit(solution)/shard_map/ppermute | solution.py:54
  37.4 14.5 %collective-permute-start.5 = (bf16[8,512]{1,0:T(8,128)(2,1)S(1)}, bf16[8,512]{1,0:T(8,128)(2,1)S(1)}, u32[]{:S(2)}, u32[]{:S(2)}) collective-permute-start(bf16[8,512]{1,0:T(8,128)(2,1)S(1)} %get-tuple-element.190), channel_id=1, source_target_pairs={{0,8},{1,9},{2,10},{3,11},{4,12},{5,13},{6,14},{7,15},{8,16},{9,17... | collective-permute-start | bytes 24584 | tf_op jit(solution)/shard_map/ppermute | solution.py:54
  47.3 7.7 %collective-permute-start.6 = (bf16[8,512]{1,0:T(8,128)(2,1)S(1)}, bf16[8,512]{1,0:T(8,128)(2,1)S(1)}, u32[]{:S(2)}, u32[]{:S(2)}) collective-permute-start(bf16[8,512]{1,0:T(8,128)(2,1)S(1)} %get-tuple-element.189), channel_id=1, source_target_pairs={{8,0},{9,1},{10,2},{11,3},{12,4},{13,5},{14,6},{15,7},{16,8},{17,9... | collective-permute-start | bytes 24584 | tf_op jit(solution)/shard_map/ppermute | solution.py:54
  55.8 7.1 %collective-permute-start.10 = (bf16[8,160,256]{2,1,0:T(8,128)(2,1)S(1)}, bf16[8,160,256]{2,1,0:T(8,128)(2,1)S(1)}, u32[]{:S(2)}, u32[]{:S(2)}) collective-permute-start(bf16[8,160,256]{2,1,0:T(8,128)(2,1)S(1)} %all-to-all-done.near_ref.refs_16_), channel_id=1, source_target_pairs={{0,8},{1,9},{2,10},{3,11},{4,12},{5,13},{6,14},{7,15},{8,0},{9,1},... | collective-permute-start | bytes 1966088 | tf_op jit(solution)/shard_map/ppermute | solution.py:54
  55.8 5.8 %collective-permute-start.11 = (bf16[512,256]{1,0:T(8,128)(2,1)S(1)}, bf16[512,256]{1,0:T(8,128)(2,1)}, u32[]{:S(2)}, u32[]{:S(2)}) collective-permute-start(bf16[512,256]{1,0:T(8,128)(2,1)S(1)} %pack_ring.1.refs_0_), channel_id=1, source_target_pairs={{0,8},{1,9},{2,10},{3,11},{4,12},{5,13},{6,14},{7,15},{8,0},{9,1},... | collective-permute-start | bytes 786440 | tf_op jit(solution)/shard_map/ppermute | solution.py:54
  56.3 6.1 %collective-permute-start.15 = (bf16[512,256]{1,0:T(8,128)(2,1)}, bf16[512,256]{1,0:T(8,128)(2,1)}, u32[]{:S(2)}, u32[]{:S(2)}) collective-permute-start(bf16[512,256]{1,0:T(8,128)(2,1)} %collective-permute-done.3.refs_4_), channel_id=1, source_target_pairs={{0,8},{1,9},{2,10},{3,11},{4,12},{5,13},{6,14},{7,15},{8,0},{9,1},... | collective-permute-start | bytes 786440 | tf_op jit(solution)/shard_map/ppermute | solution.py:54
  56.4 6.1 %collective-permute-start.12 = (bf16[512,256]{1,0:T(8,128)(2,1)S(1)}, bf16[512,256]{1,0:T(8,128)(2,1)}, u32[]{:S(2)}, u32[]{:S(2)}) collective-permute-start(bf16[512,256]{1,0:T(8,128)(2,1)S(1)} %collective-permute-done.refs_1_), channel_id=1, source_target_pairs={{0,8},{1,9},{2,10},{3,11},{4,12},{5,13},{6,14},{7,15},{8,0},{9,1},... | collective-permute-start | bytes 786440 | tf_op jit(solution)/shard_map/ppermute | solution.py:54
  56.8 8.5 %collective-permute-start.13 = (bf16[512,256]{1,0:T(8,128)(2,1)S(1)}, bf16[512,256]{1,0:T(8,128)(2,1)}, u32[]{:S(2)}, u32[]{:S(2)}) collective-permute-start(bf16[512,256]{1,0:T(8,128)(2,1)S(1)} %collective-permute-done.1.refs_2_), channel_id=1, source_target_pairs={{0,8},{1,9},{2,10},{3,11},{4,12},{5,13},{6,14},{7,15},{8,0},{9,1},... | collective-permute-start | bytes 786440 | tf_op jit(solution)/shard_map/ppermute | solution.py:54
  56.9 18.8 %all-to-all-start.1 = ((bf16[8,192,256]{2,1,0:T(8,128)(2,1)}), bf16[8,192,256]{2,1,0:T(8,128)(2,1)S(1)}, u32[]{:S(2)}, u32[]{:S(2)}) async-start(bf16[8,192,256]{2,1,0:T(8,128)(2,1)} %get-tuple-element.120), calls=%async_computation.1 | async-start | bytes 1572864 | tf_op jit(solution)/shard_map/all_to_all | solution.py:1005
  60.9 56.9 %all-gather.3.cloned.1.call-start = ((), (), s32[]{:S(2)}) async-start(), calls=%async_computation.13 | async-start | bytes 2949120 | tf_op jit(solution)/shard_map/all_gather | solution.py:1016
  61.6 3.7 %collective-permute-start.14 = (bf16[512,256]{1,0:T(8,128)(2,1)S(1)}, bf16[512,256]{1,0:T(8,128)(2,1)S(1)}, u32[]{:S(2)}, u32[]{:S(2)}) collective-permute-start(bf16[512,256]{1,0:T(8,128)(2,1)S(1)} %collective-permute-done.2.refs_3_), channel_id=1, source_target_pairs={{0,8},{1,9},{2,10},{3,11},{4,12},{5,13},{6,14},{7,15},{8,0},{9,1},... | collective-permute-start | bytes 786440 | tf_op jit(solution)/shard_map/ppermute | solution.py:54
  62.4 2.9 collective-permute-start.16
  62.5 2.8 collective-permute-start.17
  62.9 2.4 collective-permute-start.18
  75.7 2.4 collective-permute-start.19
  100.1 3.6 %collective-permute-start.20 = (bf16[8,128,256]{2,1,0:T(8,128)(2,1)S(1)}, bf16[8,128,256]{2,1,0:T(8,128)(2,1)S(1)}, u32[]{:S(2)}, u32[]{:S(2)}) collective-permute-start(bf16[8,128,256]{2,1,0:T(8,128)(2,1)S(1)} %slice.20), channel_id=1, source_target_pairs={{0,8},{1,9},{2,10},{3,11},{4,12},{5,13},{6,14},{7,15},{8,0},{9,1},... | collective-permute-start | bytes 1572872 | tf_op jit(solution)/shard_map/ppermute | solution.py:54
  117.8 12.5 %collective-permute-start.21 = (bf16[4,2,576,256]{3,2,1,0:T(8,128)(2,1)}, bf16[4,2,576,256]{3,2,1,0:T(8,128)(2,1)S(1)}, u32[]{:S(2)}, u32[]{:S(2)}) collective-permute-start(bf16[4,2,576,256]{3,2,1,0:T(8,128)(2,1)} %bitcast.48), channel_id=1, source_target_pairs={{0,8},{1,9},{2,10},{3,11},{4,12},{5,13},{6,14},{7,15},{8,0},{9,1},... | collective-permute-start | bytes 7077896 | tf_op jit(solution)/shard_map/ppermute | solution.py:54
  137.8 6.4 %collective-permute-start.22 = (bf16[256,5632]{1,0:T(8,128)(2,1)S(1)}, bf16[256,5632]{1,0:T(8,128)(2,1)}, u32[]{:S(2)}, u32[]{:S(2)}) collective-permute-start(bf16[256,5632]{1,0:T(8,128)(2,1)S(1)} %get-tuple-element.129.acts_ref), channel_id=1, source_target_pairs={{0,8},{1,9},{2,10},{3,11},{4,12},{5,13},{6,14},{7,15},{8,0},{9,1},... | collective-permute-start | bytes 8650760 | tf_op jit(solution)/shard_map/ppermute | solution.py:54
  138.9 5.4 %collective-permute-start.23 = (bf16[8,64,256]{2,1,0:T(8,128)(2,1)S(1)}, bf16[8,64,256]{2,1,0:T(8,128)(2,1)}, u32[]{:S(2)}, u32[]{:S(2)}) collective-permute-start(bf16[8,64,256]{2,1,0:T(8,128)(2,1)S(1)} %get-tuple-element.130.heads_ref), channel_id=1, source_target_pairs={{0,8},{1,9},{2,10},{3,11},{4,12},{5,13},{6,14},{7,15},{8,0},{9,1},... | collective-permute-start | bytes 786440 | tf_op jit(solution)/shard_map/ppermute | solution.py:54
  139.0 11.8 %all-to-all-start.4 = ((bf16[8,64,256]{2,1,0:T(8,128)(2,1)}), bf16[8,64,256]{2,1,0:T(8,128)(2,1)S(1)}, u32[]{:S(2)}, u32[]{:S(2)}) async-start(bf16[8,64,256]{2,1,0:T(8,128)(2,1)} %get-tuple-element.128), calls=%async_computation.4 | async-start | bytes 524288 | tf_op jit(solution)/shard_map/all_to_all | solution.py:1061
  142.4 50.7 %reduce-scatter.3.cloned.1.call-start = ((), (), s32[]{:S(2)}) async-start(), calls=%async_computation.11 | async-start | bytes 2949120 | tf_op jit(solution)/shard_map/reduce_scatter | solution.py:954
  170.3 2.9 collective-permute-start.25
  174.2 17.6 %all-to-all-start.5 = ((bf16[8,192,256]{2,1,0:T(8,128)(2,1)}), bf16[8,192,256]{2,1,0:T(8,128)(2,1)S(1)}, u32[]{:S(2)}, u32[]{:S(2)}) async-start(bf16[8,192,256]{2,1,0:T(8,128)(2,1)} %add_convert_fusion), calls=%async_computation.7 | async-start | bytes 1572864 | tf_op jit(solution)/shard_map/all_to_all | solution.py:1071
  177.8 53.5 %reduce-scatter.5.cloned.1.call-start = ((), (), s32[]{:S(2)}) async-start(), calls=%async_computation.12 | async-start | bytes 737280 | tf_op jit(solution)/shard_map/reduce_scatter | solution.py:958
  177.8 15.4 %collective-permute-start.24 = (bf16[256,2048]{1,0:T(8,128)(2,1)}, bf16[256,2048]{1,0:T(8,128)(2,1)S(1)}, u32[]{:S(2)}, u32[]{:S(2)}) collective-permute-start(bf16[256,2048]{1,0:T(8,128)(2,1)} %get-tuple-element.133.sp_ref), channel_id=1, source_target_pairs={{0,8},{1,9},{2,10},{3,11},{4,12},{5,13},{6,14},{7,15},{8,0},{9,1},... | collective-permute-start | bytes 3145736 | tf_op jit(solution)/shard_map/ppermute | solution.py:54
  191.8 14.8 %collective-permute-start.30 = (bf16[8,192,256]{2,1,0:T(8,128)(2,1)S(1)}, bf16[8,192,256]{2,1,0:T(8,128)(2,1)S(1)}, u32[]{:S(2)}, u32[]{:S(2)}) collective-permute-start(bf16[8,192,256]{2,1,0:T(8,128)(2,1)S(1)} %all-to-all-done.5.d_ref), channel_id=1, source_target_pairs={{0,8},{1,9},{2,10},{3,11},{4,12},{5,13},{6,14},{7,15},{8,0},{9,1},... | collective-permute-start | bytes 2359304 | tf_op jit(solution)/shard_map/ppermute | solution.py:54
  193.1 13.5 %collective-permute-start.29 = (bf16[256,512]{1,0:T(8,128)(2,1)S(1)}, bf16[256,512]{1,0:T(8,128)(2,1)S(1)}, u32[]{:S(2)}, u32[]{:S(2)}) collective-permute-start(bf16[256,512]{1,0:T(8,128)(2,1)S(1)} %copy-done.9), channel_id=1, source_target_pairs={{0,8},{1,9},{2,10},{3,11},{4,12},{5,13},{6,14},{7,15},{8,0},{9,1},... | collective-permute-start | bytes 786440 | tf_op jit(solution)/shard_map/ppermute | solution.py:54
  197.0 9.6 %collective-permute-start.28 = (bf16[256,256]{1,0:T(8,128)(2,1)S(1)}, bf16[256,256]{1,0:T(8,128)(2,1)S(1)}, u32[]{:S(2)}, u32[]{:S(2)}) collective-permute-start(bf16[256,256]{1,0:T(8,128)(2,1)S(1)} %get-tuple-element.147.gs_ref), channel_id=1, source_target_pairs={{0,8},{1,9},{2,10},{3,11},{4,12},{5,13},{6,14},{7,15},{8,0},{9,1},... | collective-permute-start | bytes 393224 | tf_op jit(solution)/shard_map/ppermute | solution.py:54
  197.6 4.3 %collective-permute-start.26 = (bf16[8,256]{1,0:T(8,128)(2,1)}, bf16[8,256]{1,0:T(8,128)(2,1)S(1)}, u32[]{:S(2)}, u32[]{:S(2)}) collective-permute-start(bf16[8,256]{1,0:T(8,128)(2,1)} %get-tuple-element.144), channel_id=1, source_target_pairs={{0,8},{1,9},{2,10},{3,11},{4,12},{5,13},{6,14},{7,15},{8,16},{9,17... | collective-permute-start | bytes 12296 | tf_op jit(solution)/shard_map/ppermute | solution.py:54
  200.0 6.6 %collective-permute-start.27 = (bf16[8,256]{1,0:T(8,128)(2,1)}, bf16[8,256]{1,0:T(8,128)(2,1)S(1)}, u32[]{:S(2)}, u32[]{:S(2)}) collective-permute-start(bf16[8,256]{1,0:T(8,128)(2,1)} %get-tuple-element.145), channel_id=1, source_target_pairs={{8,0},{9,1},{10,2},{11,3},{12,4},{13,5},{14,6},{15,7},{16,8},{17,9... | collective-permute-start | bytes 12296 | tf_op jit(solution)/shard_map/ppermute | solution.py:54
  210.0 34.5 %all-to-all-start.6 = ((bf16[64,80,128]{2,1,0:T(8,128)(2,1)}), bf16[64,80,128]{2,1,0:T(8,128)(2,1)}, u32[]{:S(2)}, u32[]{:S(2)}) async-start(bf16[64,80,128]{2,1,0:T(8,128)(2,1)} %bitcast.44), calls=%async_computation.8 | async-start | bytes 2621440 | tf_op jit(solution)/shard_map/all_to_all | solution.py:1091
  231.2 9.5 %collective-permute-start.32 = (bf16[256,2048]{1,0:T(8,128)(2,1)S(1)}, bf16[256,2048]{1,0:T(8,128)(2,1)S(1)}, u32[]{:S(2)}, u32[]{:S(2)}) collective-permute-start(bf16[256,2048]{1,0:T(8,128)(2,1)S(1)} %get-tuple-element.155.dw_ref), channel_id=1, source_target_pairs={{0,8},{1,9},{2,10},{3,11},{4,12},{5,13},{6,14},{7,15},{8,0},{9,1},... | collective-permute-start | bytes 3145736 | tf_op jit(solution)/shard_map/ppermute | solution.py:54
  236.8 3.8 %collective-permute-start.35 = (bf16[256,1024]{1,0:T(8,128)(2,1)S(1)}, bf16[256,1024]{1,0:T(8,128)(2,1)S(1)}, u32[]{:S(2)}, u32[]{:S(2)}) collective-permute-start(bf16[256,1024]{1,0:T(8,128)(2,1)S(1)} %get-tuple-element.167.dab_ref), channel_id=1, source_target_pairs={{0,8},{1,9},{2,10},{3,11},{4,12},{5,13},{6,14},{7,15},{8,0},{9,1},... | collective-permute-start | bytes 1572872 | tf_op jit(solution)/shard_map/ppermute | solution.py:54
  237.5 2.2 collective-permute-start.31
  237.9 2.8 collective-permute-start.36
  244.5 38.1 %all-to-all-start.7 = ((bf16[64,128,128]{2,1,0:T(8,128)(2,1)}), bf16[64,128,128]{2,1,0:T(8,128)(2,1)S(1)}, u32[]{:S(2)}, u32[]{:S(2)}) async-start(bf16[64,128,128]{2,1,0:T(8,128)(2,1)} %bitcast.43), calls=%async_computation.9 | async-start | bytes 4194304 | tf_op jit(solution)/shard_map/all_to_all | solution.py:1127
  254.4 27.1 %collective-permute-start.37 = (bf16[144,128]{1,0:T(8,128)(2,1)S(1)}, bf16[144,128]{1,0:T(8,128)(2,1)S(1)}, u32[]{:S(2)}, u32[]{:S(2)}) collective-permute-start(bf16[144,128]{1,0:T(8,128)(2,1)S(1)} %get-tuple-element.193), channel_id=1, source_target_pairs={{0,32},{1,33},{2,34},{3,35},{4,36},{5,37},{6,38},{7,39},{8,40},{9,... | collective-permute-start | bytes 110600 | tf_op jit(solution)/shard_map/ppermute | solution.py:54
  255.5 26.0 %collective-permute-start.38 = (bf16[144,128]{1,0:T(8,128)(2,1)S(1)}, bf16[144,128]{1,0:T(8,128)(2,1)S(1)}, u32[]{:S(2)}, u32[]{:S(2)}) collective-permute-start(bf16[144,128]{1,0:T(8,128)(2,1)S(1)} %get-tuple-element.192), channel_id=1, source_target_pairs={{0,64},{1,65},{2,66},{3,67},{4,68},{5,69},{6,70},{7,71},{8,72},{9,... | collective-permute-start | bytes 110600 | tf_op jit(solution)/shard_map/ppermute | solution.py:54
  258.1 23.4 %collective-permute-start.39 = (bf16[144,128]{1,0:T(8,128)(2,1)S(1)}, bf16[144,128]{1,0:T(8,128)(2,1)S(1)}, u32[]{:S(2)}, u32[]{:S(2)}) collective-permute-start(bf16[144,128]{1,0:T(8,128)(2,1)S(1)} %get-tuple-element.191), channel_id=1, source_target_pairs={{0,96},{1,97},{2,98},{3,99},{4,100},{5,101},{6,102},{7,103},{8,104... | collective-permute-start | bytes 110600 | tf_op jit(solution)/shard_map/ppermute | solution.py:54
  300.0 4.1 %collective-permute-start.40 = (bf16[8,352,128]{2,1,0:T(8,128)(2,1)S(1)}, bf16[8,352,128]{2,1,0:T(8,128)(2,1)S(1)}, u32[]{:S(2)}, u32[]{:S(2)}) collective-permute-start(bf16[8,352,128]{2,1,0:T(8,128)(2,1)S(1)} %all_to_all.47.near_ref), channel_id=1, source_target_pairs={{0,8},{1,9},{2,10},{3,11},{4,12},{5,13},{6,14},{7,15},{8,0},{9,1},... | collective-permute-start | bytes 2162696 | tf_op jit(solution)/shard_map/ppermute | solution.py:54
  (14 other events, 84.7 us)
Sparse Core Ops, SparseCore 0:
  63.4 34.7 all-gather.2
  150.9 30.0 reduce-scatter.2
  193.2 17.2 reduce-scatter.4
